TPU v7x, 512 devices: a whole 4x8x8 slice. The times are simulated.
512 devices in a mesh: region: 16 (over z, core), row: 32 (over x, y).
Axes of the slice: x: 4, y: 8, z: 8, core: 2. Of those that a mesh axis runs over, the one named last changes fastest.
Arguments:
- queries: float32 [64, 512], P('row'), may hold values from -6 to 6
- descriptors: float32 [131072, 512], P(('region', 'row')), may hold values from -6 to 6
- candidates: int32 [64, 64], replicated, may hold values from 0 to 1023
- cluster_perm: int32 [16, 8192], P('region', 'row'), may hold values from 0 to 8191, each once within a row
- tile_vals: float32 [6144, 128, 128], P(('region', 'row')), may hold values from 0 to 1, as said below
- tile_row: int32 [6144], P(('region', 'row')), may hold values from 0 to 1, as said below
- tile_col: int32 [6144], P(('region', 'row')), may hold values from 0 to 67, as said below
Outputs:
- diffused: float32 [64, 131072], P(None, ('region', 'row'))
- residual: float32 [64, 131072], P(None, ('region', 'row'))
Inputs may be any that keep to these rules, and one draw needn't show every extreme that they name: Each row of cluster_perm names every storage position of its region once. tile_row is a row tile of the owning device. In device (region r, row index i) the first 2 tiles are its diagonal tiles in order; the intra-region column tiles lie on row indices i, i + 1, i - 1, i + 3, i - 3, i + 8, i - 8 and i + 32 // 2 (modulo 32). `tile_col`: every device holds tiles with column slots in both neighbouring regions. `tile_vals`: S is symmetric with nonnegative entries and every row of S sums to at most 1.
All inputs are finite; a program needn't handle non-finite values.
Results may differ from a plain program's by a relative error of at most 0.0003.
Values sent between devices are 32-bit elements; how exact they have to be, the bound alone decides.
No kernel may reach another device: no remote copies, remote signals or barrier semaphores. Data moves between devices by JAX's collectives and lax.ppermute only.
A program may use at most 64 MiB of HBM per device.

v0:
```python
import jax
import jax.numpy as jnp
from jax import lax
from jax.sharding import PartitionSpec as P

ITERS = 3


def with_halo(block, sides, width):
    for axis, dim in sides:
        count = lax.axis_size(axis)
        forward = [(i, i + 1) for i in range(count - 1)]
        forward.append((count - 1, 0))
        backward = [(target, source) for source, target in forward]
        low = lax.ppermute(
            lax.slice_in_dim(block, block.shape[dim] - width, None, axis=dim), axis, forward
        )
        high = lax.ppermute(lax.slice_in_dim(block, 0, width, axis=dim), axis, backward)
        block = jnp.concatenate([low, block, high], axis=dim)
    return block


def apply_operator(direction, tile_vals, tile_row, tile_col):
    tile_size = tile_vals.shape[1]
    query_count = direction.shape[0]
    row_count = direction.shape[1]
    per_device = row_count // tile_size
    faces = with_halo(direction[None], (("region", 0),), 1)
    lower_face = faces[0]
    upper_face = faces[2]
    region_field = lax.all_gather(direction, "row", axis=1, tiled=True)
    joined = jnp.concatenate([region_field, lower_face, upper_face], axis=1)
    slots = joined.reshape(query_count, -1, tile_size).transpose(1, 0, 2)
    picked = slots[tile_col]
    products = jnp.einsum("tqc,trc->tqr", picked, tile_vals, precision=lax.Precision.HIGHEST)
    selector = (tile_row[None, :] == jnp.arange(per_device, dtype=jnp.int32)[:, None]).astype(
        jnp.float32
    )
    summed = jnp.einsum("at,tqr->qar", selector, products, precision=lax.Precision.HIGHEST).reshape(
        query_count, row_count
    )
    return direction - 0.9 * summed


def square_sum(residual):
    return lax.psum(jnp.sum(residual * residual, axis=1), ("region", "row"))


def local(queries, descriptors, candidates, cluster_perm, tile_vals, tile_row, tile_col):
    tile_size = tile_vals.shape[1]
    row_count = descriptors.shape[0]
    feature_width = descriptors.shape[1]
    per_device = row_count // tile_size
    n_row = lax.axis_size("row")
    device_id = lax.axis_index("region") * n_row + lax.axis_index("row")
    all_queries = lax.all_gather(queries, "row", axis=0, tiled=True)
    scores = lax.dot_general(
        all_queries,
        descriptors,
        (((1,), (1,)), ((), ())),
        precision=lax.Precision.HIGHEST,
        preferred_element_type=jnp.float32,
    ) * (1.0 / jnp.sqrt(jnp.float32(feature_width)))
    own_blocks = device_id * per_device + jnp.arange(per_device, dtype=jnp.int32)
    member = jnp.any(candidates[:, :, None] == own_blocks[None, None, :], axis=1)
    member_rows = jnp.repeat(member, tile_size, axis=1)
    stored = jnp.where(member_rows, jnp.exp(scores), jnp.float32(0.0))
    region_scores = lax.all_gather(stored, "row", axis=1, tiled=True)
    seeds = jnp.take(region_scores, cluster_perm[0], axis=1)
    diffused = jnp.zeros_like(seeds)
    residual = seeds
    direction = seeds
    norm_now = square_sum(residual)
    for step in range(ITERS):
        image = apply_operator(direction, tile_vals, tile_row, tile_col)
        curve = lax.psum(jnp.sum(direction * image, axis=1), ("region", "row"))
        alpha = norm_now / curve
        diffused = diffused + alpha[:, None] * direction
        residual = residual - alpha[:, None] * image
        if step + 1 < ITERS:
            norm_next = square_sum(residual)
            direction = residual + (norm_next / norm_now)[:, None] * direction
            norm_now = norm_next
    return (diffused, residual)


def solution(mesh):
    in_specs = (
        P("row", None),
        P(("region", "row"), None),
        P(),
        P("region", "row"),
        P(("region", "row"), None, None),
        P(("region", "row")),
        P(("region", "row")),
    )
    out_specs = (P(None, ("region", "row")), P(None, ("region", "row")))
    return jax.shard_map(local, mesh=mesh, in_specs=in_specs, out_specs=out_specs, check_vma=False)
```

profile of v0, /device:TPU:1, one launch (start us, length us, event | category | flops | bytes accessed | tf_op | source)
XLA Modules:
  0.0 883.6 jit_solution(5404740575829851799)
XLA Ops:
  7.2 1.0 compare_reduce_fusion
  8.2 0.1 copy.82
  8.4 32.4 %all-gather = f32[32,2,512]{2,1,0:T(2,128)S(1)} all-gather(f32[1,2,512]{2,1,0:T(2,128)} %bitcast.164), channel_id=1, replica_groups=mesh['region'=16,'row'=32] {'row'}, dimensions={0}, use_global_device_ids=true | all-gather | bytes 135168 | tf_op jit(solution)/shard_map/all_gather | solution.py:56
  40.8 0.1 broadcast_in_dim.27
  41.0 2.3 fusion.1
  43.3 0.7 compare_select_fusion
  44.0 0.7 compare_and_fusion.1
  44.7 85.5 %all-gather.6.cloned.1.call-done = f32[64,8192]{1,0:T(8,128)} async-done(((f32[64,256]{1,0:T(8,128)}), f32[64,8192]{1,0:T(8,128)}) %all-gather.6.cloned.1.call-update) | async-done | bytes 2097168 | tf_op jit(solution)/shard_map/all_gather | solution.py:68
  130.2 3.8 copy.83
  134.0 2.9 gather_fusion
  137.0 0.7 multiply_reduce_fusion.4
  137.9 4.8 collective-permute-start
  142.7 1.3 collective-permute-done
  144.0 2.4 collective-permute-done.1
  146.4 71.2 %all-gather.8.cloned.1.call-done = f32[64,8192]{1,0:T(8,128)} async-done(((f32[64,256]{1,0:T(8,128)}), f32[64,8192]{1,0:T(8,128)}) %all-gather.8.cloned.1.call-update) | async-done | bytes 2097168 | tf_op jit(solution)/shard_map/all_gather | solution.py:31
  217.6 1.9 bitcast_bitcast_fusion.2
  219.5 1.3 gather_fusion.1
  220.9 2.6 fusion.29
  223.5 0.6 fusion.6
  224.2 101.1 %all-reduce = (f32[64]{0:T(128)S(1)}, f32[64]{0:T(128)S(1)}) all-reduce(f32[64]{0:T(128)S(1)} %get-tuple-element.16, f32[64]{0:T(128)S(1)} %multiply_reduce_fusion.3), channel_id=1, replica_groups=mesh['region'=16,'row'=32] {'region','row'}, use_global_device_ids=true, to_apply=%region_2.3 | all-reduce | flops 128 | bytes 1024 | tf_op jit(solution)/shard_map/psum | solution.py:46
  325.3 0.2 multiply_reduce_fusion.2
  325.5 94.4 %psum.44 = f32[64]{0:T(128)S(1)} all-reduce(f32[64]{0:T(128)S(1)} %multiply_reduce_fusion.2), channel_id=1, replica_groups=mesh['region'=16,'row'=32] {'region','row'}, use_global_device_ids=true, to_apply=%region_6.7 | all-reduce | flops 64 | bytes 512 | tf_op jit(solution)/shard_map/psum | solution.py:46
  419.9 0.7 multiply_add_fusion.4
  421.0 1.2 collective-permute-start.2
  422.1 1.3 collective-permute-done.2
  423.5 2.7 collective-permute-done.3
  426.1 66.5 %all-gather.10.cloned.1.call-done = f32[64,8192]{1,0:T(8,128)} async-done(((f32[64,256]{1,0:T(8,128)}), f32[64,8192]{1,0:T(8,128)}) %all-gather.10.cloned.1.call-update) | async-done | bytes 2097168 | tf_op jit(solution)/shard_map/all_gather | solution.py:31
  492.6 1.9 bitcast_bitcast_fusion.1
  494.5 1.3 gather_fusion.2
  495.9 2.6 fusion.30
  498.5 0.6 fusion.4
  499.1 0.2 multiply_reduce_fusion.1
  499.3 101.1 %psum.45 = f32[64]{0:T(128)S(1)} all-reduce(f32[64]{0:T(128)S(1)} %multiply_reduce_fusion.1), channel_id=1, replica_groups=mesh['region'=16,'row'=32] {'region','row'}, use_global_device_ids=true, to_apply=%region_8.9 | all-reduce | flops 64 | bytes 512 | tf_op jit(solution)/shard_map/psum | solution.py:76
  600.4 0.2 multiply_reduce_fusion
  600.6 94.4 %psum.46 = f32[64]{0:T(128)S(1)} all-reduce(f32[64]{0:T(128)S(1)} %multiply_reduce_fusion), channel_id=1, replica_groups=mesh['region'=16,'row'=32] {'region','row'}, use_global_device_ids=true, to_apply=%region_10.11 | all-reduce | flops 64 | bytes 512 | tf_op jit(solution)/shard_map/psum | solution.py:46
  695.0 0.6 copy-done.13
  695.6 0.7 multiply_add_fusion.2
  696.6 1.2 collective-permute-start.4
  697.7 1.3 collective-permute-done.4
  699.1 2.7 collective-permute-done.5
  701.7 66.6 %all-gather.12.cloned.1.call-done = f32[64,8192]{1,0:T(8,128)} async-done(((f32[64,256]{1,0:T(8,128)}), f32[64,8192]{1,0:T(8,128)}) %all-gather.12.cloned.1.call-update) | async-done | bytes 2097168 | tf_op jit(solution)/shard_map/all_gather | solution.py:31
  768.3 1.9 bitcast_bitcast_fusion
  770.2 1.6 gather_fusion.3
  771.8 2.6 fusion.31
  774.4 0.6 fusion.2
  775.0 0.2 fusion.8
  775.2 101.1 %psum.47 = f32[64]{0:T(128)S(1)} all-reduce(f32[64]{0:T(128)S(1)} %fusion.8), channel_id=1, replica_groups=mesh['region'=16,'row'=32] {'region','row'}, use_global_device_ids=true, to_apply=%region_12.13 | all-reduce | flops 64 | bytes 512 | tf_op jit(solution)/shard_map/psum | solution.py:76
  876.4 0.8 fusion.10
  (62 shorter events, 1.1 us)
Async XLA Ops:
  7.2 213.7 %copy-start = (f32[12,128,128]{2,1,0:T(8,128)S(1)}, f32[12,128,128]{2,1,0:T(8,128)}, u32[]{:S(2)}) copy-start(f32[12,128,128]{2,1,0:T(8,128)} %param.11) | copy-start | bytes 2359300
  7.2 123.1 %all-gather.6.cloned.1.call-start = ((), (), s32[]{:S(2)}) async-start(), calls=%async_computation | async-start | bytes 2162688 | tf_op jit(solution)/shard_map/all_gather | solution.py:68
  43.3 174.3 %all-gather.8.cloned.1.call-start = ((), (), s32[]{:S(2)}) async-start(), calls=%async_computation.1 | async-start | bytes 2162688 | tf_op jit(solution)/shard_map/all_gather | solution.py:31
  44.7 376.1 %copy-start.4 = (pred[256]{0:T(512)(128)(4,1)}, pred[256]{0:T(512)(128)(4,1)S(1)}, u32[]{:S(2)}) copy-start(pred[256]{0:T(512)(128)(4,1)S(1)} %compare_and_fusion.1) | copy-start | bytes 772
  44.7 93.1 %copy-start.12 = (s32[12]{0:T(128)S(1)}, s32[12]{0:T(128)}, u32[]{:S(2)}) copy-start(s32[12]{0:T(128)} %param.13) | copy-start | bytes 148
  44.7 93.1 %copy-start.11 = (s32[1,256]{1,0:T(1,128)S(1)}, s32[1,256]{1,0:T(1,128)}, u32[]{:S(2)}) copy-start(s32[1,256]{1,0:T(1,128)} %param.10) | copy-start | bytes 3076
  137.8 354.8 %all-gather.10.cloned.1.call-start = ((), (), s32[]{:S(2)}) async-start(), calls=%async_computation.2 | async-start | bytes 2162688 | tf_op jit(solution)/shard_map/all_gather | solution.py:31
  137.9 6.1 collective-permute-start
  142.7 3.7 collective-permute-start.1
  142.7 351.8 %copy-start.6 = (s32[1024]{0:T(1024)}, s32[1024]{0:T(1024)S(1)}, u32[]{:S(2)}) copy-start(s32[1024]{0:T(1024)S(1)} %pad_clamp_fusion) | copy-start | bytes 12292
  219.5 4.0 copy-start.9
  219.5 200.4 %copy-start.1 = (f32[64,256]{1,0:T(8,128)S(1)}, f32[64,256]{1,0:T(8,128)}, u32[]{:S(2)}) copy-start(f32[64,256]{1,0:T(8,128)} %get-tuple-element.17) | copy-start | bytes 196612
  420.7 347.6 %all-gather.12.cloned.1.call-start = ((), (), s32[]{:S(2)}) async-start(), calls=%async_computation.3 | async-start | bytes 2162688 | tf_op jit(solution)/shard_map/all_gather | solution.py:31
  421.0 2.5 collective-permute-start.2
  422.1 4.0 collective-permute-start.3
  494.5 201.1 %copy-start.2 = (f32[64,256]{1,0:T(8,128)S(1)}, f32[64,256]{1,0:T(8,128)}, u32[]{:S(2)}) copy-start(f32[64,256]{1,0:T(8,128)} %multiply_add_fusion.4) | copy-start | bytes 196612
  495.9 200.6 %copy-start.5 = (pred[256]{0:T(512)(128)(4,1)S(1)}, pred[256]{0:T(512)(128)(4,1)}, u32[]{:S(2)}) copy-start(pred[256]{0:T(512)(128)(4,1)} %copy-done.4) | copy-start | bytes 772
  695.0 0.6 copy-start.13
  695.6 72.7 %copy-start.7 = (f32[64]{0:T(128)}, f32[64]{0:T(128)S(1)}, u32[]{:S(2)}) copy-start(f32[64]{0:T(128)S(1)} %div.18) | copy-start | bytes 772
  696.6 2.5 collective-permute-start.4
  697.7 4.0 collective-permute-start.5
  770.2 4.3 copy-start.10
  770.2 4.9 copy-start.8
  770.2 106.2 %copy-start.14 = (f32[64]{0:T(128)S(1)}, f32[64]{0:T(128)}, u32[]{:S(2)}) copy-start(f32[64]{0:T(128)} %copy-done.13) | copy-start | bytes 772
  770.2 106.2 %copy-start.3 = (f32[64,256]{1,0:T(8,128)S(1)}, f32[64,256]{1,0:T(8,128)}, u32[]{:S(2)}) copy-start(f32[64,256]{1,0:T(8,128)} %get-tuple-element.14) | copy-start | bytes 196612
Sparse Core Ops, SparseCore 0:
  43.4 86.7 all-gather.5
  137.9 79.6 all-gather.7
  420.8 71.7 all-gather.9
  696.4 71.7 all-gather.11
where the time goes:
time: 884 us
  blocking collectives  524 us (59%)
  waiting for transfers between devices  302 us (34%)
  between operations  14.1 us (2%)
  local copies, waits for them, and re-layouts  12.2 us (1%)
  other arithmetic  12.1 us (1%)
  matrix products  12 us (1%)
    psum x3, blocking collectives, square_sum(): return lax.psum(jnp.sum(residual * residual, axis=1), ('region', 'row'))  290 us
    all_gather x3, waiting for transfers between devices, apply_operator(): region_field = lax.all_gather(direction, 'row', axis=1, tiled=True)  204 us
    psum x2, blocking collectives, local(): curve = lax.psum(jnp.sum(direction * image, axis=1), ('region', 'row'))  202 us
    all_gather x1, waiting for transfers between devices, local(): region_scores = lax.all_gather(stored, 'row', axis=1, tiled=True)  85.5 us
    all_gather x1, blocking collectives, local(): all_queries = lax.all_gather(queries, 'row', axis=0, tiled=True)  32.4 us
  transfers between devices with their start and end apart: 10, of which 10 were waited for; matrix products, arithmetic and copies ran while one was open for 0% of the time, Pallas kernels for 0%

commit v1 on v0

v1 whole, which is shorter than its diff:
```python
import functools

import jax
import jax.numpy as jnp
from jax import lax
from jax.experimental import pallas as pl
from jax.experimental.pallas import tpu as pltpu
from jax.sharding import PartitionSpec as P

Q = 64
D = 512
TILE = 128
HALF = 2
ROWS = TILE * HALF
N_ROW = 32
N_REGION = 16
QS = Q // N_ROW
HOPS = (0, 1, -1, 3, -3, 8, -8, 16)
SLOTS = len(HOPS) + 2
HIGHEST = lax.Precision.HIGHEST
F32 = jnp.float32
TAU = 1.0 / 0.9


def ring(count, hop):
    return [(i, (i + hop) % count) for i in range(count)]


def scores_kernel(dev_ref, queries_ref, desc_ref, cand_ref, out_ref):
    scores = lax.dot_general(
        queries_ref[...], desc_ref[...], (((1,), (1,)), ((), ())),
        precision=HIGHEST, preferred_element_type=F32,
    ) * (1.0 / (D ** 0.5))
    stored = jnp.exp(scores)
    cand = cand_ref[...]
    for h in range(HALF):
        hit = jnp.where(cand == dev_ref[0] * HALF + h, 1.0, 0.0)
        member = jnp.max(hit, axis=1, keepdims=True) > 0.5
        out_ref[:, h * TILE:(h + 1) * TILE] = jnp.where(member, stored[:, h * TILE:(h + 1) * TILE], 0.0)


def permute_kernel(table_ref, perm_ref, out_ref, graph_ref):
    rows = N_ROW * HALF
    perm = perm_ref[...].astype(jnp.int32)
    groups = rows // 8
    low = [perm[g * 8:(g + 1) * 8] & (TILE - 1) for g in range(groups)]
    high = [perm[g * 8:(g + 1) * 8] >> 7 for g in range(groups)]

    def body(sender, acc):
        block = table_ref[sender]
        acc = [list(a) for a in acc]
        for h in range(HALF):
            hits = [high[g] == sender * HALF + h for g in range(groups)]
            for q in range(QS):
                line = jnp.broadcast_to(block[q * HALF + h][None, :], (8, TILE))
                for g in range(groups):
                    got = jnp.take_along_axis(line, low[g], axis=1)
                    acc[q][g] = jnp.where(hits[g], got, acc[q][g])
        return tuple(tuple(a) for a in acc)

    zero = tuple(tuple(jnp.zeros((8, TILE), F32) for _ in range(groups)) for _ in range(QS))
    acc = lax.fori_loop(0, N_ROW, body, zero)
    for q in range(QS):
        for g in range(groups):
            graph_ref[q, g * 8:(g + 1) * 8, :] = acc[q][g]
    width = len(HOPS) * QS * HALF
    for q in range(QS):
        for h in range(HALF):
            mine = graph_ref[q, pl.ds(h, N_ROW, stride=HALF), :]
            for k, hop in enumerate(HOPS):
                hop = hop % N_ROW
                rolled = mine if hop == 0 else jnp.concatenate([mine[hop:], mine[:hop]], axis=0)
                out_ref[pl.ds((k * QS + q) * HALF + h, N_ROW, stride=width), :] = rolled


def tile_slot(col, row_index):
    owner = col >> 1
    hop = (owner - row_index) & (N_ROW - 1)
    slot = jnp.int32(0)
    for k, h in enumerate(HOPS):
        slot = jnp.where(hop == h % N_ROW, k, slot)
    slot = slot * HALF + (col & 1)
    return jnp.where(col >= N_ROW * HALF, col - N_ROW * HALF + len(HOPS) * HALF, slot)


def multiply(place_ref, row_ref, col_ref, tiles_ref, slots_ref, acc_ref):
    acc_ref[...] = jnp.zeros_like(acc_ref)
    for t in range(tiles_ref.shape[0]):
        slot = tile_slot(col_ref[t], place_ref[0])
        part = lax.dot_general(
            slots_ref[slot], tiles_ref[t], (((1,), (1,)), ((), ())),
            precision=HIGHEST, preferred_element_type=F32,
        )
        acc_ref[row_ref[t]] += part


def spread(slots_ref, k, block_ref):
    for h in range(HALF):
        slots_ref[k * HALF + h] = block_ref[:, h * TILE:(h + 1) * TILE]


def first_kernel(place_ref, row_ref, col_ref, near_ref, low_ref, high_ref, tiles_ref, out_ref, slots_ref, acc_ref):
    width = len(HOPS) * QS * HALF
    for k in range(len(HOPS)):
        for h in range(HALF):
            for q in range(QS):
                slots_ref[k * HALF + h, q * N_ROW:(q + 1) * N_ROW, :] = near_ref[
                    pl.ds((k * QS + q) * HALF + h, N_ROW, stride=width), :]
    spread(slots_ref, len(HOPS), low_ref)
    spread(slots_ref, len(HOPS) + 1, high_ref)
    multiply(place_ref, row_ref, col_ref, tiles_ref, slots_ref, acc_ref)
    for h in range(HALF):
        out_ref[:, h * TILE:(h + 1) * TILE] = acc_ref[h]


def next_kernel(place_ref, row_ref, col_ref, *refs):
    blocks, (tiles_ref, out_ref, slots_ref, acc_ref) = refs[:SLOTS], refs[SLOTS:]
    for k, block in enumerate(blocks):
        spread(slots_ref, k, block)
    multiply(place_ref, row_ref, col_ref, tiles_ref, slots_ref, acc_ref)
    for h in range(HALF):
        out_ref[:, h * TILE:(h + 1) * TILE] = acc_ref[h]


def last_kernel(place_ref, row_ref, col_ref, *refs):
    blocks = refs[:SLOTS]
    v0_ref, v1_ref, tiles_ref, out_ref, moments_ref, slots_ref, acc_ref = refs[SLOTS:]
    next_kernel(place_ref, row_ref, col_ref, *blocks, tiles_ref, out_ref, slots_ref, acc_ref)
    vs = [v0_ref[...], v1_ref[...], blocks[0][...], out_ref[...]]
    lane = lax.broadcasted_iota(jnp.int32, (Q, TILE), 1)
    packed = [jnp.zeros((Q, TILE), F32), jnp.zeros((Q, TILE), F32)]
    for m in range(6):
        prod = vs[m // 2] * vs[(m + 1) // 2]
        total = jnp.sum(prod[:, :TILE] + prod[:, TILE:], axis=1, keepdims=True)
        packed[m % 2] = jnp.where(lane == m // 2, total, packed[m % 2])
    moments_ref[...] = jnp.concatenate(packed, axis=0).T[:4]


def finish_kernel(moments_ref, v0_ref, v1_ref, v2_ref, v3_ref, diffused_ref, residual_ref):
    parts = [moments_ref[r] for r in range(N_REGION)]
    while len(parts) > 1:
        parts = [a + b for a, b in zip(parts[::2], parts[1::2])]
    square = jnp.concatenate([parts[0], jnp.zeros((TILE - 4, TILE), F32)], axis=0).T
    m = [square[(k % 2) * Q:(k % 2 + 1) * Q, k // 2:k // 2 + 1] for k in range(6)]
    g = [None] + [x / m[0] for x in m[1:]]
    d11 = g[2] - g[1] * g[1]
    d12 = g[3] - g[1] * g[2]
    d22 = g[4] - g[2] * g[2]
    f1 = g[4] - g[1] * g[3]
    f2 = g[5] - g[2] * g[3]
    ratio = d12 / d11
    c2 = -(f2 - ratio * f1) / (d22 - ratio * d12)
    c1 = -(f1 + d12 * c2) / d11
    c0 = -(g[3] + g[1] * c1 + g[2] * c2)
    e1 = TAU + c2
    e0 = e1 * TAU + c1
    scale = 1.0 / (e0 * TAU + c0)
    v0, v1, v2 = v0_ref[...], v1_ref[...], v2_ref[...]
    diffused_ref[...] = (TAU * scale) * (v2 + e1 * v1 + e0 * v0)
    residual_ref[...] = scale * (v3_ref[...] + c2 * v2 + c1 * v1 + c0 * v0)


SMEM = pl.BlockSpec(memory_space=pltpu.SMEM)
VMEM = pl.BlockSpec(memory_space=pltpu.VMEM)
PARAMS = pltpu.CompilerParams(vmem_limit_bytes=32 * 1024 * 1024)


def shape(*dims):
    return jax.ShapeDtypeStruct(dims, F32)


def local(queries, descriptors, candidates, cluster_perm, tile_vals, tile_row, tile_col):
    row_index = lax.axis_index("row").astype(jnp.int32)
    place = row_index[None]
    device = (lax.axis_index("region").astype(jnp.int32) * N_ROW + row_index)[None]

    own = jnp.concatenate([queries, cluster_perm.reshape(HALF, TILE).astype(F32)], axis=1)
    all_own = lax.all_to_all(jnp.broadcast_to(own[None], (N_ROW,) + own.shape), "row", 0, 0, tiled=True)
    all_own = all_own.reshape(Q, D + TILE)
    stored = pl.pallas_call(
        scores_kernel, out_shape=shape(Q, ROWS), in_specs=[SMEM, VMEM, VMEM, VMEM], out_specs=VMEM,
        compiler_params=PARAMS, name="scores",
    )(device, all_own[:, :D], descriptors, candidates)
    by_query = stored.reshape(QS, N_ROW, HALF, TILE).transpose(1, 0, 2, 3).reshape(N_ROW, QS * HALF, TILE)
    table = lax.all_to_all(by_query, "row", 0, 0, tiled=True)
    width = len(HOPS) * QS * HALF
    near = pl.pallas_call(
        permute_kernel, out_shape=shape(N_ROW * width, TILE), in_specs=[VMEM, VMEM], out_specs=VMEM,
        scratch_shapes=[pltpu.VMEM((QS, N_ROW * HALF, TILE), F32)],
        compiler_params=PARAMS, name="permute",
    )(table, all_own[:, D:])
    near = lax.all_to_all(near.reshape(N_ROW, width, TILE), "row", 0, 0, tiled=True)
    v0 = near[:, :QS * HALF].reshape(N_ROW, QS, HALF, TILE).transpose(1, 0, 2, 3).reshape(Q, ROWS)

    def region_pair(v):
        return (lax.ppermute(v, "region", ring(N_REGION, 1)), lax.ppermute(v, "region", ring(N_REGION, -1)))

    def exchange(v):
        low, high = region_pair(v)
        return [v] + [lax.ppermute(v, "row", ring(N_ROW, -hop)) for hop in HOPS[1:]] + [low, high]

    scratch = [pltpu.VMEM((SLOTS * HALF, Q, TILE), F32), pltpu.VMEM((HALF, Q, TILE), F32)]
    low, high = region_pair(v0)
    v1 = pl.pallas_call(
        first_kernel, out_shape=shape(Q, ROWS), in_specs=[SMEM] * 3 + [VMEM] * 4, out_specs=VMEM,
        scratch_shapes=scratch, compiler_params=PARAMS, name="first",
    )(place, tile_row, tile_col, near.reshape(N_ROW * width, TILE), low, high, tile_vals)
    v2 = pl.pallas_call(
        next_kernel, out_shape=shape(Q, ROWS), in_specs=[SMEM] * 3 + [VMEM] * (SLOTS + 1), out_specs=VMEM,
        scratch_shapes=scratch, compiler_params=PARAMS, name="second",
    )(place, tile_row, tile_col, *exchange(v1), tile_vals)
    v3, moments = pl.pallas_call(
        last_kernel, out_shape=(shape(Q, ROWS), shape(4, TILE)),
        in_specs=[SMEM] * 3 + [VMEM] * (SLOTS + 3), out_specs=(VMEM, VMEM),
        scratch_shapes=scratch, compiler_params=PARAMS, name="third",
    )(place, tile_row, tile_col, *exchange(v2), v0, v1, tile_vals)

    moments = lax.all_to_all(jnp.broadcast_to(moments[None], (N_ROW, 4, TILE)), "row", 0, 0, tiled=True)
    moments = jnp.sum(moments.reshape(2, 2, 2, 2, 2, 4, TILE).sum(0).sum(0).sum(0).sum(0), axis=0)
    moments = lax.all_to_all(jnp.broadcast_to(moments[None], (N_REGION, 4, TILE)), "region", 0, 0, tiled=True)
    diffused, residual = pl.pallas_call(
        finish_kernel, out_shape=(shape(Q, ROWS), shape(Q, ROWS)), in_specs=[VMEM] * 5, out_specs=(VMEM, VMEM),
        compiler_params=PARAMS, name="finish",
    )(moments, v0, v1, v2, v3)
    return (diffused, residual)


def solution(mesh):
    in_specs = (
        P("row", None),
        P(("region", "row"), None),
        P(),
        P("region", "row"),
        P(("region", "row"), None, None),
        P(("region", "row")),
        P(("region", "row")),
    )
    out_specs = (P(None, ("region", "row")), P(None, ("region", "row")))
    return jax.shard_map(local, mesh=mesh, in_specs=in_specs, out_specs=out_specs, check_vma=False)
```

time: 884 us -> 179 us (0.20)
  blocking collectives: 524 us -> 46.7 us
  waiting for transfers between devices: 302 us -> 23.3 us
  starting transfers between devices: 7.29 us -> 88.4 us
  Pallas kernels: 0 us -> 14.4 us
  between operations: 14.1 us -> 1.02 us
  matrix products: 12 us -> 0 us
  other arithmetic: 12.1 us -> 1.42 us
  local copies, waits for them, and re-layouts: 12.2 us -> 3.04 us
    psum x5 -> x0, blocking collectives: 492 us -> none  [the longest x3 290 us: square_sum(): return lax.psum(jnp.sum(residual * residual, axis=1), ('region', 'row'))]
    all_gather x4 -> x0, waiting for transfers between devices: 290 us -> none  [the longest x3 204 us: apply_operator(): region_field = lax.all_gather(direction, 'row', axis=1, tiled=True)]
    ppermute x6 -> x20, starting transfers between devices: 7.13 us -> 73.2 us  [the longest x14 56.2 us: exchange(): lax.ppermute(v, 'row', ring(N_ROW, -hop))]
    all_to_all x0 -> x3, blocking collectives: none -> 46.7 us  [the longest x1 15.8 us: local(): lax.all_to_all(jnp.broadcast_to(moments[None], (N_REGION, 4, TILE)), 'reg...]
    all_gather x1 -> x0, blocking collectives: 32.4 us -> none  [local(): all_queries = lax.all_gather(queries, 'row', axis=0, tiled=True)]
    all_to_all x0 -> x2, waiting for transfers between devices: none -> 18.2 us  [the longest x1 9.36 us: local(): lax.all_to_all(jnp.broadcast_to(own[None], (N_ROW,) + own.shape), 'row',...]
    all_to_all x0 -> x2, starting transfers between devices: none -> 15.2 us  [the longest x1 10.5 us: local(): lax.all_to_all(jnp.broadcast_to(own[None], (N_ROW,) + own.shape), 'row',...]
    pallas_call x0 -> x6, Pallas kernels: none -> 14.4 us  [the longest x1 5.39 us: local(): pl.pallas_call(permute_kernel, out_shape=shape(N_ROW * width, TILE), in_s...]
  transfers between devices with their start and end apart: 10 -> 22, of which waited for: 10 -> 6; matrix products, arithmetic and copies ran while one was open for 0% -> 0% of each run, Pallas kernels for 0% -> 0%
where the time goes in v1:
time: 179 us; the launch traced here: 178 us
  starting transfers between devices  88.4 us (49%)
  blocking collectives  46.7 us (26%)
  waiting for transfers between devices  23.3 us (13%)
  Pallas kernels  14.4 us (8%)
  local copies, waits for them, and re-layouts  3.04 us (2%)
    ppermute x14, starting transfers between devices, exchange(): lax.ppermute(v, 'row', ring(N_ROW, -hop))  56.2 us
    all_to_all x1, blocking collectives, local(): lax.all_to_all(jnp.broadcast_to(moments[None], (N_REGION, 4, TILE)), 'reg...  15.8 us
    all_to_all x1, blocking collectives, local(): lax.all_to_all(near.reshape(N_ROW, width, TILE), 'row', 0, 0, tiled=True)  15.5 us
    all_to_all x1, blocking collectives, local(): lax.all_to_all(jnp.broadcast_to(moments[None], (N_ROW, 4, TILE)), 'row',...  15.4 us
    ppermute x3, starting transfers between devices, region_pair(): lax.ppermute(v, 'region', ring(N_REGION, -1))  15 us
    all_to_all x1, starting transfers between devices, local(): lax.all_to_all(jnp.broadcast_to(own[None], (N_ROW,) + own.shape), 'row',...  10.5 us
    all_to_all x1, waiting for transfers between devices, local(): lax.all_to_all(jnp.broadcast_to(own[None], (N_ROW,) + own.shape), 'row',...  9.36 us
    all_to_all x1, waiting for transfers between devices, local(): table = lax.all_to_all(by_query, 'row', 0, 0, tiled=True)  8.85 us
  transfers between devices with their start and end apart: 22, of which 6 were waited for; matrix products, arithmetic and copies ran while one was open for 0% of the time, Pallas kernels for 0%

profile of v1, /device:TPU:1, one launch (start us, length us, event | category | flops | bytes accessed | tf_op | source)
XLA Modules:
  0.0 178.3 jit_solution(3330521935667896856)
XLA Ops:
  0.6 0.7 convert_element_type.6
  1.3 0.7 pad_maximum_fusion
  2.0 0.7 broadcast_in_dim.12
  2.7 10.5 %all-to-all-start = ((f32[32,2,640]{2,1,0:T(2,128)}), f32[32,2,640]{2,1,0:T(2,128)S(1)}, u32[]{:S(2)}, u32[]{:S(2)}) async-start(f32[32,2,640]{2,1,0:T(2,128)} %broadcast_in_dim.12), calls=%async_computation | async-start | bytes 327680 | tf_op jit(solution)/shard_map/all_to_all | solution.py:178
  13.2 9.4 %all-to-all-done = f32[32,2,640]{2,1,0:T(2,128)S(1)} async-done(((f32[32,2,640]{2,1,0:T(2,128)}), f32[32,2,640]{2,1,0:T(2,128)S(1)}, u32[]{:S(2)}, u32[]{:S(2)}) %all-to-all-start) | async-done | bytes 163872 | tf_op jit(solution)/shard_map/all_to_all | solution.py:178
  22.6 0.1 reshape.31
  22.7 0.0 copy-start.2
  22.7 0.7 copy-done.2
  23.5 0.6 scores.1
  24.1 0.7 copy.20
  24.8 4.7 %all-to-all-start.1 = ((f32[32,4,128]{2,1,0:T(4,128)}), f32[32,4,128]{2,1,0:T(4,128)S(1)}, u32[]{:S(2)}, u32[]{:S(2)}) async-start(f32[32,4,128]{2,1,0:T(4,128)} %bitcast.4), calls=%async_computation.1 | async-start | bytes 131072 | tf_op jit(solution)/shard_map/all_to_all | solution.py:185
  29.4 8.9 %all-to-all-done.1.table_ref = f32[32,4,128]{2,1,0:T(4,128)S(1)} async-done(((f32[32,4,128]{2,1,0:T(4,128)}), f32[32,4,128]{2,1,0:T(4,128)S(1)}, u32[]{:S(2)}, u32[]{:S(2)}) %all-to-all-start.1) | async-done | bytes 65568 | tf_op jit(solution)/shard_map/all_to_all | solution.py:185
  38.3 5.4 %permute.1 = f32[1024,128]{1,0:T(8,128)S(1)} custom-call(f32[32,4,128]{2,1,0:T(4,128)S(1)} %all-to-all-done.1.table_ref, f32[64,128]{1,0:T(8,128)S(1)} %slice.13.perm_ref), custom_call_target="tpu_custom_call" | custom-call | tf_op jit(solution)/shard_map/permute/pallas_call | solution.py:187
  43.7 0.0 copy-start
  43.7 15.5 %all_to_all.25 = f32[32,32,128]{2,1,0:T(8,128)S(1)} all-to-all(f32[32,32,128]{2,1,0:T(8,128)S(1)} %bitcast.17), channel_id=1, replica_groups=mesh['region'=16,'row'=32] {'row'}, dimensions={0} | all-to-all | bytes 1048576 | tf_op jit(solution)/shard_map/all_to_all | solution.py:192
  59.2 0.1 copy.22
  59.3 5.4 %collective-permute-start.1 = (f32[64,256]{1,0:T(8,128)S(1)}, f32[64,256]{1,0:T(8,128)S(1)}, u32[]{:S(2)}, u32[]{:S(2)}) collective-permute-start(f32[64,256]{1,0:T(8,128)S(1)} %bitcast.18), channel_id=1, source_target_pairs={{0,480},{32,0},{64,32},{96,64},{128,96},{160,128},{192,160},{224,1... | collective-permute-start | bytes 196616 | tf_op jit(solution)/shard_map/ppermute | solution.py:196
  64.7 2.0 %collective-permute-start = (f32[64,256]{1,0:T(8,128)S(1)}, f32[64,256]{1,0:T(8,128)S(1)}, u32[]{:S(2)}, u32[]{:S(2)}) collective-permute-start(f32[64,256]{1,0:T(8,128)S(1)} %bitcast.19), channel_id=1, source_target_pairs={{0,32},{32,64},{64,96},{96,128},{128,160},{160,192},{192,224},{224... | collective-permute-start | bytes 196616 | tf_op jit(solution)/shard_map/ppermute | solution.py:196
  66.7 1.9 %collective-permute-done.1.high_ref = f32[64,256]{1,0:T(8,128)S(1)} collective-permute-done((f32[64,256]{1,0:T(8,128)S(1)}, f32[64,256]{1,0:T(8,128)S(1)}, u32[]{:S(2)}, u32[]{:S(2)}) %collective-permute-start.1) | collective-permute-done | bytes 65568 | tf_op jit(solution)/shard_map/ppermute | solution.py:196
  68.6 0.6 collective-permute-done.low_ref
  69.2 0.6 copy-done.3
  69.9 0.0 copy-done.4
  69.9 2.3 %first.1.refs_0_.refs_11_.v1_ref = f32[64,256]{1,0:T(8,128)S(1)} custom-call(s32[1]{0:T(128)} %bitcast.place_ref, s32[12]{0:T(128)S(1)} %copy-done.3, s32[12]{0:T(128)S(1)} %copy-done.4, f32[1024,128]{1,0:T(8,128)S(1)} %bitcast.16, f32[64,256]{1,0:T(8,128)S(1)} %collective-permute-done.low_ref, f32[64,256]{1,0:T(8,128)S(1)} %collective-permute-done.1.high_ref, ...), custom_call_target="tpu_custom_call" | custom-call | tf_op jit(solution)/shard_map/first/pallas_call | solution.py:204
  72.3 6.6 %collective-permute-start.10 = (f32[64,256]{1,0:T(8,128)S(1)}, f32[64,256]{1,0:T(8,128)S(1)}, u32[]{:S(2)}, u32[]{:S(2)}) collective-permute-start(f32[64,256]{1,0:T(8,128)S(1)} %first.1.refs_0_.refs_11_.v1_ref), channel_id=1, source_target_pairs={{0,480},{32,0},{64,32},{96,64},{128,96},{160,128},{192,160},{224,1... | collective-permute-start | bytes 196616 | tf_op jit(solution)/shard_map/ppermute | solution.py:196
  78.8 0.0 collective-permute-start.9
  78.8 3.3 %collective-permute-start.8 = (f32[64,256]{1,0:T(8,128)S(1)}, f32[64,256]{1,0:T(8,128)S(1)}, u32[]{:S(2)}, u32[]{:S(2)}) collective-permute-start(f32[64,256]{1,0:T(8,128)S(1)} %first.1.refs_0_.refs_11_.v1_ref), channel_id=1, source_target_pairs={{0,16},{1,17},{2,18},{3,19},{4,20},{5,21},{6,22},{7,23},{8,24},{9,... | collective-permute-start | bytes 196616 | tf_op jit(solution)/shard_map/ppermute | solution.py:200
  82.2 2.2 %collective-permute-start.7 = (f32[64,256]{1,0:T(8,128)S(1)}, f32[64,256]{1,0:T(8,128)S(1)}, u32[]{:S(2)}, u32[]{:S(2)}) collective-permute-start(f32[64,256]{1,0:T(8,128)S(1)} %first.1.refs_0_.refs_11_.v1_ref), channel_id=1, source_target_pairs={{0,8},{1,9},{2,10},{3,11},{4,12},{5,13},{6,14},{7,15},{8,16},{9,17... | collective-permute-start | bytes 196616 | tf_op jit(solution)/shard_map/ppermute | solution.py:200
  84.4 4.3 %collective-permute-start.6 = (f32[64,256]{1,0:T(8,128)S(1)}, f32[64,256]{1,0:T(8,128)S(1)}, u32[]{:S(2)}, u32[]{:S(2)}) collective-permute-start(f32[64,256]{1,0:T(8,128)S(1)} %first.1.refs_0_.refs_11_.v1_ref), channel_id=1, source_target_pairs={{0,24},{1,25},{2,26},{3,27},{4,28},{5,29},{6,30},{7,31},{8,0},{9,1... | collective-permute-start | bytes 196616 | tf_op jit(solution)/shard_map/ppermute | solution.py:200
  88.7 4.6 %collective-permute-start.5 = (f32[64,256]{1,0:T(8,128)S(1)}, f32[64,256]{1,0:T(8,128)S(1)}, u32[]{:S(2)}, u32[]{:S(2)}) collective-permute-start(f32[64,256]{1,0:T(8,128)S(1)} %first.1.refs_0_.refs_11_.v1_ref), channel_id=1, source_target_pairs={{0,3},{1,4},{2,5},{3,6},{4,7},{5,8},{6,9},{7,10},{8,11},{9,12},{10... | collective-permute-start | bytes 196616 | tf_op jit(solution)/shard_map/ppermute | solution.py:200
  93.3 5.8 %collective-permute-start.4 = (f32[64,256]{1,0:T(8,128)S(1)}, f32[64,256]{1,0:T(8,128)S(1)}, u32[]{:S(2)}, u32[]{:S(2)}) collective-permute-start(f32[64,256]{1,0:T(8,128)S(1)} %first.1.refs_0_.refs_11_.v1_ref), channel_id=1, source_target_pairs={{0,29},{1,30},{2,31},{3,0},{4,1},{5,2},{6,3},{7,4},{8,5},{9,6},{10... | collective-permute-start | bytes 196616 | tf_op jit(solution)/shard_map/ppermute | solution.py:200
  99.1 0.0 collective-permute-done.8.refs_7_
  99.1 4.1 %collective-permute-start.3 = (f32[64,256]{1,0:T(8,128)S(1)}, f32[64,256]{1,0:T(8,128)S(1)}, u32[]{:S(2)}, u32[]{:S(2)}) collective-permute-start(f32[64,256]{1,0:T(8,128)S(1)} %first.1.refs_0_.refs_11_.v1_ref), channel_id=1, source_target_pairs={{0,1},{1,2},{2,3},{3,4},{4,5},{5,6},{6,7},{7,8},{8,9},{9,10},{10,1... | collective-permute-start | bytes 196616 | tf_op jit(solution)/shard_map/ppermute | solution.py:200
  103.2 4.5 %collective-permute-start.2 = (f32[64,256]{1,0:T(8,128)S(1)}, f32[64,256]{1,0:T(8,128)S(1)}, u32[]{:S(2)}, u32[]{:S(2)}) collective-permute-start(f32[64,256]{1,0:T(8,128)S(1)} %first.1.refs_0_.refs_11_.v1_ref), channel_id=1, source_target_pairs={{0,31},{1,0},{2,1},{3,2},{4,3},{5,4},{6,5},{7,6},{8,7},{9,8},{10,9... | collective-permute-start | bytes 196616 | tf_op jit(solution)/shard_map/ppermute | solution.py:200
  107.8 1.3 collective-permute-done.2.refs_1_
  109.0 2.2 %second.1.refs_0_.v2_ref = f32[64,256]{1,0:T(8,128)S(1)} custom-call(s32[1]{0:T(128)} %bitcast.place_ref, s32[12]{0:T(128)S(1)} %copy-done.3, s32[12]{0:T(128)S(1)} %copy-done.4, f32[64,256]{1,0:T(8,128)S(1)} %first.1.refs_0_.refs_11_.v1_ref, f32[64,256]{1,0:T(8,128)S(1)} %collective-permute-done.2.refs_1_, f32[64,256]{1,0:T(8,128)S(1)} %collective-permute-done.3.refs_2_, ...), custom_call_target="tpu_custom_call" | custom-call | tf_op jit(solution)/shard_map/second/pallas_call | solution.py:208
  111.3 3.1 %collective-permute-start.19 = (f32[64,256]{1,0:T(8,128)S(1)}, f32[64,256]{1,0:T(8,128)S(1)}, u32[]{:S(2)}, u32[]{:S(2)}) collective-permute-start(f32[64,256]{1,0:T(8,128)S(1)} %second.1.refs_0_.v2_ref), channel_id=1, source_target_pairs={{0,480},{32,0},{64,32},{96,64},{128,96},{160,128},{192,160},{224,1... | collective-permute-start | bytes 196616 | tf_op jit(solution)/shard_map/ppermute | solution.py:196
  114.3 1.9 %collective-permute-start.17 = (f32[64,256]{1,0:T(8,128)S(1)}, f32[64,256]{1,0:T(8,128)S(1)}, u32[]{:S(2)}, u32[]{:S(2)}) collective-permute-start(f32[64,256]{1,0:T(8,128)S(1)} %second.1.refs_0_.v2_ref), channel_id=1, source_target_pairs={{0,16},{1,17},{2,18},{3,19},{4,20},{5,21},{6,22},{7,23},{8,24},{9,... | collective-permute-start | bytes 196616 | tf_op jit(solution)/shard_map/ppermute | solution.py:200
  116.2 1.9 %collective-permute-start.16 = (f32[64,256]{1,0:T(8,128)S(1)}, f32[64,256]{1,0:T(8,128)S(1)}, u32[]{:S(2)}, u32[]{:S(2)}) collective-permute-start(f32[64,256]{1,0:T(8,128)S(1)} %second.1.refs_0_.v2_ref), channel_id=1, source_target_pairs={{0,8},{1,9},{2,10},{3,11},{4,12},{5,13},{6,14},{7,15},{8,16},{9,17... | collective-permute-start | bytes 196616 | tf_op jit(solution)/shard_map/ppermute | solution.py:200
  118.2 4.6 %collective-permute-start.15 = (f32[64,256]{1,0:T(8,128)S(1)}, f32[64,256]{1,0:T(8,128)S(1)}, u32[]{:S(2)}, u32[]{:S(2)}) collective-permute-start(f32[64,256]{1,0:T(8,128)S(1)} %second.1.refs_0_.v2_ref), channel_id=1, source_target_pairs={{0,24},{1,25},{2,26},{3,27},{4,28},{5,29},{6,30},{7,31},{8,0},{9,1... | collective-permute-start | bytes 196616 | tf_op jit(solution)/shard_map/ppermute | solution.py:200
  122.7 1.9 %collective-permute-start.14 = (f32[64,256]{1,0:T(8,128)S(1)}, f32[64,256]{1,0:T(8,128)S(1)}, u32[]{:S(2)}, u32[]{:S(2)}) collective-permute-start(f32[64,256]{1,0:T(8,128)S(1)} %second.1.refs_0_.v2_ref), channel_id=1, source_target_pairs={{0,3},{1,4},{2,5},{3,6},{4,7},{5,8},{6,9},{7,10},{8,11},{9,12},{10... | collective-permute-start | bytes 196616 | tf_op jit(solution)/shard_map/ppermute | solution.py:200
  124.7 8.5 %collective-permute-start.13 = (f32[64,256]{1,0:T(8,128)S(1)}, f32[64,256]{1,0:T(8,128)S(1)}, u32[]{:S(2)}, u32[]{:S(2)}) collective-permute-start(f32[64,256]{1,0:T(8,128)S(1)} %second.1.refs_0_.v2_ref), channel_id=1, source_target_pairs={{0,29},{1,30},{2,31},{3,0},{4,1},{5,2},{6,3},{7,4},{8,5},{9,6},{10... | collective-permute-start | bytes 196616 | tf_op jit(solution)/shard_map/ppermute | solution.py:200
  133.2 1.9 %collective-permute-start.12 = (f32[64,256]{1,0:T(8,128)S(1)}, f32[64,256]{1,0:T(8,128)S(1)}, u32[]{:S(2)}, u32[]{:S(2)}) collective-permute-start(f32[64,256]{1,0:T(8,128)S(1)} %second.1.refs_0_.v2_ref), channel_id=1, source_target_pairs={{0,1},{1,2},{2,3},{3,4},{4,5},{5,6},{6,7},{7,8},{8,9},{9,10},{10,1... | collective-permute-start | bytes 196616 | tf_op jit(solution)/shard_map/ppermute | solution.py:200
  135.1 6.7 %collective-permute-start.11 = (f32[64,256]{1,0:T(8,128)S(1)}, f32[64,256]{1,0:T(8,128)S(1)}, u32[]{:S(2)}, u32[]{:S(2)}) collective-permute-start(f32[64,256]{1,0:T(8,128)S(1)} %second.1.refs_0_.v2_ref), channel_id=1, source_target_pairs={{0,31},{1,0},{2,1},{3,2},{4,3},{5,4},{6,5},{7,6},{8,7},{9,8},{10,9... | collective-permute-start | bytes 196616 | tf_op jit(solution)/shard_map/ppermute | solution.py:200
  141.9 1.3 collective-permute-done.11.refs_1_
  143.1 2.3 %third.1 = (f32[64,256]{1,0:T(8,128)S(1)}, f32[4,128]{1,0:T(4,128)S(1)}) custom-call(s32[1]{0:T(128)} %bitcast.place_ref, s32[12]{0:T(128)S(1)} %copy-done.3, s32[12]{0:T(128)S(1)} %copy-done.4, f32[64,256]{1,0:T(8,128)S(1)} %second.1.refs_0_.v2_ref, f32[64,256]{1,0:T(8,128)S(1)} %collective-permute-done.11.refs_1_, ...), custom_call_target="tpu_custom_call" | custom-call | tf_op jit(solution)/shard_map/third/pallas_call | solution.py:212
  145.5 15.4 %all_to_all.26 = f32[32,4,128]{2,1,0:T(4,128)S(1)} all-to-all(f32[32,4,128]{2,1,0:T(4,128)S(1)} %broadcast_in_dim.13), channel_id=1, replica_groups=mesh['region'=16,'row'=32] {'row'}, dimensions={0} | all-to-all | bytes 131072 | tf_op jit(solution)/shard_map/all_to_all | solution.py:218
  161.0 15.8 %all_to_all.27.moments_ref = f32[16,4,128]{2,1,0:T(4,128)S(1)} all-to-all(f32[16,4,128]{2,1,0:T(4,128)S(1)} %broadcast_in_dim.28), channel_id=1, replica_groups=mesh['region'=16,'row'=32] {'region'}, dimensions={0} | all-to-all | bytes 65536 | tf_op jit(solution)/shard_map/all_to_all | solution.py:220
  176.7 1.5 finish.1
  (30 shorter events, 0.2 us)
Async XLA Ops:
  2.0 20.7 %copy-start.1 = (f32[256,512]{1,0:T(8,128)S(1)}, f32[256,512]{1,0:T(8,128)}, u32[]{:S(2)}) copy-start(f32[256,512]{1,0:T(8,128)} %desc_ref.1) | copy-start | bytes 1572868
  2.7 19.9 %all-to-all-start = ((f32[32,2,640]{2,1,0:T(2,128)}), f32[32,2,640]{2,1,0:T(2,128)S(1)}, u32[]{:S(2)}, u32[]{:S(2)}) async-start(f32[32,2,640]{2,1,0:T(2,128)} %broadcast_in_dim.12), calls=%async_computation | async-start | bytes 327680 | tf_op jit(solution)/shard_map/all_to_all | solution.py:178
  22.7 0.8 copy-start.2
  24.8 13.5 %all-to-all-start.1 = ((f32[32,4,128]{2,1,0:T(4,128)}), f32[32,4,128]{2,1,0:T(4,128)S(1)}, u32[]{:S(2)}, u32[]{:S(2)}) async-start(f32[32,4,128]{2,1,0:T(4,128)} %bitcast.4), calls=%async_computation.1 | async-start | bytes 131072 | tf_op jit(solution)/shard_map/all_to_all | solution.py:185
  43.7 25.6 %copy-start = (f32[12,128,128]{2,1,0:T(8,128)S(1)}, f32[12,128,128]{2,1,0:T(8,128)}, u32[]{:S(2)}) copy-start(f32[12,128,128]{2,1,0:T(8,128)} %refs_12_.1) | copy-start | bytes 2359300
  59.3 9.3 %collective-permute-start.1 = (f32[64,256]{1,0:T(8,128)S(1)}, f32[64,256]{1,0:T(8,128)S(1)}, u32[]{:S(2)}, u32[]{:S(2)}) collective-permute-start(f32[64,256]{1,0:T(8,128)S(1)} %bitcast.18), channel_id=1, source_target_pairs={{0,480},{32,0},{64,32},{96,64},{128,96},{160,128},{192,160},{224,1... | collective-permute-start | bytes 196616 | tf_op jit(solution)/shard_map/ppermute | solution.py:196
  64.7 4.6 %collective-permute-start = (f32[64,256]{1,0:T(8,128)S(1)}, f32[64,256]{1,0:T(8,128)S(1)}, u32[]{:S(2)}, u32[]{:S(2)}) collective-permute-start(f32[64,256]{1,0:T(8,128)S(1)} %bitcast.19), channel_id=1, source_target_pairs={{0,32},{32,64},{64,96},{96,128},{128,160},{160,192},{192,224},{224... | collective-permute-start | bytes 196616 | tf_op jit(solution)/shard_map/ppermute | solution.py:196
  69.2 0.7 copy-start.3
  69.2 0.7 copy-start.4
  72.3 16.4 %collective-permute-start.10 = (f32[64,256]{1,0:T(8,128)S(1)}, f32[64,256]{1,0:T(8,128)S(1)}, u32[]{:S(2)}, u32[]{:S(2)}) collective-permute-start(f32[64,256]{1,0:T(8,128)S(1)} %first.1.refs_0_.refs_11_.v1_ref), channel_id=1, source_target_pairs={{0,480},{32,0},{64,32},{96,64},{128,96},{160,128},{192,160},{224,1... | collective-permute-start | bytes 196616 | tf_op jit(solution)/shard_map/ppermute | solution.py:196
  78.8 14.5 %collective-permute-start.9 = (f32[64,256]{1,0:T(8,128)S(1)}, f32[64,256]{1,0:T(8,128)S(1)}, u32[]{:S(2)}, u32[]{:S(2)}) collective-permute-start(f32[64,256]{1,0:T(8,128)S(1)} %first.1.refs_0_.refs_11_.v1_ref), channel_id=1, source_target_pairs={{0,32},{32,64},{64,96},{96,128},{128,160},{160,192},{192,224},{224... | collective-permute-start | bytes 196616 | tf_op jit(solution)/shard_map/ppermute | solution.py:196
  78.8 20.3 %collective-permute-start.8 = (f32[64,256]{1,0:T(8,128)S(1)}, f32[64,256]{1,0:T(8,128)S(1)}, u32[]{:S(2)}, u32[]{:S(2)}) collective-permute-start(f32[64,256]{1,0:T(8,128)S(1)} %first.1.refs_0_.refs_11_.v1_ref), channel_id=1, source_target_pairs={{0,16},{1,17},{2,18},{3,19},{4,20},{5,21},{6,22},{7,23},{8,24},{9,... | collective-permute-start | bytes 196616 | tf_op jit(solution)/shard_map/ppermute | solution.py:200
  82.2 21.0 %collective-permute-start.7 = (f32[64,256]{1,0:T(8,128)S(1)}, f32[64,256]{1,0:T(8,128)S(1)}, u32[]{:S(2)}, u32[]{:S(2)}) collective-permute-start(f32[64,256]{1,0:T(8,128)S(1)} %first.1.refs_0_.refs_11_.v1_ref), channel_id=1, source_target_pairs={{0,8},{1,9},{2,10},{3,11},{4,12},{5,13},{6,14},{7,15},{8,16},{9,17... | collective-permute-start | bytes 196616 | tf_op jit(solution)/shard_map/ppermute | solution.py:200
  84.4 23.4 %collective-permute-start.6 = (f32[64,256]{1,0:T(8,128)S(1)}, f32[64,256]{1,0:T(8,128)S(1)}, u32[]{:S(2)}, u32[]{:S(2)}) collective-permute-start(f32[64,256]{1,0:T(8,128)S(1)} %first.1.refs_0_.refs_11_.v1_ref), channel_id=1, source_target_pairs={{0,24},{1,25},{2,26},{3,27},{4,28},{5,29},{6,30},{7,31},{8,0},{9,1... | collective-permute-start | bytes 196616 | tf_op jit(solution)/shard_map/ppermute | solution.py:200
  88.7 19.1 %collective-permute-start.5 = (f32[64,256]{1,0:T(8,128)S(1)}, f32[64,256]{1,0:T(8,128)S(1)}, u32[]{:S(2)}, u32[]{:S(2)}) collective-permute-start(f32[64,256]{1,0:T(8,128)S(1)} %first.1.refs_0_.refs_11_.v1_ref), channel_id=1, source_target_pairs={{0,3},{1,4},{2,5},{3,6},{4,7},{5,8},{6,9},{7,10},{8,11},{9,12},{10... | collective-permute-start | bytes 196616 | tf_op jit(solution)/shard_map/ppermute | solution.py:200
  93.3 14.4 %collective-permute-start.4 = (f32[64,256]{1,0:T(8,128)S(1)}, f32[64,256]{1,0:T(8,128)S(1)}, u32[]{:S(2)}, u32[]{:S(2)}) collective-permute-start(f32[64,256]{1,0:T(8,128)S(1)} %first.1.refs_0_.refs_11_.v1_ref), channel_id=1, source_target_pairs={{0,29},{1,30},{2,31},{3,0},{4,1},{5,2},{6,3},{7,4},{8,5},{9,6},{10... | collective-permute-start | bytes 196616 | tf_op jit(solution)/shard_map/ppermute | solution.py:200
  99.1 8.7 %collective-permute-start.3 = (f32[64,256]{1,0:T(8,128)S(1)}, f32[64,256]{1,0:T(8,128)S(1)}, u32[]{:S(2)}, u32[]{:S(2)}) collective-permute-start(f32[64,256]{1,0:T(8,128)S(1)} %first.1.refs_0_.refs_11_.v1_ref), channel_id=1, source_target_pairs={{0,1},{1,2},{2,3},{3,4},{4,5},{5,6},{6,7},{7,8},{8,9},{9,10},{10,1... | collective-permute-start | bytes 196616 | tf_op jit(solution)/shard_map/ppermute | solution.py:200
  103.2 5.9 %collective-permute-start.2 = (f32[64,256]{1,0:T(8,128)S(1)}, f32[64,256]{1,0:T(8,128)S(1)}, u32[]{:S(2)}, u32[]{:S(2)}) collective-permute-start(f32[64,256]{1,0:T(8,128)S(1)} %first.1.refs_0_.refs_11_.v1_ref), channel_id=1, source_target_pairs={{0,31},{1,0},{2,1},{3,2},{4,3},{5,4},{6,5},{7,6},{8,7},{9,8},{10,9... | collective-permute-start | bytes 196616 | tf_op jit(solution)/shard_map/ppermute | solution.py:200
  111.3 11.5 %collective-permute-start.19 = (f32[64,256]{1,0:T(8,128)S(1)}, f32[64,256]{1,0:T(8,128)S(1)}, u32[]{:S(2)}, u32[]{:S(2)}) collective-permute-start(f32[64,256]{1,0:T(8,128)S(1)} %second.1.refs_0_.v2_ref), channel_id=1, source_target_pairs={{0,480},{32,0},{64,32},{96,64},{128,96},{160,128},{192,160},{224,1... | collective-permute-start | bytes 196616 | tf_op jit(solution)/shard_map/ppermute | solution.py:196
  114.3 10.4 %collective-permute-start.18 = (f32[64,256]{1,0:T(8,128)S(1)}, f32[64,256]{1,0:T(8,128)S(1)}, u32[]{:S(2)}, u32[]{:S(2)}) collective-permute-start(f32[64,256]{1,0:T(8,128)S(1)} %second.1.refs_0_.v2_ref), channel_id=1, source_target_pairs={{0,32},{32,64},{64,96},{96,128},{128,160},{160,192},{192,224},{224... | collective-permute-start | bytes 196616 | tf_op jit(solution)/shard_map/ppermute | solution.py:196
  114.3 18.9 %collective-permute-start.17 = (f32[64,256]{1,0:T(8,128)S(1)}, f32[64,256]{1,0:T(8,128)S(1)}, u32[]{:S(2)}, u32[]{:S(2)}) collective-permute-start(f32[64,256]{1,0:T(8,128)S(1)} %second.1.refs_0_.v2_ref), channel_id=1, source_target_pairs={{0,16},{1,17},{2,18},{3,19},{4,20},{5,21},{6,22},{7,23},{8,24},{9,... | collective-permute-start | bytes 196616 | tf_op jit(solution)/shard_map/ppermute | solution.py:200
  116.2 18.9 %collective-permute-start.16 = (f32[64,256]{1,0:T(8,128)S(1)}, f32[64,256]{1,0:T(8,128)S(1)}, u32[]{:S(2)}, u32[]{:S(2)}) collective-permute-start(f32[64,256]{1,0:T(8,128)S(1)} %second.1.refs_0_.v2_ref), channel_id=1, source_target_pairs={{0,8},{1,9},{2,10},{3,11},{4,12},{5,13},{6,14},{7,15},{8,16},{9,17... | collective-permute-start | bytes 196616 | tf_op jit(solution)/shard_map/ppermute | solution.py:200
  118.2 23.7 %collective-permute-start.15 = (f32[64,256]{1,0:T(8,128)S(1)}, f32[64,256]{1,0:T(8,128)S(1)}, u32[]{:S(2)}, u32[]{:S(2)}) collective-permute-start(f32[64,256]{1,0:T(8,128)S(1)} %second.1.refs_0_.v2_ref), channel_id=1, source_target_pairs={{0,24},{1,25},{2,26},{3,27},{4,28},{5,29},{6,30},{7,31},{8,0},{9,1... | collective-permute-start | bytes 196616 | tf_op jit(solution)/shard_map/ppermute | solution.py:200
  122.7 19.1 %collective-permute-start.14 = (f32[64,256]{1,0:T(8,128)S(1)}, f32[64,256]{1,0:T(8,128)S(1)}, u32[]{:S(2)}, u32[]{:S(2)}) collective-permute-start(f32[64,256]{1,0:T(8,128)S(1)} %second.1.refs_0_.v2_ref), channel_id=1, source_target_pairs={{0,3},{1,4},{2,5},{3,6},{4,7},{5,8},{6,9},{7,10},{8,11},{9,12},{10... | collective-permute-start | bytes 196616 | tf_op jit(solution)/shard_map/ppermute | solution.py:200
  124.7 17.2 %collective-permute-start.13 = (f32[64,256]{1,0:T(8,128)S(1)}, f32[64,256]{1,0:T(8,128)S(1)}, u32[]{:S(2)}, u32[]{:S(2)}) collective-permute-start(f32[64,256]{1,0:T(8,128)S(1)} %second.1.refs_0_.v2_ref), channel_id=1, source_target_pairs={{0,29},{1,30},{2,31},{3,0},{4,1},{5,2},{6,3},{7,4},{8,5},{9,6},{10... | collective-permute-start | bytes 196616 | tf_op jit(solution)/shard_map/ppermute | solution.py:200
  133.2 8.7 %collective-permute-start.12 = (f32[64,256]{1,0:T(8,128)S(1)}, f32[64,256]{1,0:T(8,128)S(1)}, u32[]{:S(2)}, u32[]{:S(2)}) collective-permute-start(f32[64,256]{1,0:T(8,128)S(1)} %second.1.refs_0_.v2_ref), channel_id=1, source_target_pairs={{0,1},{1,2},{2,3},{3,4},{4,5},{5,6},{6,7},{7,8},{8,9},{9,10},{10,1... | collective-permute-start | bytes 196616 | tf_op jit(solution)/shard_map/ppermute | solution.py:200
  135.1 8.0 %collective-permute-start.11 = (f32[64,256]{1,0:T(8,128)S(1)}, f32[64,256]{1,0:T(8,128)S(1)}, u32[]{:S(2)}, u32[]{:S(2)}) collective-permute-start(f32[64,256]{1,0:T(8,128)S(1)} %second.1.refs_0_.v2_ref), channel_id=1, source_target_pairs={{0,31},{1,0},{2,1},{3,2},{4,3},{5,4},{6,5},{7,6},{8,7},{9,8},{10,9... | collective-permute-start | bytes 196616 | tf_op jit(solution)/shard_map/ppermute | solution.py:200

commit v2 on v1

v2 whole, which is shorter than its diff:
```python
import jax
import jax.numpy as jnp
from jax import lax
from jax.experimental import pallas as pl
from jax.experimental.pallas import tpu as pltpu
from jax.sharding import PartitionSpec as P

Q = 64
D = 512
TILE = 128
HALF = 2
ROWS = TILE * HALF
N_ROW = 32
N_REGION = 16
QS = Q // N_ROW
HOPS = (0, 3, 8, 1, -3, -8, -1, 16)
SLOTS = len(HOPS) + 2
HIGHEST = lax.Precision.HIGHEST
F32 = jnp.float32
TAU = 1.0 / 0.9


def ring(count, hop):
    return [(i, (i + hop) % count) for i in range(count)]


def pack_kernel(queries_ref, perm_ref, out_ref):
    perm = perm_ref[...].astype(F32)
    out_ref[:, :, :D] = jnp.broadcast_to(queries_ref[...][None], (N_ROW, QS, D))
    for h in range(HALF):
        out_ref[:, h:h + 1, D:] = jnp.broadcast_to(perm[:, h * TILE:(h + 1) * TILE][None], (N_ROW, 1, TILE))


def scores_kernel(dev_ref, packed_ref, desc_ref, cand_ref, out_ref):
    scores = lax.dot_general(
        packed_ref[:, :D], desc_ref[...], (((1,), (1,)), ((), ())),
        precision=HIGHEST, preferred_element_type=F32,
    ) * (1.0 / (D ** 0.5))
    stored = jnp.exp(scores)
    cand = cand_ref[...]
    for h in range(HALF):
        hit = jnp.where(cand == dev_ref[0] * HALF + h, 1.0, 0.0)
        member = jnp.max(hit, axis=1, keepdims=True) > 0.5
        kept = jnp.where(member, stored[:, h * TILE:(h + 1) * TILE], 0.0)
        for q in range(QS):
            out_ref[pl.ds(q * HALF + h, N_ROW, stride=QS * HALF), :] = kept[q * N_ROW:(q + 1) * N_ROW]


def permute_kernel(table_ref, packed_ref, out_ref, graph_ref):
    rows = N_ROW * HALF
    perm = packed_ref[:, D:].astype(jnp.int32)
    groups = rows // 8
    low = [perm[g * 8:(g + 1) * 8] & (TILE - 1) for g in range(groups)]
    high = [perm[g * 8:(g + 1) * 8] >> 7 for g in range(groups)]

    def body(sender, acc):
        acc = [list(a) for a in acc]
        for h in range(HALF):
            hits = [high[g] == sender * HALF + h for g in range(groups)]
            for q in range(QS):
                line = jnp.broadcast_to(table_ref[pl.ds(sender * (QS * HALF) + q * HALF + h, 1), :], (8, TILE))
                for g in range(groups):
                    got = jnp.take_along_axis(line, low[g], axis=1)
                    acc[q][g] = jnp.where(hits[g], got, acc[q][g])
        return tuple(tuple(a) for a in acc)

    zero = tuple(tuple(jnp.zeros((8, TILE), F32) for _ in range(groups)) for _ in range(QS))
    acc = lax.fori_loop(0, N_ROW, body, zero)
    for q in range(QS):
        for g in range(groups):
            graph_ref[q, g * 8:(g + 1) * 8, :] = acc[q][g]
    width = len(HOPS) * QS * HALF
    for q in range(QS):
        for h in range(HALF):
            mine = graph_ref[q, pl.ds(h, N_ROW, stride=HALF), :]
            for k, hop in enumerate(HOPS):
                hop = hop % N_ROW
                rolled = mine if hop == 0 else jnp.concatenate([mine[hop:], mine[:hop]], axis=0)
                out_ref[pl.ds((k * QS + q) * HALF + h, N_ROW, stride=width), :] = rolled


def tile_slot(col, place_ref):
    hop = (((col >> 1) - place_ref[0]) * place_ref[1]) & (N_ROW - 1)
    slot = jnp.int32(0)
    for k, h in enumerate(HOPS):
        slot = jnp.where(hop == h % N_ROW, k, slot)
    slot = slot * HALF + (col & 1)
    return jnp.where(col >= N_ROW * HALF, col - N_ROW * HALF + len(HOPS) * HALF, slot)


def product(slots_ref, slot, tiles_ref, t):
    return lax.dot_general(
        slots_ref[slot], tiles_ref[t], (((1,), (1,)), ((), ())), precision=HIGHEST, preferred_element_type=F32,
    )


def spread(slots_ref, k, block):
    for h in range(HALF):
        slots_ref[k * HALF + h] = block[:, h * TILE:(h + 1) * TILE]


def inner_kernel(place_ref, row_ref, col_ref, near_ref, tiles_ref, out_ref, slots_ref):
    width = len(HOPS) * QS * HALF
    for k in range(len(HOPS)):
        for h in range(HALF):
            for q in range(QS):
                slots_ref[k * HALF + h, q * N_ROW:(q + 1) * N_ROW, :] = near_ref[
                    pl.ds((k * QS + q) * HALF + h, N_ROW, stride=width), :]
    out_ref[...] = jnp.zeros_like(out_ref)
    for t in range(tiles_ref.shape[0]):
        @pl.when(col_ref[t] < N_ROW * HALF)
        def _():
            out_ref[row_ref[t]] += product(slots_ref, tile_slot(col_ref[t], place_ref), tiles_ref, t)


def outer_kernel(row_ref, col_ref, inner_ref, low_ref, high_ref, tiles_ref, out_ref, slots_ref, acc_ref):
    spread(slots_ref, 0, low_ref[...])
    spread(slots_ref, 1, high_ref[...])
    acc_ref[...] = inner_ref[...]
    for t in range(tiles_ref.shape[0]):
        @pl.when(col_ref[t] >= N_ROW * HALF)
        def _():
            acc_ref[row_ref[t]] += product(slots_ref, col_ref[t] - N_ROW * HALF, tiles_ref, t)
    for h in range(HALF):
        out_ref[:, h * TILE:(h + 1) * TILE] = acc_ref[h]


N_BLOCKS = 8


def next_kernel(place_ref, row_ref, col_ref, *refs):
    own, a_ref, b_ref, c_ref, swapped_ref, far_ref, low_ref, high_ref = refs[:N_BLOCKS]
    tiles_ref, out_ref, slots_ref, acc_ref = refs[N_BLOCKS:]
    blocks = [own[...], a_ref[0], b_ref[0], c_ref[0], swapped_ref[0], swapped_ref[1], swapped_ref[2],
              far_ref[...], low_ref[...], high_ref[...]]
    for k, block in enumerate(blocks):
        spread(slots_ref, k, block)
    acc_ref[...] = jnp.zeros_like(acc_ref)
    for t in range(tiles_ref.shape[0]):
        acc_ref[row_ref[t]] += product(slots_ref, tile_slot(col_ref[t], place_ref), tiles_ref, t)
    for h in range(HALF):
        out_ref[:, h * TILE:(h + 1) * TILE] = acc_ref[h]


def last_kernel(place_ref, row_ref, col_ref, *refs):
    blocks = refs[:N_BLOCKS]
    v0_ref, v1_ref, tiles_ref, out_ref, moments_ref, slots_ref, acc_ref = refs[N_BLOCKS:]
    next_kernel(place_ref, row_ref, col_ref, *blocks, tiles_ref, out_ref, slots_ref, acc_ref)
    vs = [v0_ref[...], v1_ref[...], blocks[0][...], out_ref[...]]
    lane = lax.broadcasted_iota(jnp.int32, (Q, TILE), 1)
    packed = [jnp.zeros((Q, TILE), F32), jnp.zeros((Q, TILE), F32)]
    for m in range(6):
        prod = vs[m // 2] * vs[(m + 1) // 2]
        total = jnp.sum(prod[:, :TILE] + prod[:, TILE:], axis=1, keepdims=True)
        packed[m % 2] = jnp.where(lane == m // 2, total, packed[m % 2])
    moments_ref[...] = jnp.concatenate(packed, axis=0).T[:4]


def finish_kernel(moments_ref, v0_ref, v1_ref, v2_ref, v3_ref, diffused_ref, residual_ref):
    parts = [moments_ref[r] for r in range(N_REGION)]
    while len(parts) > 1:
        parts = [a + b for a, b in zip(parts[::2], parts[1::2])]
    square = jnp.concatenate([parts[0], jnp.zeros((TILE - 4, TILE), F32)], axis=0).T
    m = [square[(k % 2) * Q:(k % 2 + 1) * Q, k // 2:k // 2 + 1] for k in range(6)]
    g = [None] + [x / m[0] for x in m[1:]]
    d11 = g[2] - g[1] * g[1]
    d12 = g[3] - g[1] * g[2]
    d22 = g[4] - g[2] * g[2]
    f1 = g[4] - g[1] * g[3]
    f2 = g[5] - g[2] * g[3]
    ratio = d12 / d11
    c2 = -(f2 - ratio * f1) / (d22 - ratio * d12)
    c1 = -(f1 + d12 * c2) / d11
    c0 = -(g[3] + g[1] * c1 + g[2] * c2)
    e1 = TAU + c2
    e0 = e1 * TAU + c1
    scale = 1.0 / (e0 * TAU + c0)
    v0, v1, v2 = v0_ref[...], v1_ref[...], v2_ref[...]
    diffused_ref[...] = (TAU * scale) * (v2 + e1 * v1 + e0 * v0)
    residual_ref[...] = scale * (v3_ref[...] + c2 * v2 + c1 * v1 + c0 * v0)


SMEM = pl.BlockSpec(memory_space=pltpu.SMEM)
VMEM = pl.BlockSpec(memory_space=pltpu.VMEM)
PARAMS = pltpu.CompilerParams(vmem_limit_bytes=32 * 1024 * 1024)


def shape(*dims):
    return jax.ShapeDtypeStruct(dims, F32)


def local(queries, descriptors, candidates, cluster_perm, tile_vals, tile_row, tile_col):
    row_index = lax.axis_index("row").astype(jnp.int32)
    region = lax.axis_index("region").astype(jnp.int32)
    core = region & 1
    device = (region * N_ROW + row_index)[None]
    place = jnp.stack([row_index, 1 - 2 * core])
    upward = jnp.stack([row_index, jnp.int32(1)])

    packed = pl.pallas_call(
        pack_kernel, out_shape=shape(N_ROW, QS, D + TILE), in_specs=[VMEM, VMEM], out_specs=VMEM,
        compiler_params=PARAMS, name="pack",
    )(queries, cluster_perm)
    packed = lax.all_to_all(packed, "row", 0, 0, tiled=True).reshape(Q, D + TILE)
    by_query = pl.pallas_call(
        scores_kernel, out_shape=shape(N_ROW * QS * HALF, TILE), in_specs=[SMEM, VMEM, VMEM, VMEM], out_specs=VMEM,
        compiler_params=PARAMS, name="scores",
    )(device, packed, descriptors, candidates)
    table = lax.all_to_all(by_query.reshape(N_ROW, QS * HALF, TILE), "row", 0, 0, tiled=True)
    width = len(HOPS) * QS * HALF
    near = pl.pallas_call(
        permute_kernel, out_shape=shape(N_ROW * width, TILE), in_specs=[VMEM, VMEM], out_specs=VMEM,
        scratch_shapes=[pltpu.VMEM((QS, N_ROW * HALF, TILE), F32)],
        compiler_params=PARAMS, name="permute",
    )(table.reshape(N_ROW * QS * HALF, TILE), packed)
    near = lax.all_to_all(near.reshape(N_ROW, width, TILE), "row", 0, 0, tiled=True)
    v0 = near[:, :QS * HALF].reshape(N_ROW, QS, HALF, TILE).transpose(1, 0, 2, 3).reshape(Q, ROWS)

    def region_pair(v):
        return (lax.ppermute(v, "region", ring(N_REGION, 1)), lax.ppermute(v, "region", ring(N_REGION, -1)))

    def exchange(v):
        low, high = region_pair(v)
        far = lax.ppermute(v, "row", ring(N_ROW, 16))
        both = jnp.stack([v, jnp.where(core == 0, high, low)])
        got = []
        for hop in HOPS[1:4]:
            pairs = [(r * N_ROW + i, r * N_ROW + (i - (hop if r % 2 == 0 else -hop)) % N_ROW)
                     for r in range(N_REGION) for i in range(N_ROW)]
            got.append(lax.ppermute(both, ("region", "row"), pairs))
        swapped = lax.ppermute(jnp.stack([g[1] for g in got]), "region", [(r, r ^ 1) for r in range(N_REGION)])
        return [v] + got + [swapped, far, low, high]

    slots = pltpu.VMEM((SLOTS * HALF, Q, TILE), F32)
    acc = pltpu.VMEM((HALF, Q, TILE), F32)
    low, high = region_pair(v0)
    inner = pl.pallas_call(
        inner_kernel, out_shape=shape(HALF, Q, TILE), in_specs=[SMEM] * 3 + [VMEM] * 2, out_specs=VMEM,
        scratch_shapes=[pltpu.VMEM((len(HOPS) * HALF, Q, TILE), F32)],
        cost_estimate=pl.CostEstimate(flops=2 * 12 * Q * TILE * TILE, bytes_accessed=2000000, transcendentals=0),
        compiler_params=PARAMS, name="first_inner",
    )(upward, tile_row, tile_col, near.reshape(N_ROW * width, TILE), tile_vals)
    v1 = pl.pallas_call(
        outer_kernel, out_shape=shape(Q, ROWS), in_specs=[SMEM] * 2 + [VMEM] * 4, out_specs=VMEM,
        scratch_shapes=[pltpu.VMEM((2 * HALF, Q, TILE), F32), acc], compiler_params=PARAMS, name="first_outer",
    )(tile_row, tile_col, inner, low, high, tile_vals)
    v2 = pl.pallas_call(
        next_kernel, out_shape=shape(Q, ROWS), in_specs=[SMEM] * 3 + [VMEM] * (N_BLOCKS + 1), out_specs=VMEM,
        scratch_shapes=[slots, acc], compiler_params=PARAMS, name="second",
    )(place, tile_row, tile_col, *exchange(v1), tile_vals)
    v3, moments = pl.pallas_call(
        last_kernel, out_shape=(shape(Q, ROWS), shape(4, TILE)),
        in_specs=[SMEM] * 3 + [VMEM] * (N_BLOCKS + 3), out_specs=(VMEM, VMEM),
        scratch_shapes=[slots, acc], compiler_params=PARAMS, name="third",
    )(place, tile_row, tile_col, *exchange(v2), v0, v1, tile_vals)

    moments = lax.all_to_all(jnp.broadcast_to(moments[None], (N_ROW, 4, TILE)), "row", 0, 0, tiled=True)
    moments = jnp.sum(moments.reshape(2, 2, 2, 2, 2, 4, TILE).sum(0).sum(0).sum(0).sum(0), axis=0)
    moments = lax.all_to_all(jnp.broadcast_to(moments[None], (N_REGION, 4, TILE)), "region", 0, 0, tiled=True)
    diffused, residual = pl.pallas_call(
        finish_kernel, out_shape=(shape(Q, ROWS), shape(Q, ROWS)), in_specs=[VMEM] * 5, out_specs=(VMEM, VMEM),
        compiler_params=PARAMS, name="finish",
    )(moments, v0, v1, v2, v3)
    return (diffused, residual)


def solution(mesh):
    in_specs = (
        P("row", None),
        P(("region", "row"), None),
        P(),
        P("region", "row"),
        P(("region", "row"), None, None),
        P(("region", "row")),
        P(("region", "row")),
    )
    out_specs = (P(None, ("region", "row")), P(None, ("region", "row")))
    return jax.shard_map(local, mesh=mesh, in_specs=in_specs, out_specs=out_specs, check_vma=False)
```

time: 179 us -> 175 us (0.978)
  starting transfers between devices: 88.4 us -> 55.8 us
  waiting for transfers between devices: 23.3 us -> 35.8 us
  blocking collectives: 46.7 us -> 58 us
  local copies, waits for them, and re-layouts: 3.04 us -> 5.97 us
  Pallas kernels: 14.4 us -> 17.1 us
    ppermute x14 -> x10, starting transfers between devices: 56.2 us -> 35.3 us  [the longest x6 19.8 us: exchange(): got.append(lax.ppermute(both, ('region', 'row'), pairs))]
    ppermute x14 -> x10, waiting for transfers between devices: 2.57 us -> 17.5 us  [the longest x6 10.5 us: exchange(): got.append(lax.ppermute(both, ('region', 'row'), pairs))]
    all_to_all x0 -> x1, blocking collectives: none -> 13.3 us  [local(): lax.all_to_all(by_query.reshape(N_ROW, QS * HALF, TILE), 'row', 0, 0, til...]
    ppermute x3, starting transfers between devices: 15 us -> 2.68 us  [region_pair(): lax.ppermute(v, 'region', ring(N_REGION, -1))]
    all_to_all x2 -> x1, waiting for transfers between devices: 18.2 us -> 9.34 us  [local(): lax.all_to_all(packed, 'row', 0, 0, tiled=True).reshape(Q, D + TILE)]
    ppermute x3, starting transfers between devices: 2.01 us -> 7.36 us  [region_pair(): lax.ppermute(v, 'region', ring(N_REGION, 1))]
    all_to_all x2 -> x1, starting transfers between devices: 15.2 us -> 10.5 us  [local(): lax.all_to_all(packed, 'row', 0, 0, tiled=True).reshape(Q, D + TILE)]
    ppermute x3, waiting for transfers between devices: 0.63 us -> 4.98 us  [region_pair(): lax.ppermute(v, 'region', ring(N_REGION, 1))]
  transfers between devices with their start and end apart: 22 -> 17, of which waited for: 6 -> 12; matrix products, arithmetic and copies ran while one was open for 0% -> 0% of each run, Pallas kernels for 0% -> 2%
where the time goes in v2:
time: 175 us; the launch traced here: 174 us
  blocking collectives  58 us (33%)
  starting transfers between devices  55.8 us (32%)
  waiting for transfers between devices  35.8 us (20%)
  Pallas kernels  17.1 us (10%)
  local copies, waits for them, and re-layouts  5.97 us (3%)
    ppermute x6, starting transfers between devices, exchange(): got.append(lax.ppermute(both, ('region', 'row'), pairs))  19.8 us
    all_to_all x1, blocking collectives, local(): lax.all_to_all(near.reshape(N_ROW, width, TILE), 'row', 0, 0, tiled=True)  15.5 us
    all_to_all x1, blocking collectives, local(): lax.all_to_all(jnp.broadcast_to(moments[None], (N_ROW, 4, TILE)), 'row',...  14.8 us
    all_to_all x1, blocking collectives, local(): lax.all_to_all(jnp.broadcast_to(moments[None], (N_REGION, 4, TILE)), 'reg...  14.4 us
    all_to_all x1, blocking collectives, local(): lax.all_to_all(by_query.reshape(N_ROW, QS * HALF, TILE), 'row', 0, 0, til...  13.3 us
    all_to_all x1, starting transfers between devices, local(): lax.all_to_all(packed, 'row', 0, 0, tiled=True).reshape(Q, D + TILE)  10.5 us
    ppermute x6, waiting for transfers between devices, exchange(): got.append(lax.ppermute(both, ('region', 'row'), pairs))  10.5 us
    all_to_all x1, waiting for transfers between devices, local(): lax.all_to_all(packed, 'row', 0, 0, tiled=True).reshape(Q, D + TILE)  9.34 us
  transfers between devices with their start and end apart: 17, of which 12 were waited for; matrix products, arithmetic and copies ran while one was open for 0% of the time, Pallas kernels for 2%

profile of v2, /device:TPU:1, one launch (start us, length us, event | category | flops | bytes accessed | tf_op | source)
XLA Modules:
  0.0 173.9 jit_solution(1295326467370674387)
XLA Ops:
  0.6 0.7 copy-done.13
  1.4 0.7 copy-done.14
  2.1 0.7 pack.1
  2.7 10.5 %all-to-all-start = ((f32[32,2,640]{2,1,0:T(2,128)}), f32[32,2,640]{2,1,0:T(2,128)S(1)}, u32[]{:S(2)}, u32[]{:S(2)}) async-start(f32[32,2,640]{2,1,0:T(2,128)} %pack.1), calls=%async_computation | async-start | bytes 327680 | tf_op jit(solution)/shard_map/all_to_all | solution.py:204
  13.3 9.3 %all-to-all-done = f32[32,2,640]{2,1,0:T(2,128)S(1)} async-done(((f32[32,2,640]{2,1,0:T(2,128)}), f32[32,2,640]{2,1,0:T(2,128)S(1)}, u32[]{:S(2)}, u32[]{:S(2)}) %all-to-all-start) | async-done | bytes 163872 | tf_op jit(solution)/shard_map/all_to_all | solution.py:204
  22.6 0.1 reshape.28.packed_ref
  22.8 0.6 scores.1
  23.4 13.3 %all_to_all.25 = f32[32,4,128]{2,1,0:T(4,128)S(1)} all-to-all(f32[32,4,128]{2,1,0:T(4,128)S(1)} %bitcast.30), channel_id=1, replica_groups=mesh['region'=16,'row'=32] {'row'}, dimensions={0} | all-to-all | bytes 131072 | tf_op jit(solution)/shard_map/all_to_all | solution.py:209
  36.7 5.4 %permute.1 = f32[1024,128]{1,0:T(8,128)S(1)} custom-call(f32[128,128]{1,0:T(8,128)S(1)} %bitcast.29, f32[64,640]{1,0:T(8,128)S(1)} %reshape.28.packed_ref), custom_call_target="tpu_custom_call" | custom-call | tf_op jit(solution)/shard_map/permute/pallas_call | solution.py:211
  42.1 15.5 %all_to_all.26 = f32[32,32,128]{2,1,0:T(8,128)S(1)} all-to-all(f32[32,32,128]{2,1,0:T(8,128)S(1)} %bitcast.22), channel_id=1, replica_groups=mesh['region'=16,'row'=32] {'row'}, dimensions={0} | all-to-all | bytes 1048576 | tf_op jit(solution)/shard_map/all_to_all | solution.py:216
  57.7 7.3 %collective-permute-start = (f32[64,256]{1,0:T(8,128)S(1)}, f32[64,256]{1,0:T(8,128)S(1)}, u32[]{:S(2)}, u32[]{:S(2)}) collective-permute-start(f32[64,256]{1,0:T(8,128)S(1)} %bitcast.25), channel_id=1, source_target_pairs={{0,32},{32,64},{64,96},{96,128},{128,160},{160,192},{192,224},{224... | collective-permute-start | bytes 196616 | tf_op jit(solution)/shard_map/ppermute | solution.py:220
  65.1 0.6 copy-done.11
  65.8 3.2 %first_inner.1.inner_ref = f32[2,64,128]{2,1,0:T(8,128)S(1)} custom-call(s32[2]{0:T(128)S(1)} %pad_add_fusion.1.place_ref, s32[12]{0:T(128)S(1)} %copy-done.11, s32[12]{0:T(128)S(1)} %copy-done.12, f32[1024,128]{1,0:T(8,128)S(1)} %bitcast.21, f32[12,128,128]{2,1,0:T(8,128)S(1)} %copy-done), custom_call_target="tpu_custom_call" | custom-call | flops 25165824 | bytes 2000000 | tf_op jit(solution)/shard_map/first_inner/pallas_call | solution.py:237
  69.1 1.1 first_outer.1.refs_0_.refs_9_.v1_ref
  70.2 1.9 %collective-permute-start.2 = (f32[64,256]{1,0:T(8,128)S(1)}, f32[64,256]{1,0:T(8,128)S(1)}, u32[]{:S(2)}, u32[]{:S(2)}) collective-permute-start(f32[64,256]{1,0:T(8,128)S(1)} %first_outer.1.refs_0_.refs_9_.v1_ref), channel_id=1, source_target_pairs={{0,480},{32,0},{64,32},{96,64},{128,96},{160,128},{192,160},{224,1... | collective-permute-start | bytes 196616 | tf_op jit(solution)/shard_map/ppermute | solution.py:220
  72.1 1.8 %collective-permute-done.2.refs_7_ = f32[64,256]{1,0:T(8,128)S(1)} collective-permute-done((f32[64,256]{1,0:T(8,128)S(1)}, f32[64,256]{1,0:T(8,128)S(1)}, u32[]{:S(2)}, u32[]{:S(2)}) %collective-permute-start.2) | collective-permute-done | bytes 65568 | tf_op jit(solution)/shard_map/ppermute | solution.py:220
  73.9 4.3 %collective-permute-done.3.refs_6_ = f32[64,256]{1,0:T(8,128)S(1)} collective-permute-done((f32[64,256]{1,0:T(8,128)S(1)}, f32[64,256]{1,0:T(8,128)S(1)}, u32[]{:S(2)}, u32[]{:S(2)}) %collective-permute-start.3) | collective-permute-done | bytes 65568 | tf_op jit(solution)/shard_map/ppermute | solution.py:220
  78.2 5.0 %collective-permute-start.4 = (f32[2,64,256]{2,1,0:T(8,128)S(1)}, f32[2,64,256]{2,1,0:T(8,128)S(1)}, u32[]{:S(2)}, u32[]{:S(2)}) collective-permute-start(f32[2,64,256]{2,1,0:T(8,128)S(1)} %pad_maximum_fusion.2), channel_id=1, source_target_pairs={{0,29},{1,30},{2,31},{3,0},{4,1},{5,2},{6,3},{7,4},{8,5},{9,6},{10... | collective-permute-start | bytes 393224 | tf_op jit(solution)/shard_map/ppermute | solution.py:230
  83.1 2.2 %collective-permute-start.5 = (f32[2,64,256]{2,1,0:T(8,128)S(1)}, f32[2,64,256]{2,1,0:T(8,128)S(1)}, u32[]{:S(2)}, u32[]{:S(2)}) collective-permute-start(f32[2,64,256]{2,1,0:T(8,128)S(1)} %pad_maximum_fusion.2), channel_id=1, source_target_pairs={{0,24},{1,25},{2,26},{3,27},{4,28},{5,29},{6,30},{7,31},{8,0},{9,1... | collective-permute-start | bytes 393224 | tf_op jit(solution)/shard_map/ppermute | solution.py:230
  85.4 2.0 %collective-permute-start.6 = (f32[2,64,256]{2,1,0:T(8,128)S(1)}, f32[2,64,256]{2,1,0:T(8,128)S(1)}, u32[]{:S(2)}, u32[]{:S(2)}) collective-permute-start(f32[2,64,256]{2,1,0:T(8,128)S(1)} %pad_maximum_fusion.2), channel_id=1, source_target_pairs={{0,31},{1,0},{2,1},{3,2},{4,3},{5,4},{6,5},{7,6},{8,7},{9,8},{10,9... | collective-permute-start | bytes 393224 | tf_op jit(solution)/shard_map/ppermute | solution.py:230
  87.4 2.4 %collective-permute-done.4.refs_1_ = f32[2,64,256]{2,1,0:T(8,128)S(1)} collective-permute-done((f32[2,64,256]{2,1,0:T(8,128)S(1)}, f32[2,64,256]{2,1,0:T(8,128)S(1)}, u32[]{:S(2)}, u32[]{:S(2)}) %collective-permute-start.4) | collective-permute-done | bytes 131104 | tf_op jit(solution)/shard_map/ppermute | solution.py:230
  89.8 1.3 collective-permute-done.5.refs_2_
  91.1 0.6 copy-done.8
  91.7 2.7 %collective-permute-done.6.refs_3_ = f32[2,64,256]{2,1,0:T(8,128)S(1)} collective-permute-done((f32[2,64,256]{2,1,0:T(8,128)S(1)}, f32[2,64,256]{2,1,0:T(8,128)S(1)}, u32[]{:S(2)}, u32[]{:S(2)}) %collective-permute-start.6) | collective-permute-done | bytes 131104 | tf_op jit(solution)/shard_map/ppermute | solution.py:230
  94.4 0.8 slice-done.2
  95.3 4.7 %collective-permute-start.7 = (f32[3,64,256]{2,1,0:T(8,128)S(1)}, f32[3,64,256]{2,1,0:T(8,128)S(1)}, u32[]{:S(2)}, u32[]{:S(2)}) collective-permute-start(f32[3,64,256]{2,1,0:T(8,128)S(1)} %pad_maximum_fusion), channel_id=1, source_target_pairs={{0,32},{32,0},{64,96},{96,64},{128,160},{160,128},{192,224},{224,1... | collective-permute-start | bytes 589832 | tf_op jit(solution)/shard_map/ppermute | solution.py:231
  100.0 3.5 %collective-permute-start.8 = (f32[64,256]{1,0:T(8,128)S(1)}, f32[64,256]{1,0:T(8,128)S(1)}, u32[]{:S(2)}, u32[]{:S(2)}) collective-permute-start(f32[64,256]{1,0:T(8,128)S(1)} %first_outer.1.refs_0_.refs_9_.v1_ref), channel_id=1, source_target_pairs={{0,16},{1,17},{2,18},{3,19},{4,20},{5,21},{6,22},{7,23},{8,24},{9,... | collective-permute-start | bytes 196616 | tf_op jit(solution)/shard_map/ppermute | solution.py:224
  103.5 0.1 pad_add_fusion.place_ref
  103.6 3.5 %collective-permute-done.8.refs_5_ = f32[64,256]{1,0:T(8,128)S(1)} collective-permute-done((f32[64,256]{1,0:T(8,128)S(1)}, f32[64,256]{1,0:T(8,128)S(1)}, u32[]{:S(2)}, u32[]{:S(2)}) %collective-permute-start.8) | collective-permute-done | bytes 65568 | tf_op jit(solution)/shard_map/ppermute | solution.py:224
  107.1 2.2 %second.1.refs_0_.v2_ref = f32[64,256]{1,0:T(8,128)S(1)} custom-call(s32[2]{0:T(128)S(1)} %pad_add_fusion.place_ref, s32[12]{0:T(128)S(1)} %copy-done.11, s32[12]{0:T(128)S(1)} %copy-done.12, f32[64,256]{1,0:T(8,128)S(1)} %first_outer.1.refs_0_.refs_9_.v1_ref, f32[2,64,256]{2,1,0:T(8,128)S(1)} %copy-done.7, f32[2,64,256]{2,1,0:T(8,128)S(1)} %copy-done.9, ...), custom_call_target="tpu_custom_call" | custom-call | tf_op jit(solution)/shard_map/second/pallas_call | solution.py:247
  109.4 0.8 collective-permute-start.9
  110.2 0.7 collective-permute-done.10.refs_6_
  110.9 2.2 %collective-permute-done.9.refs_7_ = f32[64,256]{1,0:T(8,128)S(1)} collective-permute-done((f32[64,256]{1,0:T(8,128)S(1)}, f32[64,256]{1,0:T(8,128)S(1)}, u32[]{:S(2)}, u32[]{:S(2)}) %collective-permute-start.9) | collective-permute-done | bytes 65568 | tf_op jit(solution)/shard_map/ppermute | solution.py:220
  113.1 4.5 %collective-permute-start.11 = (f32[2,64,256]{2,1,0:T(8,128)S(1)}, f32[2,64,256]{2,1,0:T(8,128)S(1)}, u32[]{:S(2)}, u32[]{:S(2)}) collective-permute-start(f32[2,64,256]{2,1,0:T(8,128)S(1)} %pad_maximum_fusion.3), channel_id=1, source_target_pairs={{0,29},{1,30},{2,31},{3,0},{4,1},{5,2},{6,3},{7,4},{8,5},{9,6},{10... | collective-permute-start | bytes 393224 | tf_op jit(solution)/shard_map/ppermute | solution.py:230
  117.7 2.5 %collective-permute-start.12 = (f32[2,64,256]{2,1,0:T(8,128)S(1)}, f32[2,64,256]{2,1,0:T(8,128)S(1)}, u32[]{:S(2)}, u32[]{:S(2)}) collective-permute-start(f32[2,64,256]{2,1,0:T(8,128)S(1)} %pad_maximum_fusion.3), channel_id=1, source_target_pairs={{0,24},{1,25},{2,26},{3,27},{4,28},{5,29},{6,30},{7,31},{8,0},{9,1... | collective-permute-start | bytes 393224 | tf_op jit(solution)/shard_map/ppermute | solution.py:230
  120.1 3.6 %collective-permute-start.13 = (f32[2,64,256]{2,1,0:T(8,128)S(1)}, f32[2,64,256]{2,1,0:T(8,128)S(1)}, u32[]{:S(2)}, u32[]{:S(2)}) collective-permute-start(f32[2,64,256]{2,1,0:T(8,128)S(1)} %pad_maximum_fusion.3), channel_id=1, source_target_pairs={{0,31},{1,0},{2,1},{3,2},{4,3},{5,4},{6,5},{7,6},{8,7},{9,8},{10,9... | collective-permute-start | bytes 393224 | tf_op jit(solution)/shard_map/ppermute | solution.py:230
  123.8 3.0 %collective-permute-done.11.refs_1_ = f32[2,64,256]{2,1,0:T(8,128)S(1)} collective-permute-done((f32[2,64,256]{2,1,0:T(8,128)S(1)}, f32[2,64,256]{2,1,0:T(8,128)S(1)}, u32[]{:S(2)}, u32[]{:S(2)}) %collective-permute-start.11) | collective-permute-done | bytes 131104 | tf_op jit(solution)/shard_map/ppermute | solution.py:230
  126.7 0.6 copy-done.2
  127.4 0.6 copy-done.4
  128.0 1.1 collective-permute-done.13.refs_3_
  129.2 0.8 slice-done.1
  130.0 3.6 %collective-permute-start.14 = (f32[3,64,256]{2,1,0:T(8,128)S(1)}, f32[3,64,256]{2,1,0:T(8,128)S(1)}, u32[]{:S(2)}, u32[]{:S(2)}) collective-permute-start(f32[3,64,256]{2,1,0:T(8,128)S(1)} %pad_maximum_fusion.1), channel_id=1, source_target_pairs={{0,32},{32,0},{64,96},{96,64},{128,160},{160,128},{192,224},{224,1... | collective-permute-start | bytes 589832 | tf_op jit(solution)/shard_map/ppermute | solution.py:231
  133.7 3.6 %collective-permute-start.15 = (f32[64,256]{1,0:T(8,128)S(1)}, f32[64,256]{1,0:T(8,128)S(1)}, u32[]{:S(2)}, u32[]{:S(2)}) collective-permute-start(f32[64,256]{1,0:T(8,128)S(1)} %second.1.refs_0_.v2_ref), channel_id=1, source_target_pairs={{0,16},{1,17},{2,18},{3,19},{4,20},{5,21},{6,22},{7,23},{8,24},{9,... | collective-permute-start | bytes 196616 | tf_op jit(solution)/shard_map/ppermute | solution.py:224
  137.3 3.5 %collective-permute-done.15.refs_5_ = f32[64,256]{1,0:T(8,128)S(1)} collective-permute-done((f32[64,256]{1,0:T(8,128)S(1)}, f32[64,256]{1,0:T(8,128)S(1)}, u32[]{:S(2)}, u32[]{:S(2)}) %collective-permute-start.15) | collective-permute-done | bytes 65568 | tf_op jit(solution)/shard_map/ppermute | solution.py:224
  140.8 2.3 %third.1 = (f32[64,256]{1,0:T(8,128)S(1)}, f32[4,128]{1,0:T(4,128)S(1)}) custom-call(s32[2]{0:T(128)S(1)} %pad_add_fusion.place_ref, s32[12]{0:T(128)S(1)} %copy-done.11, s32[12]{0:T(128)S(1)} %copy-done.12, f32[64,256]{1,0:T(8,128)S(1)} %second.1.refs_0_.v2_ref, f32[2,64,256]{2,1,0:T(8,128)S(1)} %copy-done.3, f32[2,64,256]{2,1,0:T(8,128)S(1)} %copy-done.5, ...), custom_call_target="tpu_custom_call" | custom-call | tf_op jit(solution)/shard_map/third/pallas_call | solution.py:251
  143.2 14.8 %all_to_all.27 = f32[32,4,128]{2,1,0:T(4,128)S(1)} all-to-all(f32[32,4,128]{2,1,0:T(4,128)S(1)} %broadcast_in_dim.7), channel_id=1, replica_groups=mesh['region'=16,'row'=32] {'row'}, dimensions={0} | all-to-all | bytes 131072 | tf_op jit(solution)/shard_map/all_to_all | solution.py:257
  158.0 14.4 %all_to_all.28.moments_ref = f32[16,4,128]{2,1,0:T(4,128)S(1)} all-to-all(f32[16,4,128]{2,1,0:T(4,128)S(1)} %broadcast_in_dim.8), channel_id=1, replica_groups=mesh['region'=16,'row'=32] {'region'}, dimensions={0} | all-to-all | bytes 65536 | tf_op jit(solution)/shard_map/all_to_all | solution.py:259
  172.4 1.5 finish.1
  (54 shorter events, 0.4 us)
Async XLA Ops:
  0.6 22.1 %copy-start.1 = (f32[256,512]{1,0:T(8,128)S(1)}, f32[256,512]{1,0:T(8,128)}, u32[]{:S(2)}) copy-start(f32[256,512]{1,0:T(8,128)} %desc_ref.1) | copy-start | bytes 1572868
  0.6 0.7 copy-start.13
  1.4 0.7 copy-start.14
  2.7 19.9 %all-to-all-start = ((f32[32,2,640]{2,1,0:T(2,128)}), f32[32,2,640]{2,1,0:T(2,128)S(1)}, u32[]{:S(2)}, u32[]{:S(2)}) async-start(f32[32,2,640]{2,1,0:T(2,128)} %pack.1), calls=%async_computation | async-start | bytes 327680 | tf_op jit(solution)/shard_map/all_to_all | solution.py:204
  13.3 9.5 %copy-start.10 = (s32[64,64]{1,0:T(8,128)S(1)}, s32[64,64]{1,0:T(8,128)}, u32[]{:S(2)}) copy-start(s32[64,64]{1,0:T(8,128)} %cand_ref.1) | copy-start | bytes 49156
  42.1 23.1 %copy-start = (f32[12,128,128]{2,1,0:T(8,128)S(1)}, f32[12,128,128]{2,1,0:T(8,128)}, u32[]{:S(2)}) copy-start(f32[12,128,128]{2,1,0:T(8,128)} %refs_10_.1) | copy-start | bytes 2359300
  57.7 11.3 %collective-permute-start = (f32[64,256]{1,0:T(8,128)S(1)}, f32[64,256]{1,0:T(8,128)S(1)}, u32[]{:S(2)}, u32[]{:S(2)}) collective-permute-start(f32[64,256]{1,0:T(8,128)S(1)} %bitcast.25), channel_id=1, source_target_pairs={{0,32},{32,64},{64,96},{96,128},{128,160},{160,192},{192,224},{224... | collective-permute-start | bytes 196616 | tf_op jit(solution)/shard_map/ppermute | solution.py:220
  65.1 4.0 %collective-permute-start.1 = (f32[64,256]{1,0:T(8,128)S(1)}, f32[64,256]{1,0:T(8,128)S(1)}, u32[]{:S(2)}, u32[]{:S(2)}) collective-permute-start(f32[64,256]{1,0:T(8,128)S(1)} %bitcast.26), channel_id=1, source_target_pairs={{0,480},{32,0},{64,32},{96,64},{128,96},{160,128},{192,160},{224,1... | collective-permute-start | bytes 196616 | tf_op jit(solution)/shard_map/ppermute | solution.py:220
  65.1 0.7 copy-start.11
  65.1 0.7 copy-start.12
  70.2 3.7 %collective-permute-start.2 = (f32[64,256]{1,0:T(8,128)S(1)}, f32[64,256]{1,0:T(8,128)S(1)}, u32[]{:S(2)}, u32[]{:S(2)}) collective-permute-start(f32[64,256]{1,0:T(8,128)S(1)} %first_outer.1.refs_0_.refs_9_.v1_ref), channel_id=1, source_target_pairs={{0,480},{32,0},{64,32},{96,64},{128,96},{160,128},{192,160},{224,1... | collective-permute-start | bytes 196616 | tf_op jit(solution)/shard_map/ppermute | solution.py:220
  72.1 6.1 %collective-permute-start.3 = (f32[64,256]{1,0:T(8,128)S(1)}, f32[64,256]{1,0:T(8,128)S(1)}, u32[]{:S(2)}, u32[]{:S(2)}) collective-permute-start(f32[64,256]{1,0:T(8,128)S(1)} %first_outer.1.refs_0_.refs_9_.v1_ref), channel_id=1, source_target_pairs={{0,32},{32,64},{64,96},{96,128},{128,160},{160,192},{192,224},{224... | collective-permute-start | bytes 196616 | tf_op jit(solution)/shard_map/ppermute | solution.py:220
  78.2 11.6 %collective-permute-start.4 = (f32[2,64,256]{2,1,0:T(8,128)S(1)}, f32[2,64,256]{2,1,0:T(8,128)S(1)}, u32[]{:S(2)}, u32[]{:S(2)}) collective-permute-start(f32[2,64,256]{2,1,0:T(8,128)S(1)} %pad_maximum_fusion.2), channel_id=1, source_target_pairs={{0,29},{1,30},{2,31},{3,0},{4,1},{5,2},{6,3},{7,4},{8,5},{9,6},{10... | collective-permute-start | bytes 393224 | tf_op jit(solution)/shard_map/ppermute | solution.py:230
  83.1 7.9 %collective-permute-start.5 = (f32[2,64,256]{2,1,0:T(8,128)S(1)}, f32[2,64,256]{2,1,0:T(8,128)S(1)}, u32[]{:S(2)}, u32[]{:S(2)}) collective-permute-start(f32[2,64,256]{2,1,0:T(8,128)S(1)} %pad_maximum_fusion.2), channel_id=1, source_target_pairs={{0,24},{1,25},{2,26},{3,27},{4,28},{5,29},{6,30},{7,31},{8,0},{9,1... | collective-permute-start | bytes 393224 | tf_op jit(solution)/shard_map/ppermute | solution.py:230
  85.4 9.0 %collective-permute-start.6 = (f32[2,64,256]{2,1,0:T(8,128)S(1)}, f32[2,64,256]{2,1,0:T(8,128)S(1)}, u32[]{:S(2)}, u32[]{:S(2)}) collective-permute-start(f32[2,64,256]{2,1,0:T(8,128)S(1)} %pad_maximum_fusion.2), channel_id=1, source_target_pairs={{0,31},{1,0},{2,1},{3,2},{4,3},{5,4},{6,5},{7,6},{8,7},{9,8},{10,9... | collective-permute-start | bytes 393224 | tf_op jit(solution)/shard_map/ppermute | solution.py:230
  89.8 1.3 copy-start.6
  91.1 0.6 copy-start.8
  94.4 0.8 slice-start.2
  94.4 0.9 slice-start.3
  95.3 11.8 %copy-start.7 = (f32[2,64,256]{2,1,0:T(8,128)S(1)}, f32[2,64,256]{2,1,0:T(8,128)}, u32[]{:S(2)}) copy-start(f32[2,64,256]{2,1,0:T(8,128)} %copy-done.6) | copy-start | bytes 393220
  95.3 11.8 %copy-start.9 = (f32[2,64,256]{2,1,0:T(8,128)S(1)}, f32[2,64,256]{2,1,0:T(8,128)}, u32[]{:S(2)}) copy-start(f32[2,64,256]{2,1,0:T(8,128)} %copy-done.8) | copy-start | bytes 393220
  95.3 11.8 %collective-permute-start.7 = (f32[3,64,256]{2,1,0:T(8,128)S(1)}, f32[3,64,256]{2,1,0:T(8,128)S(1)}, u32[]{:S(2)}, u32[]{:S(2)}) collective-permute-start(f32[3,64,256]{2,1,0:T(8,128)S(1)} %pad_maximum_fusion), channel_id=1, source_target_pairs={{0,32},{32,0},{64,96},{96,64},{128,160},{160,128},{192,224},{224,1... | collective-permute-start | bytes 589832 | tf_op jit(solution)/shard_map/ppermute | solution.py:231
  100.0 7.1 %collective-permute-start.8 = (f32[64,256]{1,0:T(8,128)S(1)}, f32[64,256]{1,0:T(8,128)S(1)}, u32[]{:S(2)}, u32[]{:S(2)}) collective-permute-start(f32[64,256]{1,0:T(8,128)S(1)} %first_outer.1.refs_0_.refs_9_.v1_ref), channel_id=1, source_target_pairs={{0,16},{1,17},{2,18},{3,19},{4,20},{5,21},{6,22},{7,23},{8,24},{9,... | collective-permute-start | bytes 196616 | tf_op jit(solution)/shard_map/ppermute | solution.py:224
  109.3 1.6 collective-permute-start.10
  109.4 3.7 %collective-permute-start.9 = (f32[64,256]{1,0:T(8,128)S(1)}, f32[64,256]{1,0:T(8,128)S(1)}, u32[]{:S(2)}, u32[]{:S(2)}) collective-permute-start(f32[64,256]{1,0:T(8,128)S(1)} %second.1.refs_0_.v2_ref), channel_id=1, source_target_pairs={{0,480},{32,0},{64,32},{96,64},{128,96},{160,128},{192,160},{224,1... | collective-permute-start | bytes 196616 | tf_op jit(solution)/shard_map/ppermute | solution.py:220
  113.1 13.6 %collective-permute-start.11 = (f32[2,64,256]{2,1,0:T(8,128)S(1)}, f32[2,64,256]{2,1,0:T(8,128)S(1)}, u32[]{:S(2)}, u32[]{:S(2)}) collective-permute-start(f32[2,64,256]{2,1,0:T(8,128)S(1)} %pad_maximum_fusion.3), channel_id=1, source_target_pairs={{0,29},{1,30},{2,31},{3,0},{4,1},{5,2},{6,3},{7,4},{8,5},{9,6},{10... | collective-permute-start | bytes 393224 | tf_op jit(solution)/shard_map/ppermute | solution.py:230
  117.7 9.7 %collective-permute-start.12 = (f32[2,64,256]{2,1,0:T(8,128)S(1)}, f32[2,64,256]{2,1,0:T(8,128)S(1)}, u32[]{:S(2)}, u32[]{:S(2)}) collective-permute-start(f32[2,64,256]{2,1,0:T(8,128)S(1)} %pad_maximum_fusion.3), channel_id=1, source_target_pairs={{0,24},{1,25},{2,26},{3,27},{4,28},{5,29},{6,30},{7,31},{8,0},{9,1... | collective-permute-start | bytes 393224 | tf_op jit(solution)/shard_map/ppermute | solution.py:230
  120.1 9.0 %collective-permute-start.13 = (f32[2,64,256]{2,1,0:T(8,128)S(1)}, f32[2,64,256]{2,1,0:T(8,128)S(1)}, u32[]{:S(2)}, u32[]{:S(2)}) collective-permute-start(f32[2,64,256]{2,1,0:T(8,128)S(1)} %pad_maximum_fusion.3), channel_id=1, source_target_pairs={{0,31},{1,0},{2,1},{3,2},{4,3},{5,4},{6,5},{7,6},{8,7},{9,8},{10,9... | collective-permute-start | bytes 393224 | tf_op jit(solution)/shard_map/ppermute | solution.py:230
  126.7 0.6 copy-start.2
  127.4 0.7 copy-start.4
  128.0 1.1 slice-start
  129.2 0.8 slice-start.1
  130.0 10.8 %copy-start.3 = (f32[2,64,256]{2,1,0:T(8,128)S(1)}, f32[2,64,256]{2,1,0:T(8,128)}, u32[]{:S(2)}) copy-start(f32[2,64,256]{2,1,0:T(8,128)} %copy-done.2) | copy-start | bytes 393220
  130.0 10.8 %copy-start.5 = (f32[2,64,256]{2,1,0:T(8,128)S(1)}, f32[2,64,256]{2,1,0:T(8,128)}, u32[]{:S(2)}) copy-start(f32[2,64,256]{2,1,0:T(8,128)} %copy-done.4) | copy-start | bytes 393220
  130.0 10.8 %collective-permute-start.14 = (f32[3,64,256]{2,1,0:T(8,128)S(1)}, f32[3,64,256]{2,1,0:T(8,128)S(1)}, u32[]{:S(2)}, u32[]{:S(2)}) collective-permute-start(f32[3,64,256]{2,1,0:T(8,128)S(1)} %pad_maximum_fusion.1), channel_id=1, source_target_pairs={{0,32},{32,0},{64,96},{96,64},{128,160},{160,128},{192,224},{224,1... | collective-permute-start | bytes 589832 | tf_op jit(solution)/shard_map/ppermute | solution.py:231
  133.7 7.1 %collective-permute-start.15 = (f32[64,256]{1,0:T(8,128)S(1)}, f32[64,256]{1,0:T(8,128)S(1)}, u32[]{:S(2)}, u32[]{:S(2)}) collective-permute-start(f32[64,256]{1,0:T(8,128)S(1)} %second.1.refs_0_.v2_ref), channel_id=1, source_target_pairs={{0,16},{1,17},{2,18},{3,19},{4,20},{5,21},{6,22},{7,23},{8,24},{9,... | collective-permute-start | bytes 196616 | tf_op jit(solution)/shard_map/ppermute | solution.py:224

commit v3 on v2

--- a/solution.py
+++ b/solution.py
@@ -13,7 +13,7 @@
 N_ROW = 32
 N_REGION = 16
 QS = Q // N_ROW
-HOPS = (0, 3, 8, 1, -3, -8, -1, 16)
+HOPS = (0, 1, 8, 3, -1, -8, -3, 16)
 SLOTS = len(HOPS) + 2
 HIGHEST = lax.Precision.HIGHEST
 F32 = jnp.float32
@@ -24,7 +24,13 @@
     return [(i, (i + hop) % count) for i in range(count)]
 
 
-def pack_kernel(queries_ref, perm_ref, out_ref):
+def pack_kernel(queries_hbm, perm_hbm, row_hbm, col_hbm, out_ref, row_ref, col_ref, queries_ref, perm_ref, sems):
+    pairs = ((queries_hbm, queries_ref), (perm_hbm, perm_ref), (row_hbm, row_ref), (col_hbm, col_ref))
+    copies = [pltpu.make_async_copy(src, dst, sems.at[n]) for n, (src, dst) in enumerate(pairs)]
+    for copy in copies:
+        copy.start()
+    for copy in copies:
+        copy.wait()
     perm = perm_ref[...].astype(F32)
     out_ref[:, :, :D] = jnp.broadcast_to(queries_ref[...][None], (N_ROW, QS, D))
     for h in range(HALF):
@@ -46,29 +52,28 @@
             out_ref[pl.ds(q * HALF + h, N_ROW, stride=QS * HALF), :] = kept[q * N_ROW:(q + 1) * N_ROW]
 
 
+GROUPS = 2
+
+
 def permute_kernel(table_ref, packed_ref, out_ref, graph_ref):
     rows = N_ROW * HALF
     perm = packed_ref[:, D:].astype(jnp.int32)
-    groups = rows // 8
-    low = [perm[g * 8:(g + 1) * 8] & (TILE - 1) for g in range(groups)]
-    high = [perm[g * 8:(g + 1) * 8] >> 7 for g in range(groups)]
-
-    def body(sender, acc):
-        acc = [list(a) for a in acc]
-        for h in range(HALF):
-            hits = [high[g] == sender * HALF + h for g in range(groups)]
-            for q in range(QS):
-                line = jnp.broadcast_to(table_ref[pl.ds(sender * (QS * HALF) + q * HALF + h, 1), :], (8, TILE))
-                for g in range(groups):
-                    got = jnp.take_along_axis(line, low[g], axis=1)
-                    acc[q][g] = jnp.where(hits[g], got, acc[q][g])
-        return tuple(tuple(a) for a in acc)
-
-    zero = tuple(tuple(jnp.zeros((8, TILE), F32) for _ in range(groups)) for _ in range(QS))
-    acc = lax.fori_loop(0, N_ROW, body, zero)
-    for q in range(QS):
-        for g in range(groups):
-            graph_ref[q, g * 8:(g + 1) * 8, :] = acc[q][g]
+    for first in range(0, rows, 8 * GROUPS):
+        spans = [slice(first + 8 * g, first + 8 * g + 8) for g in range(GROUPS)]
+        low = [perm[span] & (TILE - 1) for span in spans]
+        high = [perm[span] >> 7 for span in spans]
+        acc = [[jnp.zeros((8, TILE), F32) for _ in spans] for _ in range(QS)]
+        for sender in range(N_ROW):
+            for h in range(HALF):
+                hits = [x == sender * HALF + h for x in high]
+                for q in range(QS):
+                    line = table_ref[(sender * QS + q) * HALF + h:(sender * QS + q) * HALF + h + 1, :]
+                    line = jnp.broadcast_to(line, (8, TILE))
+                    for g in range(GROUPS):
+                        acc[q][g] = jnp.where(hits[g], jnp.take_along_axis(line, low[g], axis=1), acc[q][g])
+        for q in range(QS):
+            for g, span in enumerate(spans):
+                graph_ref[q, span, :] = acc[q][g]
     width = len(HOPS) * QS * HALF
     for q in range(QS):
         for h in range(HALF):
@@ -88,10 +93,17 @@
     return jnp.where(col >= N_ROW * HALF, col - N_ROW * HALF + len(HOPS) * HALF, slot)
 
 
+def split(x):
+    high = x.astype(jnp.bfloat16)
+    return high, (x - high.astype(F32)).astype(jnp.bfloat16)
+
+
 def product(slots_ref, slot, tiles_ref, t):
-    return lax.dot_general(
-        slots_ref[slot], tiles_ref[t], (((1,), (1,)), ((), ())), precision=HIGHEST, preferred_element_type=F32,
-    )
+    high, low = split(slots_ref[slot])
+    tile_high, tile_low = split(tiles_ref[t])
+    contract = (((1,), (1,)), ((), ()))
+    both = lax.dot_general(jnp.concatenate([high, low], axis=0), tile_high, contract, preferred_element_type=F32)
+    return both[:Q] + both[Q:] + lax.dot_general(high, tile_low, contract, preferred_element_type=F32)
 
 
 def spread(slots_ref, k, block):
@@ -108,9 +120,9 @@
                     pl.ds((k * QS + q) * HALF + h, N_ROW, stride=width), :]
     out_ref[...] = jnp.zeros_like(out_ref)
     for t in range(tiles_ref.shape[0]):
-        @pl.when(col_ref[t] < N_ROW * HALF)
-        def _():
-            out_ref[row_ref[t]] += product(slots_ref, tile_slot(col_ref[t], place_ref), tiles_ref, t)
+        inside = col_ref[t] < N_ROW * HALF
+        slot = jnp.where(inside, tile_slot(col_ref[t], place_ref), 0)
+        out_ref[row_ref[t]] += jnp.where(inside, product(slots_ref, slot, tiles_ref, t), 0.0)
 
 
 def outer_kernel(row_ref, col_ref, inner_ref, low_ref, high_ref, tiles_ref, out_ref, slots_ref, acc_ref):
@@ -123,6 +135,16 @@
             acc_ref[row_ref[t]] += product(slots_ref, col_ref[t] - N_ROW * HALF, tiles_ref, t)
     for h in range(HALF):
         out_ref[:, h * TILE:(h + 1) * TILE] = acc_ref[h]
+
+
+def pair_kernel(core_ref, own_ref, low_ref, high_ref, out_ref):
+    out_ref[0] = own_ref[...]
+    out_ref[1] = jnp.where(core_ref[0] == 0, high_ref[...], low_ref[...])
+
+
+def swap_kernel(a_ref, b_ref, c_ref, out_ref):
+    for k, ref in enumerate((a_ref, b_ref, c_ref)):
+        out_ref[k] = ref[1]
 
 
 N_BLOCKS = 8
@@ -144,8 +166,8 @@
 
 def last_kernel(place_ref, row_ref, col_ref, *refs):
     blocks = refs[:N_BLOCKS]
-    v0_ref, v1_ref, tiles_ref, out_ref, moments_ref, slots_ref, acc_ref = refs[N_BLOCKS:]
-    next_kernel(place_ref, row_ref, col_ref, *blocks, tiles_ref, out_ref, slots_ref, acc_ref)
+    v0_ref, v1_ref, tiles_ref, out_ref, moments_ref, *scratch = refs[N_BLOCKS:]
+    next_kernel(place_ref, row_ref, col_ref, *blocks, tiles_ref, out_ref, *scratch)
     vs = [v0_ref[...], v1_ref[...], blocks[0][...], out_ref[...]]
     lane = lax.broadcasted_iota(jnp.int32, (Q, TILE), 1)
     packed = [jnp.zeros((Q, TILE), F32), jnp.zeros((Q, TILE), F32)]
@@ -182,6 +204,7 @@
 
 SMEM = pl.BlockSpec(memory_space=pltpu.SMEM)
 VMEM = pl.BlockSpec(memory_space=pltpu.VMEM)
+HBM = pl.BlockSpec(memory_space=pltpu.MemorySpace.HBM)
 PARAMS = pltpu.CompilerParams(vmem_limit_bytes=32 * 1024 * 1024)
 
 
@@ -197,10 +220,13 @@
     place = jnp.stack([row_index, 1 - 2 * core])
     upward = jnp.stack([row_index, jnp.int32(1)])
 
-    packed = pl.pallas_call(
-        pack_kernel, out_shape=shape(N_ROW, QS, D + TILE), in_specs=[VMEM, VMEM], out_specs=VMEM,
-        compiler_params=PARAMS, name="pack",
-    )(queries, cluster_perm)
+    index = jax.ShapeDtypeStruct(tile_row.shape, jnp.int32)
+    packed, tile_row, tile_col = pl.pallas_call(
+        pack_kernel, out_shape=(shape(N_ROW, QS, D + TILE), index, index), in_specs=[HBM] * 4, out_specs=(VMEM, SMEM, SMEM),
+        scratch_shapes=[pltpu.VMEM(queries.shape, F32), pltpu.VMEM(cluster_perm.shape, jnp.int32),
+                        pltpu.SemaphoreType.DMA((4,))],
+        compiler_params=pltpu.CompilerParams(vmem_limit_bytes=64 * 1024 * 1024), name="pack",
+    )(queries, cluster_perm, tile_row, tile_col)
     packed = lax.all_to_all(packed, "row", 0, 0, tiled=True).reshape(Q, D + TILE)
     by_query = pl.pallas_call(
         scores_kernel, out_shape=shape(N_ROW * QS * HALF, TILE), in_specs=[SMEM, VMEM, VMEM, VMEM], out_specs=VMEM,
@@ -220,15 +246,21 @@
         return (lax.ppermute(v, "region", ring(N_REGION, 1)), lax.ppermute(v, "region", ring(N_REGION, -1)))
 
     def exchange(v):
-        low, high = region_pair(v)
-        far = lax.ppermute(v, "row", ring(N_ROW, 16))
-        both = jnp.stack([v, jnp.where(core == 0, high, low)])
+        far, low, high = lax.optimization_barrier((lax.ppermute(v, "row", ring(N_ROW, 16)), *region_pair(v)))
+        both = pl.pallas_call(
+            pair_kernel, out_shape=shape(2, Q, ROWS), in_specs=[SMEM] + [VMEM] * 3, out_specs=VMEM,
+            compiler_params=PARAMS, name="pair",
+        )(core[None], v, low, high)
         got = []
         for hop in HOPS[1:4]:
             pairs = [(r * N_ROW + i, r * N_ROW + (i - (hop if r % 2 == 0 else -hop)) % N_ROW)
                      for r in range(N_REGION) for i in range(N_ROW)]
             got.append(lax.ppermute(both, ("region", "row"), pairs))
-        swapped = lax.ppermute(jnp.stack([g[1] for g in got]), "region", [(r, r ^ 1) for r in range(N_REGION)])
+        swapped = pl.pallas_call(
+            swap_kernel, out_shape=shape(len(got), Q, ROWS), in_specs=[VMEM] * len(got), out_specs=VMEM,
+            compiler_params=PARAMS, name="swap",
+        )(*got)
+        swapped = lax.ppermute(swapped, "region", [(r, r ^ 1) for r in range(N_REGION)])
         return [v] + got + [swapped, far, low, high]
 
     slots = pltpu.VMEM((SLOTS * HALF, Q, TILE), F32)

time: 175 us -> 158 us (0.903)
  Pallas kernels: 17.1 us -> 10.9 us
  waiting for transfers between devices: 35.8 us -> 30.7 us
  local copies, waits for them, and re-layouts: 5.97 us -> 0.91 us
  blocking collectives: 58 us -> 55.9 us
  starting transfers between devices: 55.8 us -> 57.6 us
    ppermute x3, starting transfers between devices: 2.68 us -> 12.1 us  [region_pair(): lax.ppermute(v, 'region', ring(N_REGION, -1))]
    ppermute x3, waiting for transfers between devices: 4.98 us -> 0.36 us  [region_pair(): lax.ppermute(v, 'region', ring(N_REGION, 1))]
    ppermute x3, waiting for transfers between devices: 4.01 us -> 0.01 us  [region_pair(): lax.ppermute(v, 'region', ring(N_REGION, -1))]
    ppermute x4, starting transfers between devices: 15.5 us -> 11.6 us  [the longest x2 6.6 us: exchange(): lax.ppermute(v, 'row', ring(N_ROW, 16))]
    ppermute x3, starting transfers between devices: 7.36 us -> 3.61 us  [region_pair(): lax.ppermute(v, 'region', ring(N_REGION, 1))]
    unnamed x32 -> x12, local copies, waits for them, and re-layouts: 4.06 us -> 0.7 us
    pallas_call x1, Pallas kernels: 5.39 us -> 2.25 us  [local(): pl.pallas_call(permute_kernel, out_shape=shape(N_ROW * width, TILE), in_s...]
    all_to_all x1, blocking collectives: 14.4 us -> 12.2 us  [local(): lax.all_to_all(jnp.broadcast_to(moments[None], (N_REGION, 4, TILE)), 'reg...]
  transfers between devices with their start and end apart: 17 -> 17, of which waited for: 12 -> 11; matrix products, arithmetic and copies ran while one was open for 0% -> 0% of each run, Pallas kernels for 2% -> 1%
where the time goes in v3:
time: 158 us; the launch traced here: 157 us
  starting transfers between devices  57.6 us (36%)
  blocking collectives  55.9 us (35%)
  waiting for transfers between devices  30.7 us (19%)
  Pallas kernels  10.9 us (7%)
    ppermute x6, starting transfers between devices, exchange(): got.append(lax.ppermute(both, ('region', 'row'), pairs))  19.6 us
    all_to_all x1, blocking collectives, local(): lax.all_to_all(near.reshape(N_ROW, width, TILE), 'row', 0, 0, tiled=True)  15.5 us
    all_to_all x1, blocking collectives, local(): lax.all_to_all(jnp.broadcast_to(moments[None], (N_ROW, 4, TILE)), 'row',...  14.9 us
    all_to_all x1, blocking collectives, local(): lax.all_to_all(by_query.reshape(N_ROW, QS * HALF, TILE), 'row', 0, 0, til...  13.3 us
    ppermute x6, waiting for transfers between devices, exchange(): got.append(lax.ppermute(both, ('region', 'row'), pairs))  12.4 us
    all_to_all x1, blocking collectives, local(): lax.all_to_all(jnp.broadcast_to(moments[None], (N_REGION, 4, TILE)), 'reg...  12.2 us
    ppermute x3, starting transfers between devices, region_pair(): lax.ppermute(v, 'region', ring(N_REGION, -1))  12.1 us
    all_to_all x1, starting transfers between devices, local(): lax.all_to_all(packed, 'row', 0, 0, tiled=True).reshape(Q, D + TILE)  10.6 us
  transfers between devices with their start and end apart: 17, of which 11 were waited for; matrix products, arithmetic and copies ran while one was open for 0% of the time, Pallas kernels for 1%

profile of v3, /device:TPU:1, one launch (start us, length us, event | category | flops | bytes accessed | tf_op | source)
XLA Modules:
  0.0 157.1 jit_solution(16938742744718402685)
XLA Ops:
  0.6 1.5 pack.1
  2.2 0.0 copy-start.1
  2.2 10.6 %all-to-all-start = ((f32[32,2,640]{2,1,0:T(2,128)}), f32[32,2,640]{2,1,0:T(2,128)S(1)}, u32[]{:S(2)}, u32[]{:S(2)}) async-start(f32[32,2,640]{2,1,0:T(2,128)} %get-tuple-element.15), calls=%async_computation | async-start | bytes 327680 | tf_op jit(solution)/shard_map/all_to_all | solution.py:230
  12.8 0.0 copy-start.2
  12.9 9.3 %all-to-all-done = f32[32,2,640]{2,1,0:T(2,128)S(1)} async-done(((f32[32,2,640]{2,1,0:T(2,128)}), f32[32,2,640]{2,1,0:T(2,128)S(1)}, u32[]{:S(2)}, u32[]{:S(2)}) %all-to-all-start) | async-done | bytes 163872 | tf_op jit(solution)/shard_map/all_to_all | solution.py:230
  22.2 0.1 reshape.28.packed_ref
  22.3 0.6 scores.1
  23.0 13.3 %all_to_all.25 = f32[32,4,128]{2,1,0:T(4,128)S(1)} all-to-all(f32[32,4,128]{2,1,0:T(4,128)S(1)} %bitcast.23), channel_id=1, replica_groups=mesh['region'=16,'row'=32] {'row'}, dimensions={0} | all-to-all | bytes 131072 | tf_op jit(solution)/shard_map/all_to_all | solution.py:235
  36.3 2.3 %permute.1 = f32[1024,128]{1,0:T(8,128)S(1)} custom-call(f32[128,128]{1,0:T(8,128)S(1)} %bitcast.22, f32[64,640]{1,0:T(8,128)S(1)} %reshape.28.packed_ref), custom_call_target="tpu_custom_call" | custom-call | tf_op jit(solution)/shard_map/permute/pallas_call | solution.py:237
  38.5 0.0 copy-start
  38.5 15.5 %all_to_all.26 = f32[32,32,128]{2,1,0:T(8,128)S(1)} all-to-all(f32[32,32,128]{2,1,0:T(8,128)S(1)} %bitcast.17), channel_id=1, replica_groups=mesh['region'=16,'row'=32] {'row'}, dimensions={0} | all-to-all | bytes 1048576 | tf_op jit(solution)/shard_map/all_to_all | solution.py:242
  54.1 0.1 copy.17
  54.2 5.4 %collective-permute-start.1 = (f32[64,256]{1,0:T(8,128)S(1)}, f32[64,256]{1,0:T(8,128)S(1)}, u32[]{:S(2)}, u32[]{:S(2)}) collective-permute-start(f32[64,256]{1,0:T(8,128)S(1)} %bitcast.18), channel_id=1, source_target_pairs={{0,480},{32,0},{64,32},{96,64},{128,96},{160,128},{192,160},{224,1... | collective-permute-start | bytes 196616 | tf_op jit(solution)/shard_map/ppermute | solution.py:246
  59.5 2.0 %collective-permute-start = (f32[64,256]{1,0:T(8,128)S(1)}, f32[64,256]{1,0:T(8,128)S(1)}, u32[]{:S(2)}, u32[]{:S(2)}) collective-permute-start(f32[64,256]{1,0:T(8,128)S(1)} %bitcast.19), channel_id=1, source_target_pairs={{0,32},{32,64},{64,96},{96,128},{128,160},{160,192},{192,224},{224... | collective-permute-start | bytes 196616 | tf_op jit(solution)/shard_map/ppermute | solution.py:246
  61.5 0.1 pad_add_fusion.1.place_ref
  61.6 0.6 copy-done.3
  62.3 0.0 copy-done.4
  62.3 1.4 first_inner.1.inner_ref
  63.7 0.4 collective-permute-done.low_ref
  64.1 1.0 first_outer.1.own_ref.refs_0_.refs_9_.v1_ref
  65.1 6.6 %collective-permute-start.4 = (f32[64,256]{1,0:T(8,128)S(1)}, f32[64,256]{1,0:T(8,128)S(1)}, u32[]{:S(2)}, u32[]{:S(2)}) collective-permute-start(f32[64,256]{1,0:T(8,128)S(1)} %first_outer.1.own_ref.refs_0_.refs_9_.v1_ref), channel_id=1, source_target_pairs={{0,480},{32,0},{64,32},{96,64},{128,96},{160,128},{192,160},{224,1... | collective-permute-start | bytes 196616 | tf_op jit(solution)/shard_map/ppermute | solution.py:246
  71.6 3.3 %collective-permute-start.2 = (f32[64,256]{1,0:T(8,128)S(1)}, f32[64,256]{1,0:T(8,128)S(1)}, u32[]{:S(2)}, u32[]{:S(2)}) collective-permute-start(f32[64,256]{1,0:T(8,128)S(1)} %first_outer.1.own_ref.refs_0_.refs_9_.v1_ref), channel_id=1, source_target_pairs={{0,16},{1,17},{2,18},{3,19},{4,20},{5,21},{6,22},{7,23},{8,24},{9,... | collective-permute-start | bytes 196616 | tf_op jit(solution)/shard_map/ppermute | solution.py:249
  75.0 3.1 %collective-permute-done.2.refs_5_ = f32[64,256]{1,0:T(8,128)S(1)} collective-permute-done((f32[64,256]{1,0:T(8,128)S(1)}, f32[64,256]{1,0:T(8,128)S(1)}, u32[]{:S(2)}, u32[]{:S(2)}) %collective-permute-start.2) | collective-permute-done | bytes 65568 | tf_op jit(solution)/shard_map/ppermute | solution.py:249
  78.1 5.0 %collective-permute-start.7 = (f32[2,64,256]{2,1,0:T(8,128)S(1)}, f32[2,64,256]{2,1,0:T(8,128)S(1)}, u32[]{:S(2)}, u32[]{:S(2)}) collective-permute-start(f32[2,64,256]{2,1,0:T(8,128)S(1)} %pair.2), channel_id=1, source_target_pairs={{0,29},{1,30},{2,31},{3,0},{4,1},{5,2},{6,3},{7,4},{8,5},{9,6},{10... | collective-permute-start | bytes 393224 | tf_op jit(solution)/shard_map/ppermute | solution.py:258
  83.1 2.2 %collective-permute-start.6 = (f32[2,64,256]{2,1,0:T(8,128)S(1)}, f32[2,64,256]{2,1,0:T(8,128)S(1)}, u32[]{:S(2)}, u32[]{:S(2)}) collective-permute-start(f32[2,64,256]{2,1,0:T(8,128)S(1)} %pair.2), channel_id=1, source_target_pairs={{0,24},{1,25},{2,26},{3,27},{4,28},{5,29},{6,30},{7,31},{8,0},{9,1... | collective-permute-start | bytes 393224 | tf_op jit(solution)/shard_map/ppermute | solution.py:258
  85.3 2.0 %collective-permute-start.5 = (f32[2,64,256]{2,1,0:T(8,128)S(1)}, f32[2,64,256]{2,1,0:T(8,128)S(1)}, u32[]{:S(2)}, u32[]{:S(2)}) collective-permute-start(f32[2,64,256]{2,1,0:T(8,128)S(1)} %pair.2), channel_id=1, source_target_pairs={{0,31},{1,0},{2,1},{3,2},{4,3},{5,4},{6,5},{7,6},{8,7},{9,8},{10,9... | collective-permute-start | bytes 393224 | tf_op jit(solution)/shard_map/ppermute | solution.py:258
  87.3 2.4 %collective-permute-done.7.c_ref.refs_3_ = f32[2,64,256]{2,1,0:T(8,128)S(1)} collective-permute-done((f32[2,64,256]{2,1,0:T(8,128)S(1)}, f32[2,64,256]{2,1,0:T(8,128)S(1)}, u32[]{:S(2)}, u32[]{:S(2)}) %collective-permute-start.7) | collective-permute-done | bytes 131104 | tf_op jit(solution)/shard_map/ppermute | solution.py:258
  89.7 1.3 collective-permute-done.6.b_ref.refs_2_
  91.0 3.3 %collective-permute-done.5.a_ref.refs_1_ = f32[2,64,256]{2,1,0:T(8,128)S(1)} collective-permute-done((f32[2,64,256]{2,1,0:T(8,128)S(1)}, f32[2,64,256]{2,1,0:T(8,128)S(1)}, u32[]{:S(2)}, u32[]{:S(2)}) %collective-permute-start.5) | collective-permute-done | bytes 131104 | tf_op jit(solution)/shard_map/ppermute | solution.py:258
  94.4 2.1 %collective-permute-start.8 = (f32[3,64,256]{2,1,0:T(8,128)S(1)}, f32[3,64,256]{2,1,0:T(8,128)S(1)}, u32[]{:S(2)}, u32[]{:S(2)}) collective-permute-start(f32[3,64,256]{2,1,0:T(8,128)S(1)} %swap.2), channel_id=1, source_target_pairs={{0,32},{32,0},{64,96},{96,64},{128,160},{160,128},{192,224},{224,1... | collective-permute-start | bytes 589832 | tf_op jit(solution)/shard_map/ppermute | solution.py:263
  96.5 0.1 pad_add_fusion.place_ref
  96.5 1.2 collective-permute-done.8.refs_4_
  97.7 1.2 second.1.own_ref.refs_0_.v2_ref
  98.9 0.2 collective-permute-start.11
  99.1 1.6 %collective-permute-start.10 = (f32[64,256]{1,0:T(8,128)S(1)}, f32[64,256]{1,0:T(8,128)S(1)}, u32[]{:S(2)}, u32[]{:S(2)}) collective-permute-start(f32[64,256]{1,0:T(8,128)S(1)} %second.1.own_ref.refs_0_.v2_ref), channel_id=1, source_target_pairs={{0,32},{32,64},{64,96},{96,128},{128,160},{160,192},{192,224},{224... | collective-permute-start | bytes 196616 | tf_op jit(solution)/shard_map/ppermute | solution.py:246
  100.7 3.3 %collective-permute-start.9 = (f32[64,256]{1,0:T(8,128)S(1)}, f32[64,256]{1,0:T(8,128)S(1)}, u32[]{:S(2)}, u32[]{:S(2)}) collective-permute-start(f32[64,256]{1,0:T(8,128)S(1)} %second.1.own_ref.refs_0_.v2_ref), channel_id=1, source_target_pairs={{0,16},{1,17},{2,18},{3,19},{4,20},{5,21},{6,22},{7,23},{8,24},{9,... | collective-permute-start | bytes 196616 | tf_op jit(solution)/shard_map/ppermute | solution.py:249
  104.0 3.2 %collective-permute-done.9.refs_5_ = f32[64,256]{1,0:T(8,128)S(1)} collective-permute-done((f32[64,256]{1,0:T(8,128)S(1)}, f32[64,256]{1,0:T(8,128)S(1)}, u32[]{:S(2)}, u32[]{:S(2)}) %collective-permute-start.9) | collective-permute-done | bytes 65568 | tf_op jit(solution)/shard_map/ppermute | solution.py:249
  107.2 4.3 %collective-permute-start.14 = (f32[2,64,256]{2,1,0:T(8,128)S(1)}, f32[2,64,256]{2,1,0:T(8,128)S(1)}, u32[]{:S(2)}, u32[]{:S(2)}) collective-permute-start(f32[2,64,256]{2,1,0:T(8,128)S(1)} %pair.3), channel_id=1, source_target_pairs={{0,29},{1,30},{2,31},{3,0},{4,1},{5,2},{6,3},{7,4},{8,5},{9,6},{10... | collective-permute-start | bytes 393224 | tf_op jit(solution)/shard_map/ppermute | solution.py:258
  111.5 2.5 %collective-permute-start.13 = (f32[2,64,256]{2,1,0:T(8,128)S(1)}, f32[2,64,256]{2,1,0:T(8,128)S(1)}, u32[]{:S(2)}, u32[]{:S(2)}) collective-permute-start(f32[2,64,256]{2,1,0:T(8,128)S(1)} %pair.3), channel_id=1, source_target_pairs={{0,24},{1,25},{2,26},{3,27},{4,28},{5,29},{6,30},{7,31},{8,0},{9,1... | collective-permute-start | bytes 393224 | tf_op jit(solution)/shard_map/ppermute | solution.py:258
  114.0 3.6 %collective-permute-start.12 = (f32[2,64,256]{2,1,0:T(8,128)S(1)}, f32[2,64,256]{2,1,0:T(8,128)S(1)}, u32[]{:S(2)}, u32[]{:S(2)}) collective-permute-start(f32[2,64,256]{2,1,0:T(8,128)S(1)} %pair.3), channel_id=1, source_target_pairs={{0,31},{1,0},{2,1},{3,2},{4,3},{5,4},{6,5},{7,6},{8,7},{9,8},{10,9... | collective-permute-start | bytes 393224 | tf_op jit(solution)/shard_map/ppermute | solution.py:258
  117.6 3.2 %collective-permute-done.14.c_ref.refs_3_ = f32[2,64,256]{2,1,0:T(8,128)S(1)} collective-permute-done((f32[2,64,256]{2,1,0:T(8,128)S(1)}, f32[2,64,256]{2,1,0:T(8,128)S(1)}, u32[]{:S(2)}, u32[]{:S(2)}) %collective-permute-start.14) | collective-permute-done | bytes 131104 | tf_op jit(solution)/shard_map/ppermute | solution.py:258
  120.8 2.2 %collective-permute-done.12.a_ref.refs_1_ = f32[2,64,256]{2,1,0:T(8,128)S(1)} collective-permute-done((f32[2,64,256]{2,1,0:T(8,128)S(1)}, f32[2,64,256]{2,1,0:T(8,128)S(1)}, u32[]{:S(2)}, u32[]{:S(2)}) %collective-permute-start.12) | collective-permute-done | bytes 131104 | tf_op jit(solution)/shard_map/ppermute | solution.py:258
  123.0 3.0 %collective-permute-start.15 = (f32[3,64,256]{2,1,0:T(8,128)S(1)}, f32[3,64,256]{2,1,0:T(8,128)S(1)}, u32[]{:S(2)}, u32[]{:S(2)}) collective-permute-start(f32[3,64,256]{2,1,0:T(8,128)S(1)} %swap.3), channel_id=1, source_target_pairs={{0,32},{32,0},{64,96},{96,64},{128,160},{160,128},{192,224},{224,1... | collective-permute-start | bytes 589832 | tf_op jit(solution)/shard_map/ppermute | solution.py:263
  126.1 1.0 collective-permute-done.15.refs_4_
  127.1 1.3 third.1
  128.4 14.9 %all_to_all.27 = f32[32,4,128]{2,1,0:T(4,128)S(1)} all-to-all(f32[32,4,128]{2,1,0:T(4,128)S(1)} %broadcast_in_dim.10), channel_id=1, replica_groups=mesh['region'=16,'row'=32] {'row'}, dimensions={0} | all-to-all | bytes 131072 | tf_op jit(solution)/shard_map/all_to_all | solution.py:289
  143.4 12.2 %all_to_all.28.moments_ref = f32[16,4,128]{2,1,0:T(4,128)S(1)} all-to-all(f32[16,4,128]{2,1,0:T(4,128)S(1)} %broadcast_in_dim.22), channel_id=1, replica_groups=mesh['region'=16,'row'=32] {'region'}, dimensions={0} | all-to-all | bytes 65536 | tf_op jit(solution)/shard_map/all_to_all | solution.py:291
  155.6 1.5 finish.1
  (22 shorter events, 0.2 us)
Async XLA Ops:
  2.2 20.1 %copy-start.1 = (f32[256,512]{1,0:T(8,128)S(1)}, f32[256,512]{1,0:T(8,128)}, u32[]{:S(2)}) copy-start(f32[256,512]{1,0:T(8,128)} %desc_ref.1) | copy-start | bytes 1572868
  2.2 20.0 %all-to-all-start = ((f32[32,2,640]{2,1,0:T(2,128)}), f32[32,2,640]{2,1,0:T(2,128)S(1)}, u32[]{:S(2)}, u32[]{:S(2)}) async-start(f32[32,2,640]{2,1,0:T(2,128)} %get-tuple-element.15), calls=%async_computation | async-start | bytes 327680 | tf_op jit(solution)/shard_map/all_to_all | solution.py:230
  12.8 9.5 %copy-start.2 = (s32[64,64]{1,0:T(8,128)S(1)}, s32[64,64]{1,0:T(8,128)}, u32[]{:S(2)}) copy-start(s32[64,64]{1,0:T(8,128)} %cand_ref.1) | copy-start | bytes 49156
  38.5 23.1 %copy-start = (f32[12,128,128]{2,1,0:T(8,128)S(1)}, f32[12,128,128]{2,1,0:T(8,128)}, u32[]{:S(2)}) copy-start(f32[12,128,128]{2,1,0:T(8,128)} %refs_10_.1) | copy-start | bytes 2359300
  54.2 9.6 %collective-permute-start.1 = (f32[64,256]{1,0:T(8,128)S(1)}, f32[64,256]{1,0:T(8,128)S(1)}, u32[]{:S(2)}, u32[]{:S(2)}) collective-permute-start(f32[64,256]{1,0:T(8,128)S(1)} %bitcast.18), channel_id=1, source_target_pairs={{0,480},{32,0},{64,32},{96,64},{128,96},{160,128},{192,160},{224,1... | collective-permute-start | bytes 196616 | tf_op jit(solution)/shard_map/ppermute | solution.py:246
  59.5 4.6 %collective-permute-start = (f32[64,256]{1,0:T(8,128)S(1)}, f32[64,256]{1,0:T(8,128)S(1)}, u32[]{:S(2)}, u32[]{:S(2)}) collective-permute-start(f32[64,256]{1,0:T(8,128)S(1)} %bitcast.19), channel_id=1, source_target_pairs={{0,32},{32,64},{64,96},{96,128},{128,160},{160,192},{192,224},{224... | collective-permute-start | bytes 196616 | tf_op jit(solution)/shard_map/ppermute | solution.py:246
  61.6 0.7 copy-start.3
  61.6 0.7 copy-start.4
  65.1 9.9 %collective-permute-start.4 = (f32[64,256]{1,0:T(8,128)S(1)}, f32[64,256]{1,0:T(8,128)S(1)}, u32[]{:S(2)}, u32[]{:S(2)}) collective-permute-start(f32[64,256]{1,0:T(8,128)S(1)} %first_outer.1.own_ref.refs_0_.refs_9_.v1_ref), channel_id=1, source_target_pairs={{0,480},{32,0},{64,32},{96,64},{128,96},{160,128},{192,160},{224,1... | collective-permute-start | bytes 196616 | tf_op jit(solution)/shard_map/ppermute | solution.py:246
  71.6 3.4 %collective-permute-start.3 = (f32[64,256]{1,0:T(8,128)S(1)}, f32[64,256]{1,0:T(8,128)S(1)}, u32[]{:S(2)}, u32[]{:S(2)}) collective-permute-start(f32[64,256]{1,0:T(8,128)S(1)} %first_outer.1.own_ref.refs_0_.refs_9_.v1_ref), channel_id=1, source_target_pairs={{0,32},{32,64},{64,96},{96,128},{128,160},{160,192},{192,224},{224... | collective-permute-start | bytes 196616 | tf_op jit(solution)/shard_map/ppermute | solution.py:246
  71.6 6.5 %collective-permute-start.2 = (f32[64,256]{1,0:T(8,128)S(1)}, f32[64,256]{1,0:T(8,128)S(1)}, u32[]{:S(2)}, u32[]{:S(2)}) collective-permute-start(f32[64,256]{1,0:T(8,128)S(1)} %first_outer.1.own_ref.refs_0_.refs_9_.v1_ref), channel_id=1, source_target_pairs={{0,16},{1,17},{2,18},{3,19},{4,20},{5,21},{6,22},{7,23},{8,24},{9,... | collective-permute-start | bytes 196616 | tf_op jit(solution)/shard_map/ppermute | solution.py:249
  78.1 11.6 %collective-permute-start.7 = (f32[2,64,256]{2,1,0:T(8,128)S(1)}, f32[2,64,256]{2,1,0:T(8,128)S(1)}, u32[]{:S(2)}, u32[]{:S(2)}) collective-permute-start(f32[2,64,256]{2,1,0:T(8,128)S(1)} %pair.2), channel_id=1, source_target_pairs={{0,29},{1,30},{2,31},{3,0},{4,1},{5,2},{6,3},{7,4},{8,5},{9,6},{10... | collective-permute-start | bytes 393224 | tf_op jit(solution)/shard_map/ppermute | solution.py:258
  83.1 7.9 %collective-permute-start.6 = (f32[2,64,256]{2,1,0:T(8,128)S(1)}, f32[2,64,256]{2,1,0:T(8,128)S(1)}, u32[]{:S(2)}, u32[]{:S(2)}) collective-permute-start(f32[2,64,256]{2,1,0:T(8,128)S(1)} %pair.2), channel_id=1, source_target_pairs={{0,24},{1,25},{2,26},{3,27},{4,28},{5,29},{6,30},{7,31},{8,0},{9,1... | collective-permute-start | bytes 393224 | tf_op jit(solution)/shard_map/ppermute | solution.py:258
  85.3 9.0 %collective-permute-start.5 = (f32[2,64,256]{2,1,0:T(8,128)S(1)}, f32[2,64,256]{2,1,0:T(8,128)S(1)}, u32[]{:S(2)}, u32[]{:S(2)}) collective-permute-start(f32[2,64,256]{2,1,0:T(8,128)S(1)} %pair.2), channel_id=1, source_target_pairs={{0,31},{1,0},{2,1},{3,2},{4,3},{5,4},{6,5},{7,6},{8,7},{9,8},{10,9... | collective-permute-start | bytes 393224 | tf_op jit(solution)/shard_map/ppermute | solution.py:258
  94.4 3.3 %collective-permute-start.8 = (f32[3,64,256]{2,1,0:T(8,128)S(1)}, f32[3,64,256]{2,1,0:T(8,128)S(1)}, u32[]{:S(2)}, u32[]{:S(2)}) collective-permute-start(f32[3,64,256]{2,1,0:T(8,128)S(1)} %swap.2), channel_id=1, source_target_pairs={{0,32},{32,0},{64,96},{96,64},{128,160},{160,128},{192,224},{224,1... | collective-permute-start | bytes 589832 | tf_op jit(solution)/shard_map/ppermute | solution.py:263
  98.9 5.0 %collective-permute-start.11 = (f32[64,256]{1,0:T(8,128)S(1)}, f32[64,256]{1,0:T(8,128)S(1)}, u32[]{:S(2)}, u32[]{:S(2)}) collective-permute-start(f32[64,256]{1,0:T(8,128)S(1)} %second.1.own_ref.refs_0_.v2_ref), channel_id=1, source_target_pairs={{0,480},{32,0},{64,32},{96,64},{128,96},{160,128},{192,160},{224,1... | collective-permute-start | bytes 196616 | tf_op jit(solution)/shard_map/ppermute | solution.py:246
  99.1 4.9 %collective-permute-start.10 = (f32[64,256]{1,0:T(8,128)S(1)}, f32[64,256]{1,0:T(8,128)S(1)}, u32[]{:S(2)}, u32[]{:S(2)}) collective-permute-start(f32[64,256]{1,0:T(8,128)S(1)} %second.1.own_ref.refs_0_.v2_ref), channel_id=1, source_target_pairs={{0,32},{32,64},{64,96},{96,128},{128,160},{160,192},{192,224},{224... | collective-permute-start | bytes 196616 | tf_op jit(solution)/shard_map/ppermute | solution.py:246
  100.7 6.5 %collective-permute-start.9 = (f32[64,256]{1,0:T(8,128)S(1)}, f32[64,256]{1,0:T(8,128)S(1)}, u32[]{:S(2)}, u32[]{:S(2)}) collective-permute-start(f32[64,256]{1,0:T(8,128)S(1)} %second.1.own_ref.refs_0_.v2_ref), channel_id=1, source_target_pairs={{0,16},{1,17},{2,18},{3,19},{4,20},{5,21},{6,22},{7,23},{8,24},{9,... | collective-permute-start | bytes 196616 | tf_op jit(solution)/shard_map/ppermute | solution.py:249
  107.2 13.6 %collective-permute-start.14 = (f32[2,64,256]{2,1,0:T(8,128)S(1)}, f32[2,64,256]{2,1,0:T(8,128)S(1)}, u32[]{:S(2)}, u32[]{:S(2)}) collective-permute-start(f32[2,64,256]{2,1,0:T(8,128)S(1)} %pair.3), channel_id=1, source_target_pairs={{0,29},{1,30},{2,31},{3,0},{4,1},{5,2},{6,3},{7,4},{8,5},{9,6},{10... | collective-permute-start | bytes 393224 | tf_op jit(solution)/shard_map/ppermute | solution.py:258
  111.5 9.3 %collective-permute-start.13 = (f32[2,64,256]{2,1,0:T(8,128)S(1)}, f32[2,64,256]{2,1,0:T(8,128)S(1)}, u32[]{:S(2)}, u32[]{:S(2)}) collective-permute-start(f32[2,64,256]{2,1,0:T(8,128)S(1)} %pair.3), channel_id=1, source_target_pairs={{0,24},{1,25},{2,26},{3,27},{4,28},{5,29},{6,30},{7,31},{8,0},{9,1... | collective-permute-start | bytes 393224 | tf_op jit(solution)/shard_map/ppermute | solution.py:258
  114.0 9.0 %collective-permute-start.12 = (f32[2,64,256]{2,1,0:T(8,128)S(1)}, f32[2,64,256]{2,1,0:T(8,128)S(1)}, u32[]{:S(2)}, u32[]{:S(2)}) collective-permute-start(f32[2,64,256]{2,1,0:T(8,128)S(1)} %pair.3), channel_id=1, source_target_pairs={{0,31},{1,0},{2,1},{3,2},{4,3},{5,4},{6,5},{7,6},{8,7},{9,8},{10,9... | collective-permute-start | bytes 393224 | tf_op jit(solution)/shard_map/ppermute | solution.py:258
  123.0 4.1 %collective-permute-start.15 = (f32[3,64,256]{2,1,0:T(8,128)S(1)}, f32[3,64,256]{2,1,0:T(8,128)S(1)}, u32[]{:S(2)}, u32[]{:S(2)}) collective-permute-start(f32[3,64,256]{2,1,0:T(8,128)S(1)} %swap.3), channel_id=1, source_target_pairs={{0,32},{32,0},{64,96},{96,64},{128,160},{160,128},{192,224},{224,1... | collective-permute-start | bytes 589832 | tf_op jit(solution)/shard_map/ppermute | solution.py:263

commit v4 on v3

--- a/solution.py
+++ b/solution.py
@@ -13,7 +13,10 @@
 N_ROW = 32
 N_REGION = 16
 QS = Q // N_ROW
-HOPS = (0, 1, 8, 3, -1, -8, -3, 16)
+HOPS = (0, 1, -1, 3, -3, 8, -8, 16)
+N_X = 4
+N_Y = 8
+SHARED = (1, 3)
 SLOTS = len(HOPS) + 2
 HIGHEST = lax.Precision.HIGHEST
 F32 = jnp.float32
@@ -84,13 +87,22 @@
                 out_ref[pl.ds((k * QS + q) * HALF + h, N_ROW, stride=width), :] = rolled
 
 
-def tile_slot(col, place_ref):
-    hop = (((col >> 1) - place_ref[0]) * place_ref[1]) & (N_ROW - 1)
+def near_slot(col, place_ref):
+    hop = ((col >> 1) - place_ref[0]) & (N_ROW - 1)
     slot = jnp.int32(0)
     for k, h in enumerate(HOPS):
         slot = jnp.where(hop == h % N_ROW, k, slot)
+    return slot * HALF + (col & 1)
+
+
+def any_slot(col, place_ref):
+    owner = col >> 1
+    hop = owner - place_ref[0]
+    slot = owner >> 3
+    for k, h in enumerate(SHARED + tuple(-h for h in SHARED)):
+        slot = jnp.where(((hop * place_ref[1]) & (N_ROW - 1)) == h % N_ROW, N_X + k, slot)
     slot = slot * HALF + (col & 1)
-    return jnp.where(col >= N_ROW * HALF, col - N_ROW * HALF + len(HOPS) * HALF, slot)
+    return jnp.where(col >= N_ROW * HALF, col - N_ROW * HALF + (N_X + 2 * len(SHARED)) * HALF, slot)
 
 
 def split(x):
@@ -121,7 +133,7 @@
     out_ref[...] = jnp.zeros_like(out_ref)
     for t in range(tiles_ref.shape[0]):
         inside = col_ref[t] < N_ROW * HALF
-        slot = jnp.where(inside, tile_slot(col_ref[t], place_ref), 0)
+        slot = jnp.where(inside, near_slot(col_ref[t], place_ref), 0)
         out_ref[row_ref[t]] += jnp.where(inside, product(slots_ref, slot, tiles_ref, t), 0.0)
 
 
@@ -142,24 +154,25 @@
     out_ref[1] = jnp.where(core_ref[0] == 0, high_ref[...], low_ref[...])
 
 
-def swap_kernel(a_ref, b_ref, c_ref, out_ref):
-    for k, ref in enumerate((a_ref, b_ref, c_ref)):
+def swap_kernel(*refs):
+    *got, out_ref = refs
+    for k, ref in enumerate(got):
         out_ref[k] = ref[1]
 
 
-N_BLOCKS = 8
+N_BLOCKS = 7
 
 
 def next_kernel(place_ref, row_ref, col_ref, *refs):
-    own, a_ref, b_ref, c_ref, swapped_ref, far_ref, low_ref, high_ref = refs[:N_BLOCKS]
+    _, line_ref, a_ref, b_ref, swapped_ref, low_ref, high_ref = refs[:N_BLOCKS]
     tiles_ref, out_ref, slots_ref, acc_ref = refs[N_BLOCKS:]
-    blocks = [own[...], a_ref[0], b_ref[0], c_ref[0], swapped_ref[0], swapped_ref[1], swapped_ref[2],
-              far_ref[...], low_ref[...], high_ref[...]]
+    blocks = [line_ref[x] for x in range(N_X)] + [
+        a_ref[0], b_ref[0], swapped_ref[0], swapped_ref[1], low_ref[...], high_ref[...]]
     for k, block in enumerate(blocks):
         spread(slots_ref, k, block)
     acc_ref[...] = jnp.zeros_like(acc_ref)
     for t in range(tiles_ref.shape[0]):
-        acc_ref[row_ref[t]] += product(slots_ref, tile_slot(col_ref[t], place_ref), tiles_ref, t)
+        acc_ref[row_ref[t]] += product(slots_ref, any_slot(col_ref[t], place_ref), tiles_ref, t)
     for h in range(HALF):
         out_ref[:, h * TILE:(h + 1) * TILE] = acc_ref[h]
 
@@ -218,7 +231,6 @@
     core = region & 1
     device = (region * N_ROW + row_index)[None]
     place = jnp.stack([row_index, 1 - 2 * core])
-    upward = jnp.stack([row_index, jnp.int32(1)])
 
     index = jax.ShapeDtypeStruct(tile_row.shape, jnp.int32)
     packed, tile_row, tile_col = pl.pallas_call(
@@ -246,13 +258,16 @@
         return (lax.ppermute(v, "region", ring(N_REGION, 1)), lax.ppermute(v, "region", ring(N_REGION, -1)))
 
     def exchange(v):
-        far, low, high = lax.optimization_barrier((lax.ppermute(v, "row", ring(N_ROW, 16)), *region_pair(v)))
+        low, high = region_pair(v)
+        line = lax.all_to_all(
+            jnp.broadcast_to(v[None], (N_X,) + v.shape), "row", 0, 0, tiled=True,
+            axis_index_groups=[[x * N_Y + y for x in range(N_X)] for y in range(N_Y)])
         both = pl.pallas_call(
             pair_kernel, out_shape=shape(2, Q, ROWS), in_specs=[SMEM] + [VMEM] * 3, out_specs=VMEM,
             compiler_params=PARAMS, name="pair",
         )(core[None], v, low, high)
         got = []
-        for hop in HOPS[1:4]:
+        for hop in SHARED:
             pairs = [(r * N_ROW + i, r * N_ROW + (i - (hop if r % 2 == 0 else -hop)) % N_ROW)
                      for r in range(N_REGION) for i in range(N_ROW)]
             got.append(lax.ppermute(both, ("region", "row"), pairs))
@@ -261,7 +276,7 @@
             compiler_params=PARAMS, name="swap",
         )(*got)
         swapped = lax.ppermute(swapped, "region", [(r, r ^ 1) for r in range(N_REGION)])
-        return [v] + got + [swapped, far, low, high]
+        return [v, line] + got + [swapped, low, high]
 
     slots = pltpu.VMEM((SLOTS * HALF, Q, TILE), F32)
     acc = pltpu.VMEM((HALF, Q, TILE), F32)
@@ -271,7 +286,7 @@
         scratch_shapes=[pltpu.VMEM((len(HOPS) * HALF, Q, TILE), F32)],
         cost_estimate=pl.CostEstimate(flops=2 * 12 * Q * TILE * TILE, bytes_accessed=2000000, transcendentals=0),
         compiler_params=PARAMS, name="first_inner",
-    )(upward, tile_row, tile_col, near.reshape(N_ROW * width, TILE), tile_vals)
+    )(place, tile_row, tile_col, near.reshape(N_ROW * width, TILE), tile_vals)
     v1 = pl.pallas_call(
         outer_kernel, out_shape=shape(Q, ROWS), in_specs=[SMEM] * 2 + [VMEM] * 4, out_specs=VMEM,
         scratch_shapes=[pltpu.VMEM((2 * HALF, Q, TILE), F32), acc], compiler_params=PARAMS, name="first_outer",

time: 158 us -> 155 us (0.981)
  blocking collectives: 55.9 us -> 44.4 us
  waiting for transfers between devices: 30.7 us -> 41 us
  starting transfers between devices: 57.6 us -> 53.8 us
    all_to_all x1 -> x0, blocking collectives: 15.5 us -> none  [local(): lax.all_to_all(near.reshape(N_ROW, width, TILE), 'row', 0, 0, tiled=True)]
    all_to_all x0 -> x3, waiting for transfers between devices: none -> 12.2 us  [the longest x1 12.2 us: local(): lax.all_to_all(near.reshape(N_ROW, width, TILE), 'row', 0, 0, tiled=True)]
    ppermute x3, starting transfers between devices: 12.1 us -> 0.31 us  [region_pair(): lax.ppermute(v, 'region', ring(N_REGION, -1))]
    all_to_all x0 -> x3, starting transfers between devices: none -> 10.8 us  [the longest x2 6.81 us: exchange(): lax.all_to_all(jnp.broadcast_to(v[None], (N_X,) + v.shape), 'row', 0, 0,...]
    ppermute x3, waiting for transfers between devices: 0.01 us -> 6.7 us  [region_pair(): lax.ppermute(v, 'region', ring(N_REGION, -1))]
    ppermute x2 -> x0, starting transfers between devices: 6.6 us -> none  [exchange(): lax.ppermute(v, 'row', ring(N_ROW, 16))]
    ppermute x2 -> x0, waiting for transfers between devices: 6.35 us -> none  [exchange(): lax.ppermute(v, 'row', ring(N_ROW, 16))]
    ppermute x6 -> x4, starting transfers between devices: 19.6 us -> 14 us  [exchange(): got.append(lax.ppermute(both, ('region', 'row'), pairs))]
  transfers between devices with their start and end apart: 17 -> 16, of which waited for: 11 -> 11; matrix products, arithmetic and copies ran while one was open for 0% -> 1% of each run, Pallas kernels for 1% -> 1%
where the time goes in v4:
time: 155 us; the launch traced here: 154 us
  starting transfers between devices  53.8 us (35%)
  blocking collectives  44.4 us (29%)
  waiting for transfers between devices  41 us (26%)
  Pallas kernels  11.6 us (7%)
  local copies, waits for them, and re-layouts  2.37 us (2%)
    all_to_all x1, blocking collectives, local(): lax.all_to_all(jnp.broadcast_to(moments[None], (N_REGION, 4, TILE)), 'reg...  15.8 us
    all_to_all x1, blocking collectives, local(): lax.all_to_all(jnp.broadcast_to(moments[None], (N_ROW, 4, TILE)), 'row',...  15.2 us
    ppermute x4, starting transfers between devices, exchange(): got.append(lax.ppermute(both, ('region', 'row'), pairs))  14 us
    all_to_all x1, blocking collectives, local(): lax.all_to_all(by_query.reshape(N_ROW, QS * HALF, TILE), 'row', 0, 0, til...  13.3 us
    all_to_all x1, waiting for transfers between devices, local(): lax.all_to_all(near.reshape(N_ROW, width, TILE), 'row', 0, 0, tiled=True)  12.2 us
    all_to_all x1, starting transfers between devices, local(): lax.all_to_all(packed, 'row', 0, 0, tiled=True).reshape(Q, D + TILE)  10.6 us
    ppermute x2, starting transfers between devices, exchange(): lax.ppermute(swapped, 'region', [(r, r ^ 1) for r in range(N_REGION)])  9.42 us
    all_to_all x1, waiting for transfers between devices, local(): lax.all_to_all(packed, 'row', 0, 0, tiled=True).reshape(Q, D + TILE)  9.34 us
  transfers between devices with their start and end apart: 16, of which 11 were waited for; matrix products, arithmetic and copies ran while one was open for 1% of the time, Pallas kernels for 1%

profile of v4, /device:TPU:1, one launch (start us, length us, event | category | flops | bytes accessed | tf_op | source)
XLA Modules:
  0.0 154.2 jit_solution(10082940095333512923)
XLA Ops:
  0.6 1.5 pack.1
  2.2 0.0 copy-start.1
  2.2 10.6 %all-to-all-start = ((f32[32,2,640]{2,1,0:T(2,128)}), f32[32,2,640]{2,1,0:T(2,128)S(1)}, u32[]{:S(2)}, u32[]{:S(2)}) async-start(f32[32,2,640]{2,1,0:T(2,128)} %get-tuple-element.9), calls=%async_computation | async-start | bytes 327680 | tf_op jit(solution)/shard_map/all_to_all | solution.py:242
  12.8 0.0 copy-start.2
  12.9 9.3 %all-to-all-done = f32[32,2,640]{2,1,0:T(2,128)S(1)} async-done(((f32[32,2,640]{2,1,0:T(2,128)}), f32[32,2,640]{2,1,0:T(2,128)S(1)}, u32[]{:S(2)}, u32[]{:S(2)}) %all-to-all-start) | async-done | bytes 163872 | tf_op jit(solution)/shard_map/all_to_all | solution.py:242
  22.2 0.1 reshape.30.packed_ref
  22.3 0.6 scores.1
  23.0 13.3 %all_to_all.35 = f32[32,4,128]{2,1,0:T(4,128)S(1)} all-to-all(f32[32,4,128]{2,1,0:T(4,128)S(1)} %bitcast.22), channel_id=1, replica_groups=mesh['region'=16,'row'=32] {'row'}, dimensions={0} | all-to-all | bytes 131072 | tf_op jit(solution)/shard_map/all_to_all | solution.py:247
  36.3 3.0 %permute.1 = f32[1024,128]{1,0:T(8,128)} custom-call(f32[128,128]{1,0:T(8,128)S(1)} %bitcast.21, f32[64,640]{1,0:T(8,128)S(1)} %reshape.30.packed_ref), custom_call_target="tpu_custom_call" | custom-call | tf_op jit(solution)/shard_map/permute/pallas_call | solution.py:249
  39.3 4.0 %all-to-all-start.2 = ((f32[32,32,128]{2,1,0:T(8,128)}), f32[32,32,128]{2,1,0:T(8,128)S(1)}, u32[]{:S(2)}, u32[]{:S(2)}) async-start(f32[32,32,128]{2,1,0:T(8,128)} %bitcast.5), calls=%async_computation.2 | async-start | bytes 1048576 | tf_op jit(solution)/shard_map/all_to_all | solution.py:254
  43.3 12.2 %all-to-all-done.2 = f32[32,32,128]{2,1,0:T(8,128)S(1)} async-done(((f32[32,32,128]{2,1,0:T(8,128)}), f32[32,32,128]{2,1,0:T(8,128)S(1)}, u32[]{:S(2)}, u32[]{:S(2)}) %all-to-all-start.2) | async-done | bytes 524320 | tf_op jit(solution)/shard_map/all_to_all | solution.py:254
  55.6 0.1 copy.17
  55.7 7.4 %collective-permute-start = (f32[64,256]{1,0:T(8,128)S(1)}, f32[64,256]{1,0:T(8,128)S(1)}, u32[]{:S(2)}, u32[]{:S(2)}) collective-permute-start(f32[64,256]{1,0:T(8,128)S(1)} %bitcast.17), channel_id=1, source_target_pairs={{0,32},{32,64},{64,96},{96,128},{128,160},{160,192},{192,224},{224... | collective-permute-start | bytes 196616 | tf_op jit(solution)/shard_map/ppermute | solution.py:258
  63.1 0.1 pad_add_fusion.place_ref
  63.2 0.7 copy-done.3
  63.8 0.0 copy-done.4
  63.8 1.4 first_inner.1.inner_ref
  65.3 1.5 collective-permute-done.1.high_ref
  66.8 1.0 first_outer.1.own_ref.refs_0_.refs_8_.v1_ref
  67.8 0.3 collective-permute-start.2
  68.0 0.3 collective-permute-start.3
  68.3 1.1 collective-permute-done.2.low_ref.refs_5_
  69.4 2.8 %collective-permute-done.3.high_ref.refs_6_ = f32[64,256]{1,0:T(8,128)S(1)} collective-permute-done((f32[64,256]{1,0:T(8,128)S(1)}, f32[64,256]{1,0:T(8,128)S(1)}, u32[]{:S(2)}, u32[]{:S(2)}) %collective-permute-start.3) | collective-permute-done | bytes 65568 | tf_op jit(solution)/shard_map/ppermute | solution.py:258
  72.2 4.3 %collective-permute-start.4 = (f32[2,64,256]{2,1,0:T(8,128)S(1)}, f32[2,64,256]{2,1,0:T(8,128)S(1)}, u32[]{:S(2)}, u32[]{:S(2)}) collective-permute-start(f32[2,64,256]{2,1,0:T(8,128)S(1)} %pair.2), channel_id=1, source_target_pairs={{0,31},{1,0},{2,1},{3,2},{4,3},{5,4},{6,5},{7,6},{8,7},{9,8},{10,9... | collective-permute-start | bytes 393224 | tf_op jit(solution)/shard_map/ppermute | solution.py:273
  76.5 2.6 %collective-permute-start.5 = (f32[2,64,256]{2,1,0:T(8,128)S(1)}, f32[2,64,256]{2,1,0:T(8,128)S(1)}, u32[]{:S(2)}, u32[]{:S(2)}) collective-permute-start(f32[2,64,256]{2,1,0:T(8,128)S(1)} %pair.2), channel_id=1, source_target_pairs={{0,29},{1,30},{2,31},{3,0},{4,1},{5,2},{6,3},{7,4},{8,5},{9,6},{10... | collective-permute-start | bytes 393224 | tf_op jit(solution)/shard_map/ppermute | solution.py:273
  79.1 0.7 broadcast_in_dim.13
  79.9 3.4 %all-to-all-start.3 = ((f32[4,64,256]{2,1,0:T(8,128)}), f32[4,64,256]{2,1,0:T(8,128)S(1)}, u32[]{:S(2)}, u32[]{:S(2)}) async-start(f32[4,64,256]{2,1,0:T(8,128)} %broadcast_in_dim.13), calls=%async_computation.3 | async-start | bytes 524288 | tf_op jit(solution)/shard_map/all_to_all | solution.py:262
  83.3 5.8 %collective-permute-done.5.refs_1_.refs_3_ = f32[2,64,256]{2,1,0:T(8,128)S(1)} collective-permute-done((f32[2,64,256]{2,1,0:T(8,128)S(1)}, f32[2,64,256]{2,1,0:T(8,128)S(1)}, u32[]{:S(2)}, u32[]{:S(2)}) %collective-permute-start.5) | collective-permute-done | bytes 131104 | tf_op jit(solution)/shard_map/ppermute | solution.py:273
  89.1 3.5 %collective-permute-start.6 = (f32[2,64,256]{2,1,0:T(8,128)S(1)}, f32[2,64,256]{2,1,0:T(8,128)S(1)}, u32[]{:S(2)}, u32[]{:S(2)}) collective-permute-start(f32[2,64,256]{2,1,0:T(8,128)S(1)} %swap.2), channel_id=1, source_target_pairs={{0,32},{32,0},{64,96},{96,64},{128,160},{160,128},{192,224},{224,1... | collective-permute-start | bytes 393224 | tf_op jit(solution)/shard_map/ppermute | solution.py:278
  92.6 1.0 collective-permute-done.6.refs_4_
  93.5 1.2 second.1.own_ref.refs_0_.v2_ref
  94.7 1.0 collective-permute-start.7
  95.7 0.1 collective-permute-start.8
  95.7 1.3 collective-permute-done.7.low_ref.refs_5_
  97.0 2.4 %collective-permute-done.8.high_ref.refs_6_ = f32[64,256]{1,0:T(8,128)S(1)} collective-permute-done((f32[64,256]{1,0:T(8,128)S(1)}, f32[64,256]{1,0:T(8,128)S(1)}, u32[]{:S(2)}, u32[]{:S(2)}) %collective-permute-start.8) | collective-permute-done | bytes 65568 | tf_op jit(solution)/shard_map/ppermute | solution.py:258
  99.4 1.9 %collective-permute-start.9 = (f32[2,64,256]{2,1,0:T(8,128)S(1)}, f32[2,64,256]{2,1,0:T(8,128)S(1)}, u32[]{:S(2)}, u32[]{:S(2)}) collective-permute-start(f32[2,64,256]{2,1,0:T(8,128)S(1)} %pair.3), channel_id=1, source_target_pairs={{0,31},{1,0},{2,1},{3,2},{4,3},{5,4},{6,5},{7,6},{8,7},{9,8},{10,9... | collective-permute-start | bytes 393224 | tf_op jit(solution)/shard_map/ppermute | solution.py:273
  101.3 5.2 %collective-permute-start.10 = (f32[2,64,256]{2,1,0:T(8,128)S(1)}, f32[2,64,256]{2,1,0:T(8,128)S(1)}, u32[]{:S(2)}, u32[]{:S(2)}) collective-permute-start(f32[2,64,256]{2,1,0:T(8,128)S(1)} %pair.3), channel_id=1, source_target_pairs={{0,29},{1,30},{2,31},{3,0},{4,1},{5,2},{6,3},{7,4},{8,5},{9,6},{10... | collective-permute-start | bytes 393224 | tf_op jit(solution)/shard_map/ppermute | solution.py:273
  106.5 0.7 broadcast_in_dim.15
  107.2 3.4 %all-to-all-start.4 = ((f32[4,64,256]{2,1,0:T(8,128)}), f32[4,64,256]{2,1,0:T(8,128)S(1)}, u32[]{:S(2)}, u32[]{:S(2)}) async-start(f32[4,64,256]{2,1,0:T(8,128)} %broadcast_in_dim.15), calls=%async_computation.4 | async-start | bytes 524288 | tf_op jit(solution)/shard_map/all_to_all | solution.py:262
  110.7 0.0 collective-permute-done.9.refs_0_.refs_2_
  110.7 2.7 %collective-permute-done.10.refs_1_.refs_3_ = f32[2,64,256]{2,1,0:T(8,128)S(1)} collective-permute-done((f32[2,64,256]{2,1,0:T(8,128)S(1)}, f32[2,64,256]{2,1,0:T(8,128)S(1)}, u32[]{:S(2)}, u32[]{:S(2)}) %collective-permute-start.10) | collective-permute-done | bytes 131104 | tf_op jit(solution)/shard_map/ppermute | solution.py:273
  113.3 6.0 %collective-permute-start.11 = (f32[2,64,256]{2,1,0:T(8,128)S(1)}, f32[2,64,256]{2,1,0:T(8,128)S(1)}, u32[]{:S(2)}, u32[]{:S(2)}) collective-permute-start(f32[2,64,256]{2,1,0:T(8,128)S(1)} %swap.3), channel_id=1, source_target_pairs={{0,32},{32,0},{64,96},{96,64},{128,160},{160,128},{192,224},{224,1... | collective-permute-start | bytes 393224 | tf_op jit(solution)/shard_map/ppermute | solution.py:278
  119.3 0.0 all-to-all-done.4.refs_1_
  119.3 1.0 collective-permute-done.11.refs_4_
  120.3 1.3 third.1
  121.6 15.2 %all_to_all.36 = f32[32,4,128]{2,1,0:T(4,128)S(1)} all-to-all(f32[32,4,128]{2,1,0:T(4,128)S(1)} %broadcast_in_dim.16), channel_id=1, replica_groups=mesh['region'=16,'row'=32] {'row'}, dimensions={0} | all-to-all | bytes 131072 | tf_op jit(solution)/shard_map/all_to_all | solution.py:304
  136.9 15.8 %all_to_all.37.moments_ref = f32[16,4,128]{2,1,0:T(4,128)S(1)} all-to-all(f32[16,4,128]{2,1,0:T(4,128)S(1)} %broadcast_in_dim.17), channel_id=1, replica_groups=mesh['region'=16,'row'=32] {'region'}, dimensions={0} | all-to-all | bytes 65536 | tf_op jit(solution)/shard_map/all_to_all | solution.py:306
  152.7 1.5 finish.1
  (20 shorter events, 0.2 us)
Async XLA Ops:
  2.2 20.1 %copy-start.1 = (f32[256,512]{1,0:T(8,128)S(1)}, f32[256,512]{1,0:T(8,128)}, u32[]{:S(2)}) copy-start(f32[256,512]{1,0:T(8,128)} %desc_ref.1) | copy-start | bytes 1572868
  2.2 20.0 %all-to-all-start = ((f32[32,2,640]{2,1,0:T(2,128)}), f32[32,2,640]{2,1,0:T(2,128)S(1)}, u32[]{:S(2)}, u32[]{:S(2)}) async-start(f32[32,2,640]{2,1,0:T(2,128)} %get-tuple-element.9), calls=%async_computation | async-start | bytes 327680 | tf_op jit(solution)/shard_map/all_to_all | solution.py:242
  12.8 9.5 %copy-start.2 = (s32[64,64]{1,0:T(8,128)S(1)}, s32[64,64]{1,0:T(8,128)}, u32[]{:S(2)}) copy-start(s32[64,64]{1,0:T(8,128)} %cand_ref.1) | copy-start | bytes 49156
  39.3 23.9 %copy-start = (f32[12,128,128]{2,1,0:T(8,128)S(1)}, f32[12,128,128]{2,1,0:T(8,128)}, u32[]{:S(2)}) copy-start(f32[12,128,128]{2,1,0:T(8,128)} %refs_9_.1) | copy-start | bytes 2359300
  39.3 16.3 %all-to-all-start.2 = ((f32[32,32,128]{2,1,0:T(8,128)}), f32[32,32,128]{2,1,0:T(8,128)S(1)}, u32[]{:S(2)}, u32[]{:S(2)}) async-start(f32[32,32,128]{2,1,0:T(8,128)} %bitcast.5), calls=%async_computation.2 | async-start | bytes 1048576 | tf_op jit(solution)/shard_map/all_to_all | solution.py:254
  55.7 9.6 %collective-permute-start = (f32[64,256]{1,0:T(8,128)S(1)}, f32[64,256]{1,0:T(8,128)S(1)}, u32[]{:S(2)}, u32[]{:S(2)}) collective-permute-start(f32[64,256]{1,0:T(8,128)S(1)} %bitcast.17), channel_id=1, source_target_pairs={{0,32},{32,64},{64,96},{96,128},{128,160},{160,192},{192,224},{224... | collective-permute-start | bytes 196616 | tf_op jit(solution)/shard_map/ppermute | solution.py:258
  63.1 3.7 %collective-permute-start.1 = (f32[64,256]{1,0:T(8,128)S(1)}, f32[64,256]{1,0:T(8,128)S(1)}, u32[]{:S(2)}, u32[]{:S(2)}) collective-permute-start(f32[64,256]{1,0:T(8,128)S(1)} %bitcast.18), channel_id=1, source_target_pairs={{0,480},{32,0},{64,32},{96,64},{128,96},{160,128},{192,160},{224,1... | collective-permute-start | bytes 196616 | tf_op jit(solution)/shard_map/ppermute | solution.py:258
  63.2 0.7 copy-start.3
  63.2 0.7 copy-start.4
  67.8 1.6 %collective-permute-start.2 = (f32[64,256]{1,0:T(8,128)S(1)}, f32[64,256]{1,0:T(8,128)S(1)}, u32[]{:S(2)}, u32[]{:S(2)}) collective-permute-start(f32[64,256]{1,0:T(8,128)S(1)} %first_outer.1.own_ref.refs_0_.refs_8_.v1_ref), channel_id=1, source_target_pairs={{0,32},{32,64},{64,96},{96,128},{128,160},{160,192},{192,224},{224... | collective-permute-start | bytes 196616 | tf_op jit(solution)/shard_map/ppermute | solution.py:258
  68.0 4.2 %collective-permute-start.3 = (f32[64,256]{1,0:T(8,128)S(1)}, f32[64,256]{1,0:T(8,128)S(1)}, u32[]{:S(2)}, u32[]{:S(2)}) collective-permute-start(f32[64,256]{1,0:T(8,128)S(1)} %first_outer.1.own_ref.refs_0_.refs_8_.v1_ref), channel_id=1, source_target_pairs={{0,480},{32,0},{64,32},{96,64},{128,96},{160,128},{192,160},{224,1... | collective-permute-start | bytes 196616 | tf_op jit(solution)/shard_map/ppermute | solution.py:258
  72.2 11.1 %collective-permute-start.4 = (f32[2,64,256]{2,1,0:T(8,128)S(1)}, f32[2,64,256]{2,1,0:T(8,128)S(1)}, u32[]{:S(2)}, u32[]{:S(2)}) collective-permute-start(f32[2,64,256]{2,1,0:T(8,128)S(1)} %pair.2), channel_id=1, source_target_pairs={{0,31},{1,0},{2,1},{3,2},{4,3},{5,4},{6,5},{7,6},{8,7},{9,8},{10,9... | collective-permute-start | bytes 393224 | tf_op jit(solution)/shard_map/ppermute | solution.py:273
  76.5 12.5 %collective-permute-start.5 = (f32[2,64,256]{2,1,0:T(8,128)S(1)}, f32[2,64,256]{2,1,0:T(8,128)S(1)}, u32[]{:S(2)}, u32[]{:S(2)}) collective-permute-start(f32[2,64,256]{2,1,0:T(8,128)S(1)} %pair.2), channel_id=1, source_target_pairs={{0,29},{1,30},{2,31},{3,0},{4,1},{5,2},{6,3},{7,4},{8,5},{9,6},{10... | collective-permute-start | bytes 393224 | tf_op jit(solution)/shard_map/ppermute | solution.py:273
  79.9 12.7 %all-to-all-start.3 = ((f32[4,64,256]{2,1,0:T(8,128)}), f32[4,64,256]{2,1,0:T(8,128)S(1)}, u32[]{:S(2)}, u32[]{:S(2)}) async-start(f32[4,64,256]{2,1,0:T(8,128)} %broadcast_in_dim.13), calls=%async_computation.3 | async-start | bytes 524288 | tf_op jit(solution)/shard_map/all_to_all | solution.py:262
  89.1 4.4 %collective-permute-start.6 = (f32[2,64,256]{2,1,0:T(8,128)S(1)}, f32[2,64,256]{2,1,0:T(8,128)S(1)}, u32[]{:S(2)}, u32[]{:S(2)}) collective-permute-start(f32[2,64,256]{2,1,0:T(8,128)S(1)} %swap.2), channel_id=1, source_target_pairs={{0,32},{32,0},{64,96},{96,64},{128,160},{160,128},{192,224},{224,1... | collective-permute-start | bytes 393224 | tf_op jit(solution)/shard_map/ppermute | solution.py:278
  94.7 2.3 %collective-permute-start.7 = (f32[64,256]{1,0:T(8,128)S(1)}, f32[64,256]{1,0:T(8,128)S(1)}, u32[]{:S(2)}, u32[]{:S(2)}) collective-permute-start(f32[64,256]{1,0:T(8,128)S(1)} %second.1.own_ref.refs_0_.v2_ref), channel_id=1, source_target_pairs={{0,32},{32,64},{64,96},{96,128},{128,160},{160,192},{192,224},{224... | collective-permute-start | bytes 196616 | tf_op jit(solution)/shard_map/ppermute | solution.py:258
  95.7 3.7 %collective-permute-start.8 = (f32[64,256]{1,0:T(8,128)S(1)}, f32[64,256]{1,0:T(8,128)S(1)}, u32[]{:S(2)}, u32[]{:S(2)}) collective-permute-start(f32[64,256]{1,0:T(8,128)S(1)} %second.1.own_ref.refs_0_.v2_ref), channel_id=1, source_target_pairs={{0,480},{32,0},{64,32},{96,64},{128,96},{160,128},{192,160},{224,1... | collective-permute-start | bytes 196616 | tf_op jit(solution)/shard_map/ppermute | solution.py:258
  99.4 11.3 %collective-permute-start.9 = (f32[2,64,256]{2,1,0:T(8,128)S(1)}, f32[2,64,256]{2,1,0:T(8,128)S(1)}, u32[]{:S(2)}, u32[]{:S(2)}) collective-permute-start(f32[2,64,256]{2,1,0:T(8,128)S(1)} %pair.3), channel_id=1, source_target_pairs={{0,31},{1,0},{2,1},{3,2},{4,3},{5,4},{6,5},{7,6},{8,7},{9,8},{10,9... | collective-permute-start | bytes 393224 | tf_op jit(solution)/shard_map/ppermute | solution.py:273
  101.3 12.0 %collective-permute-start.10 = (f32[2,64,256]{2,1,0:T(8,128)S(1)}, f32[2,64,256]{2,1,0:T(8,128)S(1)}, u32[]{:S(2)}, u32[]{:S(2)}) collective-permute-start(f32[2,64,256]{2,1,0:T(8,128)S(1)} %pair.3), channel_id=1, source_target_pairs={{0,29},{1,30},{2,31},{3,0},{4,1},{5,2},{6,3},{7,4},{8,5},{9,6},{10... | collective-permute-start | bytes 393224 | tf_op jit(solution)/shard_map/ppermute | solution.py:273
  107.2 12.1 %all-to-all-start.4 = ((f32[4,64,256]{2,1,0:T(8,128)}), f32[4,64,256]{2,1,0:T(8,128)S(1)}, u32[]{:S(2)}, u32[]{:S(2)}) async-start(f32[4,64,256]{2,1,0:T(8,128)} %broadcast_in_dim.15), calls=%async_computation.4 | async-start | bytes 524288 | tf_op jit(solution)/shard_map/all_to_all | solution.py:262
  113.3 6.9 %collective-permute-start.11 = (f32[2,64,256]{2,1,0:T(8,128)S(1)}, f32[2,64,256]{2,1,0:T(8,128)S(1)}, u32[]{:S(2)}, u32[]{:S(2)}) collective-permute-start(f32[2,64,256]{2,1,0:T(8,128)S(1)} %swap.3), channel_id=1, source_target_pairs={{0,32},{32,0},{64,96},{96,64},{128,160},{160,128},{192,224},{224,1... | collective-permute-start | bytes 393224 | tf_op jit(solution)/shard_map/ppermute | solution.py:278

commit v5 on v4

--- a/solution.py
+++ b/solution.py
@@ -123,6 +123,15 @@
         slots_ref[k * HALF + h] = block[:, h * TILE:(h + 1) * TILE]
 
 
+def store(acc_ref, out_ref, copies_ref=None):
+    for h in range(HALF):
+        cols = slice(h * TILE, (h + 1) * TILE)
+        out_ref[:, cols] = acc_ref[h]
+        if copies_ref is not None:
+            for x in range(N_X):
+                copies_ref[x, :, cols] = acc_ref[h]
+
+
 def inner_kernel(place_ref, row_ref, col_ref, near_ref, tiles_ref, out_ref, slots_ref):
     width = len(HOPS) * QS * HALF
     for k in range(len(HOPS)):
@@ -137,7 +146,7 @@
         out_ref[row_ref[t]] += jnp.where(inside, product(slots_ref, slot, tiles_ref, t), 0.0)
 
 
-def outer_kernel(row_ref, col_ref, inner_ref, low_ref, high_ref, tiles_ref, out_ref, slots_ref, acc_ref):
+def outer_kernel(row_ref, col_ref, inner_ref, low_ref, high_ref, tiles_ref, out_ref, copies_ref, slots_ref, acc_ref):
     spread(slots_ref, 0, low_ref[...])
     spread(slots_ref, 1, high_ref[...])
     acc_ref[...] = inner_ref[...]
@@ -145,8 +154,7 @@
         @pl.when(col_ref[t] >= N_ROW * HALF)
         def _():
             acc_ref[row_ref[t]] += product(slots_ref, col_ref[t] - N_ROW * HALF, tiles_ref, t)
-    for h in range(HALF):
-        out_ref[:, h * TILE:(h + 1) * TILE] = acc_ref[h]
+    store(acc_ref, out_ref, copies_ref)
 
 
 def pair_kernel(core_ref, own_ref, low_ref, high_ref, out_ref):
@@ -163,9 +171,8 @@
 N_BLOCKS = 7
 
 
-def next_kernel(place_ref, row_ref, col_ref, *refs):
-    _, line_ref, a_ref, b_ref, swapped_ref, low_ref, high_ref = refs[:N_BLOCKS]
-    tiles_ref, out_ref, slots_ref, acc_ref = refs[N_BLOCKS:]
+def times_s(place_ref, row_ref, col_ref, blocks, tiles_ref, slots_ref, acc_ref):
+    _, line_ref, a_ref, b_ref, swapped_ref, low_ref, high_ref = blocks
     blocks = [line_ref[x] for x in range(N_X)] + [
         a_ref[0], b_ref[0], swapped_ref[0], swapped_ref[1], low_ref[...], high_ref[...]]
     for k, block in enumerate(blocks):
@@ -173,14 +180,19 @@
     acc_ref[...] = jnp.zeros_like(acc_ref)
     for t in range(tiles_ref.shape[0]):
         acc_ref[row_ref[t]] += product(slots_ref, any_slot(col_ref[t], place_ref), tiles_ref, t)
-    for h in range(HALF):
-        out_ref[:, h * TILE:(h + 1) * TILE] = acc_ref[h]
+
+
+def next_kernel(place_ref, row_ref, col_ref, *refs):
+    tiles_ref, out_ref, copies_ref, slots_ref, acc_ref = refs[N_BLOCKS:]
+    times_s(place_ref, row_ref, col_ref, refs[:N_BLOCKS], tiles_ref, slots_ref, acc_ref)
+    store(acc_ref, out_ref, copies_ref)
 
 
 def last_kernel(place_ref, row_ref, col_ref, *refs):
     blocks = refs[:N_BLOCKS]
-    v0_ref, v1_ref, tiles_ref, out_ref, moments_ref, *scratch = refs[N_BLOCKS:]
-    next_kernel(place_ref, row_ref, col_ref, *blocks, tiles_ref, out_ref, *scratch)
+    v0_ref, v1_ref, tiles_ref, out_ref, moments_ref, slots_ref, acc_ref = refs[N_BLOCKS:]
+    times_s(place_ref, row_ref, col_ref, blocks, tiles_ref, slots_ref, acc_ref)
+    store(acc_ref, out_ref)
     vs = [v0_ref[...], v1_ref[...], blocks[0][...], out_ref[...]]
     lane = lax.broadcasted_iota(jnp.int32, (Q, TILE), 1)
     packed = [jnp.zeros((Q, TILE), F32), jnp.zeros((Q, TILE), F32)]
@@ -257,10 +269,10 @@
     def region_pair(v):
         return (lax.ppermute(v, "region", ring(N_REGION, 1)), lax.ppermute(v, "region", ring(N_REGION, -1)))
 
-    def exchange(v):
+    def exchange(v, copies):
         low, high = region_pair(v)
         line = lax.all_to_all(
-            jnp.broadcast_to(v[None], (N_X,) + v.shape), "row", 0, 0, tiled=True,
+            copies, "row", 0, 0, tiled=True,
             axis_index_groups=[[x * N_Y + y for x in range(N_X)] for y in range(N_Y)])
         both = pl.pallas_call(
             pair_kernel, out_shape=shape(2, Q, ROWS), in_specs=[SMEM] + [VMEM] * 3, out_specs=VMEM,
@@ -271,6 +283,7 @@
             pairs = [(r * N_ROW + i, r * N_ROW + (i - (hop if r % 2 == 0 else -hop)) % N_ROW)
                      for r in range(N_REGION) for i in range(N_ROW)]
             got.append(lax.ppermute(both, ("region", "row"), pairs))
+        *got, line = lax.optimization_barrier((*got, line))
         swapped = pl.pallas_call(
             swap_kernel, out_shape=shape(len(got), Q, ROWS), in_specs=[VMEM] * len(got), out_specs=VMEM,
             compiler_params=PARAMS, name="swap",
@@ -287,19 +300,20 @@
         cost_estimate=pl.CostEstimate(flops=2 * 12 * Q * TILE * TILE, bytes_accessed=2000000, transcendentals=0),
         compiler_params=PARAMS, name="first_inner",
     )(place, tile_row, tile_col, near.reshape(N_ROW * width, TILE), tile_vals)
-    v1 = pl.pallas_call(
-        outer_kernel, out_shape=shape(Q, ROWS), in_specs=[SMEM] * 2 + [VMEM] * 4, out_specs=VMEM,
+    with_copies = (shape(Q, ROWS), shape(N_X, Q, ROWS))
+    v1, copies = pl.pallas_call(
+        outer_kernel, out_shape=with_copies, in_specs=[SMEM] * 2 + [VMEM] * 4, out_specs=(VMEM, VMEM),
         scratch_shapes=[pltpu.VMEM((2 * HALF, Q, TILE), F32), acc], compiler_params=PARAMS, name="first_outer",
     )(tile_row, tile_col, inner, low, high, tile_vals)
-    v2 = pl.pallas_call(
-        next_kernel, out_shape=shape(Q, ROWS), in_specs=[SMEM] * 3 + [VMEM] * (N_BLOCKS + 1), out_specs=VMEM,
+    v2, copies = pl.pallas_call(
+        next_kernel, out_shape=with_copies, in_specs=[SMEM] * 3 + [VMEM] * (N_BLOCKS + 1), out_specs=(VMEM, VMEM),
         scratch_shapes=[slots, acc], compiler_params=PARAMS, name="second",
-    )(place, tile_row, tile_col, *exchange(v1), tile_vals)
+    )(place, tile_row, tile_col, *exchange(v1, copies), tile_vals)
     v3, moments = pl.pallas_call(
         last_kernel, out_shape=(shape(Q, ROWS), shape(4, TILE)),
         in_specs=[SMEM] * 3 + [VMEM] * (N_BLOCKS + 3), out_specs=(VMEM, VMEM),
         scratch_shapes=[slots, acc], compiler_params=PARAMS, name="third",
-    )(place, tile_row, tile_col, *exchange(v2), v0, v1, tile_vals)
+    )(place, tile_row, tile_col, *exchange(v2, copies), v0, v1, tile_vals)
 
     moments = lax.all_to_all(jnp.broadcast_to(moments[None], (N_ROW, 4, TILE)), "row", 0, 0, tiled=True)
     moments = jnp.sum(moments.reshape(2, 2, 2, 2, 2, 4, TILE).sum(0).sum(0).sum(0).sum(0), axis=0)

time: 155 us -> 152 us (0.981)
  blocking collectives: 44.4 us -> 40.2 us
    ppermute x3, starting transfers between devices: 0.31 us -> 12.1 us  [region_pair(): lax.ppermute(v, 'region', ring(N_REGION, -1))]
    ppermute x4, waiting for transfers between devices: 8.46 us -> 17.1 us  [exchange(): got.append(lax.ppermute(both, ('region', 'row'), pairs))]
    ppermute x3, waiting for transfers between devices: 6.7 us -> 0.01 us  [region_pair(): lax.ppermute(v, 'region', ring(N_REGION, -1))]
    ppermute x2, starting transfers between devices: 9.42 us -> 4.38 us  [exchange(): lax.ppermute(swapped, 'region', [(r, r ^ 1) for r in range(N_REGION)])]
    ppermute x3, starting transfers between devices: 8.61 us -> 3.61 us  [region_pair(): lax.ppermute(v, 'region', ring(N_REGION, 1))]
    all_to_all x1, blocking collectives: 15.8 us -> 12.5 us  [local(): lax.all_to_all(jnp.broadcast_to(moments[None], (N_REGION, 4, TILE)), 'reg...]
    ppermute x3, waiting for transfers between devices: 2.36 us -> 0.32 us  [region_pair(): lax.ppermute(v, 'region', ring(N_REGION, 1))]
  transfers between devices with their start and end apart: 16 -> 16, of which waited for: 11 -> 9; matrix products, arithmetic and copies ran while one was open for 1% -> 0% of each run, Pallas kernels for 1% -> 1%
where the time goes in v5:
time: 152 us; the launch traced here: 151 us
  starting transfers between devices  54.8 us (36%)
  waiting for transfers between devices  41.2 us (27%)
  blocking collectives  40.2 us (26%)
  Pallas kernels  13.1 us (9%)
    ppermute x4, waiting for transfers between devices, exchange(): got.append(lax.ppermute(both, ('region', 'row'), pairs))  17.1 us
    all_to_all x1, blocking collectives, local(): lax.all_to_all(jnp.broadcast_to(moments[None], (N_ROW, 4, TILE)), 'row',...  14.5 us
    all_to_all x1, blocking collectives, local(): lax.all_to_all(by_query.reshape(N_ROW, QS * HALF, TILE), 'row', 0, 0, til...  13.3 us
    ppermute x4, starting transfers between devices, exchange(): got.append(lax.ppermute(both, ('region', 'row'), pairs))  13.2 us
    all_to_all x1, blocking collectives, local(): lax.all_to_all(jnp.broadcast_to(moments[None], (N_REGION, 4, TILE)), 'reg...  12.5 us
    all_to_all x1, waiting for transfers between devices, local(): lax.all_to_all(near.reshape(N_ROW, width, TILE), 'row', 0, 0, tiled=True)  12.2 us
    ppermute x3, starting transfers between devices, region_pair(): lax.ppermute(v, 'region', ring(N_REGION, -1))  12.1 us
    all_to_all x1, starting transfers between devices, local(): lax.all_to_all(packed, 'row', 0, 0, tiled=True).reshape(Q, D + TILE)  10.6 us
  transfers between devices with their start and end apart: 16, of which 9 were waited for; matrix products, arithmetic and copies ran while one was open for 0% of the time, Pallas kernels for 1%

profile of v5, /device:TPU:1, one launch (start us, length us, event | category | flops | bytes accessed | tf_op | source)
XLA Modules:
  0.0 151.3 jit_solution(8632728175952620316)
XLA Ops:
  0.6 1.5 %pack.1 = (f32[32,2,640]{2,1,0:T(2,128)}, s32[12]{0:T(128)}, s32[12]{0:T(128)}) custom-call(f32[2,512]{1,0:T(2,128)} %queries_hbm.1, s32[1,256]{1,0:T(1,128)} %perm_hbm.1, s32[12]{0:T(128)} %row_hbm.1, s32[12]{0:T(128)} %col_hbm.1), custom_call_target="tpu_custom_call" | custom-call | tf_op jit(solution)/shard_map/pack/pallas_call | solution.py:248
  2.2 0.0 copy-start.1
  2.2 10.6 %all-to-all-start = ((f32[32,2,640]{2,1,0:T(2,128)}), f32[32,2,640]{2,1,0:T(2,128)S(1)}, u32[]{:S(2)}, u32[]{:S(2)}) async-start(f32[32,2,640]{2,1,0:T(2,128)} %get-tuple-element.19), calls=%async_computation | async-start | bytes 327680 | tf_op jit(solution)/shard_map/all_to_all | solution.py:254
  12.9 0.0 copy-start.2
  12.9 9.3 %all-to-all-done = f32[32,2,640]{2,1,0:T(2,128)S(1)} async-done(((f32[32,2,640]{2,1,0:T(2,128)}), f32[32,2,640]{2,1,0:T(2,128)S(1)}, u32[]{:S(2)}, u32[]{:S(2)}) %all-to-all-start) | async-done | bytes 163872 | tf_op jit(solution)/shard_map/all_to_all | solution.py:254
  22.2 0.1 reshape.28.packed_ref
  22.3 0.6 scores.1
  23.0 13.3 %all_to_all.35 = f32[32,4,128]{2,1,0:T(4,128)S(1)} all-to-all(f32[32,4,128]{2,1,0:T(4,128)S(1)} %bitcast.22), channel_id=1, replica_groups=mesh['region'=16,'row'=32] {'row'}, dimensions={0} | all-to-all | bytes 131072 | tf_op jit(solution)/shard_map/all_to_all | solution.py:259
  36.3 3.0 %permute.1 = f32[1024,128]{1,0:T(8,128)} custom-call(f32[128,128]{1,0:T(8,128)S(1)} %bitcast.21, f32[64,640]{1,0:T(8,128)S(1)} %reshape.28.packed_ref), custom_call_target="tpu_custom_call" | custom-call | tf_op jit(solution)/shard_map/permute/pallas_call | solution.py:261
  39.3 4.0 %all-to-all-start.2 = ((f32[32,32,128]{2,1,0:T(8,128)}), f32[32,32,128]{2,1,0:T(8,128)S(1)}, u32[]{:S(2)}, u32[]{:S(2)}) async-start(f32[32,32,128]{2,1,0:T(8,128)} %bitcast.5), calls=%async_computation.2 | async-start | bytes 1048576 | tf_op jit(solution)/shard_map/all_to_all | solution.py:266
  43.3 12.2 %all-to-all-done.2 = f32[32,32,128]{2,1,0:T(8,128)S(1)} async-done(((f32[32,32,128]{2,1,0:T(8,128)}), f32[32,32,128]{2,1,0:T(8,128)S(1)}, u32[]{:S(2)}, u32[]{:S(2)}) %all-to-all-start.2) | async-done | bytes 524320 | tf_op jit(solution)/shard_map/all_to_all | solution.py:266
  55.6 0.1 copy.17
  55.7 5.4 %collective-permute-start.1 = (f32[64,256]{1,0:T(8,128)S(1)}, f32[64,256]{1,0:T(8,128)S(1)}, u32[]{:S(2)}, u32[]{:S(2)}) collective-permute-start(f32[64,256]{1,0:T(8,128)S(1)} %bitcast.17), channel_id=1, source_target_pairs={{0,480},{32,0},{64,32},{96,64},{128,96},{160,128},{192,160},{224,1... | collective-permute-start | bytes 196616 | tf_op jit(solution)/shard_map/ppermute | solution.py:270
  61.1 2.0 %collective-permute-start = (f32[64,256]{1,0:T(8,128)S(1)}, f32[64,256]{1,0:T(8,128)S(1)}, u32[]{:S(2)}, u32[]{:S(2)}) collective-permute-start(f32[64,256]{1,0:T(8,128)S(1)} %bitcast.18), channel_id=1, source_target_pairs={{0,32},{32,64},{64,96},{96,128},{128,160},{160,192},{192,224},{224... | collective-permute-start | bytes 196616 | tf_op jit(solution)/shard_map/ppermute | solution.py:270
  63.1 0.1 pad_add_fusion.place_ref
  63.2 0.6 copy-done.3
  63.8 0.0 copy-done.4
  63.8 1.4 first_inner.1.inner_ref
  65.3 0.0 collective-permute-done.1.high_ref
  65.3 0.3 collective-permute-done.low_ref
  65.6 1.7 %first_outer.1 = (f32[64,256]{1,0:T(8,128)S(1)}, f32[4,64,256]{2,1,0:T(8,128)}) custom-call(s32[12]{0:T(128)S(1)} %copy-done.3, s32[12]{0:T(128)S(1)} %copy-done.4, f32[2,64,128]{2,1,0:T(8,128)S(1)} %first_inner.1.inner_ref, f32[64,256]{1,0:T(8,128)S(1)} %collective-permute-done.low_ref, f32[64,256]{1,0:T(8,128)S(1)} %collective-permute-done.1.high_ref, ...), custom_call_target="tpu_custom_call" | custom-call | tf_op jit(solution)/shard_map/first_outer/pallas_call | solution.py:304
  67.3 6.6 %collective-permute-start.3 = (f32[64,256]{1,0:T(8,128)S(1)}, f32[64,256]{1,0:T(8,128)S(1)}, u32[]{:S(2)}, u32[]{:S(2)}) collective-permute-start(f32[64,256]{1,0:T(8,128)S(1)} %get-tuple-element.20.own_ref.refs_0_.refs_8_.v1_ref), channel_id=1, source_target_pairs={{0,480},{32,0},{64,32},{96,64},{128,96},{160,128},{192,160},{224,1... | collective-permute-start | bytes 196616 | tf_op jit(solution)/shard_map/ppermute | solution.py:270
  73.9 0.0 collective-permute-start.2
  73.9 3.4 %all-to-all-start.3 = ((f32[4,64,256]{2,1,0:T(8,128)}), f32[4,64,256]{2,1,0:T(8,128)S(1)}, u32[]{:S(2)}, u32[]{:S(2)}) async-start(f32[4,64,256]{2,1,0:T(8,128)} %get-tuple-element.21), calls=%async_computation.3 | async-start | bytes 524288 | tf_op jit(solution)/shard_map/all_to_all | solution.py:274
  77.3 0.0 collective-permute-done.3.high_ref.refs_6_
  77.4 4.9 %collective-permute-start.5 = (f32[2,64,256]{2,1,0:T(8,128)S(1)}, f32[2,64,256]{2,1,0:T(8,128)S(1)}, u32[]{:S(2)}, u32[]{:S(2)}) collective-permute-start(f32[2,64,256]{2,1,0:T(8,128)S(1)} %pair.2), channel_id=1, source_target_pairs={{0,29},{1,30},{2,31},{3,0},{4,1},{5,2},{6,3},{7,4},{8,5},{9,6},{10... | collective-permute-start | bytes 393224 | tf_op jit(solution)/shard_map/ppermute | solution.py:285
  82.3 2.0 %collective-permute-start.4 = (f32[2,64,256]{2,1,0:T(8,128)S(1)}, f32[2,64,256]{2,1,0:T(8,128)S(1)}, u32[]{:S(2)}, u32[]{:S(2)}) collective-permute-start(f32[2,64,256]{2,1,0:T(8,128)S(1)} %pair.2), channel_id=1, source_target_pairs={{0,31},{1,0},{2,1},{3,2},{4,3},{5,4},{6,5},{7,6},{8,7},{9,8},{10,9... | collective-permute-start | bytes 393224 | tf_op jit(solution)/shard_map/ppermute | solution.py:285
  84.3 0.0 all-to-all-done.3.refs_1_
  84.3 5.4 %collective-permute-done.5.refs_1_.refs_3_ = f32[2,64,256]{2,1,0:T(8,128)S(1)} collective-permute-done((f32[2,64,256]{2,1,0:T(8,128)S(1)}, f32[2,64,256]{2,1,0:T(8,128)S(1)}, u32[]{:S(2)}, u32[]{:S(2)}) %collective-permute-start.5) | collective-permute-done | bytes 131104 | tf_op jit(solution)/shard_map/ppermute | solution.py:285
  89.7 3.0 %collective-permute-done.4.refs_0_.refs_2_ = f32[2,64,256]{2,1,0:T(8,128)S(1)} collective-permute-done((f32[2,64,256]{2,1,0:T(8,128)S(1)}, f32[2,64,256]{2,1,0:T(8,128)S(1)}, u32[]{:S(2)}, u32[]{:S(2)}) %collective-permute-start.4) | collective-permute-done | bytes 131104 | tf_op jit(solution)/shard_map/ppermute | solution.py:285
  92.7 1.9 %collective-permute-start.6 = (f32[2,64,256]{2,1,0:T(8,128)S(1)}, f32[2,64,256]{2,1,0:T(8,128)S(1)}, u32[]{:S(2)}, u32[]{:S(2)}) collective-permute-start(f32[2,64,256]{2,1,0:T(8,128)S(1)} %swap.2), channel_id=1, source_target_pairs={{0,32},{32,0},{64,96},{96,64},{128,160},{160,128},{192,224},{224,1... | collective-permute-start | bytes 393224 | tf_op jit(solution)/shard_map/ppermute | solution.py:291
  94.7 1.3 collective-permute-done.6.refs_4_
  96.0 1.9 %second.1 = (f32[64,256]{1,0:T(8,128)S(1)}, f32[4,64,256]{2,1,0:T(8,128)}) custom-call(s32[2]{0:T(128)S(1)} %pad_add_fusion.place_ref, s32[12]{0:T(128)S(1)} %copy-done.3, s32[12]{0:T(128)S(1)} %copy-done.4, f32[64,256]{1,0:T(8,128)S(1)} %get-tuple-element.20.own_ref.refs_0_.refs_8_.v1_ref, f32[4,64,256]{2,1,0:T(8,128)S(1)} %all-to-all-done.3.refs_1_, ...), custom_call_target="tpu_custom_call" | custom-call | tf_op jit(solution)/shard_map/second/pallas_call | solution.py:308
  97.9 0.1 collective-permute-start.8
  98.0 1.6 %collective-permute-start.7 = (f32[64,256]{1,0:T(8,128)S(1)}, f32[64,256]{1,0:T(8,128)S(1)}, u32[]{:S(2)}, u32[]{:S(2)}) collective-permute-start(f32[64,256]{1,0:T(8,128)S(1)} %get-tuple-element.25.own_ref.refs_0_.v2_ref), channel_id=1, source_target_pairs={{0,32},{32,64},{64,96},{96,128},{128,160},{160,192},{192,224},{224... | collective-permute-start | bytes 196616 | tf_op jit(solution)/shard_map/ppermute | solution.py:270
  99.6 3.4 %all-to-all-start.4 = ((f32[4,64,256]{2,1,0:T(8,128)}), f32[4,64,256]{2,1,0:T(8,128)S(1)}, u32[]{:S(2)}, u32[]{:S(2)}) async-start(f32[4,64,256]{2,1,0:T(8,128)} %get-tuple-element.26), calls=%async_computation.4 | async-start | bytes 524288 | tf_op jit(solution)/shard_map/all_to_all | solution.py:274
  103.1 0.0 collective-permute-done.8.high_ref.refs_6_
  103.1 4.4 %collective-permute-start.10 = (f32[2,64,256]{2,1,0:T(8,128)S(1)}, f32[2,64,256]{2,1,0:T(8,128)S(1)}, u32[]{:S(2)}, u32[]{:S(2)}) collective-permute-start(f32[2,64,256]{2,1,0:T(8,128)S(1)} %pair.3), channel_id=1, source_target_pairs={{0,29},{1,30},{2,31},{3,0},{4,1},{5,2},{6,3},{7,4},{8,5},{9,6},{10... | collective-permute-start | bytes 393224 | tf_op jit(solution)/shard_map/ppermute | solution.py:285
  107.5 1.9 %collective-permute-start.9 = (f32[2,64,256]{2,1,0:T(8,128)S(1)}, f32[2,64,256]{2,1,0:T(8,128)S(1)}, u32[]{:S(2)}, u32[]{:S(2)}) collective-permute-start(f32[2,64,256]{2,1,0:T(8,128)S(1)} %pair.3), channel_id=1, source_target_pairs={{0,31},{1,0},{2,1},{3,2},{4,3},{5,4},{6,5},{7,6},{8,7},{9,8},{10,9... | collective-permute-start | bytes 393224 | tf_op jit(solution)/shard_map/ppermute | solution.py:285
  109.4 0.0 all-to-all-done.4.refs_1_
  109.5 4.9 %collective-permute-done.10.refs_1_.refs_3_ = f32[2,64,256]{2,1,0:T(8,128)S(1)} collective-permute-done((f32[2,64,256]{2,1,0:T(8,128)S(1)}, f32[2,64,256]{2,1,0:T(8,128)S(1)}, u32[]{:S(2)}, u32[]{:S(2)}) %collective-permute-start.10) | collective-permute-done | bytes 131104 | tf_op jit(solution)/shard_map/ppermute | solution.py:285
  114.4 3.7 %collective-permute-done.9.refs_0_.refs_2_ = f32[2,64,256]{2,1,0:T(8,128)S(1)} collective-permute-done((f32[2,64,256]{2,1,0:T(8,128)S(1)}, f32[2,64,256]{2,1,0:T(8,128)S(1)}, u32[]{:S(2)}, u32[]{:S(2)}) %collective-permute-start.9) | collective-permute-done | bytes 131104 | tf_op jit(solution)/shard_map/ppermute | solution.py:285
  118.1 2.5 %collective-permute-start.11 = (f32[2,64,256]{2,1,0:T(8,128)S(1)}, f32[2,64,256]{2,1,0:T(8,128)S(1)}, u32[]{:S(2)}, u32[]{:S(2)}) collective-permute-start(f32[2,64,256]{2,1,0:T(8,128)S(1)} %swap.3), channel_id=1, source_target_pairs={{0,32},{32,0},{64,96},{96,64},{128,160},{160,128},{192,224},{224,1... | collective-permute-start | bytes 393224 | tf_op jit(solution)/shard_map/ppermute | solution.py:291
  120.5 1.0 collective-permute-done.11.refs_4_
  121.5 1.3 third.1
  122.8 14.5 %all_to_all.36 = f32[32,4,128]{2,1,0:T(4,128)S(1)} all-to-all(f32[32,4,128]{2,1,0:T(4,128)S(1)} %broadcast_in_dim.10), channel_id=1, replica_groups=mesh['region'=16,'row'=32] {'row'}, dimensions={0} | all-to-all | bytes 131072 | tf_op jit(solution)/shard_map/all_to_all | solution.py:318
  137.4 12.5 %all_to_all.37.moments_ref = f32[16,4,128]{2,1,0:T(4,128)S(1)} all-to-all(f32[16,4,128]{2,1,0:T(4,128)S(1)} %broadcast_in_dim.22), channel_id=1, replica_groups=mesh['region'=16,'row'=32] {'region'}, dimensions={0} | all-to-all | bytes 65536 | tf_op jit(solution)/shard_map/all_to_all | solution.py:320
  149.8 1.5 %finish.1 = (f32[64,256]{1,0:T(8,128)}, f32[64,256]{1,0:T(8,128)}) custom-call(f32[16,4,128]{2,1,0:T(4,128)S(1)} %all_to_all.37.moments_ref, f32[64,256]{1,0:T(8,128)S(1)} %bitcast.20, f32[64,256]{1,0:T(8,128)S(1)} %get-tuple-element.20.own_ref.refs_0_.refs_8_.v1_ref, f32[64,256]{1,0:T(8,128)S(1)} %get-tuple-element.25.own_ref.refs_0_.v2_ref, ...), custom_call_target="tpu_custom_call" | custom-call | tf_op jit(solution)/shard_map/finish/pallas_call | solution.py:321
  (18 shorter events, 0.2 us)
Async XLA Ops:
  2.2 20.1 %copy-start.1 = (f32[256,512]{1,0:T(8,128)S(1)}, f32[256,512]{1,0:T(8,128)}, u32[]{:S(2)}) copy-start(f32[256,512]{1,0:T(8,128)} %desc_ref.1) | copy-start | bytes 1572868
  2.2 20.0 %all-to-all-start = ((f32[32,2,640]{2,1,0:T(2,128)}), f32[32,2,640]{2,1,0:T(2,128)S(1)}, u32[]{:S(2)}, u32[]{:S(2)}) async-start(f32[32,2,640]{2,1,0:T(2,128)} %get-tuple-element.19), calls=%async_computation | async-start | bytes 327680 | tf_op jit(solution)/shard_map/all_to_all | solution.py:254
  12.9 9.5 %copy-start.2 = (s32[64,64]{1,0:T(8,128)S(1)}, s32[64,64]{1,0:T(8,128)}, u32[]{:S(2)}) copy-start(s32[64,64]{1,0:T(8,128)} %cand_ref.1) | copy-start | bytes 49156
  39.3 23.9 %copy-start = (f32[12,128,128]{2,1,0:T(8,128)S(1)}, f32[12,128,128]{2,1,0:T(8,128)}, u32[]{:S(2)}) copy-start(f32[12,128,128]{2,1,0:T(8,128)} %refs_9_.1) | copy-start | bytes 2359300
  39.3 16.3 %all-to-all-start.2 = ((f32[32,32,128]{2,1,0:T(8,128)}), f32[32,32,128]{2,1,0:T(8,128)S(1)}, u32[]{:S(2)}, u32[]{:S(2)}) async-start(f32[32,32,128]{2,1,0:T(8,128)} %bitcast.5), calls=%async_computation.2 | async-start | bytes 1048576 | tf_op jit(solution)/shard_map/all_to_all | solution.py:266
  55.7 9.6 %collective-permute-start.1 = (f32[64,256]{1,0:T(8,128)S(1)}, f32[64,256]{1,0:T(8,128)S(1)}, u32[]{:S(2)}, u32[]{:S(2)}) collective-permute-start(f32[64,256]{1,0:T(8,128)S(1)} %bitcast.17), channel_id=1, source_target_pairs={{0,480},{32,0},{64,32},{96,64},{128,96},{160,128},{192,160},{224,1... | collective-permute-start | bytes 196616 | tf_op jit(solution)/shard_map/ppermute | solution.py:270
  61.1 4.5 %collective-permute-start = (f32[64,256]{1,0:T(8,128)S(1)}, f32[64,256]{1,0:T(8,128)S(1)}, u32[]{:S(2)}, u32[]{:S(2)}) collective-permute-start(f32[64,256]{1,0:T(8,128)S(1)} %bitcast.18), channel_id=1, source_target_pairs={{0,32},{32,64},{64,96},{96,128},{128,160},{160,192},{192,224},{224... | collective-permute-start | bytes 196616 | tf_op jit(solution)/shard_map/ppermute | solution.py:270
  63.2 0.6 copy-start.3
  63.2 0.7 copy-start.4
  67.3 10.0 %collective-permute-start.3 = (f32[64,256]{1,0:T(8,128)S(1)}, f32[64,256]{1,0:T(8,128)S(1)}, u32[]{:S(2)}, u32[]{:S(2)}) collective-permute-start(f32[64,256]{1,0:T(8,128)S(1)} %get-tuple-element.20.own_ref.refs_0_.refs_8_.v1_ref), channel_id=1, source_target_pairs={{0,480},{32,0},{64,32},{96,64},{128,96},{160,128},{192,160},{224,1... | collective-permute-start | bytes 196616 | tf_op jit(solution)/shard_map/ppermute | solution.py:270
  73.9 3.4 %collective-permute-start.2 = (f32[64,256]{1,0:T(8,128)S(1)}, f32[64,256]{1,0:T(8,128)S(1)}, u32[]{:S(2)}, u32[]{:S(2)}) collective-permute-start(f32[64,256]{1,0:T(8,128)S(1)} %get-tuple-element.20.own_ref.refs_0_.refs_8_.v1_ref), channel_id=1, source_target_pairs={{0,32},{32,64},{64,96},{96,128},{128,160},{160,192},{192,224},{224... | collective-permute-start | bytes 196616 | tf_op jit(solution)/shard_map/ppermute | solution.py:270
  73.9 10.4 %all-to-all-start.3 = ((f32[4,64,256]{2,1,0:T(8,128)}), f32[4,64,256]{2,1,0:T(8,128)S(1)}, u32[]{:S(2)}, u32[]{:S(2)}) async-start(f32[4,64,256]{2,1,0:T(8,128)} %get-tuple-element.21), calls=%async_computation.3 | async-start | bytes 524288 | tf_op jit(solution)/shard_map/all_to_all | solution.py:274
  77.4 12.3 %collective-permute-start.5 = (f32[2,64,256]{2,1,0:T(8,128)S(1)}, f32[2,64,256]{2,1,0:T(8,128)S(1)}, u32[]{:S(2)}, u32[]{:S(2)}) collective-permute-start(f32[2,64,256]{2,1,0:T(8,128)S(1)} %pair.2), channel_id=1, source_target_pairs={{0,29},{1,30},{2,31},{3,0},{4,1},{5,2},{6,3},{7,4},{8,5},{9,6},{10... | collective-permute-start | bytes 393224 | tf_op jit(solution)/shard_map/ppermute | solution.py:285
  82.3 10.4 %collective-permute-start.4 = (f32[2,64,256]{2,1,0:T(8,128)S(1)}, f32[2,64,256]{2,1,0:T(8,128)S(1)}, u32[]{:S(2)}, u32[]{:S(2)}) collective-permute-start(f32[2,64,256]{2,1,0:T(8,128)S(1)} %pair.2), channel_id=1, source_target_pairs={{0,31},{1,0},{2,1},{3,2},{4,3},{5,4},{6,5},{7,6},{8,7},{9,8},{10,9... | collective-permute-start | bytes 393224 | tf_op jit(solution)/shard_map/ppermute | solution.py:285
  92.7 3.2 %collective-permute-start.6 = (f32[2,64,256]{2,1,0:T(8,128)S(1)}, f32[2,64,256]{2,1,0:T(8,128)S(1)}, u32[]{:S(2)}, u32[]{:S(2)}) collective-permute-start(f32[2,64,256]{2,1,0:T(8,128)S(1)} %swap.2), channel_id=1, source_target_pairs={{0,32},{32,0},{64,96},{96,64},{128,160},{160,128},{192,224},{224,1... | collective-permute-start | bytes 393224 | tf_op jit(solution)/shard_map/ppermute | solution.py:291
  97.9 5.2 %collective-permute-start.8 = (f32[64,256]{1,0:T(8,128)S(1)}, f32[64,256]{1,0:T(8,128)S(1)}, u32[]{:S(2)}, u32[]{:S(2)}) collective-permute-start(f32[64,256]{1,0:T(8,128)S(1)} %get-tuple-element.25.own_ref.refs_0_.v2_ref), channel_id=1, source_target_pairs={{0,480},{32,0},{64,32},{96,64},{128,96},{160,128},{192,160},{224,1... | collective-permute-start | bytes 196616 | tf_op jit(solution)/shard_map/ppermute | solution.py:270
  98.0 5.0 %collective-permute-start.7 = (f32[64,256]{1,0:T(8,128)S(1)}, f32[64,256]{1,0:T(8,128)S(1)}, u32[]{:S(2)}, u32[]{:S(2)}) collective-permute-start(f32[64,256]{1,0:T(8,128)S(1)} %get-tuple-element.25.own_ref.refs_0_.v2_ref), channel_id=1, source_target_pairs={{0,32},{32,64},{64,96},{96,128},{128,160},{160,192},{192,224},{224... | collective-permute-start | bytes 196616 | tf_op jit(solution)/shard_map/ppermute | solution.py:270
  99.6 9.8 %all-to-all-start.4 = ((f32[4,64,256]{2,1,0:T(8,128)}), f32[4,64,256]{2,1,0:T(8,128)S(1)}, u32[]{:S(2)}, u32[]{:S(2)}) async-start(f32[4,64,256]{2,1,0:T(8,128)} %get-tuple-element.26), calls=%async_computation.4 | async-start | bytes 524288 | tf_op jit(solution)/shard_map/all_to_all | solution.py:274
  103.1 11.3 %collective-permute-start.10 = (f32[2,64,256]{2,1,0:T(8,128)S(1)}, f32[2,64,256]{2,1,0:T(8,128)S(1)}, u32[]{:S(2)}, u32[]{:S(2)}) collective-permute-start(f32[2,64,256]{2,1,0:T(8,128)S(1)} %pair.3), channel_id=1, source_target_pairs={{0,29},{1,30},{2,31},{3,0},{4,1},{5,2},{6,3},{7,4},{8,5},{9,6},{10... | collective-permute-start | bytes 393224 | tf_op jit(solution)/shard_map/ppermute | solution.py:285
  107.5 10.6 %collective-permute-start.9 = (f32[2,64,256]{2,1,0:T(8,128)S(1)}, f32[2,64,256]{2,1,0:T(8,128)S(1)}, u32[]{:S(2)}, u32[]{:S(2)}) collective-permute-start(f32[2,64,256]{2,1,0:T(8,128)S(1)} %pair.3), channel_id=1, source_target_pairs={{0,31},{1,0},{2,1},{3,2},{4,3},{5,4},{6,5},{7,6},{8,7},{9,8},{10,9... | collective-permute-start | bytes 393224 | tf_op jit(solution)/shard_map/ppermute | solution.py:285
  118.1 3.4 %collective-permute-start.11 = (f32[2,64,256]{2,1,0:T(8,128)S(1)}, f32[2,64,256]{2,1,0:T(8,128)S(1)}, u32[]{:S(2)}, u32[]{:S(2)}) collective-permute-start(f32[2,64,256]{2,1,0:T(8,128)S(1)} %swap.3), channel_id=1, source_target_pairs={{0,32},{32,0},{64,96},{96,64},{128,160},{160,128},{192,224},{224,1... | collective-permute-start | bytes 393224 | tf_op jit(solution)/shard_map/ppermute | solution.py:291

commit v6 on v5

--- a/solution.py
+++ b/solution.py
@@ -27,8 +27,8 @@
     return [(i, (i + hop) % count) for i in range(count)]
 
 
-def pack_kernel(queries_hbm, perm_hbm, row_hbm, col_hbm, out_ref, row_ref, col_ref, queries_ref, perm_ref, sems):
-    pairs = ((queries_hbm, queries_ref), (perm_hbm, perm_ref), (row_hbm, row_ref), (col_hbm, col_ref))
+def pack_kernel(queries_hbm, perm_hbm, out_ref, queries_ref, perm_ref, sems):
+    pairs = ((queries_hbm, queries_ref), (perm_hbm, perm_ref))
     copies = [pltpu.make_async_copy(src, dst, sems.at[n]) for n, (src, dst) in enumerate(pairs)]
     for copy in copies:
         copy.start()
@@ -40,7 +40,10 @@
         out_ref[:, h:h + 1, D:] = jnp.broadcast_to(perm[:, h * TILE:(h + 1) * TILE][None], (N_ROW, 1, TILE))
 
 
-def scores_kernel(dev_ref, packed_ref, desc_ref, cand_ref, out_ref):
+def scores_kernel(dev_ref, row_in_ref, col_in_ref, packed_ref, desc_ref, cand_ref, out_ref, row_ref, col_ref):
+    for t in range(row_ref.shape[0]):
+        row_ref[t] = row_in_ref[t]
+        col_ref[t] = col_in_ref[t]
     scores = lax.dot_general(
         packed_ref[:, :D], desc_ref[...], (((1,), (1,)), ((), ())),
         precision=HIGHEST, preferred_element_type=F32,
@@ -58,7 +61,7 @@
 GROUPS = 2
 
 
-def permute_kernel(table_ref, packed_ref, out_ref, graph_ref):
+def permute_kernel(table_ref, packed_ref, graph_ref):
     rows = N_ROW * HALF
     perm = packed_ref[:, D:].astype(jnp.int32)
     for first in range(0, rows, 8 * GROUPS):
@@ -77,7 +80,10 @@
         for q in range(QS):
             for g, span in enumerate(spans):
                 graph_ref[q, span, :] = acc[q][g]
-    width = len(HOPS) * QS * HALF
+
+
+def payload_kernel(graph_ref, low_ref, high_ref, out_ref):
+    width = SLOTS * QS * HALF
     for q in range(QS):
         for h in range(HALF):
             mine = graph_ref[q, pl.ds(h, N_ROW, stride=HALF), :]
@@ -85,14 +91,18 @@
                 hop = hop % N_ROW
                 rolled = mine if hop == 0 else jnp.concatenate([mine[hop:], mine[:hop]], axis=0)
                 out_ref[pl.ds((k * QS + q) * HALF + h, N_ROW, stride=width), :] = rolled
-
-
-def near_slot(col, place_ref):
+            for n, ref in enumerate((low_ref, high_ref)):
+                out_ref[pl.ds(((len(HOPS) + n) * QS + q) * HALF + h, N_ROW, stride=width), :] = ref[
+                    q, pl.ds(h, N_ROW, stride=HALF), :]
+
+
+def first_slot(col, place_ref):
     hop = ((col >> 1) - place_ref[0]) & (N_ROW - 1)
     slot = jnp.int32(0)
     for k, h in enumerate(HOPS):
         slot = jnp.where(hop == h % N_ROW, k, slot)
-    return slot * HALF + (col & 1)
+    slot = slot * HALF + (col & 1)
+    return jnp.where(col >= N_ROW * HALF, col - N_ROW * HALF + len(HOPS) * HALF, slot)
 
 
 def any_slot(col, place_ref):
@@ -132,28 +142,18 @@
                 copies_ref[x, :, cols] = acc_ref[h]
 
 
-def inner_kernel(place_ref, row_ref, col_ref, near_ref, tiles_ref, out_ref, slots_ref):
-    width = len(HOPS) * QS * HALF
-    for k in range(len(HOPS)):
+def first_kernel(place_ref, row_ref, col_ref, near_ref, tiles_ref, out_ref, copies_ref, own_ref, slots_ref, acc_ref):
+    width = SLOTS * QS * HALF
+    for k in range(SLOTS):
         for h in range(HALF):
             for q in range(QS):
                 slots_ref[k * HALF + h, q * N_ROW:(q + 1) * N_ROW, :] = near_ref[
                     pl.ds((k * QS + q) * HALF + h, N_ROW, stride=width), :]
-    out_ref[...] = jnp.zeros_like(out_ref)
+    for h in range(HALF):
+        own_ref[:, h * TILE:(h + 1) * TILE] = slots_ref[h]
+    acc_ref[...] = jnp.zeros_like(acc_ref)
     for t in range(tiles_ref.shape[0]):
-        inside = col_ref[t] < N_ROW * HALF
-        slot = jnp.where(inside, near_slot(col_ref[t], place_ref), 0)
-        out_ref[row_ref[t]] += jnp.where(inside, product(slots_ref, slot, tiles_ref, t), 0.0)
-
-
-def outer_kernel(row_ref, col_ref, inner_ref, low_ref, high_ref, tiles_ref, out_ref, copies_ref, slots_ref, acc_ref):
-    spread(slots_ref, 0, low_ref[...])
-    spread(slots_ref, 1, high_ref[...])
-    acc_ref[...] = inner_ref[...]
-    for t in range(tiles_ref.shape[0]):
-        @pl.when(col_ref[t] >= N_ROW * HALF)
-        def _():
-            acc_ref[row_ref[t]] += product(slots_ref, col_ref[t] - N_ROW * HALF, tiles_ref, t)
+        acc_ref[row_ref[t]] += product(slots_ref, first_slot(col_ref[t], place_ref), tiles_ref, t)
     store(acc_ref, out_ref, copies_ref)
 
 
@@ -244,27 +244,23 @@
     device = (region * N_ROW + row_index)[None]
     place = jnp.stack([row_index, 1 - 2 * core])
 
+    packed = pl.pallas_call(
+        pack_kernel, out_shape=shape(N_ROW, QS, D + TILE), in_specs=[HBM] * 2, out_specs=VMEM,
+        scratch_shapes=[pltpu.VMEM(queries.shape, F32), pltpu.VMEM(cluster_perm.shape, jnp.int32),
+                        pltpu.SemaphoreType.DMA((2,))],
+        compiler_params=pltpu.CompilerParams(vmem_limit_bytes=64 * 1024 * 1024), name="pack",
+    )(queries, cluster_perm)
+    packed = lax.all_to_all(packed, "row", 0, 0, tiled=True).reshape(Q, D + TILE)
     index = jax.ShapeDtypeStruct(tile_row.shape, jnp.int32)
-    packed, tile_row, tile_col = pl.pallas_call(
-        pack_kernel, out_shape=(shape(N_ROW, QS, D + TILE), index, index), in_specs=[HBM] * 4, out_specs=(VMEM, SMEM, SMEM),
-        scratch_shapes=[pltpu.VMEM(queries.shape, F32), pltpu.VMEM(cluster_perm.shape, jnp.int32),
-                        pltpu.SemaphoreType.DMA((4,))],
-        compiler_params=pltpu.CompilerParams(vmem_limit_bytes=64 * 1024 * 1024), name="pack",
-    )(queries, cluster_perm, tile_row, tile_col)
-    packed = lax.all_to_all(packed, "row", 0, 0, tiled=True).reshape(Q, D + TILE)
-    by_query = pl.pallas_call(
-        scores_kernel, out_shape=shape(N_ROW * QS * HALF, TILE), in_specs=[SMEM, VMEM, VMEM, VMEM], out_specs=VMEM,
-        compiler_params=PARAMS, name="scores",
-    )(device, packed, descriptors, candidates)
+    by_query, tile_row, tile_col = pl.pallas_call(
+        scores_kernel, out_shape=(shape(N_ROW * QS * HALF, TILE), index, index),
+        in_specs=[SMEM] * 3 + [VMEM] * 3, out_specs=(VMEM, SMEM, SMEM), compiler_params=PARAMS, name="scores",
+    )(device, tile_row, tile_col, packed, descriptors, candidates)
     table = lax.all_to_all(by_query.reshape(N_ROW, QS * HALF, TILE), "row", 0, 0, tiled=True)
-    width = len(HOPS) * QS * HALF
-    near = pl.pallas_call(
-        permute_kernel, out_shape=shape(N_ROW * width, TILE), in_specs=[VMEM, VMEM], out_specs=VMEM,
-        scratch_shapes=[pltpu.VMEM((QS, N_ROW * HALF, TILE), F32)],
+    graph = pl.pallas_call(
+        permute_kernel, out_shape=shape(QS, N_ROW * HALF, TILE), in_specs=[VMEM, VMEM], out_specs=VMEM,
         compiler_params=PARAMS, name="permute",
     )(table.reshape(N_ROW * QS * HALF, TILE), packed)
-    near = lax.all_to_all(near.reshape(N_ROW, width, TILE), "row", 0, 0, tiled=True)
-    v0 = near[:, :QS * HALF].reshape(N_ROW, QS, HALF, TILE).transpose(1, 0, 2, 3).reshape(Q, ROWS)
 
     def region_pair(v):
         return (lax.ppermute(v, "region", ring(N_REGION, 1)), lax.ppermute(v, "region", ring(N_REGION, -1)))
@@ -293,18 +289,17 @@
 
     slots = pltpu.VMEM((SLOTS * HALF, Q, TILE), F32)
     acc = pltpu.VMEM((HALF, Q, TILE), F32)
-    low, high = region_pair(v0)
-    inner = pl.pallas_call(
-        inner_kernel, out_shape=shape(HALF, Q, TILE), in_specs=[SMEM] * 3 + [VMEM] * 2, out_specs=VMEM,
-        scratch_shapes=[pltpu.VMEM((len(HOPS) * HALF, Q, TILE), F32)],
-        cost_estimate=pl.CostEstimate(flops=2 * 12 * Q * TILE * TILE, bytes_accessed=2000000, transcendentals=0),
-        compiler_params=PARAMS, name="first_inner",
+    width = SLOTS * QS * HALF
+    near = pl.pallas_call(
+        payload_kernel, out_shape=shape(N_ROW * width, TILE), in_specs=[VMEM] * 3, out_specs=VMEM,
+        compiler_params=PARAMS, name="payload",
+    )(graph, *region_pair(graph))
+    near = lax.all_to_all(near.reshape(N_ROW, width, TILE), "row", 0, 0, tiled=True)
+    with_copies = (shape(Q, ROWS), shape(N_X, Q, ROWS))
+    v1, copies, v0 = pl.pallas_call(
+        first_kernel, out_shape=with_copies + (shape(Q, ROWS),), in_specs=[SMEM] * 3 + [VMEM] * 2,
+        out_specs=(VMEM, VMEM, VMEM), scratch_shapes=[slots, acc], compiler_params=PARAMS, name="first",
     )(place, tile_row, tile_col, near.reshape(N_ROW * width, TILE), tile_vals)
-    with_copies = (shape(Q, ROWS), shape(N_X, Q, ROWS))
-    v1, copies = pl.pallas_call(
-        outer_kernel, out_shape=with_copies, in_specs=[SMEM] * 2 + [VMEM] * 4, out_specs=(VMEM, VMEM),
-        scratch_shapes=[pltpu.VMEM((2 * HALF, Q, TILE), F32), acc], compiler_params=PARAMS, name="first_outer",
-    )(tile_row, tile_col, inner, low, high, tile_vals)
     v2, copies = pl.pallas_call(
         next_kernel, out_shape=with_copies, in_specs=[SMEM] * 3 + [VMEM] * (N_BLOCKS + 1), out_specs=(VMEM, VMEM),
         scratch_shapes=[slots, acc], compiler_params=PARAMS, name="second",

time: 152 us -> 158 us (1.039)
  waiting for transfers between devices: 41.2 us -> 46.5 us
    ppermute x2, starting transfers between devices: 4.38 us -> 8.04 us  [exchange(): lax.ppermute(swapped, 'region', [(r, r ^ 1) for r in range(N_REGION)])]
    ppermute x3, waiting for transfers between devices: 0.32 us -> 3.07 us  [region_pair(): lax.ppermute(v, 'region', ring(N_REGION, 1))]
    ppermute x3, waiting for transfers between devices: 0.01 us -> 1.93 us  [region_pair(): lax.ppermute(v, 'region', ring(N_REGION, -1))]
    ppermute x3, starting transfers between devices: 12.1 us -> 10.3 us  [region_pair(): lax.ppermute(v, 'region', ring(N_REGION, -1))]
    all_to_all x1, waiting for transfers between devices: 12.2 us -> 13.9 us  [local(): lax.all_to_all(near.reshape(N_ROW, width, TILE), 'row', 0, 0, tiled=True)]
  transfers between devices with their start and end apart: 16 -> 16, of which waited for: 9 -> 10; matrix products, arithmetic and copies ran while one was open for 0% -> 0% of each run, Pallas kernels for 1% -> 0%
where the time goes in v6:
time: 158 us; the launch traced here: 157 us
  starting transfers between devices  55.6 us (35%)
  waiting for transfers between devices  46.5 us (29%)
  blocking collectives  40.4 us (26%)
  Pallas kernels  12.7 us (8%)
    ppermute x4, waiting for transfers between devices, exchange(): got.append(lax.ppermute(both, ('region', 'row'), pairs))  16.3 us
    all_to_all x1, blocking collectives, local(): lax.all_to_all(jnp.broadcast_to(moments[None], (N_ROW, 4, TILE)), 'row',...  15.6 us
    all_to_all x1, waiting for transfers between devices, local(): lax.all_to_all(near.reshape(N_ROW, width, TILE), 'row', 0, 0, tiled=True)  13.9 us
    all_to_all x1, blocking collectives, local(): lax.all_to_all(by_query.reshape(N_ROW, QS * HALF, TILE), 'row', 0, 0, til...  13.3 us
    ppermute x4, starting transfers between devices, exchange(): got.append(lax.ppermute(both, ('region', 'row'), pairs))  12.4 us
    all_to_all x1, blocking collectives, local(): lax.all_to_all(jnp.broadcast_to(moments[None], (N_REGION, 4, TILE)), 'reg...  11.6 us
    all_to_all x1, starting transfers between devices, local(): lax.all_to_all(packed, 'row', 0, 0, tiled=True).reshape(Q, D + TILE)  10.6 us
    ppermute x3, starting transfers between devices, region_pair(): lax.ppermute(v, 'region', ring(N_REGION, -1))  10.3 us
  transfers between devices with their start and end apart: 16, of which 10 were waited for; matrix products, arithmetic and copies ran while one was open for 0% of the time, Pallas kernels for 0%

profile of v6, /device:TPU:1, one launch (start us, length us, event | category | flops | bytes accessed | tf_op | source)
XLA Modules:
  0.0 156.9 jit_solution(13061032421198204494)
XLA Ops:
  0.6 1.4 pack.1
  2.0 0.0 copy-start.1
  2.1 10.6 %all-to-all-start = ((f32[32,2,640]{2,1,0:T(2,128)}), f32[32,2,640]{2,1,0:T(2,128)S(1)}, u32[]{:S(2)}, u32[]{:S(2)}) async-start(f32[32,2,640]{2,1,0:T(2,128)} %pack.1), calls=%async_computation | async-start | bytes 327680 | tf_op jit(solution)/shard_map/all_to_all | solution.py:253
  12.7 0.0 copy-start.2
  12.7 9.3 %all-to-all-done = f32[32,2,640]{2,1,0:T(2,128)S(1)} async-done(((f32[32,2,640]{2,1,0:T(2,128)}), f32[32,2,640]{2,1,0:T(2,128)S(1)}, u32[]{:S(2)}, u32[]{:S(2)}) %all-to-all-start) | async-done | bytes 163872 | tf_op jit(solution)/shard_map/all_to_all | solution.py:253
  22.1 0.1 reshape.22.packed_ref
  22.2 0.0 copy-start.3
  22.2 0.0 copy-start.4
  22.2 0.6 copy-done.3
  22.8 0.0 copy-done.4
  22.9 1.6 scores.1
  24.4 13.3 %all_to_all.35 = f32[32,4,128]{2,1,0:T(4,128)S(1)} all-to-all(f32[32,4,128]{2,1,0:T(4,128)S(1)} %bitcast.10), channel_id=1, replica_groups=mesh['region'=16,'row'=32] {'row'}, dimensions={0} | all-to-all | bytes 131072 | tf_op jit(solution)/shard_map/all_to_all | solution.py:259
  37.7 2.0 %permute.1.graph_ref = f32[2,64,128]{2,1,0:T(8,128)S(1)} custom-call(f32[128,128]{1,0:T(8,128)S(1)} %bitcast.9, f32[64,640]{1,0:T(8,128)S(1)} %reshape.22.packed_ref), custom_call_target="tpu_custom_call" | custom-call | tf_op jit(solution)/shard_map/permute/pallas_call | solution.py:260
  39.7 2.9 %collective-permute-start.1 = (f32[2,64,128]{2,1,0:T(8,128)S(1)}, f32[2,64,128]{2,1,0:T(8,128)S(1)}, u32[]{:S(2)}, u32[]{:S(2)}) collective-permute-start(f32[2,64,128]{2,1,0:T(8,128)S(1)} %permute.1.graph_ref), channel_id=1, source_target_pairs={{0,480},{32,0},{64,32},{96,64},{128,96},{160,128},{192,160},{224,1... | collective-permute-start | bytes 196616 | tf_op jit(solution)/shard_map/ppermute | solution.py:266
  42.6 2.0 %collective-permute-start = (f32[2,64,128]{2,1,0:T(8,128)S(1)}, f32[2,64,128]{2,1,0:T(8,128)S(1)}, u32[]{:S(2)}, u32[]{:S(2)}) collective-permute-start(f32[2,64,128]{2,1,0:T(8,128)S(1)} %permute.1.graph_ref), channel_id=1, source_target_pairs={{0,32},{32,64},{64,96},{96,128},{128,160},{160,192},{192,224},{224... | collective-permute-start | bytes 196616 | tf_op jit(solution)/shard_map/ppermute | solution.py:266
  44.7 1.9 %collective-permute-done.1.high_ref = f32[2,64,128]{2,1,0:T(8,128)S(1)} collective-permute-done((f32[2,64,128]{2,1,0:T(8,128)S(1)}, f32[2,64,128]{2,1,0:T(8,128)S(1)}, u32[]{:S(2)}, u32[]{:S(2)}) %collective-permute-start.1) | collective-permute-done | bytes 65568 | tf_op jit(solution)/shard_map/ppermute | solution.py:266
  46.6 3.1 %collective-permute-done.low_ref = f32[2,64,128]{2,1,0:T(8,128)S(1)} collective-permute-done((f32[2,64,128]{2,1,0:T(8,128)S(1)}, f32[2,64,128]{2,1,0:T(8,128)S(1)}, u32[]{:S(2)}, u32[]{:S(2)}) %collective-permute-start) | collective-permute-done | bytes 65568 | tf_op jit(solution)/shard_map/ppermute | solution.py:266
  49.6 1.0 payload.1
  50.6 4.0 %all-to-all-start.2 = ((f32[32,40,128]{2,1,0:T(8,128)}), f32[32,40,128]{2,1,0:T(8,128)S(1)}, u32[]{:S(2)}, u32[]{:S(2)}) async-start(f32[32,40,128]{2,1,0:T(8,128)} %bitcast.5), calls=%async_computation.2 | async-start | bytes 1310720 | tf_op jit(solution)/shard_map/all_to_all | solution.py:297
  54.7 0.1 pad_add_fusion.place_ref
  54.7 13.9 %all-to-all-done.2 = f32[32,40,128]{2,1,0:T(8,128)S(1)} async-done(((f32[32,40,128]{2,1,0:T(8,128)}), f32[32,40,128]{2,1,0:T(8,128)S(1)}, u32[]{:S(2)}, u32[]{:S(2)}) %all-to-all-start.2) | async-done | bytes 655392 | tf_op jit(solution)/shard_map/all_to_all | solution.py:297
  68.6 2.0 %first.1 = (f32[64,256]{1,0:T(8,128)S(1)}, f32[4,64,256]{2,1,0:T(8,128)}, f32[64,256]{1,0:T(8,128)S(1)}) custom-call(s32[2]{0:T(128)S(1)} %pad_add_fusion.place_ref, s32[12]{0:T(128)S(1)} %get-tuple-element.18.row_ref, s32[12]{0:T(128)S(1)} %get-tuple-element.19.col_ref, f32[1280,128]{1,0:T(8,128)S(1)} %bitcast.8, f32[12,128,128]{2,1,0:T(8,128)S(1)} %copy-done), custom_call_target="tpu_custom_call" | custom-call | tf_op jit(solution)/shard_map/first/pallas_call | solution.py:299
  70.6 7.0 %collective-permute-start.3 = (f32[64,256]{1,0:T(8,128)S(1)}, f32[64,256]{1,0:T(8,128)S(1)}, u32[]{:S(2)}, u32[]{:S(2)}) collective-permute-start(f32[64,256]{1,0:T(8,128)S(1)} %get-tuple-element.21.own_ref.refs_0_.refs_8_.v1_ref), channel_id=1, source_target_pairs={{0,480},{32,0},{64,32},{96,64},{128,96},{160,128},{192,160},{224,1... | collective-permute-start | bytes 196616 | tf_op jit(solution)/shard_map/ppermute | solution.py:266
  77.6 0.0 collective-permute-start.2
  77.6 3.4 %all-to-all-start.3 = ((f32[4,64,256]{2,1,0:T(8,128)}), f32[4,64,256]{2,1,0:T(8,128)S(1)}, u32[]{:S(2)}, u32[]{:S(2)}) async-start(f32[4,64,256]{2,1,0:T(8,128)} %get-tuple-element.22), calls=%async_computation.3 | async-start | bytes 524288 | tf_op jit(solution)/shard_map/all_to_all | solution.py:270
  81.0 0.0 collective-permute-done.3.high_ref.refs_6_
  81.0 0.0 collective-permute-done.2.low_ref.refs_5_
  81.1 4.3 %collective-permute-start.5 = (f32[2,64,256]{2,1,0:T(8,128)S(1)}, f32[2,64,256]{2,1,0:T(8,128)S(1)}, u32[]{:S(2)}, u32[]{:S(2)}) collective-permute-start(f32[2,64,256]{2,1,0:T(8,128)S(1)} %pair.2), channel_id=1, source_target_pairs={{0,29},{1,30},{2,31},{3,0},{4,1},{5,2},{6,3},{7,4},{8,5},{9,6},{10... | collective-permute-start | bytes 393224 | tf_op jit(solution)/shard_map/ppermute | solution.py:281
  85.4 1.9 %collective-permute-start.4 = (f32[2,64,256]{2,1,0:T(8,128)S(1)}, f32[2,64,256]{2,1,0:T(8,128)S(1)}, u32[]{:S(2)}, u32[]{:S(2)}) collective-permute-start(f32[2,64,256]{2,1,0:T(8,128)S(1)} %pair.2), channel_id=1, source_target_pairs={{0,31},{1,0},{2,1},{3,2},{4,3},{5,4},{6,5},{7,6},{8,7},{9,8},{10,9... | collective-permute-start | bytes 393224 | tf_op jit(solution)/shard_map/ppermute | solution.py:281
  87.4 5.4 %collective-permute-done.5.refs_1_.refs_3_ = f32[2,64,256]{2,1,0:T(8,128)S(1)} collective-permute-done((f32[2,64,256]{2,1,0:T(8,128)S(1)}, f32[2,64,256]{2,1,0:T(8,128)S(1)}, u32[]{:S(2)}, u32[]{:S(2)}) %collective-permute-start.5) | collective-permute-done | bytes 131104 | tf_op jit(solution)/shard_map/ppermute | solution.py:281
  92.8 2.7 %collective-permute-done.4.refs_0_.refs_2_ = f32[2,64,256]{2,1,0:T(8,128)S(1)} collective-permute-done((f32[2,64,256]{2,1,0:T(8,128)S(1)}, f32[2,64,256]{2,1,0:T(8,128)S(1)}, u32[]{:S(2)}, u32[]{:S(2)}) %collective-permute-start.4) | collective-permute-done | bytes 131104 | tf_op jit(solution)/shard_map/ppermute | solution.py:281
  95.6 3.6 %collective-permute-start.6 = (f32[2,64,256]{2,1,0:T(8,128)S(1)}, f32[2,64,256]{2,1,0:T(8,128)S(1)}, u32[]{:S(2)}, u32[]{:S(2)}) collective-permute-start(f32[2,64,256]{2,1,0:T(8,128)S(1)} %swap.2), channel_id=1, source_target_pairs={{0,32},{32,0},{64,96},{96,64},{128,160},{160,128},{192,224},{224,1... | collective-permute-start | bytes 393224 | tf_op jit(solution)/shard_map/ppermute | solution.py:287
  99.1 1.0 collective-permute-done.6.refs_4_
  100.1 1.9 %second.1 = (f32[64,256]{1,0:T(8,128)S(1)}, f32[4,64,256]{2,1,0:T(8,128)}) custom-call(s32[2]{0:T(128)S(1)} %pad_add_fusion.place_ref, s32[12]{0:T(128)S(1)} %get-tuple-element.18.row_ref, s32[12]{0:T(128)S(1)} %get-tuple-element.19.col_ref, f32[64,256]{1,0:T(8,128)S(1)} %get-tuple-element.21.own_ref.refs_0_.refs_8_.v1_ref, ...), custom_call_target="tpu_custom_call" | custom-call | tf_op jit(solution)/shard_map/second/pallas_call | solution.py:303
  102.0 0.4 collective-permute-start.8
  102.4 1.4 collective-permute-start.7
  103.8 3.4 %all-to-all-start.4 = ((f32[4,64,256]{2,1,0:T(8,128)}), f32[4,64,256]{2,1,0:T(8,128)S(1)}, u32[]{:S(2)}, u32[]{:S(2)}) async-start(f32[4,64,256]{2,1,0:T(8,128)} %get-tuple-element.27), calls=%async_computation.4 | async-start | bytes 524288 | tf_op jit(solution)/shard_map/all_to_all | solution.py:270
  107.2 0.0 collective-permute-done.8.high_ref.refs_6_
  107.2 4.1 %collective-permute-start.10 = (f32[2,64,256]{2,1,0:T(8,128)S(1)}, f32[2,64,256]{2,1,0:T(8,128)S(1)}, u32[]{:S(2)}, u32[]{:S(2)}) collective-permute-start(f32[2,64,256]{2,1,0:T(8,128)S(1)} %pair.3), channel_id=1, source_target_pairs={{0,29},{1,30},{2,31},{3,0},{4,1},{5,2},{6,3},{7,4},{8,5},{9,6},{10... | collective-permute-start | bytes 393224 | tf_op jit(solution)/shard_map/ppermute | solution.py:281
  111.3 2.0 %collective-permute-start.9 = (f32[2,64,256]{2,1,0:T(8,128)S(1)}, f32[2,64,256]{2,1,0:T(8,128)S(1)}, u32[]{:S(2)}, u32[]{:S(2)}) collective-permute-start(f32[2,64,256]{2,1,0:T(8,128)S(1)} %pair.3), channel_id=1, source_target_pairs={{0,31},{1,0},{2,1},{3,2},{4,3},{5,4},{6,5},{7,6},{8,7},{9,8},{10,9... | collective-permute-start | bytes 393224 | tf_op jit(solution)/shard_map/ppermute | solution.py:281
  113.3 4.9 %collective-permute-done.10.refs_1_.refs_3_ = f32[2,64,256]{2,1,0:T(8,128)S(1)} collective-permute-done((f32[2,64,256]{2,1,0:T(8,128)S(1)}, f32[2,64,256]{2,1,0:T(8,128)S(1)}, u32[]{:S(2)}, u32[]{:S(2)}) %collective-permute-start.10) | collective-permute-done | bytes 131104 | tf_op jit(solution)/shard_map/ppermute | solution.py:281
  118.2 3.2 %collective-permute-done.9.refs_0_.refs_2_ = f32[2,64,256]{2,1,0:T(8,128)S(1)} collective-permute-done((f32[2,64,256]{2,1,0:T(8,128)S(1)}, f32[2,64,256]{2,1,0:T(8,128)S(1)}, u32[]{:S(2)}, u32[]{:S(2)}) %collective-permute-start.9) | collective-permute-done | bytes 131104 | tf_op jit(solution)/shard_map/ppermute | solution.py:281
  121.5 4.5 %collective-permute-start.11 = (f32[2,64,256]{2,1,0:T(8,128)S(1)}, f32[2,64,256]{2,1,0:T(8,128)S(1)}, u32[]{:S(2)}, u32[]{:S(2)}) collective-permute-start(f32[2,64,256]{2,1,0:T(8,128)S(1)} %swap.3), channel_id=1, source_target_pairs={{0,32},{32,0},{64,96},{96,64},{128,160},{160,128},{192,224},{224,1... | collective-permute-start | bytes 393224 | tf_op jit(solution)/shard_map/ppermute | solution.py:287
  125.9 1.0 collective-permute-done.11.refs_4_
  126.9 1.3 third.1
  128.2 15.6 %all_to_all.36 = f32[32,4,128]{2,1,0:T(4,128)S(1)} all-to-all(f32[32,4,128]{2,1,0:T(4,128)S(1)} %broadcast_in_dim.10), channel_id=1, replica_groups=mesh['region'=16,'row'=32] {'row'}, dimensions={0} | all-to-all | bytes 131072 | tf_op jit(solution)/shard_map/all_to_all | solution.py:313
  143.9 11.6 %all_to_all.37.moments_ref = f32[16,4,128]{2,1,0:T(4,128)S(1)} all-to-all(f32[16,4,128]{2,1,0:T(4,128)S(1)} %broadcast_in_dim.22), channel_id=1, replica_groups=mesh['region'=16,'row'=32] {'region'}, dimensions={0} | all-to-all | bytes 65536 | tf_op jit(solution)/shard_map/all_to_all | solution.py:315
  155.4 1.5 finish.1
  (14 shorter events, 0.1 us)
Async XLA Ops:
  2.0 20.2 %copy-start.1 = (f32[256,512]{1,0:T(8,128)S(1)}, f32[256,512]{1,0:T(8,128)}, u32[]{:S(2)}) copy-start(f32[256,512]{1,0:T(8,128)} %desc_ref.1) | copy-start | bytes 1572868
  2.1 20.0 %all-to-all-start = ((f32[32,2,640]{2,1,0:T(2,128)}), f32[32,2,640]{2,1,0:T(2,128)S(1)}, u32[]{:S(2)}, u32[]{:S(2)}) async-start(f32[32,2,640]{2,1,0:T(2,128)} %pack.1), calls=%async_computation | async-start | bytes 327680 | tf_op jit(solution)/shard_map/all_to_all | solution.py:253
  12.7 9.5 %copy-start.2 = (s32[64,64]{1,0:T(8,128)S(1)}, s32[64,64]{1,0:T(8,128)}, u32[]{:S(2)}) copy-start(s32[64,64]{1,0:T(8,128)} %cand_ref.1) | copy-start | bytes 49156
  22.2 0.7 copy-start.3
  22.2 0.7 copy-start.4
  39.7 6.8 %collective-permute-start.1 = (f32[2,64,128]{2,1,0:T(8,128)S(1)}, f32[2,64,128]{2,1,0:T(8,128)S(1)}, u32[]{:S(2)}, u32[]{:S(2)}) collective-permute-start(f32[2,64,128]{2,1,0:T(8,128)S(1)} %permute.1.graph_ref), channel_id=1, source_target_pairs={{0,480},{32,0},{64,32},{96,64},{128,96},{160,128},{192,160},{224,1... | collective-permute-start | bytes 196616 | tf_op jit(solution)/shard_map/ppermute | solution.py:266
  42.6 7.0 %collective-permute-start = (f32[2,64,128]{2,1,0:T(8,128)S(1)}, f32[2,64,128]{2,1,0:T(8,128)S(1)}, u32[]{:S(2)}, u32[]{:S(2)}) collective-permute-start(f32[2,64,128]{2,1,0:T(8,128)S(1)} %permute.1.graph_ref), channel_id=1, source_target_pairs={{0,32},{32,64},{64,96},{96,128},{128,160},{160,192},{192,224},{224... | collective-permute-start | bytes 196616 | tf_op jit(solution)/shard_map/ppermute | solution.py:266
  50.6 18.0 %copy-start = (f32[12,128,128]{2,1,0:T(8,128)S(1)}, f32[12,128,128]{2,1,0:T(8,128)}, u32[]{:S(2)}) copy-start(f32[12,128,128]{2,1,0:T(8,128)} %refs_9_.1) | copy-start | bytes 2359300
  50.6 18.0 %all-to-all-start.2 = ((f32[32,40,128]{2,1,0:T(8,128)}), f32[32,40,128]{2,1,0:T(8,128)S(1)}, u32[]{:S(2)}, u32[]{:S(2)}) async-start(f32[32,40,128]{2,1,0:T(8,128)} %bitcast.5), calls=%async_computation.2 | async-start | bytes 1310720 | tf_op jit(solution)/shard_map/all_to_all | solution.py:297
  70.6 10.4 %collective-permute-start.3 = (f32[64,256]{1,0:T(8,128)S(1)}, f32[64,256]{1,0:T(8,128)S(1)}, u32[]{:S(2)}, u32[]{:S(2)}) collective-permute-start(f32[64,256]{1,0:T(8,128)S(1)} %get-tuple-element.21.own_ref.refs_0_.refs_8_.v1_ref), channel_id=1, source_target_pairs={{0,480},{32,0},{64,32},{96,64},{128,96},{160,128},{192,160},{224,1... | collective-permute-start | bytes 196616 | tf_op jit(solution)/shard_map/ppermute | solution.py:266
  77.6 3.4 %collective-permute-start.2 = (f32[64,256]{1,0:T(8,128)S(1)}, f32[64,256]{1,0:T(8,128)S(1)}, u32[]{:S(2)}, u32[]{:S(2)}) collective-permute-start(f32[64,256]{1,0:T(8,128)S(1)} %get-tuple-element.21.own_ref.refs_0_.refs_8_.v1_ref), channel_id=1, source_target_pairs={{0,32},{32,64},{64,96},{96,128},{128,160},{160,192},{192,224},{224... | collective-permute-start | bytes 196616 | tf_op jit(solution)/shard_map/ppermute | solution.py:266
  77.6 9.7 %all-to-all-start.3 = ((f32[4,64,256]{2,1,0:T(8,128)}), f32[4,64,256]{2,1,0:T(8,128)S(1)}, u32[]{:S(2)}, u32[]{:S(2)}) async-start(f32[4,64,256]{2,1,0:T(8,128)} %get-tuple-element.22), calls=%async_computation.3 | async-start | bytes 524288 | tf_op jit(solution)/shard_map/all_to_all | solution.py:270
  81.1 11.7 %collective-permute-start.5 = (f32[2,64,256]{2,1,0:T(8,128)S(1)}, f32[2,64,256]{2,1,0:T(8,128)S(1)}, u32[]{:S(2)}, u32[]{:S(2)}) collective-permute-start(f32[2,64,256]{2,1,0:T(8,128)S(1)} %pair.2), channel_id=1, source_target_pairs={{0,29},{1,30},{2,31},{3,0},{4,1},{5,2},{6,3},{7,4},{8,5},{9,6},{10... | collective-permute-start | bytes 393224 | tf_op jit(solution)/shard_map/ppermute | solution.py:281
  85.4 10.1 %collective-permute-start.4 = (f32[2,64,256]{2,1,0:T(8,128)S(1)}, f32[2,64,256]{2,1,0:T(8,128)S(1)}, u32[]{:S(2)}, u32[]{:S(2)}) collective-permute-start(f32[2,64,256]{2,1,0:T(8,128)S(1)} %pair.2), channel_id=1, source_target_pairs={{0,31},{1,0},{2,1},{3,2},{4,3},{5,4},{6,5},{7,6},{8,7},{9,8},{10,9... | collective-permute-start | bytes 393224 | tf_op jit(solution)/shard_map/ppermute | solution.py:281
  95.6 4.5 %collective-permute-start.6 = (f32[2,64,256]{2,1,0:T(8,128)S(1)}, f32[2,64,256]{2,1,0:T(8,128)S(1)}, u32[]{:S(2)}, u32[]{:S(2)}) collective-permute-start(f32[2,64,256]{2,1,0:T(8,128)S(1)} %swap.2), channel_id=1, source_target_pairs={{0,32},{32,0},{64,96},{96,64},{128,160},{160,128},{192,224},{224,1... | collective-permute-start | bytes 393224 | tf_op jit(solution)/shard_map/ppermute | solution.py:287
  102.0 5.2 %collective-permute-start.8 = (f32[64,256]{1,0:T(8,128)S(1)}, f32[64,256]{1,0:T(8,128)S(1)}, u32[]{:S(2)}, u32[]{:S(2)}) collective-permute-start(f32[64,256]{1,0:T(8,128)S(1)} %get-tuple-element.26.own_ref.refs_0_.v2_ref), channel_id=1, source_target_pairs={{0,480},{32,0},{64,32},{96,64},{128,96},{160,128},{192,160},{224,1... | collective-permute-start | bytes 196616 | tf_op jit(solution)/shard_map/ppermute | solution.py:266
  102.4 4.8 %collective-permute-start.7 = (f32[64,256]{1,0:T(8,128)S(1)}, f32[64,256]{1,0:T(8,128)S(1)}, u32[]{:S(2)}, u32[]{:S(2)}) collective-permute-start(f32[64,256]{1,0:T(8,128)S(1)} %get-tuple-element.26.own_ref.refs_0_.v2_ref), channel_id=1, source_target_pairs={{0,32},{32,64},{64,96},{96,128},{128,160},{160,192},{192,224},{224... | collective-permute-start | bytes 196616 | tf_op jit(solution)/shard_map/ppermute | solution.py:266
  103.8 9.6 %all-to-all-start.4 = ((f32[4,64,256]{2,1,0:T(8,128)}), f32[4,64,256]{2,1,0:T(8,128)S(1)}, u32[]{:S(2)}, u32[]{:S(2)}) async-start(f32[4,64,256]{2,1,0:T(8,128)} %get-tuple-element.27), calls=%async_computation.4 | async-start | bytes 524288 | tf_op jit(solution)/shard_map/all_to_all | solution.py:270
  107.2 11.0 %collective-permute-start.10 = (f32[2,64,256]{2,1,0:T(8,128)S(1)}, f32[2,64,256]{2,1,0:T(8,128)S(1)}, u32[]{:S(2)}, u32[]{:S(2)}) collective-permute-start(f32[2,64,256]{2,1,0:T(8,128)S(1)} %pair.3), channel_id=1, source_target_pairs={{0,29},{1,30},{2,31},{3,0},{4,1},{5,2},{6,3},{7,4},{8,5},{9,6},{10... | collective-permute-start | bytes 393224 | tf_op jit(solution)/shard_map/ppermute | solution.py:281
  111.3 10.1 %collective-permute-start.9 = (f32[2,64,256]{2,1,0:T(8,128)S(1)}, f32[2,64,256]{2,1,0:T(8,128)S(1)}, u32[]{:S(2)}, u32[]{:S(2)}) collective-permute-start(f32[2,64,256]{2,1,0:T(8,128)S(1)} %pair.3), channel_id=1, source_target_pairs={{0,31},{1,0},{2,1},{3,2},{4,3},{5,4},{6,5},{7,6},{8,7},{9,8},{10,9... | collective-permute-start | bytes 393224 | tf_op jit(solution)/shard_map/ppermute | solution.py:281
  121.5 5.4 %collective-permute-start.11 = (f32[2,64,256]{2,1,0:T(8,128)S(1)}, f32[2,64,256]{2,1,0:T(8,128)S(1)}, u32[]{:S(2)}, u32[]{:S(2)}) collective-permute-start(f32[2,64,256]{2,1,0:T(8,128)S(1)} %swap.3), channel_id=1, source_target_pairs={{0,32},{32,0},{64,96},{96,64},{128,160},{160,128},{192,224},{224,1... | collective-permute-start | bytes 393224 | tf_op jit(solution)/shard_map/ppermute | solution.py:287

commit v7 on v5

--- a/solution.py
+++ b/solution.py
@@ -188,12 +188,31 @@
     store(acc_ref, out_ref, copies_ref)
 
 
-def last_kernel(place_ref, row_ref, col_ref, *refs):
-    blocks = refs[:N_BLOCKS]
-    v0_ref, v1_ref, tiles_ref, out_ref, moments_ref, slots_ref, acc_ref = refs[N_BLOCKS:]
-    times_s(place_ref, row_ref, col_ref, blocks, tiles_ref, slots_ref, acc_ref)
-    store(acc_ref, out_ref)
-    vs = [v0_ref[...], v1_ref[...], blocks[0][...], out_ref[...]]
+def side(col, place_ref):
+    hop = (col >> 1) - place_ref[0]
+    kind = jnp.int32(0)
+    for sign, value in ((1, 1), (-1, 2)):
+        for h in SHARED:
+            kind = jnp.where((hop & (N_ROW - 1)) == sign * h % N_ROW, value, kind)
+    return jnp.where(col >= N_ROW * HALF, 0, kind)
+
+
+def half_kernel(place_ref, row_ref, col_ref, v2_ref, line_ref, a_ref, b_ref, low_ref, high_ref, v0_ref, v1_ref, tiles_ref,
+                part_ref, moments_ref, slots_ref, acc_ref):
+    blocks = [line_ref[x] for x in range(N_X)] + [a_ref[...], b_ref[...], None, None, low_ref[...], high_ref[...]]
+    for k, block in enumerate(blocks):
+        if block is not None:
+            spread(slots_ref, k, block)
+    acc_ref[...] = jnp.zeros_like(acc_ref)
+    for t in range(tiles_ref.shape[0]):
+        kind = side(col_ref[t], place_ref)
+        slot = jnp.where(kind == 2, 0, any_slot(col_ref[t], place_ref))
+        acc_ref[kind * HALF + row_ref[t]] += product(slots_ref, slot, tiles_ref, t)
+    doubled = []
+    for h in range(HALF):
+        part_ref[h] = acc_ref[h] + acc_ref[HALF + h]
+        doubled.append(acc_ref[h] + 2.0 * acc_ref[HALF + h])
+    vs = [v0_ref[...], v1_ref[...], v2_ref[...], jnp.concatenate(doubled, axis=1)]
     lane = lax.broadcasted_iota(jnp.int32, (Q, TILE), 1)
     packed = [jnp.zeros((Q, TILE), F32), jnp.zeros((Q, TILE), F32)]
     for m in range(6):
@@ -201,6 +220,18 @@
         total = jnp.sum(prod[:, :TILE] + prod[:, TILE:], axis=1, keepdims=True)
         packed[m % 2] = jnp.where(lane == m // 2, total, packed[m % 2])
     moments_ref[...] = jnp.concatenate(packed, axis=0).T[:4]
+
+
+def rest_kernel(place_ref, row_ref, col_ref, part_ref, a_ref, b_ref, tiles_ref, out_ref, slots_ref, acc_ref):
+    spread(slots_ref, 0, a_ref[...])
+    spread(slots_ref, 1, b_ref[...])
+    acc_ref[...] = part_ref[...]
+    for t in range(tiles_ref.shape[0]):
+        @pl.when(side(col_ref[t], place_ref) == 2)
+        def _():
+            slot = any_slot(col_ref[t], place_ref) - (N_X + len(SHARED)) * HALF
+            acc_ref[row_ref[t]] += product(slots_ref, slot, tiles_ref, t)
+    store(acc_ref, out_ref)
 
 
 def finish_kernel(moments_ref, v0_ref, v1_ref, v2_ref, v3_ref, diffused_ref, residual_ref):
@@ -243,6 +274,7 @@
     core = region & 1
     device = (region * N_ROW + row_index)[None]
     place = jnp.stack([row_index, 1 - 2 * core])
+    upward = jnp.stack([row_index, jnp.int32(1)])
 
     index = jax.ShapeDtypeStruct(tile_row.shape, jnp.int32)
     packed, tile_row, tile_col = pl.pallas_call(
@@ -269,11 +301,14 @@
     def region_pair(v):
         return (lax.ppermute(v, "region", ring(N_REGION, 1)), lax.ppermute(v, "region", ring(N_REGION, -1)))
 
+    def x_line(copies):
+        return lax.all_to_all(
+            copies, "row", 0, 0, tiled=True,
+            axis_index_groups=[[x * N_Y + y for x in range(N_X)] for y in range(N_Y)])
+
     def exchange(v, copies):
         low, high = region_pair(v)
-        line = lax.all_to_all(
-            copies, "row", 0, 0, tiled=True,
-            axis_index_groups=[[x * N_Y + y for x in range(N_X)] for y in range(N_Y)])
+        line = x_line(copies)
         both = pl.pallas_call(
             pair_kernel, out_shape=shape(2, Q, ROWS), in_specs=[SMEM] + [VMEM] * 3, out_specs=VMEM,
             compiler_params=PARAMS, name="pair",
@@ -309,11 +344,20 @@
         next_kernel, out_shape=with_copies, in_specs=[SMEM] * 3 + [VMEM] * (N_BLOCKS + 1), out_specs=(VMEM, VMEM),
         scratch_shapes=[slots, acc], compiler_params=PARAMS, name="second",
     )(place, tile_row, tile_col, *exchange(v1, copies), tile_vals)
-    v3, moments = pl.pallas_call(
-        last_kernel, out_shape=(shape(Q, ROWS), shape(4, TILE)),
-        in_specs=[SMEM] * 3 + [VMEM] * (N_BLOCKS + 3), out_specs=(VMEM, VMEM),
-        scratch_shapes=[slots, acc], compiler_params=PARAMS, name="third",
-    )(place, tile_row, tile_col, *exchange(v2, copies), v0, v1, tile_vals)
+    ahead = [lax.ppermute(v2, "row", ring(N_ROW, -hop)) for hop in SHARED]
+    part, moments = pl.pallas_call(
+        half_kernel, out_shape=(shape(HALF, Q, TILE), shape(4, TILE)), in_specs=[SMEM] * 3 + [VMEM] * 9,
+        out_specs=(VMEM, VMEM), scratch_shapes=[slots, pltpu.VMEM((3 * HALF, Q, TILE), F32)],
+        compiler_params=PARAMS, name="half",
+    )(upward, tile_row, tile_col, v2, x_line(copies), *ahead, *region_pair(v2), v0, v1, tile_vals)
+    later, moments = lax.optimization_barrier((v2, moments))
+    behind = [lax.ppermute(later, "row", ring(N_ROW, hop)) for hop in SHARED]
+    v3 = pl.pallas_call(
+        rest_kernel, out_shape=shape(Q, ROWS), in_specs=[SMEM] * 3 + [VMEM] * 4, out_specs=VMEM,
+        scratch_shapes=[pltpu.VMEM((2 * HALF, Q, TILE), F32), acc],
+        cost_estimate=pl.CostEstimate(flops=2 * 12 * Q * TILE * TILE, bytes_accessed=2000000, transcendentals=0),
+        compiler_params=PARAMS, name="rest",
+    )(upward, tile_row, tile_col, part, *behind, tile_vals)
 
     moments = lax.all_to_all(jnp.broadcast_to(moments[None], (N_ROW, 4, TILE)), "row", 0, 0, tiled=True)
     moments = jnp.sum(moments.reshape(2, 2, 2, 2, 2, 4, TILE).sum(0).sum(0).sum(0).sum(0), axis=0)

time: 152 us -> 149 us (0.980)
  blocking collectives: 40.2 us -> 13.3 us
  starting transfers between devices: 54.8 us -> 75 us
  waiting for transfers between devices: 41.2 us -> 42.8 us
    all_to_all x2 -> x0, blocking collectives: 26.9 us -> none  [the longest x1 14.5 us: local(): lax.all_to_all(jnp.broadcast_to(moments[None], (N_ROW, 4, TILE)), 'row',...]
    ppermute x0 -> x4, starting transfers between devices: none -> 17.4 us  [the longest x2 9.24 us: local(): behind = [lax.ppermute(later, 'row', ring(N_ROW, hop)) for hop in SHARED]]
    all_to_all x2 -> x4, starting transfers between devices: 6.81 us -> 18.4 us  [the longest x2 6.81 us: x_line(): lax.all_to_all(copies, 'row', 0, 0, tiled=True, axis_index_groups=[[x * N...]
    ppermute x4 -> x2, waiting for transfers between devices: 17.1 us -> 8.43 us  [exchange(): got.append(lax.ppermute(both, ('region', 'row'), pairs))]
    all_to_all x2 -> x4, waiting for transfers between devices: 0.01 us -> 6.34 us  [the longest x1 6.33 us: local(): lax.all_to_all(jnp.broadcast_to(moments[None], (N_REGION, 4, TILE)), 'reg...]
    ppermute x4 -> x2, starting transfers between devices: 13.2 us -> 6.89 us  [exchange(): got.append(lax.ppermute(both, ('region', 'row'), pairs))]
    ppermute x0 -> x4, waiting for transfers between devices: none -> 4.81 us  [the longest x2 4.8 us: local(): ahead = [lax.ppermute(v2, 'row', ring(N_ROW, -hop)) for hop in SHARED]]
    ppermute x2 -> x1, starting transfers between devices: 4.38 us -> 1.92 us  [exchange(): lax.ppermute(swapped, 'region', [(r, r ^ 1) for r in range(N_REGION)])]
  transfers between devices with their start and end apart: 16 -> 19, of which waited for: 9 -> 8; matrix products, arithmetic and copies ran while one was open for 0% -> 1% of each run, Pallas kernels for 1% -> 2%
where the time goes in v7:
time: 149 us; the launch traced here: 148 us
  starting transfers between devices  75 us (50%)
  waiting for transfers between devices  42.8 us (29%)
  Pallas kernels  14.1 us (9%)
  blocking collectives  13.3 us (9%)
  local copies, waits for them, and re-layouts  2.17 us (1%)
    all_to_all x1, blocking collectives, local(): lax.all_to_all(by_query.reshape(N_ROW, QS * HALF, TILE), 'row', 0, 0, til...  13.3 us
    all_to_all x1, waiting for transfers between devices, local(): lax.all_to_all(near.reshape(N_ROW, width, TILE), 'row', 0, 0, tiled=True)  12.2 us
    ppermute x3, starting transfers between devices, region_pair(): lax.ppermute(v, 'region', ring(N_REGION, -1))  12.2 us
    all_to_all x1, starting transfers between devices, local(): lax.all_to_all(packed, 'row', 0, 0, tiled=True).reshape(Q, D + TILE)  10.6 us
    all_to_all x1, waiting for transfers between devices, local(): lax.all_to_all(packed, 'row', 0, 0, tiled=True).reshape(Q, D + TILE)  9.34 us
    ppermute x2, starting transfers between devices, local(): behind = [lax.ppermute(later, 'row', ring(N_ROW, hop)) for hop in SHARED]  9.24 us
    ppermute x2, waiting for transfers between devices, exchange(): got.append(lax.ppermute(both, ('region', 'row'), pairs))  8.43 us
    ppermute x2, starting transfers between devices, local(): ahead = [lax.ppermute(v2, 'row', ring(N_ROW, -hop)) for hop in SHARED]  8.17 us
  transfers between devices with their start and end apart: 19, of which 8 were waited for; matrix products, arithmetic and copies ran while one was open for 1% of the time, Pallas kernels for 2%

profile of v7, /device:TPU:1, one launch (start us, length us, event | category | flops | bytes accessed | tf_op | source)
XLA Modules:
  0.0 148.5 jit_solution(11112366533663282090)
XLA Ops:
  0.6 1.5 %pack.1 = (f32[32,2,640]{2,1,0:T(2,128)}, s32[12]{0:T(128)}, s32[12]{0:T(128)}) custom-call(f32[2,512]{1,0:T(2,128)} %queries_hbm.1, s32[1,256]{1,0:T(1,128)} %perm_hbm.1, s32[12]{0:T(128)} %row_hbm.1, s32[12]{0:T(128)} %col_hbm.1), custom_call_target="tpu_custom_call" | custom-call | tf_op jit(solution)/shard_map/pack/pallas_call | solution.py:280
  2.2 0.0 copy-start.1
  2.2 10.6 %all-to-all-start = ((f32[32,2,640]{2,1,0:T(2,128)}), f32[32,2,640]{2,1,0:T(2,128)S(1)}, u32[]{:S(2)}, u32[]{:S(2)}) async-start(f32[32,2,640]{2,1,0:T(2,128)} %get-tuple-element.18), calls=%async_computation | async-start | bytes 327680 | tf_op jit(solution)/shard_map/all_to_all | solution.py:286
  12.9 0.0 copy-start.2
  12.9 9.3 %all-to-all-done = f32[32,2,640]{2,1,0:T(2,128)S(1)} async-done(((f32[32,2,640]{2,1,0:T(2,128)}), f32[32,2,640]{2,1,0:T(2,128)S(1)}, u32[]{:S(2)}, u32[]{:S(2)}) %all-to-all-start) | async-done | bytes 163872 | tf_op jit(solution)/shard_map/all_to_all | solution.py:286
  22.2 0.1 reshape.28.packed_ref
  22.3 0.6 scores.1
  23.0 13.3 %all_to_all.35 = f32[32,4,128]{2,1,0:T(4,128)S(1)} all-to-all(f32[32,4,128]{2,1,0:T(4,128)S(1)} %bitcast.22), channel_id=1, replica_groups=mesh['region'=16,'row'=32] {'row'}, dimensions={0} | all-to-all | bytes 131072 | tf_op jit(solution)/shard_map/all_to_all | solution.py:291
  36.3 3.0 %permute.1 = f32[1024,128]{1,0:T(8,128)} custom-call(f32[128,128]{1,0:T(8,128)S(1)} %bitcast.21, f32[64,640]{1,0:T(8,128)S(1)} %reshape.28.packed_ref), custom_call_target="tpu_custom_call" | custom-call | tf_op jit(solution)/shard_map/permute/pallas_call | solution.py:293
  39.3 4.0 %all-to-all-start.2 = ((f32[32,32,128]{2,1,0:T(8,128)}), f32[32,32,128]{2,1,0:T(8,128)S(1)}, u32[]{:S(2)}, u32[]{:S(2)}) async-start(f32[32,32,128]{2,1,0:T(8,128)} %bitcast.5), calls=%async_computation.2 | async-start | bytes 1048576 | tf_op jit(solution)/shard_map/all_to_all | solution.py:298
  43.3 12.2 %all-to-all-done.2 = f32[32,32,128]{2,1,0:T(8,128)S(1)} async-done(((f32[32,32,128]{2,1,0:T(8,128)}), f32[32,32,128]{2,1,0:T(8,128)S(1)}, u32[]{:S(2)}, u32[]{:S(2)}) %all-to-all-start.2) | async-done | bytes 524320 | tf_op jit(solution)/shard_map/all_to_all | solution.py:298
  55.6 0.1 copy.17
  55.7 5.4 %collective-permute-start.1 = (f32[64,256]{1,0:T(8,128)S(1)}, f32[64,256]{1,0:T(8,128)S(1)}, u32[]{:S(2)}, u32[]{:S(2)}) collective-permute-start(f32[64,256]{1,0:T(8,128)S(1)} %bitcast.17), channel_id=1, source_target_pairs={{0,480},{32,0},{64,32},{96,64},{128,96},{160,128},{192,160},{224,1... | collective-permute-start | bytes 196616 | tf_op jit(solution)/shard_map/ppermute | solution.py:302
  61.1 2.0 %collective-permute-start = (f32[64,256]{1,0:T(8,128)S(1)}, f32[64,256]{1,0:T(8,128)S(1)}, u32[]{:S(2)}, u32[]{:S(2)}) collective-permute-start(f32[64,256]{1,0:T(8,128)S(1)} %bitcast.18), channel_id=1, source_target_pairs={{0,32},{32,64},{64,96},{96,128},{128,160},{160,192},{192,224},{224... | collective-permute-start | bytes 196616 | tf_op jit(solution)/shard_map/ppermute | solution.py:302
  63.1 0.1 pad_add_fusion.place_ref
  63.2 0.6 copy-done.3
  63.8 0.0 copy-done.4
  63.9 1.4 first_inner.1.inner_ref
  65.3 0.0 collective-permute-done.1.high_ref
  65.3 0.3 collective-permute-done.low_ref
  65.6 1.7 %first_outer.1 = (f32[64,256]{1,0:T(8,128)S(1)}, f32[4,64,256]{2,1,0:T(8,128)}) custom-call(s32[12]{0:T(128)S(1)} %copy-done.3, s32[12]{0:T(128)S(1)} %copy-done.4, f32[2,64,128]{2,1,0:T(8,128)S(1)} %first_inner.1.inner_ref, f32[64,256]{1,0:T(8,128)S(1)} %collective-permute-done.low_ref, f32[64,256]{1,0:T(8,128)S(1)} %collective-permute-done.1.high_ref, ...), custom_call_target="tpu_custom_call" | custom-call | tf_op jit(solution)/shard_map/first_outer/pallas_call | solution.py:339
  67.3 6.6 %collective-permute-start.3 = (f32[64,256]{1,0:T(8,128)S(1)}, f32[64,256]{1,0:T(8,128)S(1)}, u32[]{:S(2)}, u32[]{:S(2)}) collective-permute-start(f32[64,256]{1,0:T(8,128)S(1)} %get-tuple-element.19.own_ref.refs_0_.v1_ref), channel_id=1, source_target_pairs={{0,480},{32,0},{64,32},{96,64},{128,96},{160,128},{192,160},{224,1... | collective-permute-start | bytes 196616 | tf_op jit(solution)/shard_map/ppermute | solution.py:302
  73.9 0.0 collective-permute-start.2
  73.9 3.4 %all-to-all-start.3 = ((f32[4,64,256]{2,1,0:T(8,128)}), f32[4,64,256]{2,1,0:T(8,128)S(1)}, u32[]{:S(2)}, u32[]{:S(2)}) async-start(f32[4,64,256]{2,1,0:T(8,128)} %get-tuple-element.20), calls=%async_computation.3 | async-start | bytes 524288 | tf_op jit(solution)/shard_map/all_to_all | solution.py:305
  77.4 4.9 %collective-permute-start.5 = (f32[2,64,256]{2,1,0:T(8,128)S(1)}, f32[2,64,256]{2,1,0:T(8,128)S(1)}, u32[]{:S(2)}, u32[]{:S(2)}) collective-permute-start(f32[2,64,256]{2,1,0:T(8,128)S(1)} %pair.1), channel_id=1, source_target_pairs={{0,29},{1,30},{2,31},{3,0},{4,1},{5,2},{6,3},{7,4},{8,5},{9,6},{10... | collective-permute-start | bytes 393224 | tf_op jit(solution)/shard_map/ppermute | solution.py:320
  82.3 2.0 %collective-permute-start.4 = (f32[2,64,256]{2,1,0:T(8,128)S(1)}, f32[2,64,256]{2,1,0:T(8,128)S(1)}, u32[]{:S(2)}, u32[]{:S(2)}) collective-permute-start(f32[2,64,256]{2,1,0:T(8,128)S(1)} %pair.1), channel_id=1, source_target_pairs={{0,31},{1,0},{2,1},{3,2},{4,3},{5,4},{6,5},{7,6},{8,7},{9,8},{10,9... | collective-permute-start | bytes 393224 | tf_op jit(solution)/shard_map/ppermute | solution.py:320
  84.3 5.4 %collective-permute-done.5.refs_1_.refs_3_ = f32[2,64,256]{2,1,0:T(8,128)S(1)} collective-permute-done((f32[2,64,256]{2,1,0:T(8,128)S(1)}, f32[2,64,256]{2,1,0:T(8,128)S(1)}, u32[]{:S(2)}, u32[]{:S(2)}) %collective-permute-start.5) | collective-permute-done | bytes 131104 | tf_op jit(solution)/shard_map/ppermute | solution.py:320
  89.7 3.0 %collective-permute-done.4.refs_0_.refs_2_ = f32[2,64,256]{2,1,0:T(8,128)S(1)} collective-permute-done((f32[2,64,256]{2,1,0:T(8,128)S(1)}, f32[2,64,256]{2,1,0:T(8,128)S(1)}, u32[]{:S(2)}, u32[]{:S(2)}) %collective-permute-start.4) | collective-permute-done | bytes 131104 | tf_op jit(solution)/shard_map/ppermute | solution.py:320
  92.7 1.9 %collective-permute-start.6 = (f32[2,64,256]{2,1,0:T(8,128)S(1)}, f32[2,64,256]{2,1,0:T(8,128)S(1)}, u32[]{:S(2)}, u32[]{:S(2)}) collective-permute-start(f32[2,64,256]{2,1,0:T(8,128)S(1)} %swap.1), channel_id=1, source_target_pairs={{0,32},{32,0},{64,96},{96,64},{128,160},{160,128},{192,224},{224,1... | collective-permute-start | bytes 393224 | tf_op jit(solution)/shard_map/ppermute | solution.py:326
  94.7 1.3 collective-permute-done.6.refs_4_
  96.0 1.9 %second.1 = (f32[64,256]{1,0:T(8,128)S(1)}, f32[4,64,256]{2,1,0:T(8,128)}) custom-call(s32[2]{0:T(128)S(1)} %pad_add_fusion.place_ref, s32[12]{0:T(128)S(1)} %copy-done.3, s32[12]{0:T(128)S(1)} %copy-done.4, f32[64,256]{1,0:T(8,128)S(1)} %get-tuple-element.19.own_ref.refs_0_.v1_ref, f32[4,64,256]{2,1,0:T(8,128)S(1)} %all-to-all-done.3.refs_1_, ...), custom_call_target="tpu_custom_call" | custom-call | tf_op jit(solution)/shard_map/second/pallas_call | solution.py:343
  97.9 3.4 %all-to-all-start.4 = ((f32[4,64,256]{2,1,0:T(8,128)}), f32[4,64,256]{2,1,0:T(8,128)S(1)}, u32[]{:S(2)}, u32[]{:S(2)}) async-start(f32[4,64,256]{2,1,0:T(8,128)} %get-tuple-element.25), calls=%async_computation.4 | async-start | bytes 524288 | tf_op jit(solution)/shard_map/all_to_all | solution.py:305
  101.3 0.2 collective-permute-start.10
  101.5 1.6 %collective-permute-start.9 = (f32[64,256]{1,0:T(8,128)S(1)}, f32[64,256]{1,0:T(8,128)S(1)}, u32[]{:S(2)}, u32[]{:S(2)}) collective-permute-start(f32[64,256]{1,0:T(8,128)S(1)} %get-tuple-element.29.v2_ref), channel_id=1, source_target_pairs={{0,32},{32,64},{64,96},{96,128},{128,160},{160,192},{192,224},{224... | collective-permute-start | bytes 196616 | tf_op jit(solution)/shard_map/ppermute | solution.py:302
  103.1 5.1 %collective-permute-start.8 = (f32[64,256]{1,0:T(8,128)S(1)}, f32[64,256]{1,0:T(8,128)S(1)}, u32[]{:S(2)}, u32[]{:S(2)}) collective-permute-start(f32[64,256]{1,0:T(8,128)S(1)} %get-tuple-element.29.v2_ref), channel_id=1, source_target_pairs={{0,29},{1,30},{2,31},{3,0},{4,1},{5,2},{6,3},{7,4},{8,5},{9,6},{10... | collective-permute-start | bytes 196616 | tf_op jit(solution)/shard_map/ppermute | solution.py:347
  108.1 3.1 %collective-permute-start.7 = (f32[64,256]{1,0:T(8,128)S(1)}, f32[64,256]{1,0:T(8,128)S(1)}, u32[]{:S(2)}, u32[]{:S(2)}) collective-permute-start(f32[64,256]{1,0:T(8,128)S(1)} %get-tuple-element.29.v2_ref), channel_id=1, source_target_pairs={{0,31},{1,0},{2,1},{3,2},{4,3},{5,4},{6,5},{7,6},{8,7},{9,8},{10,9... | collective-permute-start | bytes 196616 | tf_op jit(solution)/shard_map/ppermute | solution.py:347
  111.3 0.1 pad_add_fusion.1.place_ref
  111.3 4.8 %collective-permute-done.7.a_ref = f32[64,256]{1,0:T(8,128)S(1)} collective-permute-done((f32[64,256]{1,0:T(8,128)S(1)}, f32[64,256]{1,0:T(8,128)S(1)}, u32[]{:S(2)}, u32[]{:S(2)}) %collective-permute-start.7) | collective-permute-done | bytes 65568 | tf_op jit(solution)/shard_map/ppermute | solution.py:347
  116.1 1.3 half.1
  117.4 0.6 broadcast_in_dim.20
  118.1 5.8 %all-to-all-start.5 = ((f32[32,4,128]{2,1,0:T(4,128)}), f32[32,4,128]{2,1,0:T(4,128)S(1)}, u32[]{:S(2)}, u32[]{:S(2)}) async-start(f32[32,4,128]{2,1,0:T(4,128)} %broadcast_in_dim.20), calls=%async_computation.5 | async-start | bytes 131072 | tf_op jit(solution)/shard_map/all_to_all | solution.py:362
  123.9 4.9 %collective-permute-start.12 = (f32[64,256]{1,0:T(8,128)S(1)}, f32[64,256]{1,0:T(8,128)S(1)}, u32[]{:S(2)}, u32[]{:S(2)}) collective-permute-start(f32[64,256]{1,0:T(8,128)S(1)} %get-tuple-element.29.v2_ref), channel_id=1, source_target_pairs={{0,3},{1,4},{2,5},{3,6},{4,7},{5,8},{6,9},{7,10},{8,11},{9,12},{10... | collective-permute-start | bytes 196616 | tf_op jit(solution)/shard_map/ppermute | solution.py:354
  128.9 4.3 %collective-permute-start.11 = (f32[64,256]{1,0:T(8,128)S(1)}, f32[64,256]{1,0:T(8,128)S(1)}, u32[]{:S(2)}, u32[]{:S(2)}) collective-permute-start(f32[64,256]{1,0:T(8,128)S(1)} %get-tuple-element.29.v2_ref), channel_id=1, source_target_pairs={{0,1},{1,2},{2,3},{3,4},{4,5},{5,6},{6,7},{7,8},{8,9},{9,10},{10,1... | collective-permute-start | bytes 196616 | tf_op jit(solution)/shard_map/ppermute | solution.py:354
  133.3 0.6 broadcast_in_dim.21
  133.9 5.7 %all-to-all-start.6 = ((f32[16,4,128]{2,1,0:T(4,128)}), f32[16,4,128]{2,1,0:T(4,128)S(1)}, u32[]{:S(2)}, u32[]{:S(2)}) async-start(f32[16,4,128]{2,1,0:T(4,128)} %broadcast_in_dim.21), calls=%async_computation.6 | async-start | bytes 65536 | tf_op jit(solution)/shard_map/all_to_all | solution.py:364
  139.6 1.0 rest.1.v3_ref
  140.6 6.3 %all-to-all-done.6.moments_ref = f32[16,4,128]{2,1,0:T(4,128)S(1)} async-done(((f32[16,4,128]{2,1,0:T(4,128)}), f32[16,4,128]{2,1,0:T(4,128)S(1)}, u32[]{:S(2)}, u32[]{:S(2)}) %all-to-all-start.6) | async-done | bytes 32800 | tf_op jit(solution)/shard_map/all_to_all | solution.py:364
  147.0 1.5 %finish.1 = (f32[64,256]{1,0:T(8,128)}, f32[64,256]{1,0:T(8,128)}) custom-call(f32[16,4,128]{2,1,0:T(4,128)S(1)} %all-to-all-done.6.moments_ref, f32[64,256]{1,0:T(8,128)S(1)} %bitcast.20, f32[64,256]{1,0:T(8,128)S(1)} %get-tuple-element.19.own_ref.refs_0_.v1_ref, f32[64,256]{1,0:T(8,128)S(1)} %get-tuple-element.29.v2_ref, f32[64,256]{1,0:T(8,128)S(1)} %rest.1.v3_ref), custom_call_target="tpu_custom_call" | custom-call | tf_op jit(solution)/shard_map/finish/pallas_call | solution.py:365
  (22 shorter events, 0.1 us)
Async XLA Ops:
  2.2 20.1 %copy-start.1 = (f32[256,512]{1,0:T(8,128)S(1)}, f32[256,512]{1,0:T(8,128)}, u32[]{:S(2)}) copy-start(f32[256,512]{1,0:T(8,128)} %desc_ref.1) | copy-start | bytes 1572868
  2.2 20.0 %all-to-all-start = ((f32[32,2,640]{2,1,0:T(2,128)}), f32[32,2,640]{2,1,0:T(2,128)S(1)}, u32[]{:S(2)}, u32[]{:S(2)}) async-start(f32[32,2,640]{2,1,0:T(2,128)} %get-tuple-element.18), calls=%async_computation | async-start | bytes 327680 | tf_op jit(solution)/shard_map/all_to_all | solution.py:286
  12.9 9.5 %copy-start.2 = (s32[64,64]{1,0:T(8,128)S(1)}, s32[64,64]{1,0:T(8,128)}, u32[]{:S(2)}) copy-start(s32[64,64]{1,0:T(8,128)} %cand_ref.1) | copy-start | bytes 49156
  39.3 23.9 %copy-start = (f32[12,128,128]{2,1,0:T(8,128)S(1)}, f32[12,128,128]{2,1,0:T(8,128)}, u32[]{:S(2)}) copy-start(f32[12,128,128]{2,1,0:T(8,128)} %tiles_ref.7) | copy-start | bytes 2359300
  39.3 16.3 %all-to-all-start.2 = ((f32[32,32,128]{2,1,0:T(8,128)}), f32[32,32,128]{2,1,0:T(8,128)S(1)}, u32[]{:S(2)}, u32[]{:S(2)}) async-start(f32[32,32,128]{2,1,0:T(8,128)} %bitcast.5), calls=%async_computation.2 | async-start | bytes 1048576 | tf_op jit(solution)/shard_map/all_to_all | solution.py:298
  55.7 9.6 %collective-permute-start.1 = (f32[64,256]{1,0:T(8,128)S(1)}, f32[64,256]{1,0:T(8,128)S(1)}, u32[]{:S(2)}, u32[]{:S(2)}) collective-permute-start(f32[64,256]{1,0:T(8,128)S(1)} %bitcast.17), channel_id=1, source_target_pairs={{0,480},{32,0},{64,32},{96,64},{128,96},{160,128},{192,160},{224,1... | collective-permute-start | bytes 196616 | tf_op jit(solution)/shard_map/ppermute | solution.py:302
  61.1 4.5 %collective-permute-start = (f32[64,256]{1,0:T(8,128)S(1)}, f32[64,256]{1,0:T(8,128)S(1)}, u32[]{:S(2)}, u32[]{:S(2)}) collective-permute-start(f32[64,256]{1,0:T(8,128)S(1)} %bitcast.18), channel_id=1, source_target_pairs={{0,32},{32,64},{64,96},{96,128},{128,160},{160,192},{192,224},{224... | collective-permute-start | bytes 196616 | tf_op jit(solution)/shard_map/ppermute | solution.py:302
  63.2 0.7 copy-start.3
  63.2 0.7 copy-start.4
  67.3 10.0 %collective-permute-start.3 = (f32[64,256]{1,0:T(8,128)S(1)}, f32[64,256]{1,0:T(8,128)S(1)}, u32[]{:S(2)}, u32[]{:S(2)}) collective-permute-start(f32[64,256]{1,0:T(8,128)S(1)} %get-tuple-element.19.own_ref.refs_0_.v1_ref), channel_id=1, source_target_pairs={{0,480},{32,0},{64,32},{96,64},{128,96},{160,128},{192,160},{224,1... | collective-permute-start | bytes 196616 | tf_op jit(solution)/shard_map/ppermute | solution.py:302
  73.9 3.4 %collective-permute-start.2 = (f32[64,256]{1,0:T(8,128)S(1)}, f32[64,256]{1,0:T(8,128)S(1)}, u32[]{:S(2)}, u32[]{:S(2)}) collective-permute-start(f32[64,256]{1,0:T(8,128)S(1)} %get-tuple-element.19.own_ref.refs_0_.v1_ref), channel_id=1, source_target_pairs={{0,32},{32,64},{64,96},{96,128},{128,160},{160,192},{192,224},{224... | collective-permute-start | bytes 196616 | tf_op jit(solution)/shard_map/ppermute | solution.py:302
  73.9 10.4 %all-to-all-start.3 = ((f32[4,64,256]{2,1,0:T(8,128)}), f32[4,64,256]{2,1,0:T(8,128)S(1)}, u32[]{:S(2)}, u32[]{:S(2)}) async-start(f32[4,64,256]{2,1,0:T(8,128)} %get-tuple-element.20), calls=%async_computation.3 | async-start | bytes 524288 | tf_op jit(solution)/shard_map/all_to_all | solution.py:305
  77.4 12.3 %collective-permute-start.5 = (f32[2,64,256]{2,1,0:T(8,128)S(1)}, f32[2,64,256]{2,1,0:T(8,128)S(1)}, u32[]{:S(2)}, u32[]{:S(2)}) collective-permute-start(f32[2,64,256]{2,1,0:T(8,128)S(1)} %pair.1), channel_id=1, source_target_pairs={{0,29},{1,30},{2,31},{3,0},{4,1},{5,2},{6,3},{7,4},{8,5},{9,6},{10... | collective-permute-start | bytes 393224 | tf_op jit(solution)/shard_map/ppermute | solution.py:320
  82.3 10.4 %collective-permute-start.4 = (f32[2,64,256]{2,1,0:T(8,128)S(1)}, f32[2,64,256]{2,1,0:T(8,128)S(1)}, u32[]{:S(2)}, u32[]{:S(2)}) collective-permute-start(f32[2,64,256]{2,1,0:T(8,128)S(1)} %pair.1), channel_id=1, source_target_pairs={{0,31},{1,0},{2,1},{3,2},{4,3},{5,4},{6,5},{7,6},{8,7},{9,8},{10,9... | collective-permute-start | bytes 393224 | tf_op jit(solution)/shard_map/ppermute | solution.py:320
  92.7 3.2 %collective-permute-start.6 = (f32[2,64,256]{2,1,0:T(8,128)S(1)}, f32[2,64,256]{2,1,0:T(8,128)S(1)}, u32[]{:S(2)}, u32[]{:S(2)}) collective-permute-start(f32[2,64,256]{2,1,0:T(8,128)S(1)} %swap.1), channel_id=1, source_target_pairs={{0,32},{32,0},{64,96},{96,64},{128,160},{160,128},{192,224},{224,1... | collective-permute-start | bytes 393224 | tf_op jit(solution)/shard_map/ppermute | solution.py:326
  97.9 18.3 %all-to-all-start.4 = ((f32[4,64,256]{2,1,0:T(8,128)}), f32[4,64,256]{2,1,0:T(8,128)S(1)}, u32[]{:S(2)}, u32[]{:S(2)}) async-start(f32[4,64,256]{2,1,0:T(8,128)} %get-tuple-element.25), calls=%async_computation.4 | async-start | bytes 524288 | tf_op jit(solution)/shard_map/all_to_all | solution.py:305
  101.3 10.0 %collective-permute-start.10 = (f32[64,256]{1,0:T(8,128)S(1)}, f32[64,256]{1,0:T(8,128)S(1)}, u32[]{:S(2)}, u32[]{:S(2)}) collective-permute-start(f32[64,256]{1,0:T(8,128)S(1)} %get-tuple-element.29.v2_ref), channel_id=1, source_target_pairs={{0,480},{32,0},{64,32},{96,64},{128,96},{160,128},{192,160},{224,1... | collective-permute-start | bytes 196616 | tf_op jit(solution)/shard_map/ppermute | solution.py:302
  101.5 9.9 %collective-permute-start.9 = (f32[64,256]{1,0:T(8,128)S(1)}, f32[64,256]{1,0:T(8,128)S(1)}, u32[]{:S(2)}, u32[]{:S(2)}) collective-permute-start(f32[64,256]{1,0:T(8,128)S(1)} %get-tuple-element.29.v2_ref), channel_id=1, source_target_pairs={{0,32},{32,64},{64,96},{96,128},{128,160},{160,192},{192,224},{224... | collective-permute-start | bytes 196616 | tf_op jit(solution)/shard_map/ppermute | solution.py:302
  103.1 8.3 %collective-permute-start.8 = (f32[64,256]{1,0:T(8,128)S(1)}, f32[64,256]{1,0:T(8,128)S(1)}, u32[]{:S(2)}, u32[]{:S(2)}) collective-permute-start(f32[64,256]{1,0:T(8,128)S(1)} %get-tuple-element.29.v2_ref), channel_id=1, source_target_pairs={{0,29},{1,30},{2,31},{3,0},{4,1},{5,2},{6,3},{7,4},{8,5},{9,6},{10... | collective-permute-start | bytes 196616 | tf_op jit(solution)/shard_map/ppermute | solution.py:347
  108.1 8.0 %collective-permute-start.7 = (f32[64,256]{1,0:T(8,128)S(1)}, f32[64,256]{1,0:T(8,128)S(1)}, u32[]{:S(2)}, u32[]{:S(2)}) collective-permute-start(f32[64,256]{1,0:T(8,128)S(1)} %get-tuple-element.29.v2_ref), channel_id=1, source_target_pairs={{0,31},{1,0},{2,1},{3,2},{4,3},{5,4},{6,5},{7,6},{8,7},{9,8},{10,9... | collective-permute-start | bytes 196616 | tf_op jit(solution)/shard_map/ppermute | solution.py:347
  118.1 15.1 %all-to-all-start.5 = ((f32[32,4,128]{2,1,0:T(4,128)}), f32[32,4,128]{2,1,0:T(4,128)S(1)}, u32[]{:S(2)}, u32[]{:S(2)}) async-start(f32[32,4,128]{2,1,0:T(4,128)} %broadcast_in_dim.20), calls=%async_computation.5 | async-start | bytes 131072 | tf_op jit(solution)/shard_map/all_to_all | solution.py:362
  123.9 15.6 %collective-permute-start.12 = (f32[64,256]{1,0:T(8,128)S(1)}, f32[64,256]{1,0:T(8,128)S(1)}, u32[]{:S(2)}, u32[]{:S(2)}) collective-permute-start(f32[64,256]{1,0:T(8,128)S(1)} %get-tuple-element.29.v2_ref), channel_id=1, source_target_pairs={{0,3},{1,4},{2,5},{3,6},{4,7},{5,8},{6,9},{7,10},{8,11},{9,12},{10... | collective-permute-start | bytes 196616 | tf_op jit(solution)/shard_map/ppermute | solution.py:354
  128.9 10.7 %collective-permute-start.11 = (f32[64,256]{1,0:T(8,128)S(1)}, f32[64,256]{1,0:T(8,128)S(1)}, u32[]{:S(2)}, u32[]{:S(2)}) collective-permute-start(f32[64,256]{1,0:T(8,128)S(1)} %get-tuple-element.29.v2_ref), channel_id=1, source_target_pairs={{0,1},{1,2},{2,3},{3,4},{4,5},{5,6},{6,7},{7,8},{8,9},{9,10},{10,1... | collective-permute-start | bytes 196616 | tf_op jit(solution)/shard_map/ppermute | solution.py:354
  133.9 13.1 %all-to-all-start.6 = ((f32[16,4,128]{2,1,0:T(4,128)}), f32[16,4,128]{2,1,0:T(4,128)S(1)}, u32[]{:S(2)}, u32[]{:S(2)}) async-start(f32[16,4,128]{2,1,0:T(4,128)} %broadcast_in_dim.21), calls=%async_computation.6 | async-start | bytes 65536 | tf_op jit(solution)/shard_map/all_to_all | solution.py:364

commit v8 on v7

--- a/solution.py
+++ b/solution.py
@@ -197,7 +197,7 @@
     return jnp.where(col >= N_ROW * HALF, 0, kind)
 
 
-def half_kernel(place_ref, row_ref, col_ref, v2_ref, line_ref, a_ref, b_ref, low_ref, high_ref, v0_ref, v1_ref, tiles_ref,
+def half_kernel(place_ref, row_ref, col_ref, v2_ref, line_ref, low_ref, high_ref, a_ref, b_ref, v0_ref, v1_ref, tiles_ref,
                 part_ref, moments_ref, slots_ref, acc_ref):
     blocks = [line_ref[x] for x in range(N_X)] + [a_ref[...], b_ref[...], None, None, low_ref[...], high_ref[...]]
     for k, block in enumerate(blocks):
@@ -344,23 +344,23 @@
         next_kernel, out_shape=with_copies, in_specs=[SMEM] * 3 + [VMEM] * (N_BLOCKS + 1), out_specs=(VMEM, VMEM),
         scratch_shapes=[slots, acc], compiler_params=PARAMS, name="second",
     )(place, tile_row, tile_col, *exchange(v1, copies), tile_vals)
+    low, high = region_pair(v2)
     ahead = [lax.ppermute(v2, "row", ring(N_ROW, -hop)) for hop in SHARED]
     part, moments = pl.pallas_call(
         half_kernel, out_shape=(shape(HALF, Q, TILE), shape(4, TILE)), in_specs=[SMEM] * 3 + [VMEM] * 9,
         out_specs=(VMEM, VMEM), scratch_shapes=[slots, pltpu.VMEM((3 * HALF, Q, TILE), F32)],
         compiler_params=PARAMS, name="half",
-    )(upward, tile_row, tile_col, v2, x_line(copies), *ahead, *region_pair(v2), v0, v1, tile_vals)
-    later, moments = lax.optimization_barrier((v2, moments))
-    behind = [lax.ppermute(later, "row", ring(N_ROW, hop)) for hop in SHARED]
+    )(upward, tile_row, tile_col, v2, x_line(copies), low, high, *ahead, v0, v1, tile_vals)
+    v2_now, moments = lax.optimization_barrier((v2, moments))
+    behind = [lax.ppermute(v2_now, "row", ring(N_ROW, hop)) for hop in SHARED]
+    moments = lax.all_to_all(jnp.broadcast_to(moments[None], (N_ROW, 4, TILE)), "row", 0, 0, tiled=True)
+    moments = jnp.sum(moments.reshape(2, 2, 2, 2, 2, 4, TILE).sum(0).sum(0).sum(0).sum(0), axis=0)
     v3 = pl.pallas_call(
         rest_kernel, out_shape=shape(Q, ROWS), in_specs=[SMEM] * 3 + [VMEM] * 4, out_specs=VMEM,
         scratch_shapes=[pltpu.VMEM((2 * HALF, Q, TILE), F32), acc],
         cost_estimate=pl.CostEstimate(flops=2 * 12 * Q * TILE * TILE, bytes_accessed=2000000, transcendentals=0),
         compiler_params=PARAMS, name="rest",
     )(upward, tile_row, tile_col, part, *behind, tile_vals)
-
-    moments = lax.all_to_all(jnp.broadcast_to(moments[None], (N_ROW, 4, TILE)), "row", 0, 0, tiled=True)
-    moments = jnp.sum(moments.reshape(2, 2, 2, 2, 2, 4, TILE).sum(0).sum(0).sum(0).sum(0), axis=0)
     moments = lax.all_to_all(jnp.broadcast_to(moments[None], (N_REGION, 4, TILE)), "region", 0, 0, tiled=True)
     diffused, residual = pl.pallas_call(
         finish_kernel, out_shape=(shape(Q, ROWS), shape(Q, ROWS)), in_specs=[VMEM] * 5, out_specs=(VMEM, VMEM),

time: 149 us -> 150 us (level)
  starting transfers between devices: 75 us -> 78.2 us
  waiting for transfers between devices: 42.8 us -> 40.5 us
    all_to_all x1, starting transfers between devices: 5.7 us -> 8.27 us  [local(): lax.all_to_all(jnp.broadcast_to(moments[None], (N_REGION, 4, TILE)), 'reg...]
    ppermute x2, waiting for transfers between devices: 4.8 us -> 2.5 us  [local(): ahead = [lax.ppermute(v2, 'row', ring(N_ROW, -hop)) for hop in SHARED]]
where the time goes in v8:
time: 150 us; the launch traced here: 149 us
  starting transfers between devices  78.2 us (52%)
  waiting for transfers between devices  40.5 us (27%)
  Pallas kernels  14.1 us (9%)
  blocking collectives  13.3 us (9%)
  local copies, waits for them, and re-layouts  2.17 us (1%)
    all_to_all x1, blocking collectives, local(): lax.all_to_all(by_query.reshape(N_ROW, QS * HALF, TILE), 'row', 0, 0, til...  13.3 us
    ppermute x3, starting transfers between devices, region_pair(): lax.ppermute(v, 'region', ring(N_REGION, -1))  13.3 us
    all_to_all x1, waiting for transfers between devices, local(): lax.all_to_all(near.reshape(N_ROW, width, TILE), 'row', 0, 0, tiled=True)  12.2 us
    all_to_all x1, starting transfers between devices, local(): lax.all_to_all(packed, 'row', 0, 0, tiled=True).reshape(Q, D + TILE)  10.6 us
    all_to_all x1, waiting for transfers between devices, local(): lax.all_to_all(packed, 'row', 0, 0, tiled=True).reshape(Q, D + TILE)  9.34 us
    ppermute x2, starting transfers between devices, local(): behind = [lax.ppermute(v2_now, 'row', ring(N_ROW, hop)) for hop in SHARED]  9.24 us
    ppermute x2, waiting for transfers between devices, exchange(): got.append(lax.ppermute(both, ('region', 'row'), pairs))  8.44 us
    all_to_all x1, starting transfers between devices, local(): lax.all_to_all(jnp.broadcast_to(moments[None], (N_REGION, 4, TILE)), 'reg...  8.27 us
  transfers between devices with their start and end apart: 19, of which 8 were waited for; matrix products, arithmetic and copies ran while one was open for 1% of the time, Pallas kernels for 2%

profile of v8, /device:TPU:1, one launch (start us, length us, event | category | flops | bytes accessed | tf_op | source)
XLA Modules:
  0.0 149.4 jit_solution(15715422041958671193)
XLA Ops:
  0.6 1.5 %pack.1 = (f32[32,2,640]{2,1,0:T(2,128)}, s32[12]{0:T(128)}, s32[12]{0:T(128)}) custom-call(f32[2,512]{1,0:T(2,128)} %queries_hbm.1, s32[1,256]{1,0:T(1,128)} %perm_hbm.1, s32[12]{0:T(128)} %row_hbm.1, s32[12]{0:T(128)} %col_hbm.1), custom_call_target="tpu_custom_call" | custom-call | tf_op jit(solution)/shard_map/pack/pallas_call | solution.py:280
  2.2 0.0 copy-start.1
  2.2 10.6 %all-to-all-start = ((f32[32,2,640]{2,1,0:T(2,128)}), f32[32,2,640]{2,1,0:T(2,128)S(1)}, u32[]{:S(2)}, u32[]{:S(2)}) async-start(f32[32,2,640]{2,1,0:T(2,128)} %get-tuple-element.18), calls=%async_computation | async-start | bytes 327680 | tf_op jit(solution)/shard_map/all_to_all | solution.py:286
  12.9 0.0 copy-start.2
  12.9 9.3 %all-to-all-done = f32[32,2,640]{2,1,0:T(2,128)S(1)} async-done(((f32[32,2,640]{2,1,0:T(2,128)}), f32[32,2,640]{2,1,0:T(2,128)S(1)}, u32[]{:S(2)}, u32[]{:S(2)}) %all-to-all-start) | async-done | bytes 163872 | tf_op jit(solution)/shard_map/all_to_all | solution.py:286
  22.2 0.1 reshape.28.packed_ref
  22.3 0.6 scores.1
  23.0 13.3 %all_to_all.35 = f32[32,4,128]{2,1,0:T(4,128)S(1)} all-to-all(f32[32,4,128]{2,1,0:T(4,128)S(1)} %bitcast.22), channel_id=1, replica_groups=mesh['region'=16,'row'=32] {'row'}, dimensions={0} | all-to-all | bytes 131072 | tf_op jit(solution)/shard_map/all_to_all | solution.py:291
  36.3 3.0 %permute.1 = f32[1024,128]{1,0:T(8,128)} custom-call(f32[128,128]{1,0:T(8,128)S(1)} %bitcast.21, f32[64,640]{1,0:T(8,128)S(1)} %reshape.28.packed_ref), custom_call_target="tpu_custom_call" | custom-call | tf_op jit(solution)/shard_map/permute/pallas_call | solution.py:293
  39.3 4.0 %all-to-all-start.2 = ((f32[32,32,128]{2,1,0:T(8,128)}), f32[32,32,128]{2,1,0:T(8,128)S(1)}, u32[]{:S(2)}, u32[]{:S(2)}) async-start(f32[32,32,128]{2,1,0:T(8,128)} %bitcast.5), calls=%async_computation.2 | async-start | bytes 1048576 | tf_op jit(solution)/shard_map/all_to_all | solution.py:298
  43.3 12.2 %all-to-all-done.2 = f32[32,32,128]{2,1,0:T(8,128)S(1)} async-done(((f32[32,32,128]{2,1,0:T(8,128)}), f32[32,32,128]{2,1,0:T(8,128)S(1)}, u32[]{:S(2)}, u32[]{:S(2)}) %all-to-all-start.2) | async-done | bytes 524320 | tf_op jit(solution)/shard_map/all_to_all | solution.py:298
  55.6 0.1 copy.17
  55.7 5.4 %collective-permute-start.1 = (f32[64,256]{1,0:T(8,128)S(1)}, f32[64,256]{1,0:T(8,128)S(1)}, u32[]{:S(2)}, u32[]{:S(2)}) collective-permute-start(f32[64,256]{1,0:T(8,128)S(1)} %bitcast.17), channel_id=1, source_target_pairs={{0,480},{32,0},{64,32},{96,64},{128,96},{160,128},{192,160},{224,1... | collective-permute-start | bytes 196616 | tf_op jit(solution)/shard_map/ppermute | solution.py:302
  61.1 2.0 %collective-permute-start = (f32[64,256]{1,0:T(8,128)S(1)}, f32[64,256]{1,0:T(8,128)S(1)}, u32[]{:S(2)}, u32[]{:S(2)}) collective-permute-start(f32[64,256]{1,0:T(8,128)S(1)} %bitcast.18), channel_id=1, source_target_pairs={{0,32},{32,64},{64,96},{96,128},{128,160},{160,192},{192,224},{224... | collective-permute-start | bytes 196616 | tf_op jit(solution)/shard_map/ppermute | solution.py:302
  63.1 0.1 pad_add_fusion.place_ref
  63.2 0.6 copy-done.3
  63.8 0.0 copy-done.4
  63.9 1.4 first_inner.1.inner_ref
  65.3 0.0 collective-permute-done.1.high_ref
  65.3 0.3 collective-permute-done.low_ref
  65.6 1.7 %first_outer.1 = (f32[64,256]{1,0:T(8,128)S(1)}, f32[4,64,256]{2,1,0:T(8,128)}) custom-call(s32[12]{0:T(128)S(1)} %copy-done.3, s32[12]{0:T(128)S(1)} %copy-done.4, f32[2,64,128]{2,1,0:T(8,128)S(1)} %first_inner.1.inner_ref, f32[64,256]{1,0:T(8,128)S(1)} %collective-permute-done.low_ref, f32[64,256]{1,0:T(8,128)S(1)} %collective-permute-done.1.high_ref, ...), custom_call_target="tpu_custom_call" | custom-call | tf_op jit(solution)/shard_map/first_outer/pallas_call | solution.py:339
  67.3 6.6 %collective-permute-start.3 = (f32[64,256]{1,0:T(8,128)S(1)}, f32[64,256]{1,0:T(8,128)S(1)}, u32[]{:S(2)}, u32[]{:S(2)}) collective-permute-start(f32[64,256]{1,0:T(8,128)S(1)} %get-tuple-element.19.own_ref.refs_0_.v1_ref), channel_id=1, source_target_pairs={{0,480},{32,0},{64,32},{96,64},{128,96},{160,128},{192,160},{224,1... | collective-permute-start | bytes 196616 | tf_op jit(solution)/shard_map/ppermute | solution.py:302
  73.9 0.0 collective-permute-start.2
  73.9 3.4 %all-to-all-start.3 = ((f32[4,64,256]{2,1,0:T(8,128)}), f32[4,64,256]{2,1,0:T(8,128)S(1)}, u32[]{:S(2)}, u32[]{:S(2)}) async-start(f32[4,64,256]{2,1,0:T(8,128)} %get-tuple-element.20), calls=%async_computation.3 | async-start | bytes 524288 | tf_op jit(solution)/shard_map/all_to_all | solution.py:305
  77.4 4.9 %collective-permute-start.5 = (f32[2,64,256]{2,1,0:T(8,128)S(1)}, f32[2,64,256]{2,1,0:T(8,128)S(1)}, u32[]{:S(2)}, u32[]{:S(2)}) collective-permute-start(f32[2,64,256]{2,1,0:T(8,128)S(1)} %pair.1), channel_id=1, source_target_pairs={{0,29},{1,30},{2,31},{3,0},{4,1},{5,2},{6,3},{7,4},{8,5},{9,6},{10... | collective-permute-start | bytes 393224 | tf_op jit(solution)/shard_map/ppermute | solution.py:320
  82.3 2.0 %collective-permute-start.4 = (f32[2,64,256]{2,1,0:T(8,128)S(1)}, f32[2,64,256]{2,1,0:T(8,128)S(1)}, u32[]{:S(2)}, u32[]{:S(2)}) collective-permute-start(f32[2,64,256]{2,1,0:T(8,128)S(1)} %pair.1), channel_id=1, source_target_pairs={{0,31},{1,0},{2,1},{3,2},{4,3},{5,4},{6,5},{7,6},{8,7},{9,8},{10,9... | collective-permute-start | bytes 393224 | tf_op jit(solution)/shard_map/ppermute | solution.py:320
  84.3 5.4 %collective-permute-done.5.refs_1_.refs_3_ = f32[2,64,256]{2,1,0:T(8,128)S(1)} collective-permute-done((f32[2,64,256]{2,1,0:T(8,128)S(1)}, f32[2,64,256]{2,1,0:T(8,128)S(1)}, u32[]{:S(2)}, u32[]{:S(2)}) %collective-permute-start.5) | collective-permute-done | bytes 131104 | tf_op jit(solution)/shard_map/ppermute | solution.py:320
  89.7 3.0 %collective-permute-done.4.refs_0_.refs_2_ = f32[2,64,256]{2,1,0:T(8,128)S(1)} collective-permute-done((f32[2,64,256]{2,1,0:T(8,128)S(1)}, f32[2,64,256]{2,1,0:T(8,128)S(1)}, u32[]{:S(2)}, u32[]{:S(2)}) %collective-permute-start.4) | collective-permute-done | bytes 131104 | tf_op jit(solution)/shard_map/ppermute | solution.py:320
  92.7 1.9 %collective-permute-start.6 = (f32[2,64,256]{2,1,0:T(8,128)S(1)}, f32[2,64,256]{2,1,0:T(8,128)S(1)}, u32[]{:S(2)}, u32[]{:S(2)}) collective-permute-start(f32[2,64,256]{2,1,0:T(8,128)S(1)} %swap.1), channel_id=1, source_target_pairs={{0,32},{32,0},{64,96},{96,64},{128,160},{160,128},{192,224},{224,1... | collective-permute-start | bytes 393224 | tf_op jit(solution)/shard_map/ppermute | solution.py:326
  94.7 1.3 collective-permute-done.6.refs_4_
  96.0 1.9 %second.1 = (f32[64,256]{1,0:T(8,128)S(1)}, f32[4,64,256]{2,1,0:T(8,128)}) custom-call(s32[2]{0:T(128)S(1)} %pad_add_fusion.place_ref, s32[12]{0:T(128)S(1)} %copy-done.3, s32[12]{0:T(128)S(1)} %copy-done.4, f32[64,256]{1,0:T(8,128)S(1)} %get-tuple-element.19.own_ref.refs_0_.v1_ref, f32[4,64,256]{2,1,0:T(8,128)S(1)} %all-to-all-done.3.refs_1_, ...), custom_call_target="tpu_custom_call" | custom-call | tf_op jit(solution)/shard_map/second/pallas_call | solution.py:343
  97.9 3.4 %all-to-all-start.4 = ((f32[4,64,256]{2,1,0:T(8,128)}), f32[4,64,256]{2,1,0:T(8,128)S(1)}, u32[]{:S(2)}, u32[]{:S(2)}) async-start(f32[4,64,256]{2,1,0:T(8,128)} %get-tuple-element.25), calls=%async_computation.4 | async-start | bytes 524288 | tf_op jit(solution)/shard_map/all_to_all | solution.py:305
  101.3 5.1 %collective-permute-start.10 = (f32[64,256]{1,0:T(8,128)S(1)}, f32[64,256]{1,0:T(8,128)S(1)}, u32[]{:S(2)}, u32[]{:S(2)}) collective-permute-start(f32[64,256]{1,0:T(8,128)S(1)} %get-tuple-element.29.v2_ref), channel_id=1, source_target_pairs={{0,29},{1,30},{2,31},{3,0},{4,1},{5,2},{6,3},{7,4},{8,5},{9,6},{10... | collective-permute-start | bytes 196616 | tf_op jit(solution)/shard_map/ppermute | solution.py:348
  106.4 3.1 %collective-permute-start.9 = (f32[64,256]{1,0:T(8,128)S(1)}, f32[64,256]{1,0:T(8,128)S(1)}, u32[]{:S(2)}, u32[]{:S(2)}) collective-permute-start(f32[64,256]{1,0:T(8,128)S(1)} %get-tuple-element.29.v2_ref), channel_id=1, source_target_pairs={{0,31},{1,0},{2,1},{3,2},{4,3},{5,4},{6,5},{7,6},{8,7},{9,8},{10,9... | collective-permute-start | bytes 196616 | tf_op jit(solution)/shard_map/ppermute | solution.py:348
  109.5 1.3 collective-permute-start.8
  110.8 0.5 collective-permute-start.7
  111.3 0.1 pad_add_fusion.1.place_ref
  111.3 2.5 %collective-permute-done.9.a_ref = f32[64,256]{1,0:T(8,128)S(1)} collective-permute-done((f32[64,256]{1,0:T(8,128)S(1)}, f32[64,256]{1,0:T(8,128)S(1)}, u32[]{:S(2)}, u32[]{:S(2)}) %collective-permute-start.9) | collective-permute-done | bytes 65568 | tf_op jit(solution)/shard_map/ppermute | solution.py:348
  113.9 1.3 half.1
  115.2 0.6 broadcast_in_dim.20
  115.8 6.5 %all-to-all-start.5 = ((f32[32,4,128]{2,1,0:T(4,128)}), f32[32,4,128]{2,1,0:T(4,128)S(1)}, u32[]{:S(2)}, u32[]{:S(2)}) async-start(f32[32,4,128]{2,1,0:T(4,128)} %broadcast_in_dim.20), calls=%async_computation.5 | async-start | bytes 131072 | tf_op jit(solution)/shard_map/all_to_all | solution.py:356
  122.3 4.9 %collective-permute-start.12 = (f32[64,256]{1,0:T(8,128)S(1)}, f32[64,256]{1,0:T(8,128)S(1)}, u32[]{:S(2)}, u32[]{:S(2)}) collective-permute-start(f32[64,256]{1,0:T(8,128)S(1)} %get-tuple-element.29.v2_ref), channel_id=1, source_target_pairs={{0,3},{1,4},{2,5},{3,6},{4,7},{5,8},{6,9},{7,10},{8,11},{9,12},{10... | collective-permute-start | bytes 196616 | tf_op jit(solution)/shard_map/ppermute | solution.py:355
  127.2 4.3 %collective-permute-start.11 = (f32[64,256]{1,0:T(8,128)S(1)}, f32[64,256]{1,0:T(8,128)S(1)}, u32[]{:S(2)}, u32[]{:S(2)}) collective-permute-start(f32[64,256]{1,0:T(8,128)S(1)} %get-tuple-element.29.v2_ref), channel_id=1, source_target_pairs={{0,1},{1,2},{2,3},{3,4},{4,5},{5,6},{6,7},{7,8},{8,9},{9,10},{10,1... | collective-permute-start | bytes 196616 | tf_op jit(solution)/shard_map/ppermute | solution.py:355
  131.6 0.6 broadcast_in_dim.21
  132.2 8.3 %all-to-all-start.6 = ((f32[16,4,128]{2,1,0:T(4,128)}), f32[16,4,128]{2,1,0:T(4,128)S(1)}, u32[]{:S(2)}, u32[]{:S(2)}) async-start(f32[16,4,128]{2,1,0:T(4,128)} %broadcast_in_dim.21), calls=%async_computation.6 | async-start | bytes 65536 | tf_op jit(solution)/shard_map/all_to_all | solution.py:364
  140.5 1.0 rest.1.v3_ref
  141.5 6.3 %all-to-all-done.6.moments_ref = f32[16,4,128]{2,1,0:T(4,128)S(1)} async-done(((f32[16,4,128]{2,1,0:T(4,128)}), f32[16,4,128]{2,1,0:T(4,128)S(1)}, u32[]{:S(2)}, u32[]{:S(2)}) %all-to-all-start.6) | async-done | bytes 32800 | tf_op jit(solution)/shard_map/all_to_all | solution.py:364
  147.9 1.5 %finish.1 = (f32[64,256]{1,0:T(8,128)}, f32[64,256]{1,0:T(8,128)}) custom-call(f32[16,4,128]{2,1,0:T(4,128)S(1)} %all-to-all-done.6.moments_ref, f32[64,256]{1,0:T(8,128)S(1)} %bitcast.20, f32[64,256]{1,0:T(8,128)S(1)} %get-tuple-element.19.own_ref.refs_0_.v1_ref, f32[64,256]{1,0:T(8,128)S(1)} %get-tuple-element.29.v2_ref, f32[64,256]{1,0:T(8,128)S(1)} %rest.1.v3_ref), custom_call_target="tpu_custom_call" | custom-call | tf_op jit(solution)/shard_map/finish/pallas_call | solution.py:365
  (22 shorter events, 0.1 us)
Async XLA Ops:
  2.2 20.1 %copy-start.1 = (f32[256,512]{1,0:T(8,128)S(1)}, f32[256,512]{1,0:T(8,128)}, u32[]{:S(2)}) copy-start(f32[256,512]{1,0:T(8,128)} %desc_ref.1) | copy-start | bytes 1572868
  2.2 20.0 %all-to-all-start = ((f32[32,2,640]{2,1,0:T(2,128)}), f32[32,2,640]{2,1,0:T(2,128)S(1)}, u32[]{:S(2)}, u32[]{:S(2)}) async-start(f32[32,2,640]{2,1,0:T(2,128)} %get-tuple-element.18), calls=%async_computation | async-start | bytes 327680 | tf_op jit(solution)/shard_map/all_to_all | solution.py:286
  12.9 9.5 %copy-start.2 = (s32[64,64]{1,0:T(8,128)S(1)}, s32[64,64]{1,0:T(8,128)}, u32[]{:S(2)}) copy-start(s32[64,64]{1,0:T(8,128)} %cand_ref.1) | copy-start | bytes 49156
  39.3 23.9 %copy-start = (f32[12,128,128]{2,1,0:T(8,128)S(1)}, f32[12,128,128]{2,1,0:T(8,128)}, u32[]{:S(2)}) copy-start(f32[12,128,128]{2,1,0:T(8,128)} %tiles_ref.7) | copy-start | bytes 2359300
  39.3 16.3 %all-to-all-start.2 = ((f32[32,32,128]{2,1,0:T(8,128)}), f32[32,32,128]{2,1,0:T(8,128)S(1)}, u32[]{:S(2)}, u32[]{:S(2)}) async-start(f32[32,32,128]{2,1,0:T(8,128)} %bitcast.5), calls=%async_computation.2 | async-start | bytes 1048576 | tf_op jit(solution)/shard_map/all_to_all | solution.py:298
  55.7 9.6 %collective-permute-start.1 = (f32[64,256]{1,0:T(8,128)S(1)}, f32[64,256]{1,0:T(8,128)S(1)}, u32[]{:S(2)}, u32[]{:S(2)}) collective-permute-start(f32[64,256]{1,0:T(8,128)S(1)} %bitcast.17), channel_id=1, source_target_pairs={{0,480},{32,0},{64,32},{96,64},{128,96},{160,128},{192,160},{224,1... | collective-permute-start | bytes 196616 | tf_op jit(solution)/shard_map/ppermute | solution.py:302
  61.1 4.5 %collective-permute-start = (f32[64,256]{1,0:T(8,128)S(1)}, f32[64,256]{1,0:T(8,128)S(1)}, u32[]{:S(2)}, u32[]{:S(2)}) collective-permute-start(f32[64,256]{1,0:T(8,128)S(1)} %bitcast.18), channel_id=1, source_target_pairs={{0,32},{32,64},{64,96},{96,128},{128,160},{160,192},{192,224},{224... | collective-permute-start | bytes 196616 | tf_op jit(solution)/shard_map/ppermute | solution.py:302
  63.2 0.7 copy-start.3
  63.2 0.7 copy-start.4
  67.3 10.0 %collective-permute-start.3 = (f32[64,256]{1,0:T(8,128)S(1)}, f32[64,256]{1,0:T(8,128)S(1)}, u32[]{:S(2)}, u32[]{:S(2)}) collective-permute-start(f32[64,256]{1,0:T(8,128)S(1)} %get-tuple-element.19.own_ref.refs_0_.v1_ref), channel_id=1, source_target_pairs={{0,480},{32,0},{64,32},{96,64},{128,96},{160,128},{192,160},{224,1... | collective-permute-start | bytes 196616 | tf_op jit(solution)/shard_map/ppermute | solution.py:302
  73.9 3.4 %collective-permute-start.2 = (f32[64,256]{1,0:T(8,128)S(1)}, f32[64,256]{1,0:T(8,128)S(1)}, u32[]{:S(2)}, u32[]{:S(2)}) collective-permute-start(f32[64,256]{1,0:T(8,128)S(1)} %get-tuple-element.19.own_ref.refs_0_.v1_ref), channel_id=1, source_target_pairs={{0,32},{32,64},{64,96},{96,128},{128,160},{160,192},{192,224},{224... | collective-permute-start | bytes 196616 | tf_op jit(solution)/shard_map/ppermute | solution.py:302
  73.9 10.4 %all-to-all-start.3 = ((f32[4,64,256]{2,1,0:T(8,128)}), f32[4,64,256]{2,1,0:T(8,128)S(1)}, u32[]{:S(2)}, u32[]{:S(2)}) async-start(f32[4,64,256]{2,1,0:T(8,128)} %get-tuple-element.20), calls=%async_computation.3 | async-start | bytes 524288 | tf_op jit(solution)/shard_map/all_to_all | solution.py:305
  77.4 12.3 %collective-permute-start.5 = (f32[2,64,256]{2,1,0:T(8,128)S(1)}, f32[2,64,256]{2,1,0:T(8,128)S(1)}, u32[]{:S(2)}, u32[]{:S(2)}) collective-permute-start(f32[2,64,256]{2,1,0:T(8,128)S(1)} %pair.1), channel_id=1, source_target_pairs={{0,29},{1,30},{2,31},{3,0},{4,1},{5,2},{6,3},{7,4},{8,5},{9,6},{10... | collective-permute-start | bytes 393224 | tf_op jit(solution)/shard_map/ppermute | solution.py:320
  82.3 10.4 %collective-permute-start.4 = (f32[2,64,256]{2,1,0:T(8,128)S(1)}, f32[2,64,256]{2,1,0:T(8,128)S(1)}, u32[]{:S(2)}, u32[]{:S(2)}) collective-permute-start(f32[2,64,256]{2,1,0:T(8,128)S(1)} %pair.1), channel_id=1, source_target_pairs={{0,31},{1,0},{2,1},{3,2},{4,3},{5,4},{6,5},{7,6},{8,7},{9,8},{10,9... | collective-permute-start | bytes 393224 | tf_op jit(solution)/shard_map/ppermute | solution.py:320
  92.7 3.2 %collective-permute-start.6 = (f32[2,64,256]{2,1,0:T(8,128)S(1)}, f32[2,64,256]{2,1,0:T(8,128)S(1)}, u32[]{:S(2)}, u32[]{:S(2)}) collective-permute-start(f32[2,64,256]{2,1,0:T(8,128)S(1)} %swap.1), channel_id=1, source_target_pairs={{0,32},{32,0},{64,96},{96,64},{128,160},{160,128},{192,224},{224,1... | collective-permute-start | bytes 393224 | tf_op jit(solution)/shard_map/ppermute | solution.py:326
  97.9 16.0 %all-to-all-start.4 = ((f32[4,64,256]{2,1,0:T(8,128)}), f32[4,64,256]{2,1,0:T(8,128)S(1)}, u32[]{:S(2)}, u32[]{:S(2)}) async-start(f32[4,64,256]{2,1,0:T(8,128)} %get-tuple-element.25), calls=%async_computation.4 | async-start | bytes 524288 | tf_op jit(solution)/shard_map/all_to_all | solution.py:305
  101.3 10.0 %collective-permute-start.10 = (f32[64,256]{1,0:T(8,128)S(1)}, f32[64,256]{1,0:T(8,128)S(1)}, u32[]{:S(2)}, u32[]{:S(2)}) collective-permute-start(f32[64,256]{1,0:T(8,128)S(1)} %get-tuple-element.29.v2_ref), channel_id=1, source_target_pairs={{0,29},{1,30},{2,31},{3,0},{4,1},{5,2},{6,3},{7,4},{8,5},{9,6},{10... | collective-permute-start | bytes 196616 | tf_op jit(solution)/shard_map/ppermute | solution.py:348
  106.4 7.5 %collective-permute-start.9 = (f32[64,256]{1,0:T(8,128)S(1)}, f32[64,256]{1,0:T(8,128)S(1)}, u32[]{:S(2)}, u32[]{:S(2)}) collective-permute-start(f32[64,256]{1,0:T(8,128)S(1)} %get-tuple-element.29.v2_ref), channel_id=1, source_target_pairs={{0,31},{1,0},{2,1},{3,2},{4,3},{5,4},{6,5},{7,6},{8,7},{9,8},{10,9... | collective-permute-start | bytes 196616 | tf_op jit(solution)/shard_map/ppermute | solution.py:348
  109.5 4.3 %collective-permute-start.8 = (f32[64,256]{1,0:T(8,128)S(1)}, f32[64,256]{1,0:T(8,128)S(1)}, u32[]{:S(2)}, u32[]{:S(2)}) collective-permute-start(f32[64,256]{1,0:T(8,128)S(1)} %get-tuple-element.29.v2_ref), channel_id=1, source_target_pairs={{0,480},{32,0},{64,32},{96,64},{128,96},{160,128},{192,160},{224,1... | collective-permute-start | bytes 196616 | tf_op jit(solution)/shard_map/ppermute | solution.py:302
  110.8 3.0 %collective-permute-start.7 = (f32[64,256]{1,0:T(8,128)S(1)}, f32[64,256]{1,0:T(8,128)S(1)}, u32[]{:S(2)}, u32[]{:S(2)}) collective-permute-start(f32[64,256]{1,0:T(8,128)S(1)} %get-tuple-element.29.v2_ref), channel_id=1, source_target_pairs={{0,32},{32,64},{64,96},{96,128},{128,160},{160,192},{192,224},{224... | collective-permute-start | bytes 196616 | tf_op jit(solution)/shard_map/ppermute | solution.py:302
  115.8 15.7 %all-to-all-start.5 = ((f32[32,4,128]{2,1,0:T(4,128)}), f32[32,4,128]{2,1,0:T(4,128)S(1)}, u32[]{:S(2)}, u32[]{:S(2)}) async-start(f32[32,4,128]{2,1,0:T(4,128)} %broadcast_in_dim.20), calls=%async_computation.5 | async-start | bytes 131072 | tf_op jit(solution)/shard_map/all_to_all | solution.py:356
  122.3 18.2 %collective-permute-start.12 = (f32[64,256]{1,0:T(8,128)S(1)}, f32[64,256]{1,0:T(8,128)S(1)}, u32[]{:S(2)}, u32[]{:S(2)}) collective-permute-start(f32[64,256]{1,0:T(8,128)S(1)} %get-tuple-element.29.v2_ref), channel_id=1, source_target_pairs={{0,3},{1,4},{2,5},{3,6},{4,7},{5,8},{6,9},{7,10},{8,11},{9,12},{10... | collective-permute-start | bytes 196616 | tf_op jit(solution)/shard_map/ppermute | solution.py:355
  127.2 13.3 %collective-permute-start.11 = (f32[64,256]{1,0:T(8,128)S(1)}, f32[64,256]{1,0:T(8,128)S(1)}, u32[]{:S(2)}, u32[]{:S(2)}) collective-permute-start(f32[64,256]{1,0:T(8,128)S(1)} %get-tuple-element.29.v2_ref), channel_id=1, source_target_pairs={{0,1},{1,2},{2,3},{3,4},{4,5},{5,6},{6,7},{7,8},{8,9},{9,10},{10,1... | collective-permute-start | bytes 196616 | tf_op jit(solution)/shard_map/ppermute | solution.py:355
  132.2 15.7 %all-to-all-start.6 = ((f32[16,4,128]{2,1,0:T(4,128)}), f32[16,4,128]{2,1,0:T(4,128)S(1)}, u32[]{:S(2)}, u32[]{:S(2)}) async-start(f32[16,4,128]{2,1,0:T(4,128)} %broadcast_in_dim.21), calls=%async_computation.6 | async-start | bytes 65536 | tf_op jit(solution)/shard_map/all_to_all | solution.py:364

commit v9 on v8

--- a/solution.py
+++ b/solution.py
@@ -189,7 +189,7 @@
 
 
 def side(col, place_ref):
-    hop = (col >> 1) - place_ref[0]
+    hop = ((col >> 1) - place_ref[0]) * place_ref[1]
     kind = jnp.int32(0)
     for sign, value in ((1, 1), (-1, 2)):
         for h in SHARED:
@@ -199,7 +199,7 @@
 
 def half_kernel(place_ref, row_ref, col_ref, v2_ref, line_ref, low_ref, high_ref, a_ref, b_ref, v0_ref, v1_ref, tiles_ref,
                 part_ref, moments_ref, slots_ref, acc_ref):
-    blocks = [line_ref[x] for x in range(N_X)] + [a_ref[...], b_ref[...], None, None, low_ref[...], high_ref[...]]
+    blocks = [line_ref[x] for x in range(N_X)] + [a_ref[0], b_ref[0], None, None, low_ref[...], high_ref[...]]
     for k, block in enumerate(blocks):
         if block is not None:
             spread(slots_ref, k, block)
@@ -222,9 +222,9 @@
     moments_ref[...] = jnp.concatenate(packed, axis=0).T[:4]
 
 
-def rest_kernel(place_ref, row_ref, col_ref, part_ref, a_ref, b_ref, tiles_ref, out_ref, slots_ref, acc_ref):
-    spread(slots_ref, 0, a_ref[...])
-    spread(slots_ref, 1, b_ref[...])
+def rest_kernel(place_ref, row_ref, col_ref, part_ref, swapped_ref, tiles_ref, out_ref, slots_ref, acc_ref):
+    for k in range(len(SHARED)):
+        spread(slots_ref, k, swapped_ref[k])
     acc_ref[...] = part_ref[...]
     for t in range(tiles_ref.shape[0]):
         @pl.when(side(col_ref[t], place_ref) == 2)
@@ -274,7 +274,6 @@
     core = region & 1
     device = (region * N_ROW + row_index)[None]
     place = jnp.stack([row_index, 1 - 2 * core])
-    upward = jnp.stack([row_index, jnp.int32(1)])
 
     index = jax.ShapeDtypeStruct(tile_row.shape, jnp.int32)
     packed, tile_row, tile_col = pl.pallas_call(
@@ -306,7 +305,7 @@
             copies, "row", 0, 0, tiled=True,
             axis_index_groups=[[x * N_Y + y for x in range(N_X)] for y in range(N_Y)])
 
-    def exchange(v, copies):
+    def fetch(v, copies):
         low, high = region_pair(v)
         line = x_line(copies)
         both = pl.pallas_call(
@@ -319,12 +318,14 @@
                      for r in range(N_REGION) for i in range(N_ROW)]
             got.append(lax.ppermute(both, ("region", "row"), pairs))
         *got, line = lax.optimization_barrier((*got, line))
+        return line, low, high, got
+
+    def swap(got):
         swapped = pl.pallas_call(
             swap_kernel, out_shape=shape(len(got), Q, ROWS), in_specs=[VMEM] * len(got), out_specs=VMEM,
             compiler_params=PARAMS, name="swap",
         )(*got)
-        swapped = lax.ppermute(swapped, "region", [(r, r ^ 1) for r in range(N_REGION)])
-        return [v, line] + got + [swapped, low, high]
+        return lax.ppermute(swapped, "region", [(r, r ^ 1) for r in range(N_REGION)])
 
     slots = pltpu.VMEM((SLOTS * HALF, Q, TILE), F32)
     acc = pltpu.VMEM((HALF, Q, TILE), F32)
@@ -340,27 +341,26 @@
         outer_kernel, out_shape=with_copies, in_specs=[SMEM] * 2 + [VMEM] * 4, out_specs=(VMEM, VMEM),
         scratch_shapes=[pltpu.VMEM((2 * HALF, Q, TILE), F32), acc], compiler_params=PARAMS, name="first_outer",
     )(tile_row, tile_col, inner, low, high, tile_vals)
+    line, low, high, got = fetch(v1, copies)
     v2, copies = pl.pallas_call(
         next_kernel, out_shape=with_copies, in_specs=[SMEM] * 3 + [VMEM] * (N_BLOCKS + 1), out_specs=(VMEM, VMEM),
         scratch_shapes=[slots, acc], compiler_params=PARAMS, name="second",
-    )(place, tile_row, tile_col, *exchange(v1, copies), tile_vals)
-    low, high = region_pair(v2)
-    ahead = [lax.ppermute(v2, "row", ring(N_ROW, -hop)) for hop in SHARED]
+    )(place, tile_row, tile_col, v1, line, *got, swap(got), low, high, tile_vals)
+    line, low, high, got = fetch(v2, copies)
     part, moments = pl.pallas_call(
         half_kernel, out_shape=(shape(HALF, Q, TILE), shape(4, TILE)), in_specs=[SMEM] * 3 + [VMEM] * 9,
         out_specs=(VMEM, VMEM), scratch_shapes=[slots, pltpu.VMEM((3 * HALF, Q, TILE), F32)],
         compiler_params=PARAMS, name="half",
-    )(upward, tile_row, tile_col, v2, x_line(copies), low, high, *ahead, v0, v1, tile_vals)
-    v2_now, moments = lax.optimization_barrier((v2, moments))
-    behind = [lax.ppermute(v2_now, "row", ring(N_ROW, hop)) for hop in SHARED]
+    )(place, tile_row, tile_col, v2, line, low, high, *got, v0, v1, tile_vals)
+    *got, moments = lax.optimization_barrier((*got, moments))
     moments = lax.all_to_all(jnp.broadcast_to(moments[None], (N_ROW, 4, TILE)), "row", 0, 0, tiled=True)
     moments = jnp.sum(moments.reshape(2, 2, 2, 2, 2, 4, TILE).sum(0).sum(0).sum(0).sum(0), axis=0)
     v3 = pl.pallas_call(
-        rest_kernel, out_shape=shape(Q, ROWS), in_specs=[SMEM] * 3 + [VMEM] * 4, out_specs=VMEM,
+        rest_kernel, out_shape=shape(Q, ROWS), in_specs=[SMEM] * 3 + [VMEM] * 3, out_specs=VMEM,
         scratch_shapes=[pltpu.VMEM((2 * HALF, Q, TILE), F32), acc],
         cost_estimate=pl.CostEstimate(flops=2 * 12 * Q * TILE * TILE, bytes_accessed=2000000, transcendentals=0),
         compiler_params=PARAMS, name="rest",
-    )(upward, tile_row, tile_col, part, *behind, tile_vals)
+    )(place, tile_row, tile_col, part, swap(got), tile_vals)
     moments = lax.all_to_all(jnp.broadcast_to(moments[None], (N_REGION, 4, TILE)), "region", 0, 0, tiled=True)
     diffused, residual = pl.pallas_call(
         finish_kernel, out_shape=(shape(Q, ROWS), shape(Q, ROWS)), in_specs=[VMEM] * 5, out_specs=(VMEM, VMEM),

time: 150 us -> 151 us (level)
  waiting for transfers between devices: 40.5 us -> 50.8 us
  starting transfers between devices: 78.2 us -> 68.3 us
    ppermute x7 -> x6, starting transfers between devices: 26.2 us -> 19.8 us  [the longest x4 13.2 us: fetch(): got.append(lax.ppermute(both, ('region', 'row'), pairs))]
    ppermute x7 -> x6, waiting for transfers between devices: 12.3 us -> 18.4 us  [the longest x4 17 us: fetch(): got.append(lax.ppermute(both, ('region', 'row'), pairs))]
    all_to_all x1, waiting for transfers between devices: 0.01 us -> 4.22 us  [local(): lax.all_to_all(jnp.broadcast_to(moments[None], (N_ROW, 4, TILE)), 'row',...]
    all_to_all x1, starting transfers between devices: 6.46 us -> 3.86 us  [local(): lax.all_to_all(jnp.broadcast_to(moments[None], (N_ROW, 4, TILE)), 'row',...]
  transfers between devices with their start and end apart: 19 -> 18, of which waited for: 8 -> 10; matrix products, arithmetic and copies ran while one was open for 1% -> 0% of each run, Pallas kernels for 2% -> 2%
where the time goes in v9:
time: 151 us; the launch traced here: 150 us
  starting transfers between devices  68.3 us (45%)
  waiting for transfers between devices  50.8 us (34%)
  Pallas kernels  14.2 us (9%)
  blocking collectives  13.3 us (9%)
  local copies, waits for them, and re-layouts  2.16 us (1%)
    ppermute x4, waiting for transfers between devices, fetch(): got.append(lax.ppermute(both, ('region', 'row'), pairs))  17 us
    all_to_all x1, blocking collectives, local(): lax.all_to_all(by_query.reshape(N_ROW, QS * HALF, TILE), 'row', 0, 0, til...  13.3 us
    ppermute x4, starting transfers between devices, fetch(): got.append(lax.ppermute(both, ('region', 'row'), pairs))  13.2 us
    all_to_all x1, waiting for transfers between devices, local(): lax.all_to_all(near.reshape(N_ROW, width, TILE), 'row', 0, 0, tiled=True)  12.2 us
    ppermute x3, starting transfers between devices, region_pair(): lax.ppermute(v, 'region', ring(N_REGION, -1))  12.2 us
    all_to_all x1, starting transfers between devices, local(): lax.all_to_all(packed, 'row', 0, 0, tiled=True).reshape(Q, D + TILE)  10.6 us
    all_to_all x1, waiting for transfers between devices, local(): lax.all_to_all(packed, 'row', 0, 0, tiled=True).reshape(Q, D + TILE)  9.34 us
    all_to_all x1, starting transfers between devices, local(): lax.all_to_all(jnp.broadcast_to(moments[None], (N_REGION, 4, TILE)), 'reg...  7.44 us
  transfers between devices with their start and end apart: 18, of which 10 were waited for; matrix products, arithmetic and copies ran while one was open for 0% of the time, Pallas kernels for 2%

profile of v9, /device:TPU:1, one launch (start us, length us, event | category | flops | bytes accessed | tf_op | source)
XLA Modules:
  0.0 149.8 jit_solution(7667417519236603671)
XLA Ops:
  0.6 1.5 %pack.1 = (f32[32,2,640]{2,1,0:T(2,128)}, s32[12]{0:T(128)}, s32[12]{0:T(128)}) custom-call(f32[2,512]{1,0:T(2,128)} %queries_hbm.1, s32[1,256]{1,0:T(1,128)} %perm_hbm.1, s32[12]{0:T(128)} %row_hbm.1, s32[12]{0:T(128)} %col_hbm.1), custom_call_target="tpu_custom_call" | custom-call | tf_op jit(solution)/shard_map/pack/pallas_call | solution.py:279
  2.2 0.0 copy-start.1
  2.2 10.6 %all-to-all-start = ((f32[32,2,640]{2,1,0:T(2,128)}), f32[32,2,640]{2,1,0:T(2,128)S(1)}, u32[]{:S(2)}, u32[]{:S(2)}) async-start(f32[32,2,640]{2,1,0:T(2,128)} %get-tuple-element.22), calls=%async_computation | async-start | bytes 327680 | tf_op jit(solution)/shard_map/all_to_all | solution.py:285
  12.9 0.0 copy-start.2
  12.9 9.3 %all-to-all-done = f32[32,2,640]{2,1,0:T(2,128)S(1)} async-done(((f32[32,2,640]{2,1,0:T(2,128)}), f32[32,2,640]{2,1,0:T(2,128)S(1)}, u32[]{:S(2)}, u32[]{:S(2)}) %all-to-all-start) | async-done | bytes 163872 | tf_op jit(solution)/shard_map/all_to_all | solution.py:285
  22.2 0.1 reshape.28.packed_ref
  22.3 0.6 scores.1
  23.0 13.3 %all_to_all.35 = f32[32,4,128]{2,1,0:T(4,128)S(1)} all-to-all(f32[32,4,128]{2,1,0:T(4,128)S(1)} %bitcast.22), channel_id=1, replica_groups=mesh['region'=16,'row'=32] {'row'}, dimensions={0} | all-to-all | bytes 131072 | tf_op jit(solution)/shard_map/all_to_all | solution.py:290
  36.3 3.0 %permute.1 = f32[1024,128]{1,0:T(8,128)} custom-call(f32[128,128]{1,0:T(8,128)S(1)} %bitcast.21, f32[64,640]{1,0:T(8,128)S(1)} %reshape.28.packed_ref), custom_call_target="tpu_custom_call" | custom-call | tf_op jit(solution)/shard_map/permute/pallas_call | solution.py:292
  39.3 4.0 %all-to-all-start.2 = ((f32[32,32,128]{2,1,0:T(8,128)}), f32[32,32,128]{2,1,0:T(8,128)S(1)}, u32[]{:S(2)}, u32[]{:S(2)}) async-start(f32[32,32,128]{2,1,0:T(8,128)} %bitcast.6), calls=%async_computation.2 | async-start | bytes 1048576 | tf_op jit(solution)/shard_map/all_to_all | solution.py:297
  43.4 12.2 %all-to-all-done.2 = f32[32,32,128]{2,1,0:T(8,128)S(1)} async-done(((f32[32,32,128]{2,1,0:T(8,128)}), f32[32,32,128]{2,1,0:T(8,128)S(1)}, u32[]{:S(2)}, u32[]{:S(2)}) %all-to-all-start.2) | async-done | bytes 524320 | tf_op jit(solution)/shard_map/all_to_all | solution.py:297
  55.6 0.1 copy.17
  55.7 5.4 %collective-permute-start.1 = (f32[64,256]{1,0:T(8,128)S(1)}, f32[64,256]{1,0:T(8,128)S(1)}, u32[]{:S(2)}, u32[]{:S(2)}) collective-permute-start(f32[64,256]{1,0:T(8,128)S(1)} %bitcast.17), channel_id=1, source_target_pairs={{0,480},{32,0},{64,32},{96,64},{128,96},{160,128},{192,160},{224,1... | collective-permute-start | bytes 196616 | tf_op jit(solution)/shard_map/ppermute | solution.py:301
  61.1 2.0 %collective-permute-start = (f32[64,256]{1,0:T(8,128)S(1)}, f32[64,256]{1,0:T(8,128)S(1)}, u32[]{:S(2)}, u32[]{:S(2)}) collective-permute-start(f32[64,256]{1,0:T(8,128)S(1)} %bitcast.18), channel_id=1, source_target_pairs={{0,32},{32,64},{64,96},{96,128},{128,160},{160,192},{192,224},{224... | collective-permute-start | bytes 196616 | tf_op jit(solution)/shard_map/ppermute | solution.py:301
  63.1 0.1 pad_add_fusion.place_ref
  63.2 0.7 copy-done.3
  63.9 0.0 copy-done.4
  63.9 1.4 first_inner.1.inner_ref
  65.3 0.0 collective-permute-done.1.high_ref
  65.3 0.3 collective-permute-done.low_ref
  65.6 1.7 %first_outer.1 = (f32[64,256]{1,0:T(8,128)S(1)}, f32[4,64,256]{2,1,0:T(8,128)}) custom-call(s32[12]{0:T(128)S(1)} %copy-done.3, s32[12]{0:T(128)S(1)} %copy-done.4, f32[2,64,128]{2,1,0:T(8,128)S(1)} %first_inner.1.inner_ref, f32[64,256]{1,0:T(8,128)S(1)} %collective-permute-done.low_ref, f32[64,256]{1,0:T(8,128)S(1)} %collective-permute-done.1.high_ref, ...), custom_call_target="tpu_custom_call" | custom-call | tf_op jit(solution)/shard_map/first_outer/pallas_call | solution.py:340
  67.3 6.6 %collective-permute-start.3 = (f32[64,256]{1,0:T(8,128)S(1)}, f32[64,256]{1,0:T(8,128)S(1)}, u32[]{:S(2)}, u32[]{:S(2)}) collective-permute-start(f32[64,256]{1,0:T(8,128)S(1)} %get-tuple-element.23.own_ref.refs_0_.v1_ref), channel_id=1, source_target_pairs={{0,480},{32,0},{64,32},{96,64},{128,96},{160,128},{192,160},{224,1... | collective-permute-start | bytes 196616 | tf_op jit(solution)/shard_map/ppermute | solution.py:301
  73.9 0.0 collective-permute-start.2
  73.9 3.4 %all-to-all-start.3 = ((f32[4,64,256]{2,1,0:T(8,128)}), f32[4,64,256]{2,1,0:T(8,128)S(1)}, u32[]{:S(2)}, u32[]{:S(2)}) async-start(f32[4,64,256]{2,1,0:T(8,128)} %get-tuple-element.24), calls=%async_computation.3 | async-start | bytes 524288 | tf_op jit(solution)/shard_map/all_to_all | solution.py:304
  77.4 4.9 %collective-permute-start.5 = (f32[2,64,256]{2,1,0:T(8,128)S(1)}, f32[2,64,256]{2,1,0:T(8,128)S(1)}, u32[]{:S(2)}, u32[]{:S(2)}) collective-permute-start(f32[2,64,256]{2,1,0:T(8,128)S(1)} %pair.2), channel_id=1, source_target_pairs={{0,29},{1,30},{2,31},{3,0},{4,1},{5,2},{6,3},{7,4},{8,5},{9,6},{10... | collective-permute-start | bytes 393224 | tf_op jit(solution)/shard_map/ppermute | solution.py:319
  82.3 2.0 %collective-permute-start.4 = (f32[2,64,256]{2,1,0:T(8,128)S(1)}, f32[2,64,256]{2,1,0:T(8,128)S(1)}, u32[]{:S(2)}, u32[]{:S(2)}) collective-permute-start(f32[2,64,256]{2,1,0:T(8,128)S(1)} %pair.2), channel_id=1, source_target_pairs={{0,31},{1,0},{2,1},{3,2},{4,3},{5,4},{6,5},{7,6},{8,7},{9,8},{10,9... | collective-permute-start | bytes 393224 | tf_op jit(solution)/shard_map/ppermute | solution.py:319
  84.3 5.4 %collective-permute-done.5.refs_1_.refs_3_ = f32[2,64,256]{2,1,0:T(8,128)S(1)} collective-permute-done((f32[2,64,256]{2,1,0:T(8,128)S(1)}, f32[2,64,256]{2,1,0:T(8,128)S(1)}, u32[]{:S(2)}, u32[]{:S(2)}) %collective-permute-start.5) | collective-permute-done | bytes 131104 | tf_op jit(solution)/shard_map/ppermute | solution.py:319
  89.7 3.0 %collective-permute-done.4.refs_0_.refs_2_ = f32[2,64,256]{2,1,0:T(8,128)S(1)} collective-permute-done((f32[2,64,256]{2,1,0:T(8,128)S(1)}, f32[2,64,256]{2,1,0:T(8,128)S(1)}, u32[]{:S(2)}, u32[]{:S(2)}) %collective-permute-start.4) | collective-permute-done | bytes 131104 | tf_op jit(solution)/shard_map/ppermute | solution.py:319
  92.8 1.9 %collective-permute-start.6 = (f32[2,64,256]{2,1,0:T(8,128)S(1)}, f32[2,64,256]{2,1,0:T(8,128)S(1)}, u32[]{:S(2)}, u32[]{:S(2)}) collective-permute-start(f32[2,64,256]{2,1,0:T(8,128)S(1)} %swap.2), channel_id=1, source_target_pairs={{0,32},{32,0},{64,96},{96,64},{128,160},{160,128},{192,224},{224,1... | collective-permute-start | bytes 393224 | tf_op jit(solution)/shard_map/ppermute | solution.py:328
  94.7 1.3 collective-permute-done.6.refs_4_
  96.0 1.9 %second.1 = (f32[64,256]{1,0:T(8,128)S(1)}, f32[4,64,256]{2,1,0:T(8,128)}) custom-call(s32[2]{0:T(128)S(1)} %pad_add_fusion.place_ref, s32[12]{0:T(128)S(1)} %copy-done.3, s32[12]{0:T(128)S(1)} %copy-done.4, f32[64,256]{1,0:T(8,128)S(1)} %get-tuple-element.23.own_ref.refs_0_.v1_ref, f32[4,64,256]{2,1,0:T(8,128)S(1)} %all-to-all-done.3.refs_1_, ...), custom_call_target="tpu_custom_call" | custom-call | tf_op jit(solution)/shard_map/second/pallas_call | solution.py:345
  97.9 0.2 collective-permute-start.8
  98.1 1.6 %collective-permute-start.7 = (f32[64,256]{1,0:T(8,128)S(1)}, f32[64,256]{1,0:T(8,128)S(1)}, u32[]{:S(2)}, u32[]{:S(2)}) collective-permute-start(f32[64,256]{1,0:T(8,128)S(1)} %get-tuple-element.28.own_ref.v2_ref), channel_id=1, source_target_pairs={{0,32},{32,64},{64,96},{96,128},{128,160},{160,192},{192,224},{224... | collective-permute-start | bytes 196616 | tf_op jit(solution)/shard_map/ppermute | solution.py:301
  99.7 3.4 %all-to-all-start.4 = ((f32[4,64,256]{2,1,0:T(8,128)}), f32[4,64,256]{2,1,0:T(8,128)S(1)}, u32[]{:S(2)}, u32[]{:S(2)}) async-start(f32[4,64,256]{2,1,0:T(8,128)} %get-tuple-element.29), calls=%async_computation.4 | async-start | bytes 524288 | tf_op jit(solution)/shard_map/all_to_all | solution.py:304
  103.1 4.4 %collective-permute-start.10 = (f32[2,64,256]{2,1,0:T(8,128)S(1)}, f32[2,64,256]{2,1,0:T(8,128)S(1)}, u32[]{:S(2)}, u32[]{:S(2)}) collective-permute-start(f32[2,64,256]{2,1,0:T(8,128)S(1)} %pair.3), channel_id=1, source_target_pairs={{0,29},{1,30},{2,31},{3,0},{4,1},{5,2},{6,3},{7,4},{8,5},{9,6},{10... | collective-permute-start | bytes 393224 | tf_op jit(solution)/shard_map/ppermute | solution.py:319
  107.6 1.9 %collective-permute-start.9 = (f32[2,64,256]{2,1,0:T(8,128)S(1)}, f32[2,64,256]{2,1,0:T(8,128)S(1)}, u32[]{:S(2)}, u32[]{:S(2)}) collective-permute-start(f32[2,64,256]{2,1,0:T(8,128)S(1)} %pair.3), channel_id=1, source_target_pairs={{0,31},{1,0},{2,1},{3,2},{4,3},{5,4},{6,5},{7,6},{8,7},{9,8},{10,9... | collective-permute-start | bytes 393224 | tf_op jit(solution)/shard_map/ppermute | solution.py:319
  109.5 4.9 %collective-permute-done.10.b_ref.refs_1_ = f32[2,64,256]{2,1,0:T(8,128)S(1)} collective-permute-done((f32[2,64,256]{2,1,0:T(8,128)S(1)}, f32[2,64,256]{2,1,0:T(8,128)S(1)}, u32[]{:S(2)}, u32[]{:S(2)}) %collective-permute-start.10) | collective-permute-done | bytes 131104 | tf_op jit(solution)/shard_map/ppermute | solution.py:319
  114.4 3.7 %collective-permute-done.9.a_ref.refs_0_ = f32[2,64,256]{2,1,0:T(8,128)S(1)} collective-permute-done((f32[2,64,256]{2,1,0:T(8,128)S(1)}, f32[2,64,256]{2,1,0:T(8,128)S(1)}, u32[]{:S(2)}, u32[]{:S(2)}) %collective-permute-start.9) | collective-permute-done | bytes 131104 | tf_op jit(solution)/shard_map/ppermute | solution.py:319
  118.1 1.3 half.1
  119.4 0.6 broadcast_in_dim.10
  120.0 3.9 %all-to-all-start.5 = ((f32[32,4,128]{2,1,0:T(4,128)}), f32[32,4,128]{2,1,0:T(4,128)S(1)}, u32[]{:S(2)}, u32[]{:S(2)}) async-start(f32[32,4,128]{2,1,0:T(4,128)} %broadcast_in_dim.10), calls=%async_computation.5 | async-start | bytes 131072 | tf_op jit(solution)/shard_map/all_to_all | solution.py:356
  123.9 4.6 %collective-permute-start.11 = (f32[2,64,256]{2,1,0:T(8,128)S(1)}, f32[2,64,256]{2,1,0:T(8,128)S(1)}, u32[]{:S(2)}, u32[]{:S(2)}) collective-permute-start(f32[2,64,256]{2,1,0:T(8,128)S(1)} %swap.3), channel_id=1, source_target_pairs={{0,32},{32,0},{64,96},{96,64},{128,160},{160,128},{192,224},{224,1... | collective-permute-start | bytes 393224 | tf_op jit(solution)/shard_map/ppermute | solution.py:328
  128.5 4.2 %all-to-all-done.5 = f32[32,4,128]{2,1,0:T(4,128)S(1)} async-done(((f32[32,4,128]{2,1,0:T(4,128)}), f32[32,4,128]{2,1,0:T(4,128)S(1)}, u32[]{:S(2)}, u32[]{:S(2)}) %all-to-all-start.5) | async-done | bytes 65568 | tf_op jit(solution)/shard_map/all_to_all | solution.py:356
  132.8 0.6 broadcast_in_dim.22
  133.4 7.4 %all-to-all-start.6 = ((f32[16,4,128]{2,1,0:T(4,128)}), f32[16,4,128]{2,1,0:T(4,128)S(1)}, u32[]{:S(2)}, u32[]{:S(2)}) async-start(f32[16,4,128]{2,1,0:T(4,128)} %broadcast_in_dim.22), calls=%async_computation.6 | async-start | bytes 65536 | tf_op jit(solution)/shard_map/all_to_all | solution.py:364
  140.9 1.0 rest.1.v3_ref
  141.9 6.3 %all-to-all-done.6.moments_ref = f32[16,4,128]{2,1,0:T(4,128)S(1)} async-done(((f32[16,4,128]{2,1,0:T(4,128)}), f32[16,4,128]{2,1,0:T(4,128)S(1)}, u32[]{:S(2)}, u32[]{:S(2)}) %all-to-all-start.6) | async-done | bytes 32800 | tf_op jit(solution)/shard_map/all_to_all | solution.py:364
  148.3 1.5 %finish.1 = (f32[64,256]{1,0:T(8,128)}, f32[64,256]{1,0:T(8,128)}) custom-call(f32[16,4,128]{2,1,0:T(4,128)S(1)} %all-to-all-done.6.moments_ref, f32[64,256]{1,0:T(8,128)S(1)} %bitcast.20, f32[64,256]{1,0:T(8,128)S(1)} %get-tuple-element.23.own_ref.refs_0_.v1_ref, f32[64,256]{1,0:T(8,128)S(1)} %get-tuple-element.28.own_ref.v2_ref, f32[64,256]{1,0:T(8,128)S(1)} %rest.1.v3_ref), custom_call_target="tpu_custom_call" | custom-call | tf_op jit(solution)/shard_map/finish/pallas_call | solution.py:365
  (21 shorter events, 0.2 us)
Async XLA Ops:
  2.2 20.1 %copy-start.1 = (f32[256,512]{1,0:T(8,128)S(1)}, f32[256,512]{1,0:T(8,128)}, u32[]{:S(2)}) copy-start(f32[256,512]{1,0:T(8,128)} %desc_ref.1) | copy-start | bytes 1572868
  2.2 20.0 %all-to-all-start = ((f32[32,2,640]{2,1,0:T(2,128)}), f32[32,2,640]{2,1,0:T(2,128)S(1)}, u32[]{:S(2)}, u32[]{:S(2)}) async-start(f32[32,2,640]{2,1,0:T(2,128)} %get-tuple-element.22), calls=%async_computation | async-start | bytes 327680 | tf_op jit(solution)/shard_map/all_to_all | solution.py:285
  12.9 9.5 %copy-start.2 = (s32[64,64]{1,0:T(8,128)S(1)}, s32[64,64]{1,0:T(8,128)}, u32[]{:S(2)}) copy-start(s32[64,64]{1,0:T(8,128)} %cand_ref.1) | copy-start | bytes 49156
  39.3 23.9 %copy-start = (f32[12,128,128]{2,1,0:T(8,128)S(1)}, f32[12,128,128]{2,1,0:T(8,128)}, u32[]{:S(2)}) copy-start(f32[12,128,128]{2,1,0:T(8,128)} %tiles_ref.7) | copy-start | bytes 2359300
  39.3 16.3 %all-to-all-start.2 = ((f32[32,32,128]{2,1,0:T(8,128)}), f32[32,32,128]{2,1,0:T(8,128)S(1)}, u32[]{:S(2)}, u32[]{:S(2)}) async-start(f32[32,32,128]{2,1,0:T(8,128)} %bitcast.6), calls=%async_computation.2 | async-start | bytes 1048576 | tf_op jit(solution)/shard_map/all_to_all | solution.py:297
  55.7 9.6 %collective-permute-start.1 = (f32[64,256]{1,0:T(8,128)S(1)}, f32[64,256]{1,0:T(8,128)S(1)}, u32[]{:S(2)}, u32[]{:S(2)}) collective-permute-start(f32[64,256]{1,0:T(8,128)S(1)} %bitcast.17), channel_id=1, source_target_pairs={{0,480},{32,0},{64,32},{96,64},{128,96},{160,128},{192,160},{224,1... | collective-permute-start | bytes 196616 | tf_op jit(solution)/shard_map/ppermute | solution.py:301
  61.1 4.5 %collective-permute-start = (f32[64,256]{1,0:T(8,128)S(1)}, f32[64,256]{1,0:T(8,128)S(1)}, u32[]{:S(2)}, u32[]{:S(2)}) collective-permute-start(f32[64,256]{1,0:T(8,128)S(1)} %bitcast.18), channel_id=1, source_target_pairs={{0,32},{32,64},{64,96},{96,128},{128,160},{160,192},{192,224},{224... | collective-permute-start | bytes 196616 | tf_op jit(solution)/shard_map/ppermute | solution.py:301
  63.2 0.7 copy-start.3
  63.2 0.7 copy-start.4
  67.3 10.0 %collective-permute-start.3 = (f32[64,256]{1,0:T(8,128)S(1)}, f32[64,256]{1,0:T(8,128)S(1)}, u32[]{:S(2)}, u32[]{:S(2)}) collective-permute-start(f32[64,256]{1,0:T(8,128)S(1)} %get-tuple-element.23.own_ref.refs_0_.v1_ref), channel_id=1, source_target_pairs={{0,480},{32,0},{64,32},{96,64},{128,96},{160,128},{192,160},{224,1... | collective-permute-start | bytes 196616 | tf_op jit(solution)/shard_map/ppermute | solution.py:301
  73.9 3.4 %collective-permute-start.2 = (f32[64,256]{1,0:T(8,128)S(1)}, f32[64,256]{1,0:T(8,128)S(1)}, u32[]{:S(2)}, u32[]{:S(2)}) collective-permute-start(f32[64,256]{1,0:T(8,128)S(1)} %get-tuple-element.23.own_ref.refs_0_.v1_ref), channel_id=1, source_target_pairs={{0,32},{32,64},{64,96},{96,128},{128,160},{160,192},{192,224},{224... | collective-permute-start | bytes 196616 | tf_op jit(solution)/shard_map/ppermute | solution.py:301
  73.9 10.4 %all-to-all-start.3 = ((f32[4,64,256]{2,1,0:T(8,128)}), f32[4,64,256]{2,1,0:T(8,128)S(1)}, u32[]{:S(2)}, u32[]{:S(2)}) async-start(f32[4,64,256]{2,1,0:T(8,128)} %get-tuple-element.24), calls=%async_computation.3 | async-start | bytes 524288 | tf_op jit(solution)/shard_map/all_to_all | solution.py:304
  77.4 12.3 %collective-permute-start.5 = (f32[2,64,256]{2,1,0:T(8,128)S(1)}, f32[2,64,256]{2,1,0:T(8,128)S(1)}, u32[]{:S(2)}, u32[]{:S(2)}) collective-permute-start(f32[2,64,256]{2,1,0:T(8,128)S(1)} %pair.2), channel_id=1, source_target_pairs={{0,29},{1,30},{2,31},{3,0},{4,1},{5,2},{6,3},{7,4},{8,5},{9,6},{10... | collective-permute-start | bytes 393224 | tf_op jit(solution)/shard_map/ppermute | solution.py:319
  82.3 10.4 %collective-permute-start.4 = (f32[2,64,256]{2,1,0:T(8,128)S(1)}, f32[2,64,256]{2,1,0:T(8,128)S(1)}, u32[]{:S(2)}, u32[]{:S(2)}) collective-permute-start(f32[2,64,256]{2,1,0:T(8,128)S(1)} %pair.2), channel_id=1, source_target_pairs={{0,31},{1,0},{2,1},{3,2},{4,3},{5,4},{6,5},{7,6},{8,7},{9,8},{10,9... | collective-permute-start | bytes 393224 | tf_op jit(solution)/shard_map/ppermute | solution.py:319
  92.8 3.2 %collective-permute-start.6 = (f32[2,64,256]{2,1,0:T(8,128)S(1)}, f32[2,64,256]{2,1,0:T(8,128)S(1)}, u32[]{:S(2)}, u32[]{:S(2)}) collective-permute-start(f32[2,64,256]{2,1,0:T(8,128)S(1)} %swap.2), channel_id=1, source_target_pairs={{0,32},{32,0},{64,96},{96,64},{128,160},{160,128},{192,224},{224,1... | collective-permute-start | bytes 393224 | tf_op jit(solution)/shard_map/ppermute | solution.py:328
  97.9 5.2 %collective-permute-start.8 = (f32[64,256]{1,0:T(8,128)S(1)}, f32[64,256]{1,0:T(8,128)S(1)}, u32[]{:S(2)}, u32[]{:S(2)}) collective-permute-start(f32[64,256]{1,0:T(8,128)S(1)} %get-tuple-element.28.own_ref.v2_ref), channel_id=1, source_target_pairs={{0,480},{32,0},{64,32},{96,64},{128,96},{160,128},{192,160},{224,1... | collective-permute-start | bytes 196616 | tf_op jit(solution)/shard_map/ppermute | solution.py:301
  98.1 5.0 %collective-permute-start.7 = (f32[64,256]{1,0:T(8,128)S(1)}, f32[64,256]{1,0:T(8,128)S(1)}, u32[]{:S(2)}, u32[]{:S(2)}) collective-permute-start(f32[64,256]{1,0:T(8,128)S(1)} %get-tuple-element.28.own_ref.v2_ref), channel_id=1, source_target_pairs={{0,32},{32,64},{64,96},{96,128},{128,160},{160,192},{192,224},{224... | collective-permute-start | bytes 196616 | tf_op jit(solution)/shard_map/ppermute | solution.py:301
  99.7 9.8 %all-to-all-start.4 = ((f32[4,64,256]{2,1,0:T(8,128)}), f32[4,64,256]{2,1,0:T(8,128)S(1)}, u32[]{:S(2)}, u32[]{:S(2)}) async-start(f32[4,64,256]{2,1,0:T(8,128)} %get-tuple-element.29), calls=%async_computation.4 | async-start | bytes 524288 | tf_op jit(solution)/shard_map/all_to_all | solution.py:304
  103.1 11.3 %collective-permute-start.10 = (f32[2,64,256]{2,1,0:T(8,128)S(1)}, f32[2,64,256]{2,1,0:T(8,128)S(1)}, u32[]{:S(2)}, u32[]{:S(2)}) collective-permute-start(f32[2,64,256]{2,1,0:T(8,128)S(1)} %pair.3), channel_id=1, source_target_pairs={{0,29},{1,30},{2,31},{3,0},{4,1},{5,2},{6,3},{7,4},{8,5},{9,6},{10... | collective-permute-start | bytes 393224 | tf_op jit(solution)/shard_map/ppermute | solution.py:319
  107.6 10.5 %collective-permute-start.9 = (f32[2,64,256]{2,1,0:T(8,128)S(1)}, f32[2,64,256]{2,1,0:T(8,128)S(1)}, u32[]{:S(2)}, u32[]{:S(2)}) collective-permute-start(f32[2,64,256]{2,1,0:T(8,128)S(1)} %pair.3), channel_id=1, source_target_pairs={{0,31},{1,0},{2,1},{3,2},{4,3},{5,4},{6,5},{7,6},{8,7},{9,8},{10,9... | collective-permute-start | bytes 393224 | tf_op jit(solution)/shard_map/ppermute | solution.py:319
  120.0 12.7 %all-to-all-start.5 = ((f32[32,4,128]{2,1,0:T(4,128)}), f32[32,4,128]{2,1,0:T(4,128)S(1)}, u32[]{:S(2)}, u32[]{:S(2)}) async-start(f32[32,4,128]{2,1,0:T(4,128)} %broadcast_in_dim.10), calls=%async_computation.5 | async-start | bytes 131072 | tf_op jit(solution)/shard_map/all_to_all | solution.py:356
  123.9 16.9 %collective-permute-start.11 = (f32[2,64,256]{2,1,0:T(8,128)S(1)}, f32[2,64,256]{2,1,0:T(8,128)S(1)}, u32[]{:S(2)}, u32[]{:S(2)}) collective-permute-start(f32[2,64,256]{2,1,0:T(8,128)S(1)} %swap.3), channel_id=1, source_target_pairs={{0,32},{32,0},{64,96},{96,64},{128,160},{160,128},{192,224},{224,1... | collective-permute-start | bytes 393224 | tf_op jit(solution)/shard_map/ppermute | solution.py:328
  133.4 14.8 %all-to-all-start.6 = ((f32[16,4,128]{2,1,0:T(4,128)}), f32[16,4,128]{2,1,0:T(4,128)S(1)}, u32[]{:S(2)}, u32[]{:S(2)}) async-start(f32[16,4,128]{2,1,0:T(4,128)} %broadcast_in_dim.22), calls=%async_computation.6 | async-start | bytes 65536 | tf_op jit(solution)/shard_map/all_to_all | solution.py:364

commit v10 on v9

--- a/solution.py
+++ b/solution.py
@@ -87,20 +87,24 @@
                 out_ref[pl.ds((k * QS + q) * HALF + h, N_ROW, stride=width), :] = rolled
 
 
-def near_slot(col, place_ref):
-    hop = ((col >> 1) - place_ref[0]) & (N_ROW - 1)
+def place(dev_ref):
+    return dev_ref[0] & (N_ROW - 1), 1 - 2 * ((dev_ref[0] >> 5) & 1)
+
+
+def near_slot(col, here):
+    hop = ((col >> 1) - here[0]) & (N_ROW - 1)
     slot = jnp.int32(0)
     for k, h in enumerate(HOPS):
         slot = jnp.where(hop == h % N_ROW, k, slot)
     return slot * HALF + (col & 1)
 
 
-def any_slot(col, place_ref):
+def any_slot(col, here):
     owner = col >> 1
-    hop = owner - place_ref[0]
+    hop = owner - here[0]
     slot = owner >> 3
     for k, h in enumerate(SHARED + tuple(-h for h in SHARED)):
-        slot = jnp.where(((hop * place_ref[1]) & (N_ROW - 1)) == h % N_ROW, N_X + k, slot)
+        slot = jnp.where(((hop * here[1]) & (N_ROW - 1)) == h % N_ROW, N_X + k, slot)
     slot = slot * HALF + (col & 1)
     return jnp.where(col >= N_ROW * HALF, col - N_ROW * HALF + (N_X + 2 * len(SHARED)) * HALF, slot)
 
@@ -132,7 +136,7 @@
                 copies_ref[x, :, cols] = acc_ref[h]
 
 
-def inner_kernel(place_ref, row_ref, col_ref, near_ref, tiles_ref, out_ref, slots_ref):
+def inner_kernel(dev_ref, row_ref, col_ref, near_ref, tiles_ref, out_ref, slots_ref):
     width = len(HOPS) * QS * HALF
     for k in range(len(HOPS)):
         for h in range(HALF):
@@ -142,7 +146,7 @@
     out_ref[...] = jnp.zeros_like(out_ref)
     for t in range(tiles_ref.shape[0]):
         inside = col_ref[t] < N_ROW * HALF
-        slot = jnp.where(inside, near_slot(col_ref[t], place_ref), 0)
+        slot = jnp.where(inside, near_slot(col_ref[t], place(dev_ref)), 0)
         out_ref[row_ref[t]] += jnp.where(inside, product(slots_ref, slot, tiles_ref, t), 0.0)
 
 
@@ -157,9 +161,9 @@
     store(acc_ref, out_ref, copies_ref)
 
 
-def pair_kernel(core_ref, own_ref, low_ref, high_ref, out_ref):
+def pair_kernel(dev_ref, own_ref, low_ref, high_ref, out_ref):
     out_ref[0] = own_ref[...]
-    out_ref[1] = jnp.where(core_ref[0] == 0, high_ref[...], low_ref[...])
+    out_ref[1] = jnp.where(place(dev_ref)[1] == 1, high_ref[...], low_ref[...])
 
 
 def swap_kernel(*refs):
@@ -171,7 +175,7 @@
 N_BLOCKS = 7
 
 
-def times_s(place_ref, row_ref, col_ref, blocks, tiles_ref, slots_ref, acc_ref):
+def times_s(dev_ref, row_ref, col_ref, blocks, tiles_ref, slots_ref, acc_ref):
     _, line_ref, a_ref, b_ref, swapped_ref, low_ref, high_ref = blocks
     blocks = [line_ref[x] for x in range(N_X)] + [
         a_ref[0], b_ref[0], swapped_ref[0], swapped_ref[1], low_ref[...], high_ref[...]]
@@ -179,17 +183,17 @@
         spread(slots_ref, k, block)
     acc_ref[...] = jnp.zeros_like(acc_ref)
     for t in range(tiles_ref.shape[0]):
-        acc_ref[row_ref[t]] += product(slots_ref, any_slot(col_ref[t], place_ref), tiles_ref, t)
-
-
-def next_kernel(place_ref, row_ref, col_ref, *refs):
+        acc_ref[row_ref[t]] += product(slots_ref, any_slot(col_ref[t], place(dev_ref)), tiles_ref, t)
+
+
+def next_kernel(dev_ref, row_ref, col_ref, *refs):
     tiles_ref, out_ref, copies_ref, slots_ref, acc_ref = refs[N_BLOCKS:]
-    times_s(place_ref, row_ref, col_ref, refs[:N_BLOCKS], tiles_ref, slots_ref, acc_ref)
+    times_s(dev_ref, row_ref, col_ref, refs[:N_BLOCKS], tiles_ref, slots_ref, acc_ref)
     store(acc_ref, out_ref, copies_ref)
 
 
-def side(col, place_ref):
-    hop = ((col >> 1) - place_ref[0]) * place_ref[1]
+def side(col, here):
+    hop = ((col >> 1) - here[0]) * here[1]
     kind = jnp.int32(0)
     for sign, value in ((1, 1), (-1, 2)):
         for h in SHARED:
@@ -197,7 +201,7 @@
     return jnp.where(col >= N_ROW * HALF, 0, kind)
 
 
-def half_kernel(place_ref, row_ref, col_ref, v2_ref, line_ref, low_ref, high_ref, a_ref, b_ref, v0_ref, v1_ref, tiles_ref,
+def half_kernel(dev_ref, row_ref, col_ref, v2_ref, line_ref, low_ref, high_ref, a_ref, b_ref, v0_ref, v1_ref, tiles_ref,
                 part_ref, moments_ref, slots_ref, acc_ref):
     blocks = [line_ref[x] for x in range(N_X)] + [a_ref[0], b_ref[0], None, None, low_ref[...], high_ref[...]]
     for k, block in enumerate(blocks):
@@ -205,8 +209,8 @@
             spread(slots_ref, k, block)
     acc_ref[...] = jnp.zeros_like(acc_ref)
     for t in range(tiles_ref.shape[0]):
-        kind = side(col_ref[t], place_ref)
-        slot = jnp.where(kind == 2, 0, any_slot(col_ref[t], place_ref))
+        kind = side(col_ref[t], place(dev_ref))
+        slot = jnp.where(kind == 2, 0, any_slot(col_ref[t], place(dev_ref)))
         acc_ref[kind * HALF + row_ref[t]] += product(slots_ref, slot, tiles_ref, t)
     doubled = []
     for h in range(HALF):
@@ -222,14 +226,14 @@
     moments_ref[...] = jnp.concatenate(packed, axis=0).T[:4]
 
 
-def rest_kernel(place_ref, row_ref, col_ref, part_ref, swapped_ref, tiles_ref, out_ref, slots_ref, acc_ref):
+def rest_kernel(dev_ref, row_ref, col_ref, part_ref, swapped_ref, tiles_ref, out_ref, slots_ref, acc_ref):
     for k in range(len(SHARED)):
         spread(slots_ref, k, swapped_ref[k])
     acc_ref[...] = part_ref[...]
     for t in range(tiles_ref.shape[0]):
-        @pl.when(side(col_ref[t], place_ref) == 2)
+        @pl.when(side(col_ref[t], place(dev_ref)) == 2)
         def _():
-            slot = any_slot(col_ref[t], place_ref) - (N_X + len(SHARED)) * HALF
+            slot = any_slot(col_ref[t], place(dev_ref)) - (N_X + len(SHARED)) * HALF
             acc_ref[row_ref[t]] += product(slots_ref, slot, tiles_ref, t)
     store(acc_ref, out_ref)
 
@@ -271,9 +275,7 @@
 def local(queries, descriptors, candidates, cluster_perm, tile_vals, tile_row, tile_col):
     row_index = lax.axis_index("row").astype(jnp.int32)
     region = lax.axis_index("region").astype(jnp.int32)
-    core = region & 1
     device = (region * N_ROW + row_index)[None]
-    place = jnp.stack([row_index, 1 - 2 * core])
 
     index = jax.ShapeDtypeStruct(tile_row.shape, jnp.int32)
     packed, tile_row, tile_col = pl.pallas_call(
@@ -311,7 +313,7 @@
         both = pl.pallas_call(
             pair_kernel, out_shape=shape(2, Q, ROWS), in_specs=[SMEM] + [VMEM] * 3, out_specs=VMEM,
             compiler_params=PARAMS, name="pair",
-        )(core[None], v, low, high)
+        )(device, v, low, high)
         got = []
         for hop in SHARED:
             pairs = [(r * N_ROW + i, r * N_ROW + (i - (hop if r % 2 == 0 else -hop)) % N_ROW)
@@ -335,7 +337,7 @@
         scratch_shapes=[pltpu.VMEM((len(HOPS) * HALF, Q, TILE), F32)],
         cost_estimate=pl.CostEstimate(flops=2 * 12 * Q * TILE * TILE, bytes_accessed=2000000, transcendentals=0),
         compiler_params=PARAMS, name="first_inner",
-    )(place, tile_row, tile_col, near.reshape(N_ROW * width, TILE), tile_vals)
+    )(device, tile_row, tile_col, near.reshape(N_ROW * width, TILE), tile_vals)
     with_copies = (shape(Q, ROWS), shape(N_X, Q, ROWS))
     v1, copies = pl.pallas_call(
         outer_kernel, out_shape=with_copies, in_specs=[SMEM] * 2 + [VMEM] * 4, out_specs=(VMEM, VMEM),
@@ -345,13 +347,13 @@
     v2, copies = pl.pallas_call(
         next_kernel, out_shape=with_copies, in_specs=[SMEM] * 3 + [VMEM] * (N_BLOCKS + 1), out_specs=(VMEM, VMEM),
         scratch_shapes=[slots, acc], compiler_params=PARAMS, name="second",
-    )(place, tile_row, tile_col, v1, line, *got, swap(got), low, high, tile_vals)
+    )(device, tile_row, tile_col, v1, line, *got, swap(got), low, high, tile_vals)
     line, low, high, got = fetch(v2, copies)
     part, moments = pl.pallas_call(
         half_kernel, out_shape=(shape(HALF, Q, TILE), shape(4, TILE)), in_specs=[SMEM] * 3 + [VMEM] * 9,
         out_specs=(VMEM, VMEM), scratch_shapes=[slots, pltpu.VMEM((3 * HALF, Q, TILE), F32)],
         compiler_params=PARAMS, name="half",
-    )(place, tile_row, tile_col, v2, line, low, high, *got, v0, v1, tile_vals)
+    )(device, tile_row, tile_col, v2, line, low, high, *got, v0, v1, tile_vals)
     *got, moments = lax.optimization_barrier((*got, moments))
     moments = lax.all_to_all(jnp.broadcast_to(moments[None], (N_ROW, 4, TILE)), "row", 0, 0, tiled=True)
     moments = jnp.sum(moments.reshape(2, 2, 2, 2, 2, 4, TILE).sum(0).sum(0).sum(0).sum(0), axis=0)
@@ -360,7 +362,7 @@
         scratch_shapes=[pltpu.VMEM((2 * HALF, Q, TILE), F32), acc],
         cost_estimate=pl.CostEstimate(flops=2 * 12 * Q * TILE * TILE, bytes_accessed=2000000, transcendentals=0),
         compiler_params=PARAMS, name="rest",
-    )(place, tile_row, tile_col, part, swap(got), tile_vals)
+    )(device, tile_row, tile_col, part, swap(got), tile_vals)
     moments = lax.all_to_all(jnp.broadcast_to(moments[None], (N_REGION, 4, TILE)), "region", 0, 0, tiled=True)
     diffused, residual = pl.pallas_call(
         finish_kernel, out_shape=(shape(Q, ROWS), shape(Q, ROWS)), in_specs=[VMEM] * 5, out_specs=(VMEM, VMEM),

time: 151 us -> 149 us (0.987)
  blocking collectives: 13.3 us -> 28.8 us
  waiting for transfers between devices: 50.8 us -> 38.2 us
  starting transfers between devices: 68.3 us -> 64.8 us
    all_to_all x0 -> x1, blocking collectives: none -> 15.5 us  [local(): lax.all_to_all(near.reshape(N_ROW, width, TILE), 'row', 0, 0, tiled=True)]
    all_to_all x1 -> x0, waiting for transfers between devices: 12.2 us -> none  [local(): lax.all_to_all(near.reshape(N_ROW, width, TILE), 'row', 0, 0, tiled=True)]
    all_to_all x1 -> x0, starting transfers between devices: 4.02 us -> none  [local(): lax.all_to_all(near.reshape(N_ROW, width, TILE), 'row', 0, 0, tiled=True)]
  transfers between devices with their start and end apart: 18 -> 17, of which waited for: 10 -> 9; matrix products, arithmetic and copies ran while one was open for 0% -> 0% of each run, Pallas kernels for 2% -> 2%
where the time goes in v10:
time: 149 us; the launch traced here: 148 us
  starting transfers between devices  64.8 us (43%)
  waiting for transfers between devices  38.2 us (26%)
  blocking collectives  28.8 us (19%)
  Pallas kernels  13.4 us (9%)
  local copies, waits for them, and re-layouts  2.14 us (1%)
    ppermute x4, waiting for transfers between devices, fetch(): got.append(lax.ppermute(both, ('region', 'row'), pairs))  16.7 us
    all_to_all x1, blocking collectives, local(): lax.all_to_all(near.reshape(N_ROW, width, TILE), 'row', 0, 0, tiled=True)  15.5 us
    ppermute x4, starting transfers between devices, fetch(): got.append(lax.ppermute(both, ('region', 'row'), pairs))  13.4 us
    all_to_all x1, blocking collectives, local(): lax.all_to_all(by_query.reshape(N_ROW, QS * HALF, TILE), 'row', 0, 0, til...  13.3 us
    ppermute x3, starting transfers between devices, region_pair(): lax.ppermute(v, 'region', ring(N_REGION, -1))  12.1 us
    all_to_all x1, starting transfers between devices, local(): lax.all_to_all(packed, 'row', 0, 0, tiled=True).reshape(Q, D + TILE)  10.6 us
    all_to_all x1, waiting for transfers between devices, local(): lax.all_to_all(packed, 'row', 0, 0, tiled=True).reshape(Q, D + TILE)  9.34 us
    all_to_all x1, starting transfers between devices, local(): lax.all_to_all(jnp.broadcast_to(moments[None], (N_REGION, 4, TILE)), 'reg...  7.69 us
  transfers between devices with their start and end apart: 17, of which 9 were waited for; matrix products, arithmetic and copies ran while one was open for 0% of the time, Pallas kernels for 2%

profile of v10, /device:TPU:1, one launch (start us, length us, event | category | flops | bytes accessed | tf_op | source)
XLA Modules:
  0.0 148.3 jit_solution(12244974816001021153)
XLA Ops:
  0.6 1.5 %pack.1 = (f32[32,2,640]{2,1,0:T(2,128)}, s32[12]{0:T(128)}, s32[12]{0:T(128)}) custom-call(f32[2,512]{1,0:T(2,128)} %queries_hbm.1, s32[1,256]{1,0:T(1,128)} %perm_hbm.1, s32[12]{0:T(128)} %row_hbm.1, s32[12]{0:T(128)} %col_hbm.1), custom_call_target="tpu_custom_call" | custom-call | tf_op jit(solution)/shard_map/pack/pallas_call | solution.py:281
  2.2 0.0 copy-start.1
  2.2 10.6 %all-to-all-start = ((f32[32,2,640]{2,1,0:T(2,128)}), f32[32,2,640]{2,1,0:T(2,128)S(1)}, u32[]{:S(2)}, u32[]{:S(2)}) async-start(f32[32,2,640]{2,1,0:T(2,128)} %get-tuple-element.22), calls=%async_computation | async-start | bytes 327680 | tf_op jit(solution)/shard_map/all_to_all | solution.py:287
  12.9 0.0 copy-start.2
  12.9 9.3 %all-to-all-done = f32[32,2,640]{2,1,0:T(2,128)S(1)} async-done(((f32[32,2,640]{2,1,0:T(2,128)}), f32[32,2,640]{2,1,0:T(2,128)S(1)}, u32[]{:S(2)}, u32[]{:S(2)}) %all-to-all-start) | async-done | bytes 163872 | tf_op jit(solution)/shard_map/all_to_all | solution.py:287
  22.2 0.1 reshape.28.packed_ref
  22.3 0.6 scores.1
  23.0 13.3 %all_to_all.35 = f32[32,4,128]{2,1,0:T(4,128)S(1)} all-to-all(f32[32,4,128]{2,1,0:T(4,128)S(1)} %bitcast.20), channel_id=1, replica_groups=mesh['region'=16,'row'=32] {'row'}, dimensions={0} | all-to-all | bytes 131072 | tf_op jit(solution)/shard_map/all_to_all | solution.py:292
  36.3 2.2 %permute.1 = f32[1024,128]{1,0:T(8,128)S(1)} custom-call(f32[128,128]{1,0:T(8,128)S(1)} %bitcast.19, f32[64,640]{1,0:T(8,128)S(1)} %reshape.28.packed_ref), custom_call_target="tpu_custom_call" | custom-call | tf_op jit(solution)/shard_map/permute/pallas_call | solution.py:294
  38.5 0.0 copy-start
  38.5 15.5 %all_to_all.36 = f32[32,32,128]{2,1,0:T(8,128)S(1)} all-to-all(f32[32,32,128]{2,1,0:T(8,128)S(1)} %bitcast.14), channel_id=1, replica_groups=mesh['region'=16,'row'=32] {'row'}, dimensions={0} | all-to-all | bytes 1048576 | tf_op jit(solution)/shard_map/all_to_all | solution.py:299
  54.1 0.1 copy.17
  54.2 5.4 %collective-permute-start.1 = (f32[64,256]{1,0:T(8,128)S(1)}, f32[64,256]{1,0:T(8,128)S(1)}, u32[]{:S(2)}, u32[]{:S(2)}) collective-permute-start(f32[64,256]{1,0:T(8,128)S(1)} %bitcast.15), channel_id=1, source_target_pairs={{0,480},{32,0},{64,32},{96,64},{128,96},{160,128},{192,160},{224,1... | collective-permute-start | bytes 196616 | tf_op jit(solution)/shard_map/ppermute | solution.py:303
  59.5 2.0 %collective-permute-start = (f32[64,256]{1,0:T(8,128)S(1)}, f32[64,256]{1,0:T(8,128)S(1)}, u32[]{:S(2)}, u32[]{:S(2)}) collective-permute-start(f32[64,256]{1,0:T(8,128)S(1)} %bitcast.16), channel_id=1, source_target_pairs={{0,32},{32,64},{64,96},{96,128},{128,160},{160,192},{192,224},{224... | collective-permute-start | bytes 196616 | tf_op jit(solution)/shard_map/ppermute | solution.py:303
  61.5 0.6 copy-done.3
  62.2 1.4 first_inner.1.inner_ref
  63.6 0.5 collective-permute-done.low_ref
  64.1 1.7 %first_outer.1 = (f32[64,256]{1,0:T(8,128)S(1)}, f32[4,64,256]{2,1,0:T(8,128)}) custom-call(s32[12]{0:T(128)S(1)} %copy-done.3, s32[12]{0:T(128)S(1)} %copy-done.4, f32[2,64,128]{2,1,0:T(8,128)S(1)} %first_inner.1.inner_ref, f32[64,256]{1,0:T(8,128)S(1)} %collective-permute-done.low_ref, f32[64,256]{1,0:T(8,128)S(1)} %collective-permute-done.1.high_ref, ...), custom_call_target="tpu_custom_call" | custom-call | tf_op jit(solution)/shard_map/first_outer/pallas_call | solution.py:342
  65.8 6.5 %collective-permute-start.3 = (f32[64,256]{1,0:T(8,128)S(1)}, f32[64,256]{1,0:T(8,128)S(1)}, u32[]{:S(2)}, u32[]{:S(2)}) collective-permute-start(f32[64,256]{1,0:T(8,128)S(1)} %get-tuple-element.23.own_ref.refs_0_.v1_ref), channel_id=1, source_target_pairs={{0,480},{32,0},{64,32},{96,64},{128,96},{160,128},{192,160},{224,1... | collective-permute-start | bytes 196616 | tf_op jit(solution)/shard_map/ppermute | solution.py:303
  72.3 0.0 collective-permute-start.2
  72.3 3.4 %all-to-all-start.3 = ((f32[4,64,256]{2,1,0:T(8,128)}), f32[4,64,256]{2,1,0:T(8,128)S(1)}, u32[]{:S(2)}, u32[]{:S(2)}) async-start(f32[4,64,256]{2,1,0:T(8,128)} %get-tuple-element.24), calls=%async_computation.3 | async-start | bytes 524288 | tf_op jit(solution)/shard_map/all_to_all | solution.py:306
  75.8 0.0 collective-permute-done.2.low_ref.refs_5_
  75.8 5.0 %collective-permute-start.5 = (f32[2,64,256]{2,1,0:T(8,128)S(1)}, f32[2,64,256]{2,1,0:T(8,128)S(1)}, u32[]{:S(2)}, u32[]{:S(2)}) collective-permute-start(f32[2,64,256]{2,1,0:T(8,128)S(1)} %pair.2), channel_id=1, source_target_pairs={{0,29},{1,30},{2,31},{3,0},{4,1},{5,2},{6,3},{7,4},{8,5},{9,6},{10... | collective-permute-start | bytes 393224 | tf_op jit(solution)/shard_map/ppermute | solution.py:321
  80.8 2.0 %collective-permute-start.4 = (f32[2,64,256]{2,1,0:T(8,128)S(1)}, f32[2,64,256]{2,1,0:T(8,128)S(1)}, u32[]{:S(2)}, u32[]{:S(2)}) collective-permute-start(f32[2,64,256]{2,1,0:T(8,128)S(1)} %pair.2), channel_id=1, source_target_pairs={{0,31},{1,0},{2,1},{3,2},{4,3},{5,4},{6,5},{7,6},{8,7},{9,8},{10,9... | collective-permute-start | bytes 393224 | tf_op jit(solution)/shard_map/ppermute | solution.py:321
  82.7 0.0 all-to-all-done.3.refs_1_
  82.8 5.4 %collective-permute-done.5.refs_1_.refs_3_ = f32[2,64,256]{2,1,0:T(8,128)S(1)} collective-permute-done((f32[2,64,256]{2,1,0:T(8,128)S(1)}, f32[2,64,256]{2,1,0:T(8,128)S(1)}, u32[]{:S(2)}, u32[]{:S(2)}) %collective-permute-start.5) | collective-permute-done | bytes 131104 | tf_op jit(solution)/shard_map/ppermute | solution.py:321
  88.2 2.8 %collective-permute-done.4.refs_0_.refs_2_ = f32[2,64,256]{2,1,0:T(8,128)S(1)} collective-permute-done((f32[2,64,256]{2,1,0:T(8,128)S(1)}, f32[2,64,256]{2,1,0:T(8,128)S(1)}, u32[]{:S(2)}, u32[]{:S(2)}) %collective-permute-start.4) | collective-permute-done | bytes 131104 | tf_op jit(solution)/shard_map/ppermute | solution.py:321
  91.0 1.9 %collective-permute-start.6 = (f32[2,64,256]{2,1,0:T(8,128)S(1)}, f32[2,64,256]{2,1,0:T(8,128)S(1)}, u32[]{:S(2)}, u32[]{:S(2)}) collective-permute-start(f32[2,64,256]{2,1,0:T(8,128)S(1)} %swap.2), channel_id=1, source_target_pairs={{0,32},{32,0},{64,96},{96,64},{128,160},{160,128},{192,224},{224,1... | collective-permute-start | bytes 393224 | tf_op jit(solution)/shard_map/ppermute | solution.py:330
  92.9 1.3 collective-permute-done.6.refs_4_
  94.2 1.9 %second.1 = (f32[64,256]{1,0:T(8,128)S(1)}, f32[4,64,256]{2,1,0:T(8,128)}) custom-call(s32[1]{0:T(128)} %bitcast.dev_ref, s32[12]{0:T(128)S(1)} %copy-done.3, s32[12]{0:T(128)S(1)} %copy-done.4, f32[64,256]{1,0:T(8,128)S(1)} %get-tuple-element.23.own_ref.refs_0_.v1_ref, f32[4,64,256]{2,1,0:T(8,128)S(1)} %all-to-all-done.3.refs_1_, ...), custom_call_target="tpu_custom_call" | custom-call | tf_op jit(solution)/shard_map/second/pallas_call | solution.py:347
  96.1 0.1 collective-permute-start.8
  96.3 1.6 %collective-permute-start.7 = (f32[64,256]{1,0:T(8,128)S(1)}, f32[64,256]{1,0:T(8,128)S(1)}, u32[]{:S(2)}, u32[]{:S(2)}) collective-permute-start(f32[64,256]{1,0:T(8,128)S(1)} %get-tuple-element.28.own_ref.v2_ref), channel_id=1, source_target_pairs={{0,32},{32,64},{64,96},{96,128},{128,160},{160,192},{192,224},{224... | collective-permute-start | bytes 196616 | tf_op jit(solution)/shard_map/ppermute | solution.py:303
  97.9 3.4 %all-to-all-start.4 = ((f32[4,64,256]{2,1,0:T(8,128)}), f32[4,64,256]{2,1,0:T(8,128)S(1)}, u32[]{:S(2)}, u32[]{:S(2)}) async-start(f32[4,64,256]{2,1,0:T(8,128)} %get-tuple-element.29), calls=%async_computation.4 | async-start | bytes 524288 | tf_op jit(solution)/shard_map/all_to_all | solution.py:306
  101.3 0.0 collective-permute-done.7.low_ref
  101.3 4.5 %collective-permute-start.10 = (f32[2,64,256]{2,1,0:T(8,128)S(1)}, f32[2,64,256]{2,1,0:T(8,128)S(1)}, u32[]{:S(2)}, u32[]{:S(2)}) collective-permute-start(f32[2,64,256]{2,1,0:T(8,128)S(1)} %pair.3), channel_id=1, source_target_pairs={{0,29},{1,30},{2,31},{3,0},{4,1},{5,2},{6,3},{7,4},{8,5},{9,6},{10... | collective-permute-start | bytes 393224 | tf_op jit(solution)/shard_map/ppermute | solution.py:321
  105.9 1.9 %collective-permute-start.9 = (f32[2,64,256]{2,1,0:T(8,128)S(1)}, f32[2,64,256]{2,1,0:T(8,128)S(1)}, u32[]{:S(2)}, u32[]{:S(2)}) collective-permute-start(f32[2,64,256]{2,1,0:T(8,128)S(1)} %pair.3), channel_id=1, source_target_pairs={{0,31},{1,0},{2,1},{3,2},{4,3},{5,4},{6,5},{7,6},{8,7},{9,8},{10,9... | collective-permute-start | bytes 393224 | tf_op jit(solution)/shard_map/ppermute | solution.py:321
  107.8 4.8 %collective-permute-done.10.b_ref.refs_1_ = f32[2,64,256]{2,1,0:T(8,128)S(1)} collective-permute-done((f32[2,64,256]{2,1,0:T(8,128)S(1)}, f32[2,64,256]{2,1,0:T(8,128)S(1)}, u32[]{:S(2)}, u32[]{:S(2)}) %collective-permute-start.10) | collective-permute-done | bytes 131104 | tf_op jit(solution)/shard_map/ppermute | solution.py:321
  112.6 3.8 %collective-permute-done.9.a_ref.refs_0_ = f32[2,64,256]{2,1,0:T(8,128)S(1)} collective-permute-done((f32[2,64,256]{2,1,0:T(8,128)S(1)}, f32[2,64,256]{2,1,0:T(8,128)S(1)}, u32[]{:S(2)}, u32[]{:S(2)}) %collective-permute-start.9) | collective-permute-done | bytes 131104 | tf_op jit(solution)/shard_map/ppermute | solution.py:321
  116.4 1.3 half.1
  117.6 0.6 broadcast_in_dim.7
  118.3 3.9 %all-to-all-start.5 = ((f32[32,4,128]{2,1,0:T(4,128)}), f32[32,4,128]{2,1,0:T(4,128)S(1)}, u32[]{:S(2)}, u32[]{:S(2)}) async-start(f32[32,4,128]{2,1,0:T(4,128)} %broadcast_in_dim.7), calls=%async_computation.5 | async-start | bytes 131072 | tf_op jit(solution)/shard_map/all_to_all | solution.py:358
  122.2 4.9 %collective-permute-start.11 = (f32[2,64,256]{2,1,0:T(8,128)S(1)}, f32[2,64,256]{2,1,0:T(8,128)S(1)}, u32[]{:S(2)}, u32[]{:S(2)}) collective-permute-start(f32[2,64,256]{2,1,0:T(8,128)S(1)} %swap.3), channel_id=1, source_target_pairs={{0,32},{32,0},{64,96},{96,64},{128,160},{160,128},{192,224},{224,1... | collective-permute-start | bytes 393224 | tf_op jit(solution)/shard_map/ppermute | solution.py:330
  127.0 4.0 %all-to-all-done.5 = f32[32,4,128]{2,1,0:T(4,128)S(1)} async-done(((f32[32,4,128]{2,1,0:T(4,128)}), f32[32,4,128]{2,1,0:T(4,128)S(1)}, u32[]{:S(2)}, u32[]{:S(2)}) %all-to-all-start.5) | async-done | bytes 65568 | tf_op jit(solution)/shard_map/all_to_all | solution.py:358
  131.1 0.6 broadcast_in_dim.8
  131.7 7.7 %all-to-all-start.6 = ((f32[16,4,128]{2,1,0:T(4,128)}), f32[16,4,128]{2,1,0:T(4,128)S(1)}, u32[]{:S(2)}, u32[]{:S(2)}) async-start(f32[16,4,128]{2,1,0:T(4,128)} %broadcast_in_dim.8), calls=%async_computation.6 | async-start | bytes 65536 | tf_op jit(solution)/shard_map/all_to_all | solution.py:366
  139.4 1.1 rest.1.v3_ref
  140.5 6.3 %all-to-all-done.6.moments_ref = f32[16,4,128]{2,1,0:T(4,128)S(1)} async-done(((f32[16,4,128]{2,1,0:T(4,128)}), f32[16,4,128]{2,1,0:T(4,128)S(1)}, u32[]{:S(2)}, u32[]{:S(2)}) %all-to-all-start.6) | async-done | bytes 32800 | tf_op jit(solution)/shard_map/all_to_all | solution.py:366
  146.8 1.5 %finish.1 = (f32[64,256]{1,0:T(8,128)}, f32[64,256]{1,0:T(8,128)}) custom-call(f32[16,4,128]{2,1,0:T(4,128)S(1)} %all-to-all-done.6.moments_ref, f32[64,256]{1,0:T(8,128)S(1)} %bitcast.18, f32[64,256]{1,0:T(8,128)S(1)} %get-tuple-element.23.own_ref.refs_0_.v1_ref, f32[64,256]{1,0:T(8,128)S(1)} %get-tuple-element.28.own_ref.v2_ref, f32[64,256]{1,0:T(8,128)S(1)} %rest.1.v3_ref), custom_call_target="tpu_custom_call" | custom-call | tf_op jit(solution)/shard_map/finish/pallas_call | solution.py:367
  (19 shorter events, 0.2 us)
Async XLA Ops:
  2.2 20.1 %copy-start.1 = (f32[256,512]{1,0:T(8,128)S(1)}, f32[256,512]{1,0:T(8,128)}, u32[]{:S(2)}) copy-start(f32[256,512]{1,0:T(8,128)} %desc_ref.1) | copy-start | bytes 1572868
  2.2 20.0 %all-to-all-start = ((f32[32,2,640]{2,1,0:T(2,128)}), f32[32,2,640]{2,1,0:T(2,128)S(1)}, u32[]{:S(2)}, u32[]{:S(2)}) async-start(f32[32,2,640]{2,1,0:T(2,128)} %get-tuple-element.22), calls=%async_computation | async-start | bytes 327680 | tf_op jit(solution)/shard_map/all_to_all | solution.py:287
  12.9 9.5 %copy-start.2 = (s32[64,64]{1,0:T(8,128)S(1)}, s32[64,64]{1,0:T(8,128)}, u32[]{:S(2)}) copy-start(s32[64,64]{1,0:T(8,128)} %cand_ref.1) | copy-start | bytes 49156
  38.5 23.0 %copy-start = (f32[12,128,128]{2,1,0:T(8,128)S(1)}, f32[12,128,128]{2,1,0:T(8,128)}, u32[]{:S(2)}) copy-start(f32[12,128,128]{2,1,0:T(8,128)} %tiles_ref.7) | copy-start | bytes 2359300
  54.2 9.5 %collective-permute-start.1 = (f32[64,256]{1,0:T(8,128)S(1)}, f32[64,256]{1,0:T(8,128)S(1)}, u32[]{:S(2)}, u32[]{:S(2)}) collective-permute-start(f32[64,256]{1,0:T(8,128)S(1)} %bitcast.15), channel_id=1, source_target_pairs={{0,480},{32,0},{64,32},{96,64},{128,96},{160,128},{192,160},{224,1... | collective-permute-start | bytes 196616 | tf_op jit(solution)/shard_map/ppermute | solution.py:303
  59.5 4.6 %collective-permute-start = (f32[64,256]{1,0:T(8,128)S(1)}, f32[64,256]{1,0:T(8,128)S(1)}, u32[]{:S(2)}, u32[]{:S(2)}) collective-permute-start(f32[64,256]{1,0:T(8,128)S(1)} %bitcast.16), channel_id=1, source_target_pairs={{0,32},{32,64},{64,96},{96,128},{128,160},{160,192},{192,224},{224... | collective-permute-start | bytes 196616 | tf_op jit(solution)/shard_map/ppermute | solution.py:303
  61.5 0.7 copy-start.3
  61.5 0.7 copy-start.4
  65.8 10.0 %collective-permute-start.3 = (f32[64,256]{1,0:T(8,128)S(1)}, f32[64,256]{1,0:T(8,128)S(1)}, u32[]{:S(2)}, u32[]{:S(2)}) collective-permute-start(f32[64,256]{1,0:T(8,128)S(1)} %get-tuple-element.23.own_ref.refs_0_.v1_ref), channel_id=1, source_target_pairs={{0,480},{32,0},{64,32},{96,64},{128,96},{160,128},{192,160},{224,1... | collective-permute-start | bytes 196616 | tf_op jit(solution)/shard_map/ppermute | solution.py:303
  72.3 3.4 %collective-permute-start.2 = (f32[64,256]{1,0:T(8,128)S(1)}, f32[64,256]{1,0:T(8,128)S(1)}, u32[]{:S(2)}, u32[]{:S(2)}) collective-permute-start(f32[64,256]{1,0:T(8,128)S(1)} %get-tuple-element.23.own_ref.refs_0_.v1_ref), channel_id=1, source_target_pairs={{0,32},{32,64},{64,96},{96,128},{128,160},{160,192},{192,224},{224... | collective-permute-start | bytes 196616 | tf_op jit(solution)/shard_map/ppermute | solution.py:303
  72.3 10.4 %all-to-all-start.3 = ((f32[4,64,256]{2,1,0:T(8,128)}), f32[4,64,256]{2,1,0:T(8,128)S(1)}, u32[]{:S(2)}, u32[]{:S(2)}) async-start(f32[4,64,256]{2,1,0:T(8,128)} %get-tuple-element.24), calls=%async_computation.3 | async-start | bytes 524288 | tf_op jit(solution)/shard_map/all_to_all | solution.py:306
  75.8 12.4 %collective-permute-start.5 = (f32[2,64,256]{2,1,0:T(8,128)S(1)}, f32[2,64,256]{2,1,0:T(8,128)S(1)}, u32[]{:S(2)}, u32[]{:S(2)}) collective-permute-start(f32[2,64,256]{2,1,0:T(8,128)S(1)} %pair.2), channel_id=1, source_target_pairs={{0,29},{1,30},{2,31},{3,0},{4,1},{5,2},{6,3},{7,4},{8,5},{9,6},{10... | collective-permute-start | bytes 393224 | tf_op jit(solution)/shard_map/ppermute | solution.py:321
  80.8 10.2 %collective-permute-start.4 = (f32[2,64,256]{2,1,0:T(8,128)S(1)}, f32[2,64,256]{2,1,0:T(8,128)S(1)}, u32[]{:S(2)}, u32[]{:S(2)}) collective-permute-start(f32[2,64,256]{2,1,0:T(8,128)S(1)} %pair.2), channel_id=1, source_target_pairs={{0,31},{1,0},{2,1},{3,2},{4,3},{5,4},{6,5},{7,6},{8,7},{9,8},{10,9... | collective-permute-start | bytes 393224 | tf_op jit(solution)/shard_map/ppermute | solution.py:321
  91.0 3.2 %collective-permute-start.6 = (f32[2,64,256]{2,1,0:T(8,128)S(1)}, f32[2,64,256]{2,1,0:T(8,128)S(1)}, u32[]{:S(2)}, u32[]{:S(2)}) collective-permute-start(f32[2,64,256]{2,1,0:T(8,128)S(1)} %swap.2), channel_id=1, source_target_pairs={{0,32},{32,0},{64,96},{96,64},{128,160},{160,128},{192,224},{224,1... | collective-permute-start | bytes 393224 | tf_op jit(solution)/shard_map/ppermute | solution.py:330
  96.1 5.2 %collective-permute-start.8 = (f32[64,256]{1,0:T(8,128)S(1)}, f32[64,256]{1,0:T(8,128)S(1)}, u32[]{:S(2)}, u32[]{:S(2)}) collective-permute-start(f32[64,256]{1,0:T(8,128)S(1)} %get-tuple-element.28.own_ref.v2_ref), channel_id=1, source_target_pairs={{0,480},{32,0},{64,32},{96,64},{128,96},{160,128},{192,160},{224,1... | collective-permute-start | bytes 196616 | tf_op jit(solution)/shard_map/ppermute | solution.py:303
  96.3 5.0 %collective-permute-start.7 = (f32[64,256]{1,0:T(8,128)S(1)}, f32[64,256]{1,0:T(8,128)S(1)}, u32[]{:S(2)}, u32[]{:S(2)}) collective-permute-start(f32[64,256]{1,0:T(8,128)S(1)} %get-tuple-element.28.own_ref.v2_ref), channel_id=1, source_target_pairs={{0,32},{32,64},{64,96},{96,128},{128,160},{160,192},{192,224},{224... | collective-permute-start | bytes 196616 | tf_op jit(solution)/shard_map/ppermute | solution.py:303
  97.9 9.9 %all-to-all-start.4 = ((f32[4,64,256]{2,1,0:T(8,128)}), f32[4,64,256]{2,1,0:T(8,128)S(1)}, u32[]{:S(2)}, u32[]{:S(2)}) async-start(f32[4,64,256]{2,1,0:T(8,128)} %get-tuple-element.29), calls=%async_computation.4 | async-start | bytes 524288 | tf_op jit(solution)/shard_map/all_to_all | solution.py:306
  101.3 11.2 %collective-permute-start.10 = (f32[2,64,256]{2,1,0:T(8,128)S(1)}, f32[2,64,256]{2,1,0:T(8,128)S(1)}, u32[]{:S(2)}, u32[]{:S(2)}) collective-permute-start(f32[2,64,256]{2,1,0:T(8,128)S(1)} %pair.3), channel_id=1, source_target_pairs={{0,29},{1,30},{2,31},{3,0},{4,1},{5,2},{6,3},{7,4},{8,5},{9,6},{10... | collective-permute-start | bytes 393224 | tf_op jit(solution)/shard_map/ppermute | solution.py:321
  105.9 10.5 %collective-permute-start.9 = (f32[2,64,256]{2,1,0:T(8,128)S(1)}, f32[2,64,256]{2,1,0:T(8,128)S(1)}, u32[]{:S(2)}, u32[]{:S(2)}) collective-permute-start(f32[2,64,256]{2,1,0:T(8,128)S(1)} %pair.3), channel_id=1, source_target_pairs={{0,31},{1,0},{2,1},{3,2},{4,3},{5,4},{6,5},{7,6},{8,7},{9,8},{10,9... | collective-permute-start | bytes 393224 | tf_op jit(solution)/shard_map/ppermute | solution.py:321
  118.3 12.7 %all-to-all-start.5 = ((f32[32,4,128]{2,1,0:T(4,128)}), f32[32,4,128]{2,1,0:T(4,128)S(1)}, u32[]{:S(2)}, u32[]{:S(2)}) async-start(f32[32,4,128]{2,1,0:T(4,128)} %broadcast_in_dim.7), calls=%async_computation.5 | async-start | bytes 131072 | tf_op jit(solution)/shard_map/all_to_all | solution.py:358
  122.2 17.2 %collective-permute-start.11 = (f32[2,64,256]{2,1,0:T(8,128)S(1)}, f32[2,64,256]{2,1,0:T(8,128)S(1)}, u32[]{:S(2)}, u32[]{:S(2)}) collective-permute-start(f32[2,64,256]{2,1,0:T(8,128)S(1)} %swap.3), channel_id=1, source_target_pairs={{0,32},{32,0},{64,96},{96,64},{128,160},{160,128},{192,224},{224,1... | collective-permute-start | bytes 393224 | tf_op jit(solution)/shard_map/ppermute | solution.py:330
  131.7 15.1 %all-to-all-start.6 = ((f32[16,4,128]{2,1,0:T(4,128)}), f32[16,4,128]{2,1,0:T(4,128)S(1)}, u32[]{:S(2)}, u32[]{:S(2)}) async-start(f32[16,4,128]{2,1,0:T(4,128)} %broadcast_in_dim.8), calls=%async_computation.6 | async-start | bytes 65536 | tf_op jit(solution)/shard_map/all_to_all | solution.py:366

commit v11 on v10

--- a/solution.py
+++ b/solution.py
@@ -203,14 +203,14 @@
 
 def half_kernel(dev_ref, row_ref, col_ref, v2_ref, line_ref, low_ref, high_ref, a_ref, b_ref, v0_ref, v1_ref, tiles_ref,
                 part_ref, moments_ref, slots_ref, acc_ref):
-    blocks = [line_ref[x] for x in range(N_X)] + [a_ref[0], b_ref[0], None, None, low_ref[...], high_ref[...]]
+    blocks = [line_ref[x] for x in range(N_X)] + [a_ref[...], b_ref[...], None, None, low_ref[...], high_ref[...]]
     for k, block in enumerate(blocks):
         if block is not None:
             spread(slots_ref, k, block)
     acc_ref[...] = jnp.zeros_like(acc_ref)
     for t in range(tiles_ref.shape[0]):
-        kind = side(col_ref[t], place(dev_ref))
-        slot = jnp.where(kind == 2, 0, any_slot(col_ref[t], place(dev_ref)))
+        kind = side(col_ref[t], (place(dev_ref)[0], 1))
+        slot = jnp.where(kind == 2, 0, any_slot(col_ref[t], (place(dev_ref)[0], 1)))
         acc_ref[kind * HALF + row_ref[t]] += product(slots_ref, slot, tiles_ref, t)
     doubled = []
     for h in range(HALF):
@@ -226,14 +226,14 @@
     moments_ref[...] = jnp.concatenate(packed, axis=0).T[:4]
 
 
-def rest_kernel(dev_ref, row_ref, col_ref, part_ref, swapped_ref, tiles_ref, out_ref, slots_ref, acc_ref):
-    for k in range(len(SHARED)):
-        spread(slots_ref, k, swapped_ref[k])
+def rest_kernel(dev_ref, row_ref, col_ref, part_ref, a_ref, b_ref, tiles_ref, out_ref, slots_ref, acc_ref):
+    spread(slots_ref, 0, a_ref[...])
+    spread(slots_ref, 1, b_ref[...])
     acc_ref[...] = part_ref[...]
     for t in range(tiles_ref.shape[0]):
-        @pl.when(side(col_ref[t], place(dev_ref)) == 2)
+        @pl.when(side(col_ref[t], (place(dev_ref)[0], 1)) == 2)
         def _():
-            slot = any_slot(col_ref[t], place(dev_ref)) - (N_X + len(SHARED)) * HALF
+            slot = any_slot(col_ref[t], (place(dev_ref)[0], 1)) - (N_X + len(SHARED)) * HALF
             acc_ref[row_ref[t]] += product(slots_ref, slot, tiles_ref, t)
     store(acc_ref, out_ref)
 
@@ -348,21 +348,23 @@
         next_kernel, out_shape=with_copies, in_specs=[SMEM] * 3 + [VMEM] * (N_BLOCKS + 1), out_specs=(VMEM, VMEM),
         scratch_shapes=[slots, acc], compiler_params=PARAMS, name="second",
     )(device, tile_row, tile_col, v1, line, *got, swap(got), low, high, tile_vals)
-    line, low, high, got = fetch(v2, copies)
+    low, high = region_pair(v2)
+    ahead = [lax.ppermute(v2, "row", ring(N_ROW, -hop)) for hop in SHARED]
     part, moments = pl.pallas_call(
         half_kernel, out_shape=(shape(HALF, Q, TILE), shape(4, TILE)), in_specs=[SMEM] * 3 + [VMEM] * 9,
         out_specs=(VMEM, VMEM), scratch_shapes=[slots, pltpu.VMEM((3 * HALF, Q, TILE), F32)],
         compiler_params=PARAMS, name="half",
-    )(device, tile_row, tile_col, v2, line, low, high, *got, v0, v1, tile_vals)
-    *got, moments = lax.optimization_barrier((*got, moments))
+    )(device, tile_row, tile_col, v2, x_line(copies), low, high, *ahead, v0, v1, tile_vals)
+    later, moments = lax.optimization_barrier((v2, moments))
+    behind = [lax.ppermute(later, "row", ring(N_ROW, hop)) for hop in SHARED]
     moments = lax.all_to_all(jnp.broadcast_to(moments[None], (N_ROW, 4, TILE)), "row", 0, 0, tiled=True)
     moments = jnp.sum(moments.reshape(2, 2, 2, 2, 2, 4, TILE).sum(0).sum(0).sum(0).sum(0), axis=0)
     v3 = pl.pallas_call(
-        rest_kernel, out_shape=shape(Q, ROWS), in_specs=[SMEM] * 3 + [VMEM] * 3, out_specs=VMEM,
+        rest_kernel, out_shape=shape(Q, ROWS), in_specs=[SMEM] * 3 + [VMEM] * 4, out_specs=VMEM,
         scratch_shapes=[pltpu.VMEM((2 * HALF, Q, TILE), F32), acc],
         cost_estimate=pl.CostEstimate(flops=2 * 12 * Q * TILE * TILE, bytes_accessed=2000000, transcendentals=0),
         compiler_params=PARAMS, name="rest",
-    )(device, tile_row, tile_col, part, swap(got), tile_vals)
+    )(device, tile_row, tile_col, part, *behind, tile_vals)
     moments = lax.all_to_all(jnp.broadcast_to(moments[None], (N_REGION, 4, TILE)), "region", 0, 0, tiled=True)
     diffused, residual = pl.pallas_call(
         finish_kernel, out_shape=(shape(Q, ROWS), shape(Q, ROWS)), in_specs=[VMEM] * 5, out_specs=(VMEM, VMEM),

time: 149 us -> 148 us (level)
  waiting for transfers between devices: 38.2 us -> 28.2 us
  starting transfers between devices: 64.8 us -> 73.9 us
    ppermute x0 -> x4, starting transfers between devices: none -> 17.6 us  [the longest x2 9.24 us: local(): behind = [lax.ppermute(later, 'row', ring(N_ROW, hop)) for hop in SHARED]]
    ppermute x4 -> x2, waiting for transfers between devices: 16.7 us -> 8.18 us  [fetch(): got.append(lax.ppermute(both, ('region', 'row'), pairs))]
    ppermute x4 -> x2, starting transfers between devices: 13.4 us -> 6.93 us  [fetch(): got.append(lax.ppermute(both, ('region', 'row'), pairs))]
    ppermute x2 -> x1, starting transfers between devices: 6.78 us -> 1.92 us  [swap(): lax.ppermute(swapped, 'region', [(r, r ^ 1) for r in range(N_REGION)])]
    all_to_all x1, waiting for transfers between devices: 3.98 us -> 0.01 us  [local(): lax.all_to_all(jnp.broadcast_to(moments[None], (N_ROW, 4, TILE)), 'row',...]
    all_to_all x1, starting transfers between devices: 3.86 us -> 6.51 us  [local(): lax.all_to_all(jnp.broadcast_to(moments[None], (N_ROW, 4, TILE)), 'row',...]
    ppermute x0 -> x4, waiting for transfers between devices: none -> 2.59 us  [the longest x2 2.59 us: local(): ahead = [lax.ppermute(v2, 'row', ring(N_ROW, -hop)) for hop in SHARED]]
  transfers between devices with their start and end apart: 17 -> 18, of which waited for: 9 -> 7; matrix products, arithmetic and copies ran while one was open for 0% -> 0% of each run, Pallas kernels for 2% -> 2%
where the time goes in v11:
time: 148 us; the launch traced here: 147 us
  starting transfers between devices  73.9 us (50%)
  blocking collectives  28.8 us (19%)
  waiting for transfers between devices  28.2 us (19%)
  Pallas kernels  13.3 us (9%)
  local copies, waits for them, and re-layouts  2.14 us (1%)
    all_to_all x1, blocking collectives, local(): lax.all_to_all(near.reshape(N_ROW, width, TILE), 'row', 0, 0, tiled=True)  15.5 us
    ppermute x3, starting transfers between devices, region_pair(): lax.ppermute(v, 'region', ring(N_REGION, -1))  13.3 us
    all_to_all x1, blocking collectives, local(): lax.all_to_all(by_query.reshape(N_ROW, QS * HALF, TILE), 'row', 0, 0, til...  13.3 us
    all_to_all x1, starting transfers between devices, local(): lax.all_to_all(packed, 'row', 0, 0, tiled=True).reshape(Q, D + TILE)  10.6 us
    all_to_all x1, waiting for transfers between devices, local(): lax.all_to_all(packed, 'row', 0, 0, tiled=True).reshape(Q, D + TILE)  9.34 us
    ppermute x2, starting transfers between devices, local(): behind = [lax.ppermute(later, 'row', ring(N_ROW, hop)) for hop in SHARED]  9.24 us
    ppermute x2, starting transfers between devices, local(): ahead = [lax.ppermute(v2, 'row', ring(N_ROW, -hop)) for hop in SHARED]  8.32 us
    ppermute x2, waiting for transfers between devices, fetch(): got.append(lax.ppermute(both, ('region', 'row'), pairs))  8.18 us
  transfers between devices with their start and end apart: 18, of which 7 were waited for; matrix products, arithmetic and copies ran while one was open for 0% of the time, Pallas kernels for 2%

profile of v11, /device:TPU:1, one launch (start us, length us, event | category | flops | bytes accessed | tf_op | source)
XLA Modules:
  0.0 147.4 jit_solution(15090936612405479192)
XLA Ops:
  0.6 1.5 %pack.1 = (f32[32,2,640]{2,1,0:T(2,128)}, s32[12]{0:T(128)}, s32[12]{0:T(128)}) custom-call(f32[2,512]{1,0:T(2,128)} %queries_hbm.1, s32[1,256]{1,0:T(1,128)} %perm_hbm.1, s32[12]{0:T(128)} %row_hbm.1, s32[12]{0:T(128)} %col_hbm.1), custom_call_target="tpu_custom_call" | custom-call | tf_op jit(solution)/shard_map/pack/pallas_call | solution.py:281
  2.2 0.0 copy-start.1
  2.2 10.6 %all-to-all-start = ((f32[32,2,640]{2,1,0:T(2,128)}), f32[32,2,640]{2,1,0:T(2,128)S(1)}, u32[]{:S(2)}, u32[]{:S(2)}) async-start(f32[32,2,640]{2,1,0:T(2,128)} %get-tuple-element.18), calls=%async_computation | async-start | bytes 327680 | tf_op jit(solution)/shard_map/all_to_all | solution.py:287
  12.8 0.0 copy-start.2
  12.9 9.3 %all-to-all-done = f32[32,2,640]{2,1,0:T(2,128)S(1)} async-done(((f32[32,2,640]{2,1,0:T(2,128)}), f32[32,2,640]{2,1,0:T(2,128)S(1)}, u32[]{:S(2)}, u32[]{:S(2)}) %all-to-all-start) | async-done | bytes 163872 | tf_op jit(solution)/shard_map/all_to_all | solution.py:287
  22.2 0.1 reshape.28.packed_ref
  22.3 0.6 scores.1
  23.0 13.3 %all_to_all.35 = f32[32,4,128]{2,1,0:T(4,128)S(1)} all-to-all(f32[32,4,128]{2,1,0:T(4,128)S(1)} %bitcast.20), channel_id=1, replica_groups=mesh['region'=16,'row'=32] {'row'}, dimensions={0} | all-to-all | bytes 131072 | tf_op jit(solution)/shard_map/all_to_all | solution.py:292
  36.3 2.2 %permute.1 = f32[1024,128]{1,0:T(8,128)S(1)} custom-call(f32[128,128]{1,0:T(8,128)S(1)} %bitcast.19, f32[64,640]{1,0:T(8,128)S(1)} %reshape.28.packed_ref), custom_call_target="tpu_custom_call" | custom-call | tf_op jit(solution)/shard_map/permute/pallas_call | solution.py:294
  38.5 0.0 copy-start
  38.5 15.5 %all_to_all.36 = f32[32,32,128]{2,1,0:T(8,128)S(1)} all-to-all(f32[32,32,128]{2,1,0:T(8,128)S(1)} %bitcast.14), channel_id=1, replica_groups=mesh['region'=16,'row'=32] {'row'}, dimensions={0} | all-to-all | bytes 1048576 | tf_op jit(solution)/shard_map/all_to_all | solution.py:299
  54.1 0.1 copy.17
  54.2 5.4 %collective-permute-start.1 = (f32[64,256]{1,0:T(8,128)S(1)}, f32[64,256]{1,0:T(8,128)S(1)}, u32[]{:S(2)}, u32[]{:S(2)}) collective-permute-start(f32[64,256]{1,0:T(8,128)S(1)} %bitcast.15), channel_id=1, source_target_pairs={{0,480},{32,0},{64,32},{96,64},{128,96},{160,128},{192,160},{224,1... | collective-permute-start | bytes 196616 | tf_op jit(solution)/shard_map/ppermute | solution.py:303
  59.5 2.0 %collective-permute-start = (f32[64,256]{1,0:T(8,128)S(1)}, f32[64,256]{1,0:T(8,128)S(1)}, u32[]{:S(2)}, u32[]{:S(2)}) collective-permute-start(f32[64,256]{1,0:T(8,128)S(1)} %bitcast.16), channel_id=1, source_target_pairs={{0,32},{32,64},{64,96},{96,128},{128,160},{160,192},{192,224},{224... | collective-permute-start | bytes 196616 | tf_op jit(solution)/shard_map/ppermute | solution.py:303
  61.5 0.6 copy-done.3
  62.2 1.4 first_inner.1.inner_ref
  63.6 0.0 collective-permute-done.1.high_ref
  63.6 0.5 collective-permute-done.low_ref
  64.1 1.7 %first_outer.1 = (f32[64,256]{1,0:T(8,128)S(1)}, f32[4,64,256]{2,1,0:T(8,128)}) custom-call(s32[12]{0:T(128)S(1)} %copy-done.3, s32[12]{0:T(128)S(1)} %copy-done.4, f32[2,64,128]{2,1,0:T(8,128)S(1)} %first_inner.1.inner_ref, f32[64,256]{1,0:T(8,128)S(1)} %collective-permute-done.low_ref, f32[64,256]{1,0:T(8,128)S(1)} %collective-permute-done.1.high_ref, ...), custom_call_target="tpu_custom_call" | custom-call | tf_op jit(solution)/shard_map/first_outer/pallas_call | solution.py:342
  65.8 6.5 %collective-permute-start.3 = (f32[64,256]{1,0:T(8,128)S(1)}, f32[64,256]{1,0:T(8,128)S(1)}, u32[]{:S(2)}, u32[]{:S(2)}) collective-permute-start(f32[64,256]{1,0:T(8,128)S(1)} %get-tuple-element.19.own_ref.refs_0_.v1_ref), channel_id=1, source_target_pairs={{0,480},{32,0},{64,32},{96,64},{128,96},{160,128},{192,160},{224,1... | collective-permute-start | bytes 196616 | tf_op jit(solution)/shard_map/ppermute | solution.py:303
  72.3 0.0 collective-permute-start.2
  72.3 3.4 %all-to-all-start.3 = ((f32[4,64,256]{2,1,0:T(8,128)}), f32[4,64,256]{2,1,0:T(8,128)S(1)}, u32[]{:S(2)}, u32[]{:S(2)}) async-start(f32[4,64,256]{2,1,0:T(8,128)} %get-tuple-element.20), calls=%async_computation.3 | async-start | bytes 524288 | tf_op jit(solution)/shard_map/all_to_all | solution.py:306
  75.7 0.0 collective-permute-done.2.low_ref.refs_5_
  75.8 5.0 %collective-permute-start.5 = (f32[2,64,256]{2,1,0:T(8,128)S(1)}, f32[2,64,256]{2,1,0:T(8,128)S(1)}, u32[]{:S(2)}, u32[]{:S(2)}) collective-permute-start(f32[2,64,256]{2,1,0:T(8,128)S(1)} %pair.1), channel_id=1, source_target_pairs={{0,29},{1,30},{2,31},{3,0},{4,1},{5,2},{6,3},{7,4},{8,5},{9,6},{10... | collective-permute-start | bytes 393224 | tf_op jit(solution)/shard_map/ppermute | solution.py:321
  80.7 2.0 %collective-permute-start.4 = (f32[2,64,256]{2,1,0:T(8,128)S(1)}, f32[2,64,256]{2,1,0:T(8,128)S(1)}, u32[]{:S(2)}, u32[]{:S(2)}) collective-permute-start(f32[2,64,256]{2,1,0:T(8,128)S(1)} %pair.1), channel_id=1, source_target_pairs={{0,31},{1,0},{2,1},{3,2},{4,3},{5,4},{6,5},{7,6},{8,7},{9,8},{10,9... | collective-permute-start | bytes 393224 | tf_op jit(solution)/shard_map/ppermute | solution.py:321
  82.7 0.0 all-to-all-done.3.refs_1_
  82.7 5.4 %collective-permute-done.5.refs_1_.refs_3_ = f32[2,64,256]{2,1,0:T(8,128)S(1)} collective-permute-done((f32[2,64,256]{2,1,0:T(8,128)S(1)}, f32[2,64,256]{2,1,0:T(8,128)S(1)}, u32[]{:S(2)}, u32[]{:S(2)}) %collective-permute-start.5) | collective-permute-done | bytes 131104 | tf_op jit(solution)/shard_map/ppermute | solution.py:321
  88.1 2.8 %collective-permute-done.4.refs_0_.refs_2_ = f32[2,64,256]{2,1,0:T(8,128)S(1)} collective-permute-done((f32[2,64,256]{2,1,0:T(8,128)S(1)}, f32[2,64,256]{2,1,0:T(8,128)S(1)}, u32[]{:S(2)}, u32[]{:S(2)}) %collective-permute-start.4) | collective-permute-done | bytes 131104 | tf_op jit(solution)/shard_map/ppermute | solution.py:321
  90.9 1.9 %collective-permute-start.6 = (f32[2,64,256]{2,1,0:T(8,128)S(1)}, f32[2,64,256]{2,1,0:T(8,128)S(1)}, u32[]{:S(2)}, u32[]{:S(2)}) collective-permute-start(f32[2,64,256]{2,1,0:T(8,128)S(1)} %swap.1), channel_id=1, source_target_pairs={{0,32},{32,0},{64,96},{96,64},{128,160},{160,128},{192,224},{224,1... | collective-permute-start | bytes 393224 | tf_op jit(solution)/shard_map/ppermute | solution.py:330
  92.9 1.3 collective-permute-done.6.refs_4_
  94.2 1.9 %second.1 = (f32[64,256]{1,0:T(8,128)S(1)}, f32[4,64,256]{2,1,0:T(8,128)}) custom-call(s32[1]{0:T(128)} %bitcast.dev_ref, s32[12]{0:T(128)S(1)} %copy-done.3, s32[12]{0:T(128)S(1)} %copy-done.4, f32[64,256]{1,0:T(8,128)S(1)} %get-tuple-element.19.own_ref.refs_0_.v1_ref, f32[4,64,256]{2,1,0:T(8,128)S(1)} %all-to-all-done.3.refs_1_, ...), custom_call_target="tpu_custom_call" | custom-call | tf_op jit(solution)/shard_map/second/pallas_call | solution.py:347
  96.1 3.4 %all-to-all-start.4 = ((f32[4,64,256]{2,1,0:T(8,128)}), f32[4,64,256]{2,1,0:T(8,128)S(1)}, u32[]{:S(2)}, u32[]{:S(2)}) async-start(f32[4,64,256]{2,1,0:T(8,128)} %get-tuple-element.25), calls=%async_computation.4 | async-start | bytes 524288 | tf_op jit(solution)/shard_map/all_to_all | solution.py:306
  99.5 5.2 %collective-permute-start.10 = (f32[64,256]{1,0:T(8,128)S(1)}, f32[64,256]{1,0:T(8,128)S(1)}, u32[]{:S(2)}, u32[]{:S(2)}) collective-permute-start(f32[64,256]{1,0:T(8,128)S(1)} %get-tuple-element.29.v2_ref), channel_id=1, source_target_pairs={{0,29},{1,30},{2,31},{3,0},{4,1},{5,2},{6,3},{7,4},{8,5},{9,6},{10... | collective-permute-start | bytes 196616 | tf_op jit(solution)/shard_map/ppermute | solution.py:352
  104.7 3.1 %collective-permute-start.9 = (f32[64,256]{1,0:T(8,128)S(1)}, f32[64,256]{1,0:T(8,128)S(1)}, u32[]{:S(2)}, u32[]{:S(2)}) collective-permute-start(f32[64,256]{1,0:T(8,128)S(1)} %get-tuple-element.29.v2_ref), channel_id=1, source_target_pairs={{0,31},{1,0},{2,1},{3,2},{4,3},{5,4},{6,5},{7,6},{8,7},{9,8},{10,9... | collective-permute-start | bytes 196616 | tf_op jit(solution)/shard_map/ppermute | solution.py:352
  107.8 1.4 collective-permute-start.8
  109.2 0.3 collective-permute-start.7
  109.6 0.0 collective-permute-done.10.b_ref
  109.6 2.6 %collective-permute-done.9.a_ref = f32[64,256]{1,0:T(8,128)S(1)} collective-permute-done((f32[64,256]{1,0:T(8,128)S(1)}, f32[64,256]{1,0:T(8,128)S(1)}, u32[]{:S(2)}, u32[]{:S(2)}) %collective-permute-start.9) | collective-permute-done | bytes 65568 | tf_op jit(solution)/shard_map/ppermute | solution.py:352
  112.2 1.3 half.1
  113.5 0.6 broadcast_in_dim.7
  114.1 6.5 %all-to-all-start.5 = ((f32[32,4,128]{2,1,0:T(4,128)}), f32[32,4,128]{2,1,0:T(4,128)S(1)}, u32[]{:S(2)}, u32[]{:S(2)}) async-start(f32[32,4,128]{2,1,0:T(4,128)} %broadcast_in_dim.7), calls=%async_computation.5 | async-start | bytes 131072 | tf_op jit(solution)/shard_map/all_to_all | solution.py:360
  120.6 4.9 %collective-permute-start.12 = (f32[64,256]{1,0:T(8,128)S(1)}, f32[64,256]{1,0:T(8,128)S(1)}, u32[]{:S(2)}, u32[]{:S(2)}) collective-permute-start(f32[64,256]{1,0:T(8,128)S(1)} %get-tuple-element.29.v2_ref), channel_id=1, source_target_pairs={{0,3},{1,4},{2,5},{3,6},{4,7},{5,8},{6,9},{7,10},{8,11},{9,12},{10... | collective-permute-start | bytes 196616 | tf_op jit(solution)/shard_map/ppermute | solution.py:359
  125.6 4.3 %collective-permute-start.11 = (f32[64,256]{1,0:T(8,128)S(1)}, f32[64,256]{1,0:T(8,128)S(1)}, u32[]{:S(2)}, u32[]{:S(2)}) collective-permute-start(f32[64,256]{1,0:T(8,128)S(1)} %get-tuple-element.29.v2_ref), channel_id=1, source_target_pairs={{0,1},{1,2},{2,3},{3,4},{4,5},{5,6},{6,7},{7,8},{8,9},{9,10},{10,1... | collective-permute-start | bytes 196616 | tf_op jit(solution)/shard_map/ppermute | solution.py:359
  130.0 0.6 broadcast_in_dim.8
  130.6 7.9 %all-to-all-start.6 = ((f32[16,4,128]{2,1,0:T(4,128)}), f32[16,4,128]{2,1,0:T(4,128)S(1)}, u32[]{:S(2)}, u32[]{:S(2)}) async-start(f32[16,4,128]{2,1,0:T(4,128)} %broadcast_in_dim.8), calls=%async_computation.6 | async-start | bytes 65536 | tf_op jit(solution)/shard_map/all_to_all | solution.py:368
  138.5 1.0 rest.1.v3_ref
  139.5 6.3 %all-to-all-done.6.moments_ref = f32[16,4,128]{2,1,0:T(4,128)S(1)} async-done(((f32[16,4,128]{2,1,0:T(4,128)}), f32[16,4,128]{2,1,0:T(4,128)S(1)}, u32[]{:S(2)}, u32[]{:S(2)}) %all-to-all-start.6) | async-done | bytes 32800 | tf_op jit(solution)/shard_map/all_to_all | solution.py:368
  145.8 1.5 %finish.1 = (f32[64,256]{1,0:T(8,128)}, f32[64,256]{1,0:T(8,128)}) custom-call(f32[16,4,128]{2,1,0:T(4,128)S(1)} %all-to-all-done.6.moments_ref, f32[64,256]{1,0:T(8,128)S(1)} %bitcast.18, f32[64,256]{1,0:T(8,128)S(1)} %get-tuple-element.19.own_ref.refs_0_.v1_ref, f32[64,256]{1,0:T(8,128)S(1)} %get-tuple-element.29.v2_ref, f32[64,256]{1,0:T(8,128)S(1)} %rest.1.v3_ref), custom_call_target="tpu_custom_call" | custom-call | tf_op jit(solution)/shard_map/finish/pallas_call | solution.py:369
  (19 shorter events, 0.1 us)
Async XLA Ops:
  2.2 20.1 %copy-start.1 = (f32[256,512]{1,0:T(8,128)S(1)}, f32[256,512]{1,0:T(8,128)}, u32[]{:S(2)}) copy-start(f32[256,512]{1,0:T(8,128)} %desc_ref.1) | copy-start | bytes 1572868
  2.2 20.0 %all-to-all-start = ((f32[32,2,640]{2,1,0:T(2,128)}), f32[32,2,640]{2,1,0:T(2,128)S(1)}, u32[]{:S(2)}, u32[]{:S(2)}) async-start(f32[32,2,640]{2,1,0:T(2,128)} %get-tuple-element.18), calls=%async_computation | async-start | bytes 327680 | tf_op jit(solution)/shard_map/all_to_all | solution.py:287
  12.8 9.5 %copy-start.2 = (s32[64,64]{1,0:T(8,128)S(1)}, s32[64,64]{1,0:T(8,128)}, u32[]{:S(2)}) copy-start(s32[64,64]{1,0:T(8,128)} %cand_ref.1) | copy-start | bytes 49156
  38.5 23.0 %copy-start = (f32[12,128,128]{2,1,0:T(8,128)S(1)}, f32[12,128,128]{2,1,0:T(8,128)}, u32[]{:S(2)}) copy-start(f32[12,128,128]{2,1,0:T(8,128)} %tiles_ref.7) | copy-start | bytes 2359300
  54.2 9.5 %collective-permute-start.1 = (f32[64,256]{1,0:T(8,128)S(1)}, f32[64,256]{1,0:T(8,128)S(1)}, u32[]{:S(2)}, u32[]{:S(2)}) collective-permute-start(f32[64,256]{1,0:T(8,128)S(1)} %bitcast.15), channel_id=1, source_target_pairs={{0,480},{32,0},{64,32},{96,64},{128,96},{160,128},{192,160},{224,1... | collective-permute-start | bytes 196616 | tf_op jit(solution)/shard_map/ppermute | solution.py:303
  59.5 4.6 %collective-permute-start = (f32[64,256]{1,0:T(8,128)S(1)}, f32[64,256]{1,0:T(8,128)S(1)}, u32[]{:S(2)}, u32[]{:S(2)}) collective-permute-start(f32[64,256]{1,0:T(8,128)S(1)} %bitcast.16), channel_id=1, source_target_pairs={{0,32},{32,64},{64,96},{96,128},{128,160},{160,192},{192,224},{224... | collective-permute-start | bytes 196616 | tf_op jit(solution)/shard_map/ppermute | solution.py:303
  61.5 0.7 copy-start.3
  61.5 0.7 copy-start.4
  65.8 10.0 %collective-permute-start.3 = (f32[64,256]{1,0:T(8,128)S(1)}, f32[64,256]{1,0:T(8,128)S(1)}, u32[]{:S(2)}, u32[]{:S(2)}) collective-permute-start(f32[64,256]{1,0:T(8,128)S(1)} %get-tuple-element.19.own_ref.refs_0_.v1_ref), channel_id=1, source_target_pairs={{0,480},{32,0},{64,32},{96,64},{128,96},{160,128},{192,160},{224,1... | collective-permute-start | bytes 196616 | tf_op jit(solution)/shard_map/ppermute | solution.py:303
  72.3 3.4 %collective-permute-start.2 = (f32[64,256]{1,0:T(8,128)S(1)}, f32[64,256]{1,0:T(8,128)S(1)}, u32[]{:S(2)}, u32[]{:S(2)}) collective-permute-start(f32[64,256]{1,0:T(8,128)S(1)} %get-tuple-element.19.own_ref.refs_0_.v1_ref), channel_id=1, source_target_pairs={{0,32},{32,64},{64,96},{96,128},{128,160},{160,192},{192,224},{224... | collective-permute-start | bytes 196616 | tf_op jit(solution)/shard_map/ppermute | solution.py:303
  72.3 10.4 %all-to-all-start.3 = ((f32[4,64,256]{2,1,0:T(8,128)}), f32[4,64,256]{2,1,0:T(8,128)S(1)}, u32[]{:S(2)}, u32[]{:S(2)}) async-start(f32[4,64,256]{2,1,0:T(8,128)} %get-tuple-element.20), calls=%async_computation.3 | async-start | bytes 524288 | tf_op jit(solution)/shard_map/all_to_all | solution.py:306
  75.8 12.3 %collective-permute-start.5 = (f32[2,64,256]{2,1,0:T(8,128)S(1)}, f32[2,64,256]{2,1,0:T(8,128)S(1)}, u32[]{:S(2)}, u32[]{:S(2)}) collective-permute-start(f32[2,64,256]{2,1,0:T(8,128)S(1)} %pair.1), channel_id=1, source_target_pairs={{0,29},{1,30},{2,31},{3,0},{4,1},{5,2},{6,3},{7,4},{8,5},{9,6},{10... | collective-permute-start | bytes 393224 | tf_op jit(solution)/shard_map/ppermute | solution.py:321
  80.7 10.2 %collective-permute-start.4 = (f32[2,64,256]{2,1,0:T(8,128)S(1)}, f32[2,64,256]{2,1,0:T(8,128)S(1)}, u32[]{:S(2)}, u32[]{:S(2)}) collective-permute-start(f32[2,64,256]{2,1,0:T(8,128)S(1)} %pair.1), channel_id=1, source_target_pairs={{0,31},{1,0},{2,1},{3,2},{4,3},{5,4},{6,5},{7,6},{8,7},{9,8},{10,9... | collective-permute-start | bytes 393224 | tf_op jit(solution)/shard_map/ppermute | solution.py:321
  90.9 3.2 %collective-permute-start.6 = (f32[2,64,256]{2,1,0:T(8,128)S(1)}, f32[2,64,256]{2,1,0:T(8,128)S(1)}, u32[]{:S(2)}, u32[]{:S(2)}) collective-permute-start(f32[2,64,256]{2,1,0:T(8,128)S(1)} %swap.1), channel_id=1, source_target_pairs={{0,32},{32,0},{64,96},{96,64},{128,160},{160,128},{192,224},{224,1... | collective-permute-start | bytes 393224 | tf_op jit(solution)/shard_map/ppermute | solution.py:330
  96.1 16.1 %all-to-all-start.4 = ((f32[4,64,256]{2,1,0:T(8,128)}), f32[4,64,256]{2,1,0:T(8,128)S(1)}, u32[]{:S(2)}, u32[]{:S(2)}) async-start(f32[4,64,256]{2,1,0:T(8,128)} %get-tuple-element.25), calls=%async_computation.4 | async-start | bytes 524288 | tf_op jit(solution)/shard_map/all_to_all | solution.py:306
  99.5 10.1 %collective-permute-start.10 = (f32[64,256]{1,0:T(8,128)S(1)}, f32[64,256]{1,0:T(8,128)S(1)}, u32[]{:S(2)}, u32[]{:S(2)}) collective-permute-start(f32[64,256]{1,0:T(8,128)S(1)} %get-tuple-element.29.v2_ref), channel_id=1, source_target_pairs={{0,29},{1,30},{2,31},{3,0},{4,1},{5,2},{6,3},{7,4},{8,5},{9,6},{10... | collective-permute-start | bytes 196616 | tf_op jit(solution)/shard_map/ppermute | solution.py:352
  104.7 7.4 %collective-permute-start.9 = (f32[64,256]{1,0:T(8,128)S(1)}, f32[64,256]{1,0:T(8,128)S(1)}, u32[]{:S(2)}, u32[]{:S(2)}) collective-permute-start(f32[64,256]{1,0:T(8,128)S(1)} %get-tuple-element.29.v2_ref), channel_id=1, source_target_pairs={{0,31},{1,0},{2,1},{3,2},{4,3},{5,4},{6,5},{7,6},{8,7},{9,8},{10,9... | collective-permute-start | bytes 196616 | tf_op jit(solution)/shard_map/ppermute | solution.py:352
  107.8 4.4 %collective-permute-start.8 = (f32[64,256]{1,0:T(8,128)S(1)}, f32[64,256]{1,0:T(8,128)S(1)}, u32[]{:S(2)}, u32[]{:S(2)}) collective-permute-start(f32[64,256]{1,0:T(8,128)S(1)} %get-tuple-element.29.v2_ref), channel_id=1, source_target_pairs={{0,480},{32,0},{64,32},{96,64},{128,96},{160,128},{192,160},{224,1... | collective-permute-start | bytes 196616 | tf_op jit(solution)/shard_map/ppermute | solution.py:303
  109.2 2.9 %collective-permute-start.7 = (f32[64,256]{1,0:T(8,128)S(1)}, f32[64,256]{1,0:T(8,128)S(1)}, u32[]{:S(2)}, u32[]{:S(2)}) collective-permute-start(f32[64,256]{1,0:T(8,128)S(1)} %get-tuple-element.29.v2_ref), channel_id=1, source_target_pairs={{0,32},{32,64},{64,96},{96,128},{128,160},{160,192},{192,224},{224... | collective-permute-start | bytes 196616 | tf_op jit(solution)/shard_map/ppermute | solution.py:303
  114.1 15.8 %all-to-all-start.5 = ((f32[32,4,128]{2,1,0:T(4,128)}), f32[32,4,128]{2,1,0:T(4,128)S(1)}, u32[]{:S(2)}, u32[]{:S(2)}) async-start(f32[32,4,128]{2,1,0:T(4,128)} %broadcast_in_dim.7), calls=%async_computation.5 | async-start | bytes 131072 | tf_op jit(solution)/shard_map/all_to_all | solution.py:360
  120.6 17.8 %collective-permute-start.12 = (f32[64,256]{1,0:T(8,128)S(1)}, f32[64,256]{1,0:T(8,128)S(1)}, u32[]{:S(2)}, u32[]{:S(2)}) collective-permute-start(f32[64,256]{1,0:T(8,128)S(1)} %get-tuple-element.29.v2_ref), channel_id=1, source_target_pairs={{0,3},{1,4},{2,5},{3,6},{4,7},{5,8},{6,9},{7,10},{8,11},{9,12},{10... | collective-permute-start | bytes 196616 | tf_op jit(solution)/shard_map/ppermute | solution.py:359
  125.6 12.9 %collective-permute-start.11 = (f32[64,256]{1,0:T(8,128)S(1)}, f32[64,256]{1,0:T(8,128)S(1)}, u32[]{:S(2)}, u32[]{:S(2)}) collective-permute-start(f32[64,256]{1,0:T(8,128)S(1)} %get-tuple-element.29.v2_ref), channel_id=1, source_target_pairs={{0,1},{1,2},{2,3},{3,4},{4,5},{5,6},{6,7},{7,8},{8,9},{9,10},{10,1... | collective-permute-start | bytes 196616 | tf_op jit(solution)/shard_map/ppermute | solution.py:359
  130.6 15.3 %all-to-all-start.6 = ((f32[16,4,128]{2,1,0:T(4,128)}), f32[16,4,128]{2,1,0:T(4,128)S(1)}, u32[]{:S(2)}, u32[]{:S(2)}) async-start(f32[16,4,128]{2,1,0:T(4,128)} %broadcast_in_dim.8), calls=%async_computation.6 | async-start | bytes 65536 | tf_op jit(solution)/shard_map/all_to_all | solution.py:368

commit v12 on v11

--- a/solution.py
+++ b/solution.py
@@ -16,7 +16,7 @@
 HOPS = (0, 1, -1, 3, -3, 8, -8, 16)
 N_X = 4
 N_Y = 8
-SHARED = (1, 3)
+SHARED = (3, 1)
 SLOTS = len(HOPS) + 2
 HIGHEST = lax.Precision.HIGHEST
 F32 = jnp.float32

time: 148 us -> 151 us (1.020)
  waiting for transfers between devices: 28.2 us -> 30.2 us
    ppermute x2, starting transfers between devices: 8.32 us -> 10.1 us  [local(): ahead = [lax.ppermute(v2, 'row', ring(N_ROW, -hop)) for hop in SHARED]]
    ppermute x2, waiting for transfers between devices: 8.18 us -> 9.85 us  [fetch(): got.append(lax.ppermute(both, ('region', 'row'), pairs))]
where the time goes in v12:
time: 151 us
  starting transfers between devices  75.3 us (50%)
  waiting for transfers between devices  30.2 us (20%)
  blocking collectives  28.8 us (19%)
  Pallas kernels  13.3 us (9%)
  local copies, waits for them, and re-layouts  2.14 us (1%)
    all_to_all x1, blocking collectives, local(): lax.all_to_all(near.reshape(N_ROW, width, TILE), 'row', 0, 0, tiled=True)  15.5 us
    all_to_all x1, blocking collectives, local(): lax.all_to_all(by_query.reshape(N_ROW, QS * HALF, TILE), 'row', 0, 0, til...  13.3 us
    ppermute x3, starting transfers between devices, region_pair(): lax.ppermute(v, 'region', ring(N_REGION, -1))  13.1 us
    all_to_all x1, starting transfers between devices, local(): lax.all_to_all(packed, 'row', 0, 0, tiled=True).reshape(Q, D + TILE)  10.6 us
    ppermute x2, starting transfers between devices, local(): ahead = [lax.ppermute(v2, 'row', ring(N_ROW, -hop)) for hop in SHARED]  10.1 us
    ppermute x2, waiting for transfers between devices, fetch(): got.append(lax.ppermute(both, ('region', 'row'), pairs))  9.85 us
    all_to_all x1, waiting for transfers between devices, local(): lax.all_to_all(packed, 'row', 0, 0, tiled=True).reshape(Q, D + TILE)  9.34 us
    ppermute x2, starting transfers between devices, local(): behind = [lax.ppermute(later, 'row', ring(N_ROW, hop)) for hop in SHARED]  9.24 us
  transfers between devices with their start and end apart: 18, of which 7 were waited for; matrix products, arithmetic and copies ran while one was open for 0% of the time, Pallas kernels for 2%

profile of v12, /device:TPU:1, one launch (start us, length us, event | category | flops | bytes accessed | tf_op | source)
XLA Modules:
  0.0 150.7 jit_solution(14775989581655602462)
XLA Ops:
  0.6 1.5 %pack.1 = (f32[32,2,640]{2,1,0:T(2,128)}, s32[12]{0:T(128)}, s32[12]{0:T(128)}) custom-call(f32[2,512]{1,0:T(2,128)} %queries_hbm.1, s32[1,256]{1,0:T(1,128)} %perm_hbm.1, s32[12]{0:T(128)} %row_hbm.1, s32[12]{0:T(128)} %col_hbm.1), custom_call_target="tpu_custom_call" | custom-call | tf_op jit(solution)/shard_map/pack/pallas_call | solution.py:281
  2.2 0.0 copy-start.1
  2.2 10.6 %all-to-all-start = ((f32[32,2,640]{2,1,0:T(2,128)}), f32[32,2,640]{2,1,0:T(2,128)S(1)}, u32[]{:S(2)}, u32[]{:S(2)}) async-start(f32[32,2,640]{2,1,0:T(2,128)} %get-tuple-element.18), calls=%async_computation | async-start | bytes 327680 | tf_op jit(solution)/shard_map/all_to_all | solution.py:287
  12.8 0.0 copy-start.2
  12.9 9.3 %all-to-all-done = f32[32,2,640]{2,1,0:T(2,128)S(1)} async-done(((f32[32,2,640]{2,1,0:T(2,128)}), f32[32,2,640]{2,1,0:T(2,128)S(1)}, u32[]{:S(2)}, u32[]{:S(2)}) %all-to-all-start) | async-done | bytes 163872 | tf_op jit(solution)/shard_map/all_to_all | solution.py:287
  22.2 0.1 reshape.28.packed_ref
  22.3 0.6 scores.1
  23.0 13.3 %all_to_all.35 = f32[32,4,128]{2,1,0:T(4,128)S(1)} all-to-all(f32[32,4,128]{2,1,0:T(4,128)S(1)} %bitcast.20), channel_id=1, replica_groups=mesh['region'=16,'row'=32] {'row'}, dimensions={0} | all-to-all | bytes 131072 | tf_op jit(solution)/shard_map/all_to_all | solution.py:292
  36.3 2.2 %permute.1 = f32[1024,128]{1,0:T(8,128)S(1)} custom-call(f32[128,128]{1,0:T(8,128)S(1)} %bitcast.19, f32[64,640]{1,0:T(8,128)S(1)} %reshape.28.packed_ref), custom_call_target="tpu_custom_call" | custom-call | tf_op jit(solution)/shard_map/permute/pallas_call | solution.py:294
  38.5 0.0 copy-start
  38.5 15.5 %all_to_all.36 = f32[32,32,128]{2,1,0:T(8,128)S(1)} all-to-all(f32[32,32,128]{2,1,0:T(8,128)S(1)} %bitcast.14), channel_id=1, replica_groups=mesh['region'=16,'row'=32] {'row'}, dimensions={0} | all-to-all | bytes 1048576 | tf_op jit(solution)/shard_map/all_to_all | solution.py:299
  54.1 0.1 copy.17
  54.2 5.4 %collective-permute-start.1 = (f32[64,256]{1,0:T(8,128)S(1)}, f32[64,256]{1,0:T(8,128)S(1)}, u32[]{:S(2)}, u32[]{:S(2)}) collective-permute-start(f32[64,256]{1,0:T(8,128)S(1)} %bitcast.15), channel_id=1, source_target_pairs={{0,480},{32,0},{64,32},{96,64},{128,96},{160,128},{192,160},{224,1... | collective-permute-start | bytes 196616 | tf_op jit(solution)/shard_map/ppermute | solution.py:303
  59.5 2.0 %collective-permute-start = (f32[64,256]{1,0:T(8,128)S(1)}, f32[64,256]{1,0:T(8,128)S(1)}, u32[]{:S(2)}, u32[]{:S(2)}) collective-permute-start(f32[64,256]{1,0:T(8,128)S(1)} %bitcast.16), channel_id=1, source_target_pairs={{0,32},{32,64},{64,96},{96,128},{128,160},{160,192},{192,224},{224... | collective-permute-start | bytes 196616 | tf_op jit(solution)/shard_map/ppermute | solution.py:303
  61.5 0.6 copy-done.3
  62.2 1.4 first_inner.1.inner_ref
  63.6 0.0 collective-permute-done.1.high_ref
  63.6 0.5 collective-permute-done.low_ref
  64.1 1.7 %first_outer.1 = (f32[64,256]{1,0:T(8,128)S(1)}, f32[4,64,256]{2,1,0:T(8,128)}) custom-call(s32[12]{0:T(128)S(1)} %copy-done.3, s32[12]{0:T(128)S(1)} %copy-done.4, f32[2,64,128]{2,1,0:T(8,128)S(1)} %first_inner.1.inner_ref, f32[64,256]{1,0:T(8,128)S(1)} %collective-permute-done.low_ref, f32[64,256]{1,0:T(8,128)S(1)} %collective-permute-done.1.high_ref, ...), custom_call_target="tpu_custom_call" | custom-call | tf_op jit(solution)/shard_map/first_outer/pallas_call | solution.py:342
  65.8 6.5 %collective-permute-start.3 = (f32[64,256]{1,0:T(8,128)S(1)}, f32[64,256]{1,0:T(8,128)S(1)}, u32[]{:S(2)}, u32[]{:S(2)}) collective-permute-start(f32[64,256]{1,0:T(8,128)S(1)} %get-tuple-element.19.own_ref.refs_0_.v1_ref), channel_id=1, source_target_pairs={{0,480},{32,0},{64,32},{96,64},{128,96},{160,128},{192,160},{224,1... | collective-permute-start | bytes 196616 | tf_op jit(solution)/shard_map/ppermute | solution.py:303
  72.3 3.4 %all-to-all-start.3 = ((f32[4,64,256]{2,1,0:T(8,128)}), f32[4,64,256]{2,1,0:T(8,128)S(1)}, u32[]{:S(2)}, u32[]{:S(2)}) async-start(f32[4,64,256]{2,1,0:T(8,128)} %get-tuple-element.20), calls=%async_computation.3 | async-start | bytes 524288 | tf_op jit(solution)/shard_map/all_to_all | solution.py:306
  75.7 0.0 collective-permute-done.3.high_ref.refs_6_
  75.8 4.4 %collective-permute-start.5 = (f32[2,64,256]{2,1,0:T(8,128)S(1)}, f32[2,64,256]{2,1,0:T(8,128)S(1)}, u32[]{:S(2)}, u32[]{:S(2)}) collective-permute-start(f32[2,64,256]{2,1,0:T(8,128)S(1)} %pair.1), channel_id=1, source_target_pairs={{0,31},{1,0},{2,1},{3,2},{4,3},{5,4},{6,5},{7,6},{8,7},{9,8},{10,9... | collective-permute-start | bytes 393224 | tf_op jit(solution)/shard_map/ppermute | solution.py:321
  80.2 2.6 %collective-permute-start.4 = (f32[2,64,256]{2,1,0:T(8,128)S(1)}, f32[2,64,256]{2,1,0:T(8,128)S(1)}, u32[]{:S(2)}, u32[]{:S(2)}) collective-permute-start(f32[2,64,256]{2,1,0:T(8,128)S(1)} %pair.1), channel_id=1, source_target_pairs={{0,29},{1,30},{2,31},{3,0},{4,1},{5,2},{6,3},{7,4},{8,5},{9,6},{10... | collective-permute-start | bytes 393224 | tf_op jit(solution)/shard_map/ppermute | solution.py:321
  82.7 2.1 %collective-permute-done.5.refs_1_.refs_3_ = f32[2,64,256]{2,1,0:T(8,128)S(1)} collective-permute-done((f32[2,64,256]{2,1,0:T(8,128)S(1)}, f32[2,64,256]{2,1,0:T(8,128)S(1)}, u32[]{:S(2)}, u32[]{:S(2)}) %collective-permute-start.5) | collective-permute-done | bytes 131104 | tf_op jit(solution)/shard_map/ppermute | solution.py:321
  84.8 7.8 %collective-permute-done.4.refs_0_.refs_2_ = f32[2,64,256]{2,1,0:T(8,128)S(1)} collective-permute-done((f32[2,64,256]{2,1,0:T(8,128)S(1)}, f32[2,64,256]{2,1,0:T(8,128)S(1)}, u32[]{:S(2)}, u32[]{:S(2)}) %collective-permute-start.4) | collective-permute-done | bytes 131104 | tf_op jit(solution)/shard_map/ppermute | solution.py:321
  92.6 2.0 %collective-permute-start.6 = (f32[2,64,256]{2,1,0:T(8,128)S(1)}, f32[2,64,256]{2,1,0:T(8,128)S(1)}, u32[]{:S(2)}, u32[]{:S(2)}) collective-permute-start(f32[2,64,256]{2,1,0:T(8,128)S(1)} %swap.1), channel_id=1, source_target_pairs={{0,32},{32,0},{64,96},{96,64},{128,160},{160,128},{192,224},{224,1... | collective-permute-start | bytes 393224 | tf_op jit(solution)/shard_map/ppermute | solution.py:330
  94.7 1.2 collective-permute-done.6.refs_4_
  95.8 1.9 %second.1 = (f32[64,256]{1,0:T(8,128)S(1)}, f32[4,64,256]{2,1,0:T(8,128)}) custom-call(s32[1]{0:T(128)} %bitcast.dev_ref, s32[12]{0:T(128)S(1)} %copy-done.3, s32[12]{0:T(128)S(1)} %copy-done.4, f32[64,256]{1,0:T(8,128)S(1)} %get-tuple-element.19.own_ref.refs_0_.v1_ref, f32[4,64,256]{2,1,0:T(8,128)S(1)} %all-to-all-done.3.refs_1_, ...), custom_call_target="tpu_custom_call" | custom-call | tf_op jit(solution)/shard_map/second/pallas_call | solution.py:347
  97.7 3.4 %all-to-all-start.4 = ((f32[4,64,256]{2,1,0:T(8,128)}), f32[4,64,256]{2,1,0:T(8,128)S(1)}, u32[]{:S(2)}, u32[]{:S(2)}) async-start(f32[4,64,256]{2,1,0:T(8,128)} %get-tuple-element.25), calls=%async_computation.4 | async-start | bytes 524288 | tf_op jit(solution)/shard_map/all_to_all | solution.py:306
  101.2 8.0 %collective-permute-start.10 = (f32[64,256]{1,0:T(8,128)S(1)}, f32[64,256]{1,0:T(8,128)S(1)}, u32[]{:S(2)}, u32[]{:S(2)}) collective-permute-start(f32[64,256]{1,0:T(8,128)S(1)} %get-tuple-element.29.v2_ref), channel_id=1, source_target_pairs={{0,31},{1,0},{2,1},{3,2},{4,3},{5,4},{6,5},{7,6},{8,7},{9,8},{10,9... | collective-permute-start | bytes 196616 | tf_op jit(solution)/shard_map/ppermute | solution.py:352
  109.2 2.0 %collective-permute-start.9 = (f32[64,256]{1,0:T(8,128)S(1)}, f32[64,256]{1,0:T(8,128)S(1)}, u32[]{:S(2)}, u32[]{:S(2)}) collective-permute-start(f32[64,256]{1,0:T(8,128)S(1)} %get-tuple-element.29.v2_ref), channel_id=1, source_target_pairs={{0,29},{1,30},{2,31},{3,0},{4,1},{5,2},{6,3},{7,4},{8,5},{9,6},{10... | collective-permute-start | bytes 196616 | tf_op jit(solution)/shard_map/ppermute | solution.py:352
  111.2 1.2 collective-permute-start.8
  112.4 0.5 collective-permute-start.7
  113.0 0.0 collective-permute-done.10.b_ref
  113.0 3.0 %collective-permute-done.9.a_ref = f32[64,256]{1,0:T(8,128)S(1)} collective-permute-done((f32[64,256]{1,0:T(8,128)S(1)}, f32[64,256]{1,0:T(8,128)S(1)}, u32[]{:S(2)}, u32[]{:S(2)}) %collective-permute-start.9) | collective-permute-done | bytes 65568 | tf_op jit(solution)/shard_map/ppermute | solution.py:352
  116.0 0.0 all-to-all-done.4.line_ref
  116.0 1.3 half.1
  117.3 0.6 broadcast_in_dim.7
  118.0 5.8 %all-to-all-start.5 = ((f32[32,4,128]{2,1,0:T(4,128)}), f32[32,4,128]{2,1,0:T(4,128)S(1)}, u32[]{:S(2)}, u32[]{:S(2)}) async-start(f32[32,4,128]{2,1,0:T(4,128)} %broadcast_in_dim.7), calls=%async_computation.5 | async-start | bytes 131072 | tf_op jit(solution)/shard_map/all_to_all | solution.py:360
  123.8 3.1 %collective-permute-start.12 = (f32[64,256]{1,0:T(8,128)S(1)}, f32[64,256]{1,0:T(8,128)S(1)}, u32[]{:S(2)}, u32[]{:S(2)}) collective-permute-start(f32[64,256]{1,0:T(8,128)S(1)} %get-tuple-element.29.v2_ref), channel_id=1, source_target_pairs={{0,1},{1,2},{2,3},{3,4},{4,5},{5,6},{6,7},{7,8},{8,9},{9,10},{10,1... | collective-permute-start | bytes 196616 | tf_op jit(solution)/shard_map/ppermute | solution.py:359
  127.0 6.1 %collective-permute-start.11 = (f32[64,256]{1,0:T(8,128)S(1)}, f32[64,256]{1,0:T(8,128)S(1)}, u32[]{:S(2)}, u32[]{:S(2)}) collective-permute-start(f32[64,256]{1,0:T(8,128)S(1)} %get-tuple-element.29.v2_ref), channel_id=1, source_target_pairs={{0,3},{1,4},{2,5},{3,6},{4,7},{5,8},{6,9},{7,10},{8,11},{9,12},{10... | collective-permute-start | bytes 196616 | tf_op jit(solution)/shard_map/ppermute | solution.py:359
  133.1 0.6 broadcast_in_dim.8
  133.7 8.1 %all-to-all-start.6 = ((f32[16,4,128]{2,1,0:T(4,128)}), f32[16,4,128]{2,1,0:T(4,128)S(1)}, u32[]{:S(2)}, u32[]{:S(2)}) async-start(f32[16,4,128]{2,1,0:T(4,128)} %broadcast_in_dim.8), calls=%async_computation.6 | async-start | bytes 65536 | tf_op jit(solution)/shard_map/all_to_all | solution.py:368
  141.8 0.0 collective-permute-done.11.a_ref
  141.8 1.0 rest.1.v3_ref
  142.9 6.3 %all-to-all-done.6.moments_ref = f32[16,4,128]{2,1,0:T(4,128)S(1)} async-done(((f32[16,4,128]{2,1,0:T(4,128)}), f32[16,4,128]{2,1,0:T(4,128)S(1)}, u32[]{:S(2)}, u32[]{:S(2)}) %all-to-all-start.6) | async-done | bytes 32800 | tf_op jit(solution)/shard_map/all_to_all | solution.py:368
  149.2 1.5 %finish.1 = (f32[64,256]{1,0:T(8,128)}, f32[64,256]{1,0:T(8,128)}) custom-call(f32[16,4,128]{2,1,0:T(4,128)S(1)} %all-to-all-done.6.moments_ref, f32[64,256]{1,0:T(8,128)S(1)} %bitcast.18, f32[64,256]{1,0:T(8,128)S(1)} %get-tuple-element.19.own_ref.refs_0_.v1_ref, f32[64,256]{1,0:T(8,128)S(1)} %get-tuple-element.29.v2_ref, f32[64,256]{1,0:T(8,128)S(1)} %rest.1.v3_ref), custom_call_target="tpu_custom_call" | custom-call | tf_op jit(solution)/shard_map/finish/pallas_call | solution.py:369
  (19 shorter events, 0.1 us)
Async XLA Ops:
  2.2 20.1 %copy-start.1 = (f32[256,512]{1,0:T(8,128)S(1)}, f32[256,512]{1,0:T(8,128)}, u32[]{:S(2)}) copy-start(f32[256,512]{1,0:T(8,128)} %desc_ref.1) | copy-start | bytes 1572868
  2.2 20.0 %all-to-all-start = ((f32[32,2,640]{2,1,0:T(2,128)}), f32[32,2,640]{2,1,0:T(2,128)S(1)}, u32[]{:S(2)}, u32[]{:S(2)}) async-start(f32[32,2,640]{2,1,0:T(2,128)} %get-tuple-element.18), calls=%async_computation | async-start | bytes 327680 | tf_op jit(solution)/shard_map/all_to_all | solution.py:287
  12.8 9.5 %copy-start.2 = (s32[64,64]{1,0:T(8,128)S(1)}, s32[64,64]{1,0:T(8,128)}, u32[]{:S(2)}) copy-start(s32[64,64]{1,0:T(8,128)} %cand_ref.1) | copy-start | bytes 49156
  38.5 23.0 %copy-start = (f32[12,128,128]{2,1,0:T(8,128)S(1)}, f32[12,128,128]{2,1,0:T(8,128)}, u32[]{:S(2)}) copy-start(f32[12,128,128]{2,1,0:T(8,128)} %tiles_ref.7) | copy-start | bytes 2359300
  54.2 9.5 %collective-permute-start.1 = (f32[64,256]{1,0:T(8,128)S(1)}, f32[64,256]{1,0:T(8,128)S(1)}, u32[]{:S(2)}, u32[]{:S(2)}) collective-permute-start(f32[64,256]{1,0:T(8,128)S(1)} %bitcast.15), channel_id=1, source_target_pairs={{0,480},{32,0},{64,32},{96,64},{128,96},{160,128},{192,160},{224,1... | collective-permute-start | bytes 196616 | tf_op jit(solution)/shard_map/ppermute | solution.py:303
  59.5 4.6 %collective-permute-start = (f32[64,256]{1,0:T(8,128)S(1)}, f32[64,256]{1,0:T(8,128)S(1)}, u32[]{:S(2)}, u32[]{:S(2)}) collective-permute-start(f32[64,256]{1,0:T(8,128)S(1)} %bitcast.16), channel_id=1, source_target_pairs={{0,32},{32,64},{64,96},{96,128},{128,160},{160,192},{192,224},{224... | collective-permute-start | bytes 196616 | tf_op jit(solution)/shard_map/ppermute | solution.py:303
  61.5 0.7 copy-start.3
  61.5 0.7 copy-start.4
  65.8 10.0 %collective-permute-start.3 = (f32[64,256]{1,0:T(8,128)S(1)}, f32[64,256]{1,0:T(8,128)S(1)}, u32[]{:S(2)}, u32[]{:S(2)}) collective-permute-start(f32[64,256]{1,0:T(8,128)S(1)} %get-tuple-element.19.own_ref.refs_0_.v1_ref), channel_id=1, source_target_pairs={{0,480},{32,0},{64,32},{96,64},{128,96},{160,128},{192,160},{224,1... | collective-permute-start | bytes 196616 | tf_op jit(solution)/shard_map/ppermute | solution.py:303
  72.3 3.4 %collective-permute-start.2 = (f32[64,256]{1,0:T(8,128)S(1)}, f32[64,256]{1,0:T(8,128)S(1)}, u32[]{:S(2)}, u32[]{:S(2)}) collective-permute-start(f32[64,256]{1,0:T(8,128)S(1)} %get-tuple-element.19.own_ref.refs_0_.v1_ref), channel_id=1, source_target_pairs={{0,32},{32,64},{64,96},{96,128},{128,160},{160,192},{192,224},{224... | collective-permute-start | bytes 196616 | tf_op jit(solution)/shard_map/ppermute | solution.py:303
  72.3 10.4 %all-to-all-start.3 = ((f32[4,64,256]{2,1,0:T(8,128)}), f32[4,64,256]{2,1,0:T(8,128)S(1)}, u32[]{:S(2)}, u32[]{:S(2)}) async-start(f32[4,64,256]{2,1,0:T(8,128)} %get-tuple-element.20), calls=%async_computation.3 | async-start | bytes 524288 | tf_op jit(solution)/shard_map/all_to_all | solution.py:306
  75.8 9.0 %collective-permute-start.5 = (f32[2,64,256]{2,1,0:T(8,128)S(1)}, f32[2,64,256]{2,1,0:T(8,128)S(1)}, u32[]{:S(2)}, u32[]{:S(2)}) collective-permute-start(f32[2,64,256]{2,1,0:T(8,128)S(1)} %pair.1), channel_id=1, source_target_pairs={{0,31},{1,0},{2,1},{3,2},{4,3},{5,4},{6,5},{7,6},{8,7},{9,8},{10,9... | collective-permute-start | bytes 393224 | tf_op jit(solution)/shard_map/ppermute | solution.py:321
  80.2 12.4 %collective-permute-start.4 = (f32[2,64,256]{2,1,0:T(8,128)S(1)}, f32[2,64,256]{2,1,0:T(8,128)S(1)}, u32[]{:S(2)}, u32[]{:S(2)}) collective-permute-start(f32[2,64,256]{2,1,0:T(8,128)S(1)} %pair.1), channel_id=1, source_target_pairs={{0,29},{1,30},{2,31},{3,0},{4,1},{5,2},{6,3},{7,4},{8,5},{9,6},{10... | collective-permute-start | bytes 393224 | tf_op jit(solution)/shard_map/ppermute | solution.py:321
  92.6 3.2 %collective-permute-start.6 = (f32[2,64,256]{2,1,0:T(8,128)S(1)}, f32[2,64,256]{2,1,0:T(8,128)S(1)}, u32[]{:S(2)}, u32[]{:S(2)}) collective-permute-start(f32[2,64,256]{2,1,0:T(8,128)S(1)} %swap.1), channel_id=1, source_target_pairs={{0,32},{32,0},{64,96},{96,64},{128,160},{160,128},{192,224},{224,1... | collective-permute-start | bytes 393224 | tf_op jit(solution)/shard_map/ppermute | solution.py:330
  97.7 18.3 %all-to-all-start.4 = ((f32[4,64,256]{2,1,0:T(8,128)}), f32[4,64,256]{2,1,0:T(8,128)S(1)}, u32[]{:S(2)}, u32[]{:S(2)}) async-start(f32[4,64,256]{2,1,0:T(8,128)} %get-tuple-element.25), calls=%async_computation.4 | async-start | bytes 524288 | tf_op jit(solution)/shard_map/all_to_all | solution.py:306
  101.2 11.8 %collective-permute-start.10 = (f32[64,256]{1,0:T(8,128)S(1)}, f32[64,256]{1,0:T(8,128)S(1)}, u32[]{:S(2)}, u32[]{:S(2)}) collective-permute-start(f32[64,256]{1,0:T(8,128)S(1)} %get-tuple-element.29.v2_ref), channel_id=1, source_target_pairs={{0,31},{1,0},{2,1},{3,2},{4,3},{5,4},{6,5},{7,6},{8,7},{9,8},{10,9... | collective-permute-start | bytes 196616 | tf_op jit(solution)/shard_map/ppermute | solution.py:352
  109.2 6.9 %collective-permute-start.9 = (f32[64,256]{1,0:T(8,128)S(1)}, f32[64,256]{1,0:T(8,128)S(1)}, u32[]{:S(2)}, u32[]{:S(2)}) collective-permute-start(f32[64,256]{1,0:T(8,128)S(1)} %get-tuple-element.29.v2_ref), channel_id=1, source_target_pairs={{0,29},{1,30},{2,31},{3,0},{4,1},{5,2},{6,3},{7,4},{8,5},{9,6},{10... | collective-permute-start | bytes 196616 | tf_op jit(solution)/shard_map/ppermute | solution.py:352
  111.2 4.8 %collective-permute-start.8 = (f32[64,256]{1,0:T(8,128)S(1)}, f32[64,256]{1,0:T(8,128)S(1)}, u32[]{:S(2)}, u32[]{:S(2)}) collective-permute-start(f32[64,256]{1,0:T(8,128)S(1)} %get-tuple-element.29.v2_ref), channel_id=1, source_target_pairs={{0,480},{32,0},{64,32},{96,64},{128,96},{160,128},{192,160},{224,1... | collective-permute-start | bytes 196616 | tf_op jit(solution)/shard_map/ppermute | solution.py:303
  112.4 3.6 %collective-permute-start.7 = (f32[64,256]{1,0:T(8,128)S(1)}, f32[64,256]{1,0:T(8,128)S(1)}, u32[]{:S(2)}, u32[]{:S(2)}) collective-permute-start(f32[64,256]{1,0:T(8,128)S(1)} %get-tuple-element.29.v2_ref), channel_id=1, source_target_pairs={{0,32},{32,64},{64,96},{96,128},{128,160},{160,192},{192,224},{224... | collective-permute-start | bytes 196616 | tf_op jit(solution)/shard_map/ppermute | solution.py:303
  118.0 15.1 %all-to-all-start.5 = ((f32[32,4,128]{2,1,0:T(4,128)}), f32[32,4,128]{2,1,0:T(4,128)S(1)}, u32[]{:S(2)}, u32[]{:S(2)}) async-start(f32[32,4,128]{2,1,0:T(4,128)} %broadcast_in_dim.7), calls=%async_computation.5 | async-start | bytes 131072 | tf_op jit(solution)/shard_map/all_to_all | solution.py:360
  123.8 18.0 %collective-permute-start.12 = (f32[64,256]{1,0:T(8,128)S(1)}, f32[64,256]{1,0:T(8,128)S(1)}, u32[]{:S(2)}, u32[]{:S(2)}) collective-permute-start(f32[64,256]{1,0:T(8,128)S(1)} %get-tuple-element.29.v2_ref), channel_id=1, source_target_pairs={{0,1},{1,2},{2,3},{3,4},{4,5},{5,6},{6,7},{7,8},{8,9},{9,10},{10,1... | collective-permute-start | bytes 196616 | tf_op jit(solution)/shard_map/ppermute | solution.py:359
  127.0 14.9 %collective-permute-start.11 = (f32[64,256]{1,0:T(8,128)S(1)}, f32[64,256]{1,0:T(8,128)S(1)}, u32[]{:S(2)}, u32[]{:S(2)}) collective-permute-start(f32[64,256]{1,0:T(8,128)S(1)} %get-tuple-element.29.v2_ref), channel_id=1, source_target_pairs={{0,3},{1,4},{2,5},{3,6},{4,7},{5,8},{6,9},{7,10},{8,11},{9,12},{10... | collective-permute-start | bytes 196616 | tf_op jit(solution)/shard_map/ppermute | solution.py:359
  133.7 15.5 %all-to-all-start.6 = ((f32[16,4,128]{2,1,0:T(4,128)}), f32[16,4,128]{2,1,0:T(4,128)S(1)}, u32[]{:S(2)}, u32[]{:S(2)}) async-start(f32[16,4,128]{2,1,0:T(4,128)} %broadcast_in_dim.8), calls=%async_computation.6 | async-start | bytes 65536 | tf_op jit(solution)/shard_map/all_to_all | solution.py:368

commit v13 on v11

--- a/solution.py
+++ b/solution.py
@@ -27,13 +27,17 @@
     return [(i, (i + hop) % count) for i in range(count)]
 
 
-def pack_kernel(queries_hbm, perm_hbm, row_hbm, col_hbm, out_ref, row_ref, col_ref, queries_ref, perm_ref, sems):
+def pack_kernel(queries_hbm, perm_hbm, row_hbm, col_hbm, out_ref, where_ref, queries_ref, perm_ref, row_ref, col_ref, sems):
     pairs = ((queries_hbm, queries_ref), (perm_hbm, perm_ref), (row_hbm, row_ref), (col_hbm, col_ref))
     copies = [pltpu.make_async_copy(src, dst, sems.at[n]) for n, (src, dst) in enumerate(pairs)]
     for copy in copies:
         copy.start()
     for copy in copies:
         copy.wait()
+    count = row_ref.shape[0]
+    for t in range(count):
+        where_ref[t] = row_ref[t]
+        where_ref[count + t] = col_ref[t]
     perm = perm_ref[...].astype(F32)
     out_ref[:, :, :D] = jnp.broadcast_to(queries_ref[...][None], (N_ROW, QS, D))
     for h in range(HALF):
@@ -136,7 +140,7 @@
                 copies_ref[x, :, cols] = acc_ref[h]
 
 
-def inner_kernel(dev_ref, row_ref, col_ref, near_ref, tiles_ref, out_ref, slots_ref):
+def inner_kernel(dev_ref, where_ref, near_ref, tiles_ref, out_ref, slots_ref):
     width = len(HOPS) * QS * HALF
     for k in range(len(HOPS)):
         for h in range(HALF):
@@ -145,19 +149,19 @@
                     pl.ds((k * QS + q) * HALF + h, N_ROW, stride=width), :]
     out_ref[...] = jnp.zeros_like(out_ref)
     for t in range(tiles_ref.shape[0]):
-        inside = col_ref[t] < N_ROW * HALF
-        slot = jnp.where(inside, near_slot(col_ref[t], place(dev_ref)), 0)
-        out_ref[row_ref[t]] += jnp.where(inside, product(slots_ref, slot, tiles_ref, t), 0.0)
-
-
-def outer_kernel(row_ref, col_ref, inner_ref, low_ref, high_ref, tiles_ref, out_ref, copies_ref, slots_ref, acc_ref):
+        inside = where_ref[tiles_ref.shape[0] + t] < N_ROW * HALF
+        slot = jnp.where(inside, near_slot(where_ref[tiles_ref.shape[0] + t], place(dev_ref)), 0)
+        out_ref[where_ref[t]] += jnp.where(inside, product(slots_ref, slot, tiles_ref, t), 0.0)
+
+
+def outer_kernel(where_ref, inner_ref, low_ref, high_ref, tiles_ref, out_ref, copies_ref, slots_ref, acc_ref):
     spread(slots_ref, 0, low_ref[...])
     spread(slots_ref, 1, high_ref[...])
     acc_ref[...] = inner_ref[...]
     for t in range(tiles_ref.shape[0]):
-        @pl.when(col_ref[t] >= N_ROW * HALF)
+        @pl.when(where_ref[tiles_ref.shape[0] + t] >= N_ROW * HALF)
         def _():
-            acc_ref[row_ref[t]] += product(slots_ref, col_ref[t] - N_ROW * HALF, tiles_ref, t)
+            acc_ref[where_ref[t]] += product(slots_ref, where_ref[tiles_ref.shape[0] + t] - N_ROW * HALF, tiles_ref, t)
     store(acc_ref, out_ref, copies_ref)
 
 
@@ -175,7 +179,7 @@
 N_BLOCKS = 7
 
 
-def times_s(dev_ref, row_ref, col_ref, blocks, tiles_ref, slots_ref, acc_ref):
+def times_s(dev_ref, where_ref, blocks, tiles_ref, slots_ref, acc_ref):
     _, line_ref, a_ref, b_ref, swapped_ref, low_ref, high_ref = blocks
     blocks = [line_ref[x] for x in range(N_X)] + [
         a_ref[0], b_ref[0], swapped_ref[0], swapped_ref[1], low_ref[...], high_ref[...]]
@@ -183,12 +187,12 @@
         spread(slots_ref, k, block)
     acc_ref[...] = jnp.zeros_like(acc_ref)
     for t in range(tiles_ref.shape[0]):
-        acc_ref[row_ref[t]] += product(slots_ref, any_slot(col_ref[t], place(dev_ref)), tiles_ref, t)
-
-
-def next_kernel(dev_ref, row_ref, col_ref, *refs):
+        acc_ref[where_ref[t]] += product(slots_ref, any_slot(where_ref[tiles_ref.shape[0] + t], place(dev_ref)), tiles_ref, t)
+
+
+def next_kernel(dev_ref, where_ref, *refs):
     tiles_ref, out_ref, copies_ref, slots_ref, acc_ref = refs[N_BLOCKS:]
-    times_s(dev_ref, row_ref, col_ref, refs[:N_BLOCKS], tiles_ref, slots_ref, acc_ref)
+    times_s(dev_ref, where_ref, refs[:N_BLOCKS], tiles_ref, slots_ref, acc_ref)
     store(acc_ref, out_ref, copies_ref)
 
 
@@ -201,7 +205,7 @@
     return jnp.where(col >= N_ROW * HALF, 0, kind)
 
 
-def half_kernel(dev_ref, row_ref, col_ref, v2_ref, line_ref, low_ref, high_ref, a_ref, b_ref, v0_ref, v1_ref, tiles_ref,
+def half_kernel(dev_ref, where_ref, v2_ref, line_ref, low_ref, high_ref, a_ref, b_ref, v0_ref, v1_ref, tiles_ref,
                 part_ref, moments_ref, slots_ref, acc_ref):
     blocks = [line_ref[x] for x in range(N_X)] + [a_ref[...], b_ref[...], None, None, low_ref[...], high_ref[...]]
     for k, block in enumerate(blocks):
@@ -209,9 +213,9 @@
             spread(slots_ref, k, block)
     acc_ref[...] = jnp.zeros_like(acc_ref)
     for t in range(tiles_ref.shape[0]):
-        kind = side(col_ref[t], (place(dev_ref)[0], 1))
-        slot = jnp.where(kind == 2, 0, any_slot(col_ref[t], (place(dev_ref)[0], 1)))
-        acc_ref[kind * HALF + row_ref[t]] += product(slots_ref, slot, tiles_ref, t)
+        kind = side(where_ref[tiles_ref.shape[0] + t], (place(dev_ref)[0], 1))
+        slot = jnp.where(kind == 2, 0, any_slot(where_ref[tiles_ref.shape[0] + t], (place(dev_ref)[0], 1)))
+        acc_ref[kind * HALF + where_ref[t]] += product(slots_ref, slot, tiles_ref, t)
     doubled = []
     for h in range(HALF):
         part_ref[h] = acc_ref[h] + acc_ref[HALF + h]
@@ -226,15 +230,15 @@
     moments_ref[...] = jnp.concatenate(packed, axis=0).T[:4]
 
 
-def rest_kernel(dev_ref, row_ref, col_ref, part_ref, a_ref, b_ref, tiles_ref, out_ref, slots_ref, acc_ref):
+def rest_kernel(dev_ref, where_ref, part_ref, a_ref, b_ref, tiles_ref, out_ref, slots_ref, acc_ref):
     spread(slots_ref, 0, a_ref[...])
     spread(slots_ref, 1, b_ref[...])
     acc_ref[...] = part_ref[...]
     for t in range(tiles_ref.shape[0]):
-        @pl.when(side(col_ref[t], (place(dev_ref)[0], 1)) == 2)
+        @pl.when(side(where_ref[tiles_ref.shape[0] + t], (place(dev_ref)[0], 1)) == 2)
         def _():
-            slot = any_slot(col_ref[t], (place(dev_ref)[0], 1)) - (N_X + len(SHARED)) * HALF
-            acc_ref[row_ref[t]] += product(slots_ref, slot, tiles_ref, t)
+            slot = any_slot(where_ref[tiles_ref.shape[0] + t], (place(dev_ref)[0], 1)) - (N_X + len(SHARED)) * HALF
+            acc_ref[where_ref[t]] += product(slots_ref, slot, tiles_ref, t)
     store(acc_ref, out_ref)
 
 
@@ -277,10 +281,11 @@
     region = lax.axis_index("region").astype(jnp.int32)
     device = (region * N_ROW + row_index)[None]
 
-    index = jax.ShapeDtypeStruct(tile_row.shape, jnp.int32)
-    packed, tile_row, tile_col = pl.pallas_call(
-        pack_kernel, out_shape=(shape(N_ROW, QS, D + TILE), index, index), in_specs=[HBM] * 4, out_specs=(VMEM, SMEM, SMEM),
+    index = jax.ShapeDtypeStruct((2 * tile_row.shape[0],), jnp.int32)
+    packed, where = pl.pallas_call(
+        pack_kernel, out_shape=(shape(N_ROW, QS, D + TILE), index), in_specs=[HBM] * 4, out_specs=(VMEM, SMEM),
         scratch_shapes=[pltpu.VMEM(queries.shape, F32), pltpu.VMEM(cluster_perm.shape, jnp.int32),
+                        pltpu.SMEM(tile_row.shape, jnp.int32), pltpu.SMEM(tile_col.shape, jnp.int32),
                         pltpu.SemaphoreType.DMA((4,))],
         compiler_params=pltpu.CompilerParams(vmem_limit_bytes=64 * 1024 * 1024), name="pack",
     )(queries, cluster_perm, tile_row, tile_col)
@@ -333,38 +338,38 @@
     acc = pltpu.VMEM((HALF, Q, TILE), F32)
     low, high = region_pair(v0)
     inner = pl.pallas_call(
-        inner_kernel, out_shape=shape(HALF, Q, TILE), in_specs=[SMEM] * 3 + [VMEM] * 2, out_specs=VMEM,
+        inner_kernel, out_shape=shape(HALF, Q, TILE), in_specs=[SMEM] * 2 + [VMEM] * 2, out_specs=VMEM,
         scratch_shapes=[pltpu.VMEM((len(HOPS) * HALF, Q, TILE), F32)],
         cost_estimate=pl.CostEstimate(flops=2 * 12 * Q * TILE * TILE, bytes_accessed=2000000, transcendentals=0),
         compiler_params=PARAMS, name="first_inner",
-    )(device, tile_row, tile_col, near.reshape(N_ROW * width, TILE), tile_vals)
+    )(device, where, near.reshape(N_ROW * width, TILE), tile_vals)
     with_copies = (shape(Q, ROWS), shape(N_X, Q, ROWS))
     v1, copies = pl.pallas_call(
-        outer_kernel, out_shape=with_copies, in_specs=[SMEM] * 2 + [VMEM] * 4, out_specs=(VMEM, VMEM),
+        outer_kernel, out_shape=with_copies, in_specs=[SMEM] + [VMEM] * 4, out_specs=(VMEM, VMEM),
         scratch_shapes=[pltpu.VMEM((2 * HALF, Q, TILE), F32), acc], compiler_params=PARAMS, name="first_outer",
-    )(tile_row, tile_col, inner, low, high, tile_vals)
+    )(where, inner, low, high, tile_vals)
     line, low, high, got = fetch(v1, copies)
     v2, copies = pl.pallas_call(
-        next_kernel, out_shape=with_copies, in_specs=[SMEM] * 3 + [VMEM] * (N_BLOCKS + 1), out_specs=(VMEM, VMEM),
+        next_kernel, out_shape=with_copies, in_specs=[SMEM] * 2 + [VMEM] * (N_BLOCKS + 1), out_specs=(VMEM, VMEM),
         scratch_shapes=[slots, acc], compiler_params=PARAMS, name="second",
-    )(device, tile_row, tile_col, v1, line, *got, swap(got), low, high, tile_vals)
+    )(device, where, v1, line, *got, swap(got), low, high, tile_vals)
     low, high = region_pair(v2)
     ahead = [lax.ppermute(v2, "row", ring(N_ROW, -hop)) for hop in SHARED]
     part, moments = pl.pallas_call(
-        half_kernel, out_shape=(shape(HALF, Q, TILE), shape(4, TILE)), in_specs=[SMEM] * 3 + [VMEM] * 9,
+        half_kernel, out_shape=(shape(HALF, Q, TILE), shape(4, TILE)), in_specs=[SMEM] * 2 + [VMEM] * 9,
         out_specs=(VMEM, VMEM), scratch_shapes=[slots, pltpu.VMEM((3 * HALF, Q, TILE), F32)],
         compiler_params=PARAMS, name="half",
-    )(device, tile_row, tile_col, v2, x_line(copies), low, high, *ahead, v0, v1, tile_vals)
+    )(device, where, v2, x_line(copies), low, high, *ahead, v0, v1, tile_vals)
     later, moments = lax.optimization_barrier((v2, moments))
     behind = [lax.ppermute(later, "row", ring(N_ROW, hop)) for hop in SHARED]
     moments = lax.all_to_all(jnp.broadcast_to(moments[None], (N_ROW, 4, TILE)), "row", 0, 0, tiled=True)
     moments = jnp.sum(moments.reshape(2, 2, 2, 2, 2, 4, TILE).sum(0).sum(0).sum(0).sum(0), axis=0)
     v3 = pl.pallas_call(
-        rest_kernel, out_shape=shape(Q, ROWS), in_specs=[SMEM] * 3 + [VMEM] * 4, out_specs=VMEM,
+        rest_kernel, out_shape=shape(Q, ROWS), in_specs=[SMEM] * 2 + [VMEM] * 4, out_specs=VMEM,
         scratch_shapes=[pltpu.VMEM((2 * HALF, Q, TILE), F32), acc],
         cost_estimate=pl.CostEstimate(flops=2 * 12 * Q * TILE * TILE, bytes_accessed=2000000, transcendentals=0),
         compiler_params=PARAMS, name="rest",
-    )(device, tile_row, tile_col, part, *behind, tile_vals)
+    )(device, where, part, *behind, tile_vals)
     moments = lax.all_to_all(jnp.broadcast_to(moments[None], (N_REGION, 4, TILE)), "region", 0, 0, tiled=True)
     diffused, residual = pl.pallas_call(
         finish_kernel, out_shape=(shape(Q, ROWS), shape(Q, ROWS)), in_specs=[VMEM] * 5, out_specs=(VMEM, VMEM),

time: 148 us -> 148 us (level)
  no operation moved by 1% of the time
where the time goes in v13:
time: 148 us; the launch traced here: 147 us
  starting transfers between devices  73.9 us (50%)
  blocking collectives  28.8 us (19%)
  waiting for transfers between devices  28.3 us (19%)
  Pallas kernels  13.3 us (9%)
  local copies, waits for them, and re-layouts  2.14 us (1%)
    all_to_all x1, blocking collectives, local(): lax.all_to_all(near.reshape(N_ROW, width, TILE), 'row', 0, 0, tiled=True)  15.5 us
    ppermute x3, starting transfers between devices, region_pair(): lax.ppermute(v, 'region', ring(N_REGION, -1))  13.3 us
    all_to_all x1, blocking collectives, local(): lax.all_to_all(by_query.reshape(N_ROW, QS * HALF, TILE), 'row', 0, 0, til...  13.3 us
    all_to_all x1, starting transfers between devices, local(): lax.all_to_all(packed, 'row', 0, 0, tiled=True).reshape(Q, D + TILE)  10.6 us
    all_to_all x1, waiting for transfers between devices, local(): lax.all_to_all(packed, 'row', 0, 0, tiled=True).reshape(Q, D + TILE)  9.34 us
    ppermute x2, starting transfers between devices, local(): behind = [lax.ppermute(later, 'row', ring(N_ROW, hop)) for hop in SHARED]  9.24 us
    ppermute x2, starting transfers between devices, local(): ahead = [lax.ppermute(v2, 'row', ring(N_ROW, -hop)) for hop in SHARED]  8.3 us
    ppermute x2, waiting for transfers between devices, fetch(): got.append(lax.ppermute(both, ('region', 'row'), pairs))  8.18 us
  transfers between devices with their start and end apart: 18, of which 7 were waited for; matrix products, arithmetic and copies ran while one was open for 0% of the time, Pallas kernels for 2%

profile of v13, /device:TPU:1, one launch (start us, length us, event | category | flops | bytes accessed | tf_op | source)
XLA Modules:
  0.0 147.4 jit_solution(5284949484779166117)
XLA Ops:
  0.6 1.5 %pack.1 = (f32[32,2,640]{2,1,0:T(2,128)}, s32[24]{0:T(128)}) custom-call(f32[2,512]{1,0:T(2,128)} %queries_hbm.1, s32[1,256]{1,0:T(1,128)} %perm_hbm.1, s32[12]{0:T(128)} %row_hbm.1, s32[12]{0:T(128)} %col_hbm.1), custom_call_target="tpu_custom_call" | custom-call | tf_op jit(solution)/shard_map/pack/pallas_call | solution.py:285
  2.2 0.0 copy-start.1
  2.2 10.6 %all-to-all-start = ((f32[32,2,640]{2,1,0:T(2,128)}), f32[32,2,640]{2,1,0:T(2,128)S(1)}, u32[]{:S(2)}, u32[]{:S(2)}) async-start(f32[32,2,640]{2,1,0:T(2,128)} %get-tuple-element.16), calls=%async_computation | async-start | bytes 327680 | tf_op jit(solution)/shard_map/all_to_all | solution.py:292
  12.8 0.0 copy-start.2
  12.9 9.3 %all-to-all-done = f32[32,2,640]{2,1,0:T(2,128)S(1)} async-done(((f32[32,2,640]{2,1,0:T(2,128)}), f32[32,2,640]{2,1,0:T(2,128)S(1)}, u32[]{:S(2)}, u32[]{:S(2)}) %all-to-all-start) | async-done | bytes 163872 | tf_op jit(solution)/shard_map/all_to_all | solution.py:292
  22.2 0.1 reshape.28.packed_ref
  22.3 0.6 scores.1
  23.0 13.3 %all_to_all.35 = f32[32,4,128]{2,1,0:T(4,128)S(1)} all-to-all(f32[32,4,128]{2,1,0:T(4,128)S(1)} %bitcast.20), channel_id=1, replica_groups=mesh['region'=16,'row'=32] {'row'}, dimensions={0} | all-to-all | bytes 131072 | tf_op jit(solution)/shard_map/all_to_all | solution.py:297
  36.3 2.2 %permute.1 = f32[1024,128]{1,0:T(8,128)S(1)} custom-call(f32[128,128]{1,0:T(8,128)S(1)} %bitcast.19, f32[64,640]{1,0:T(8,128)S(1)} %reshape.28.packed_ref), custom_call_target="tpu_custom_call" | custom-call | tf_op jit(solution)/shard_map/permute/pallas_call | solution.py:299
  38.5 0.0 copy-start
  38.5 15.5 %all_to_all.36 = f32[32,32,128]{2,1,0:T(8,128)S(1)} all-to-all(f32[32,32,128]{2,1,0:T(8,128)S(1)} %bitcast.14), channel_id=1, replica_groups=mesh['region'=16,'row'=32] {'row'}, dimensions={0} | all-to-all | bytes 1048576 | tf_op jit(solution)/shard_map/all_to_all | solution.py:304
  54.1 0.1 copy.17
  54.2 5.4 %collective-permute-start.1 = (f32[64,256]{1,0:T(8,128)S(1)}, f32[64,256]{1,0:T(8,128)S(1)}, u32[]{:S(2)}, u32[]{:S(2)}) collective-permute-start(f32[64,256]{1,0:T(8,128)S(1)} %bitcast.15), channel_id=1, source_target_pairs={{0,480},{32,0},{64,32},{96,64},{128,96},{160,128},{192,160},{224,1... | collective-permute-start | bytes 196616 | tf_op jit(solution)/shard_map/ppermute | solution.py:308
  59.5 2.0 %collective-permute-start = (f32[64,256]{1,0:T(8,128)S(1)}, f32[64,256]{1,0:T(8,128)S(1)}, u32[]{:S(2)}, u32[]{:S(2)}) collective-permute-start(f32[64,256]{1,0:T(8,128)S(1)} %bitcast.16), channel_id=1, source_target_pairs={{0,32},{32,64},{64,96},{96,128},{128,160},{160,192},{192,224},{224... | collective-permute-start | bytes 196616 | tf_op jit(solution)/shard_map/ppermute | solution.py:308
  61.5 0.7 copy-done.3
  62.2 1.4 first_inner.1.inner_ref
  63.6 0.0 collective-permute-done.1.high_ref
  63.6 0.5 collective-permute-done.low_ref
  64.1 1.7 %first_outer.1 = (f32[64,256]{1,0:T(8,128)S(1)}, f32[4,64,256]{2,1,0:T(8,128)}) custom-call(s32[24]{0:T(128)S(1)} %copy-done.3, f32[2,64,128]{2,1,0:T(8,128)S(1)} %first_inner.1.inner_ref, f32[64,256]{1,0:T(8,128)S(1)} %collective-permute-done.low_ref, f32[64,256]{1,0:T(8,128)S(1)} %collective-permute-done.1.high_ref, f32[12,128,128]{2,1,0:T(8,128)S(1)} %copy-done), custom_call_target="tpu_custom_call" | custom-call | tf_op jit(solution)/shard_map/first_outer/pallas_call | solution.py:347
  65.8 6.5 %collective-permute-start.3 = (f32[64,256]{1,0:T(8,128)S(1)}, f32[64,256]{1,0:T(8,128)S(1)}, u32[]{:S(2)}, u32[]{:S(2)}) collective-permute-start(f32[64,256]{1,0:T(8,128)S(1)} %get-tuple-element.17.own_ref.refs_0_.v1_ref), channel_id=1, source_target_pairs={{0,480},{32,0},{64,32},{96,64},{128,96},{160,128},{192,160},{224,1... | collective-permute-start | bytes 196616 | tf_op jit(solution)/shard_map/ppermute | solution.py:308
  72.3 0.0 collective-permute-start.2
  72.3 3.4 %all-to-all-start.3 = ((f32[4,64,256]{2,1,0:T(8,128)}), f32[4,64,256]{2,1,0:T(8,128)S(1)}, u32[]{:S(2)}, u32[]{:S(2)}) async-start(f32[4,64,256]{2,1,0:T(8,128)} %get-tuple-element.18), calls=%async_computation.3 | async-start | bytes 524288 | tf_op jit(solution)/shard_map/all_to_all | solution.py:311
  75.7 0.0 collective-permute-done.3.high_ref.refs_6_
  75.8 5.0 %collective-permute-start.5 = (f32[2,64,256]{2,1,0:T(8,128)S(1)}, f32[2,64,256]{2,1,0:T(8,128)S(1)}, u32[]{:S(2)}, u32[]{:S(2)}) collective-permute-start(f32[2,64,256]{2,1,0:T(8,128)S(1)} %pair.1), channel_id=1, source_target_pairs={{0,29},{1,30},{2,31},{3,0},{4,1},{5,2},{6,3},{7,4},{8,5},{9,6},{10... | collective-permute-start | bytes 393224 | tf_op jit(solution)/shard_map/ppermute | solution.py:326
  80.8 2.0 %collective-permute-start.4 = (f32[2,64,256]{2,1,0:T(8,128)S(1)}, f32[2,64,256]{2,1,0:T(8,128)S(1)}, u32[]{:S(2)}, u32[]{:S(2)}) collective-permute-start(f32[2,64,256]{2,1,0:T(8,128)S(1)} %pair.1), channel_id=1, source_target_pairs={{0,31},{1,0},{2,1},{3,2},{4,3},{5,4},{6,5},{7,6},{8,7},{9,8},{10,9... | collective-permute-start | bytes 393224 | tf_op jit(solution)/shard_map/ppermute | solution.py:326
  82.7 0.0 all-to-all-done.3.refs_1_
  82.8 5.4 %collective-permute-done.5.refs_1_.refs_3_ = f32[2,64,256]{2,1,0:T(8,128)S(1)} collective-permute-done((f32[2,64,256]{2,1,0:T(8,128)S(1)}, f32[2,64,256]{2,1,0:T(8,128)S(1)}, u32[]{:S(2)}, u32[]{:S(2)}) %collective-permute-start.5) | collective-permute-done | bytes 131104 | tf_op jit(solution)/shard_map/ppermute | solution.py:326
  88.1 2.8 %collective-permute-done.4.refs_0_.refs_2_ = f32[2,64,256]{2,1,0:T(8,128)S(1)} collective-permute-done((f32[2,64,256]{2,1,0:T(8,128)S(1)}, f32[2,64,256]{2,1,0:T(8,128)S(1)}, u32[]{:S(2)}, u32[]{:S(2)}) %collective-permute-start.4) | collective-permute-done | bytes 131104 | tf_op jit(solution)/shard_map/ppermute | solution.py:326
  91.0 1.9 %collective-permute-start.6 = (f32[2,64,256]{2,1,0:T(8,128)S(1)}, f32[2,64,256]{2,1,0:T(8,128)S(1)}, u32[]{:S(2)}, u32[]{:S(2)}) collective-permute-start(f32[2,64,256]{2,1,0:T(8,128)S(1)} %swap.1), channel_id=1, source_target_pairs={{0,32},{32,0},{64,96},{96,64},{128,160},{160,128},{192,224},{224,1... | collective-permute-start | bytes 393224 | tf_op jit(solution)/shard_map/ppermute | solution.py:335
  92.9 1.3 collective-permute-done.6.refs_4_
  94.2 1.9 %second.1 = (f32[64,256]{1,0:T(8,128)S(1)}, f32[4,64,256]{2,1,0:T(8,128)}) custom-call(s32[1]{0:T(128)} %bitcast.dev_ref, s32[24]{0:T(128)S(1)} %copy-done.3, f32[64,256]{1,0:T(8,128)S(1)} %get-tuple-element.17.own_ref.refs_0_.v1_ref, f32[4,64,256]{2,1,0:T(8,128)S(1)} %all-to-all-done.3.refs_1_, f32[2,64,256]{2,1,0:T(8,128)S(1)} %collective-permute-done.4.refs_0_.refs_2_, ...), custom_call_target="tpu_custom_call" | custom-call | tf_op jit(solution)/shard_map/second/pallas_call | solution.py:352
  96.1 3.4 %all-to-all-start.4 = ((f32[4,64,256]{2,1,0:T(8,128)}), f32[4,64,256]{2,1,0:T(8,128)S(1)}, u32[]{:S(2)}, u32[]{:S(2)}) async-start(f32[4,64,256]{2,1,0:T(8,128)} %get-tuple-element.23), calls=%async_computation.4 | async-start | bytes 524288 | tf_op jit(solution)/shard_map/all_to_all | solution.py:311
  99.5 5.2 %collective-permute-start.10 = (f32[64,256]{1,0:T(8,128)S(1)}, f32[64,256]{1,0:T(8,128)S(1)}, u32[]{:S(2)}, u32[]{:S(2)}) collective-permute-start(f32[64,256]{1,0:T(8,128)S(1)} %get-tuple-element.27.v2_ref), channel_id=1, source_target_pairs={{0,29},{1,30},{2,31},{3,0},{4,1},{5,2},{6,3},{7,4},{8,5},{9,6},{10... | collective-permute-start | bytes 196616 | tf_op jit(solution)/shard_map/ppermute | solution.py:357
  104.7 3.1 %collective-permute-start.9 = (f32[64,256]{1,0:T(8,128)S(1)}, f32[64,256]{1,0:T(8,128)S(1)}, u32[]{:S(2)}, u32[]{:S(2)}) collective-permute-start(f32[64,256]{1,0:T(8,128)S(1)} %get-tuple-element.27.v2_ref), channel_id=1, source_target_pairs={{0,31},{1,0},{2,1},{3,2},{4,3},{5,4},{6,5},{7,6},{8,7},{9,8},{10,9... | collective-permute-start | bytes 196616 | tf_op jit(solution)/shard_map/ppermute | solution.py:357
  107.8 1.4 collective-permute-start.8
  109.3 0.3 collective-permute-start.7
  109.6 2.6 %collective-permute-done.9.a_ref = f32[64,256]{1,0:T(8,128)S(1)} collective-permute-done((f32[64,256]{1,0:T(8,128)S(1)}, f32[64,256]{1,0:T(8,128)S(1)}, u32[]{:S(2)}, u32[]{:S(2)}) %collective-permute-start.9) | collective-permute-done | bytes 65568 | tf_op jit(solution)/shard_map/ppermute | solution.py:357
  112.2 0.0 collective-permute-done.7.low_ref
  112.2 1.3 half.1
  113.5 0.7 broadcast_in_dim.7
  114.1 6.4 %all-to-all-start.5 = ((f32[32,4,128]{2,1,0:T(4,128)}), f32[32,4,128]{2,1,0:T(4,128)S(1)}, u32[]{:S(2)}, u32[]{:S(2)}) async-start(f32[32,4,128]{2,1,0:T(4,128)} %broadcast_in_dim.7), calls=%async_computation.5 | async-start | bytes 131072 | tf_op jit(solution)/shard_map/all_to_all | solution.py:365
  120.6 4.9 %collective-permute-start.12 = (f32[64,256]{1,0:T(8,128)S(1)}, f32[64,256]{1,0:T(8,128)S(1)}, u32[]{:S(2)}, u32[]{:S(2)}) collective-permute-start(f32[64,256]{1,0:T(8,128)S(1)} %get-tuple-element.27.v2_ref), channel_id=1, source_target_pairs={{0,3},{1,4},{2,5},{3,6},{4,7},{5,8},{6,9},{7,10},{8,11},{9,12},{10... | collective-permute-start | bytes 196616 | tf_op jit(solution)/shard_map/ppermute | solution.py:364
  125.5 4.3 %collective-permute-start.11 = (f32[64,256]{1,0:T(8,128)S(1)}, f32[64,256]{1,0:T(8,128)S(1)}, u32[]{:S(2)}, u32[]{:S(2)}) collective-permute-start(f32[64,256]{1,0:T(8,128)S(1)} %get-tuple-element.27.v2_ref), channel_id=1, source_target_pairs={{0,1},{1,2},{2,3},{3,4},{4,5},{5,6},{6,7},{7,8},{8,9},{9,10},{10,1... | collective-permute-start | bytes 196616 | tf_op jit(solution)/shard_map/ppermute | solution.py:364
  129.9 0.6 broadcast_in_dim.8
  130.5 8.0 %all-to-all-start.6 = ((f32[16,4,128]{2,1,0:T(4,128)}), f32[16,4,128]{2,1,0:T(4,128)S(1)}, u32[]{:S(2)}, u32[]{:S(2)}) async-start(f32[16,4,128]{2,1,0:T(4,128)} %broadcast_in_dim.8), calls=%async_computation.6 | async-start | bytes 65536 | tf_op jit(solution)/shard_map/all_to_all | solution.py:373
  138.5 1.0 rest.1.v3_ref
  139.5 6.3 %all-to-all-done.6.moments_ref = f32[16,4,128]{2,1,0:T(4,128)S(1)} async-done(((f32[16,4,128]{2,1,0:T(4,128)}), f32[16,4,128]{2,1,0:T(4,128)S(1)}, u32[]{:S(2)}, u32[]{:S(2)}) %all-to-all-start.6) | async-done | bytes 32800 | tf_op jit(solution)/shard_map/all_to_all | solution.py:373
  145.8 1.5 %finish.1 = (f32[64,256]{1,0:T(8,128)}, f32[64,256]{1,0:T(8,128)}) custom-call(f32[16,4,128]{2,1,0:T(4,128)S(1)} %all-to-all-done.6.moments_ref, f32[64,256]{1,0:T(8,128)S(1)} %bitcast.18, f32[64,256]{1,0:T(8,128)S(1)} %get-tuple-element.17.own_ref.refs_0_.v1_ref, f32[64,256]{1,0:T(8,128)S(1)} %get-tuple-element.27.v2_ref, f32[64,256]{1,0:T(8,128)S(1)} %rest.1.v3_ref), custom_call_target="tpu_custom_call" | custom-call | tf_op jit(solution)/shard_map/finish/pallas_call | solution.py:374
  (17 shorter events, 0.1 us)
Async XLA Ops:
  2.2 20.1 %copy-start.1 = (f32[256,512]{1,0:T(8,128)S(1)}, f32[256,512]{1,0:T(8,128)}, u32[]{:S(2)}) copy-start(f32[256,512]{1,0:T(8,128)} %desc_ref.1) | copy-start | bytes 1572868
  2.2 20.0 %all-to-all-start = ((f32[32,2,640]{2,1,0:T(2,128)}), f32[32,2,640]{2,1,0:T(2,128)S(1)}, u32[]{:S(2)}, u32[]{:S(2)}) async-start(f32[32,2,640]{2,1,0:T(2,128)} %get-tuple-element.16), calls=%async_computation | async-start | bytes 327680 | tf_op jit(solution)/shard_map/all_to_all | solution.py:292
  12.8 9.5 %copy-start.2 = (s32[64,64]{1,0:T(8,128)S(1)}, s32[64,64]{1,0:T(8,128)}, u32[]{:S(2)}) copy-start(s32[64,64]{1,0:T(8,128)} %cand_ref.1) | copy-start | bytes 49156
  38.5 23.0 %copy-start = (f32[12,128,128]{2,1,0:T(8,128)S(1)}, f32[12,128,128]{2,1,0:T(8,128)}, u32[]{:S(2)}) copy-start(f32[12,128,128]{2,1,0:T(8,128)} %tiles_ref.7) | copy-start | bytes 2359300
  54.2 9.5 %collective-permute-start.1 = (f32[64,256]{1,0:T(8,128)S(1)}, f32[64,256]{1,0:T(8,128)S(1)}, u32[]{:S(2)}, u32[]{:S(2)}) collective-permute-start(f32[64,256]{1,0:T(8,128)S(1)} %bitcast.15), channel_id=1, source_target_pairs={{0,480},{32,0},{64,32},{96,64},{128,96},{160,128},{192,160},{224,1... | collective-permute-start | bytes 196616 | tf_op jit(solution)/shard_map/ppermute | solution.py:308
  59.5 4.6 %collective-permute-start = (f32[64,256]{1,0:T(8,128)S(1)}, f32[64,256]{1,0:T(8,128)S(1)}, u32[]{:S(2)}, u32[]{:S(2)}) collective-permute-start(f32[64,256]{1,0:T(8,128)S(1)} %bitcast.16), channel_id=1, source_target_pairs={{0,32},{32,64},{64,96},{96,128},{128,160},{160,192},{192,224},{224... | collective-permute-start | bytes 196616 | tf_op jit(solution)/shard_map/ppermute | solution.py:308
  61.5 0.7 copy-start.3
  65.8 10.0 %collective-permute-start.3 = (f32[64,256]{1,0:T(8,128)S(1)}, f32[64,256]{1,0:T(8,128)S(1)}, u32[]{:S(2)}, u32[]{:S(2)}) collective-permute-start(f32[64,256]{1,0:T(8,128)S(1)} %get-tuple-element.17.own_ref.refs_0_.v1_ref), channel_id=1, source_target_pairs={{0,480},{32,0},{64,32},{96,64},{128,96},{160,128},{192,160},{224,1... | collective-permute-start | bytes 196616 | tf_op jit(solution)/shard_map/ppermute | solution.py:308
  72.3 3.4 %collective-permute-start.2 = (f32[64,256]{1,0:T(8,128)S(1)}, f32[64,256]{1,0:T(8,128)S(1)}, u32[]{:S(2)}, u32[]{:S(2)}) collective-permute-start(f32[64,256]{1,0:T(8,128)S(1)} %get-tuple-element.17.own_ref.refs_0_.v1_ref), channel_id=1, source_target_pairs={{0,32},{32,64},{64,96},{96,128},{128,160},{160,192},{192,224},{224... | collective-permute-start | bytes 196616 | tf_op jit(solution)/shard_map/ppermute | solution.py:308
  72.3 10.4 %all-to-all-start.3 = ((f32[4,64,256]{2,1,0:T(8,128)}), f32[4,64,256]{2,1,0:T(8,128)S(1)}, u32[]{:S(2)}, u32[]{:S(2)}) async-start(f32[4,64,256]{2,1,0:T(8,128)} %get-tuple-element.18), calls=%async_computation.3 | async-start | bytes 524288 | tf_op jit(solution)/shard_map/all_to_all | solution.py:311
  75.8 12.3 %collective-permute-start.5 = (f32[2,64,256]{2,1,0:T(8,128)S(1)}, f32[2,64,256]{2,1,0:T(8,128)S(1)}, u32[]{:S(2)}, u32[]{:S(2)}) collective-permute-start(f32[2,64,256]{2,1,0:T(8,128)S(1)} %pair.1), channel_id=1, source_target_pairs={{0,29},{1,30},{2,31},{3,0},{4,1},{5,2},{6,3},{7,4},{8,5},{9,6},{10... | collective-permute-start | bytes 393224 | tf_op jit(solution)/shard_map/ppermute | solution.py:326
  80.8 10.2 %collective-permute-start.4 = (f32[2,64,256]{2,1,0:T(8,128)S(1)}, f32[2,64,256]{2,1,0:T(8,128)S(1)}, u32[]{:S(2)}, u32[]{:S(2)}) collective-permute-start(f32[2,64,256]{2,1,0:T(8,128)S(1)} %pair.1), channel_id=1, source_target_pairs={{0,31},{1,0},{2,1},{3,2},{4,3},{5,4},{6,5},{7,6},{8,7},{9,8},{10,9... | collective-permute-start | bytes 393224 | tf_op jit(solution)/shard_map/ppermute | solution.py:326
  91.0 3.2 %collective-permute-start.6 = (f32[2,64,256]{2,1,0:T(8,128)S(1)}, f32[2,64,256]{2,1,0:T(8,128)S(1)}, u32[]{:S(2)}, u32[]{:S(2)}) collective-permute-start(f32[2,64,256]{2,1,0:T(8,128)S(1)} %swap.1), channel_id=1, source_target_pairs={{0,32},{32,0},{64,96},{96,64},{128,160},{160,128},{192,224},{224,1... | collective-permute-start | bytes 393224 | tf_op jit(solution)/shard_map/ppermute | solution.py:335
  96.1 16.1 %all-to-all-start.4 = ((f32[4,64,256]{2,1,0:T(8,128)}), f32[4,64,256]{2,1,0:T(8,128)S(1)}, u32[]{:S(2)}, u32[]{:S(2)}) async-start(f32[4,64,256]{2,1,0:T(8,128)} %get-tuple-element.23), calls=%async_computation.4 | async-start | bytes 524288 | tf_op jit(solution)/shard_map/all_to_all | solution.py:311
  99.5 10.1 %collective-permute-start.10 = (f32[64,256]{1,0:T(8,128)S(1)}, f32[64,256]{1,0:T(8,128)S(1)}, u32[]{:S(2)}, u32[]{:S(2)}) collective-permute-start(f32[64,256]{1,0:T(8,128)S(1)} %get-tuple-element.27.v2_ref), channel_id=1, source_target_pairs={{0,29},{1,30},{2,31},{3,0},{4,1},{5,2},{6,3},{7,4},{8,5},{9,6},{10... | collective-permute-start | bytes 196616 | tf_op jit(solution)/shard_map/ppermute | solution.py:357
  104.7 7.4 %collective-permute-start.9 = (f32[64,256]{1,0:T(8,128)S(1)}, f32[64,256]{1,0:T(8,128)S(1)}, u32[]{:S(2)}, u32[]{:S(2)}) collective-permute-start(f32[64,256]{1,0:T(8,128)S(1)} %get-tuple-element.27.v2_ref), channel_id=1, source_target_pairs={{0,31},{1,0},{2,1},{3,2},{4,3},{5,4},{6,5},{7,6},{8,7},{9,8},{10,9... | collective-permute-start | bytes 196616 | tf_op jit(solution)/shard_map/ppermute | solution.py:357
  107.8 4.4 %collective-permute-start.8 = (f32[64,256]{1,0:T(8,128)S(1)}, f32[64,256]{1,0:T(8,128)S(1)}, u32[]{:S(2)}, u32[]{:S(2)}) collective-permute-start(f32[64,256]{1,0:T(8,128)S(1)} %get-tuple-element.27.v2_ref), channel_id=1, source_target_pairs={{0,480},{32,0},{64,32},{96,64},{128,96},{160,128},{192,160},{224,1... | collective-permute-start | bytes 196616 | tf_op jit(solution)/shard_map/ppermute | solution.py:308
  109.3 2.9 %collective-permute-start.7 = (f32[64,256]{1,0:T(8,128)S(1)}, f32[64,256]{1,0:T(8,128)S(1)}, u32[]{:S(2)}, u32[]{:S(2)}) collective-permute-start(f32[64,256]{1,0:T(8,128)S(1)} %get-tuple-element.27.v2_ref), channel_id=1, source_target_pairs={{0,32},{32,64},{64,96},{96,128},{128,160},{160,192},{192,224},{224... | collective-permute-start | bytes 196616 | tf_op jit(solution)/shard_map/ppermute | solution.py:308
  114.1 15.7 %all-to-all-start.5 = ((f32[32,4,128]{2,1,0:T(4,128)}), f32[32,4,128]{2,1,0:T(4,128)S(1)}, u32[]{:S(2)}, u32[]{:S(2)}) async-start(f32[32,4,128]{2,1,0:T(4,128)} %broadcast_in_dim.7), calls=%async_computation.5 | async-start | bytes 131072 | tf_op jit(solution)/shard_map/all_to_all | solution.py:365
  120.6 17.9 %collective-permute-start.12 = (f32[64,256]{1,0:T(8,128)S(1)}, f32[64,256]{1,0:T(8,128)S(1)}, u32[]{:S(2)}, u32[]{:S(2)}) collective-permute-start(f32[64,256]{1,0:T(8,128)S(1)} %get-tuple-element.27.v2_ref), channel_id=1, source_target_pairs={{0,3},{1,4},{2,5},{3,6},{4,7},{5,8},{6,9},{7,10},{8,11},{9,12},{10... | collective-permute-start | bytes 196616 | tf_op jit(solution)/shard_map/ppermute | solution.py:364
  125.5 13.0 %collective-permute-start.11 = (f32[64,256]{1,0:T(8,128)S(1)}, f32[64,256]{1,0:T(8,128)S(1)}, u32[]{:S(2)}, u32[]{:S(2)}) collective-permute-start(f32[64,256]{1,0:T(8,128)S(1)} %get-tuple-element.27.v2_ref), channel_id=1, source_target_pairs={{0,1},{1,2},{2,3},{3,4},{4,5},{5,6},{6,7},{7,8},{8,9},{9,10},{10,1... | collective-permute-start | bytes 196616 | tf_op jit(solution)/shard_map/ppermute | solution.py:364
  130.5 15.3 %all-to-all-start.6 = ((f32[16,4,128]{2,1,0:T(4,128)}), f32[16,4,128]{2,1,0:T(4,128)S(1)}, u32[]{:S(2)}, u32[]{:S(2)}) async-start(f32[16,4,128]{2,1,0:T(4,128)} %broadcast_in_dim.8), calls=%async_computation.6 | async-start | bytes 65536 | tf_op jit(solution)/shard_map/all_to_all | solution.py:373
